TPU v7x, 128 devices: a whole 4x4x4 slice. The times are simulated.
128 devices in a mesh: pts: 64 (over x, y, z), grp: 2 (over core).
Axes of the slice: x: 4, y: 4, z: 4, core: 2. Of those that a mesh axis runs over, the one named last changes fastest.
Arguments:
- points: bfloat16 [65536, 256], P(('pts', 'grp')), may hold values from -56 to 56
- rotated_place: int32 [65536], P(('pts', 'grp')), may hold values from 0 to 65535, as said below
- rotated_source: int32 [65536], P(('pts', 'grp')), may hold values from 0 to 65535, as said below
- ball_counts: int32 [256], replicated, may hold values from 64 to 256
- fine_projection: bfloat16 [256, 768], replicated, may hold values from -12 to 12
- fine_output: bfloat16 [256, 256], replicated, may hold values from -0.375 to 0.375
- pool_weight: bfloat16 [512, 512], replicated, may hold values from -0.25 to 0.25
- coarse_projection: bfloat16 [512, 1536], replicated, may hold values from -12 to 12
- coarse_output: bfloat16 [512, 512], replicated, may hold values from -0.25 to 0.25
- coarse_cotangent: bfloat16 [32768, 512], P(('pts', 'grp')), may hold values from -6 to 6
Outputs:
- coarse_result: bfloat16 [32768, 512], P(('pts', 'grp'))
- points_gradient: bfloat16 [65536, 256], P(('pts', 'grp'))
- fine_projection_gradient: float32 [256, 768], replicated
- fine_output_gradient: float32 [256, 256], replicated
- pool_gradient: float32 [512, 512], replicated
- coarse_projection_gradient: float32 [512, 1536], replicated
- coarse_output_gradient: float32 [512, 512], replicated
Inputs may be any that keep to these rules, and one draw needn't show every extreme that they name: `rotated_place`: A permutation. Reading rows in blocks of 512, the tokens of one block that go to one block number at most 8, and every block sends exactly 8 to some block. `rotated_source`: the inverse permutation of rotated_place.
All inputs are finite; a program needn't handle non-finite values.
Results may differ from a plain program's by a relative error of at most 0.034.
The roundings to bfloat16 on the way count: a program that leaves them out, or rounds other values in their place, can miss the bound.
Values may be sent and summed in bfloat16 or wider, within the bound.
No kernel may reach another device: no remote copies, remote signals or barrier semaphores. Data moves between devices by JAX's collectives and lax.ppermute only.
A program may use at most 64 MiB of HBM per device.

v0:
```python
import math

import jax
import jax.numpy as jnp
from jax import lax
from jax.sharding import PartitionSpec as P

HD = 64
BALL = 256


epsilon = 1e-05


def normalize(values):
    floats = values.astype(jnp.float32)
    center = floats - jnp.mean(floats, axis=-1, keepdims=True)
    inverse = lax.rsqrt(jnp.mean(center * center, axis=-1, keepdims=True) + epsilon)
    return (center * inverse, inverse)


def norm_backward(incoming, normed, inverse):
    first_mean = jnp.mean(incoming, axis=-1, keepdims=True)
    second_mean = jnp.mean(incoming * normed, axis=-1, keepdims=True)
    return inverse * (incoming - first_mean - normed * second_mean)


def split_heads(blocked):
    row_count, features = blocked.shape
    return jnp.transpose(blocked.reshape(row_count, features // HD, HD), (1, 0, 2))


def merge_heads(blocked):
    head_count, row_count, head_size = blocked.shape
    return jnp.transpose(blocked, (1, 0, 2)).reshape(row_count, head_count * head_size)


def head_forward(query_rows, key_rows, value_rows, key_live):
    scores = jnp.dot(query_rows, key_rows.T, preferred_element_type=jnp.float32) * HD ** (-0.5)
    scores = jnp.where(key_live[None, :], scores, -1e30)
    highest = jnp.max(scores, axis=-1, keepdims=True)
    raised = jnp.exp(scores - highest)
    weights = (raised / jnp.sum(raised, axis=-1, keepdims=True)).astype(jnp.bfloat16)
    mixture = jnp.dot(weights, value_rows, preferred_element_type=jnp.float32).astype(jnp.bfloat16)
    return (mixture, weights)


def head_backward(query_rows, key_rows, value_rows, weights, incoming):
    against = jnp.dot(incoming, value_rows.T, preferred_element_type=jnp.float32)
    wide_weights = weights.astype(jnp.float32)
    diagonal = jnp.sum(wide_weights * against, axis=-1, keepdims=True)
    slopes = (wide_weights * (against - diagonal) * HD ** (-0.5)).astype(jnp.bfloat16)
    query_grad = jnp.dot(slopes, key_rows, preferred_element_type=jnp.float32)
    key_grad = jnp.dot(slopes.T, query_rows, preferred_element_type=jnp.float32)
    value_grad = jnp.dot(weights.T, incoming, preferred_element_type=jnp.float32)
    return (query_grad, key_grad, value_grad)


def attention(query_rows, key_rows, value_rows, key_live):

    def one_head(pieces):
        return head_forward(pieces[0], pieces[1], pieces[2], key_live)

    mixture, weights = lax.map(
        one_head, (split_heads(query_rows), split_heads(key_rows), split_heads(value_rows))
    )
    return (merge_heads(mixture), weights)


def attention_backward(query_rows, key_rows, value_rows, weights, incoming):

    def one_head(pieces):
        return head_backward(pieces[0], pieces[1], pieces[2], pieces[3], pieces[4])

    query_grad, key_grad, value_grad = lax.map(
        one_head,
        (
            split_heads(query_rows),
            split_heads(key_rows),
            split_heads(value_rows),
            weights,
            split_heads(incoming),
        ),
    )
    return (merge_heads(query_grad), merge_heads(key_grad), merge_heads(value_grad))


def fine_forward(rotated_balls, live_balls, projection, output):
    ball_total, ball_size, features = rotated_balls.shape
    normed, inverse = normalize(rotated_balls)
    unit_rows = normed.astype(jnp.bfloat16)
    projected = jnp.dot(
        unit_rows.reshape(ball_total * ball_size, features),
        projection,
        preferred_element_type=jnp.float32,
    )
    projected = projected.astype(jnp.bfloat16).reshape(ball_total, ball_size, 3 * features)

    def one_ball(pieces):
        rows_in = pieces[0]
        return attention(
            rows_in[:, :features],
            rows_in[:, features : 2 * features],
            rows_in[:, 2 * features :],
            pieces[1],
        )

    mixture, weights = lax.map(one_ball, (projected, live_balls))
    update = jnp.dot(
        mixture.reshape(ball_total * ball_size, features),
        output,
        preferred_element_type=jnp.float32,
    )
    result = (
        rotated_balls.astype(jnp.float32) + update.reshape(ball_total, ball_size, features)
    ).astype(jnp.bfloat16)
    return (result, (unit_rows, normed, inverse, projected, mixture, weights))


def fine_backward(stored, incoming, projection, output):
    unit_rows, normed, inverse, projected, mixture, weights = stored
    ball_total, ball_size, features = incoming.shape
    incoming_flat = incoming.reshape(ball_total * ball_size, features)
    output_term = jnp.dot(
        mixture.reshape(ball_total * ball_size, features).T,
        incoming_flat,
        preferred_element_type=jnp.float32,
    )
    mixed_grad = jnp.dot(incoming_flat, output.T, preferred_element_type=jnp.float32).astype(
        jnp.bfloat16
    )
    mixed_grad = mixed_grad.reshape(ball_total, ball_size, features)

    def one_ball(pieces):
        rows_in = pieces[0]
        query_grad, key_grad, value_grad = attention_backward(
            rows_in[:, :features],
            rows_in[:, features : 2 * features],
            rows_in[:, 2 * features :],
            pieces[1],
            pieces[2],
        )
        return jnp.concatenate([query_grad, key_grad, value_grad], axis=1).astype(jnp.bfloat16)

    grad_projected = lax.map(one_ball, (projected, weights, mixed_grad))
    grad_flat = grad_projected.reshape(ball_total * ball_size, 3 * features)
    projection_term = jnp.dot(
        unit_rows.reshape(ball_total * ball_size, features).T,
        grad_flat,
        preferred_element_type=jnp.float32,
    )
    spread_back = jnp.dot(grad_flat, projection.T, preferred_element_type=jnp.float32).reshape(
        ball_total, ball_size, features
    )
    grad_input = (
        incoming.astype(jnp.float32) + norm_backward(spread_back, normed, inverse)
    ).astype(jnp.bfloat16)
    return (grad_input, projection_term, output_term)


def run_rank(groups, ordering):
    same_run = (groups[:, None] == groups[None, :]) & (ordering[None, :] < ordering[:, None])
    return jnp.sum(same_run.astype(jnp.int32), axis=1)


def route_out(values):
    senders, capacity, features = values.shape
    arrived = lax.all_to_all(values, ("pts", "grp"), split_axis=0, concat_axis=0, tiled=True)
    return arrived.reshape(senders * capacity, features)


def route_back(values):
    senders, capacity, features = values.shape
    arrived = lax.all_to_all(values, ("pts", "grp"), split_axis=0, concat_axis=0, tiled=True)
    return arrived.reshape(senders * capacity, features)


def on_device(
    points,
    rotated_place,
    rotated_source,
    ball_counts,
    fine_projection,
    fine_output,
    pool_weight,
    coarse_projection,
    coarse_output,
    coarse_cotangent,
):
    row_count, features = points.shape
    devices = lax.axis_size(("pts", "grp"))
    capacity = 2 * row_count // devices
    scaling = 1.0 / math.sqrt(row_count * devices)
    positions = jnp.arange(row_count, dtype=jnp.int32)
    destination = rotated_place // row_count
    send_slot = destination * capacity + run_rank(destination, positions)
    source_device = rotated_source // row_count
    receive_slot = source_device * capacity + run_rank(source_device, rotated_source)
    ball_index = jnp.arange(ball_counts.shape[0], dtype=jnp.int32)
    filled = jnp.sum(
        jnp.where(
            (rotated_source // BALL)[:, None] == ball_index[None, :], ball_counts[None, :], 0
        ),
        axis=1,
    )
    live_rows = rotated_source % BALL < filled

    def to_owners(values):
        buffer = jnp.zeros((devices * capacity, features), jnp.bfloat16).at[send_slot].set(values)
        return route_out(buffer.reshape(devices, capacity, features))[receive_slot]

    def to_senders(values):
        buffer = (
            jnp.zeros((devices * capacity, features), jnp.bfloat16).at[receive_slot].set(values)
        )
        return route_back(buffer.reshape(devices, capacity, features))[send_slot]

    ball_total = row_count // BALL
    rotated = to_owners(points).reshape(ball_total, BALL, features)
    fine_rotated, stored = fine_forward(
        rotated, live_rows.reshape(ball_total, BALL), fine_projection, fine_output
    )
    fine_tree = to_senders(fine_rotated.reshape(row_count, features))
    joined = fine_tree.reshape(row_count // 2, 2 * features)
    coarse = jnp.dot(joined, pool_weight, preferred_element_type=jnp.float32).astype(jnp.bfloat16)
    wide = coarse.shape[1]
    normed, inverse = normalize(coarse)
    unit_rows = normed.astype(jnp.bfloat16)
    query_rows = jnp.dot(
        unit_rows, coarse_projection[:, :wide], preferred_element_type=jnp.float32
    ).astype(jnp.bfloat16)
    own_rows = jnp.dot(
        unit_rows, coarse_projection[:, wide:], preferred_element_type=jnp.float32
    ).astype(jnp.bfloat16)
    pair_rows = lax.all_gather(own_rows, "grp", axis=0, tiled=True)
    key_rows = pair_rows[:, :wide]
    value_rows = pair_rows[:, wide:]
    everyone = jnp.arange(pair_rows.shape[0]) >= 0
    mixture, weights = attention(query_rows, key_rows, value_rows, everyone)
    incoming = jnp.dot(
        coarse_cotangent, coarse_output.T, preferred_element_type=jnp.float32
    ).astype(jnp.bfloat16)
    query_grad, key_grad, value_grad = attention_backward(
        query_rows, key_rows, value_rows, weights, incoming
    )
    own_key_grad, own_value_grad = (
        lax.psum_scatter(
            key_grad.astype(jnp.bfloat16), "grp", scatter_dimension=0, tiled=True
        ).astype(jnp.float32),
        lax.psum_scatter(
            value_grad.astype(jnp.bfloat16), "grp", scatter_dimension=0, tiled=True
        ).astype(jnp.float32),
    )
    grad_projected = jnp.concatenate(
        [
            query_grad.astype(jnp.bfloat16),
            own_key_grad.astype(jnp.bfloat16),
            own_value_grad.astype(jnp.bfloat16),
        ],
        axis=1,
    )
    coarse_result = (
        coarse.astype(jnp.float32)
        + jnp.dot(mixture, coarse_output, preferred_element_type=jnp.float32)
    ).astype(jnp.bfloat16)
    spread_back = jnp.dot(grad_projected, coarse_projection.T, preferred_element_type=jnp.float32)
    coarse_grad = (
        coarse_cotangent.astype(jnp.float32) + norm_backward(spread_back, normed, inverse)
    ).astype(jnp.bfloat16)
    coarse_projection_term = (
        jnp.dot(unit_rows.T, grad_projected, preferred_element_type=jnp.float32) * scaling
    )
    coarse_output_term = (
        jnp.dot(mixture.T, coarse_cotangent, preferred_element_type=jnp.float32) * scaling
    )
    pool_term = jnp.dot(joined.T, coarse_grad, preferred_element_type=jnp.float32) * scaling
    fine_grad = (
        jnp.dot(coarse_grad, pool_weight.T, preferred_element_type=jnp.float32)
        .astype(jnp.bfloat16)
        .reshape(row_count, features)
    )
    grad_rotated = to_owners(fine_grad).reshape(ball_total, BALL, features)
    grad_back, fine_projection_term, fine_output_term = fine_backward(
        stored, grad_rotated, fine_projection, fine_output
    )
    points_gradient = to_senders(grad_back.reshape(row_count, features))
    fine_projection_sum, fine_output_sum, pool_sum, coarse_projection_sum, coarse_output_sum = (
        lax.psum(
            (
                fine_projection_term * scaling,
                fine_output_term * scaling,
                pool_term,
                coarse_projection_term,
                coarse_output_term,
            ),
            ("pts", "grp"),
        )
    )
    return (
        coarse_result,
        points_gradient,
        fine_projection_sum,
        fine_output_sum,
        pool_sum,
        coarse_projection_sum,
        coarse_output_sum,
    )


def solution(mesh):
    in_specs = (
        P(("pts", "grp"), None),
        P(("pts", "grp")),
        P(("pts", "grp")),
        P(),
        P(),
        P(),
        P(),
        P(),
        P(),
        P(("pts", "grp"), None),
    )
    out_specs = (P(("pts", "grp"), None), P(("pts", "grp"), None), P(), P(), P(), P(), P())
    return jax.shard_map(
        on_device, mesh=mesh, in_specs=in_specs, out_specs=out_specs, check_vma=False
    )
```

profile of v0, /device:TPU:1, one launch (start us, length us, event | category | flops | bytes accessed | tf_op | source)
XLA Modules:
  0.0 452.1 jit_solution(1309923759119752645)
XLA Ops:
  8.9 3.5 scatter_custom_fusion
  12.4 11.5 %all-to-all-start = ((bf16[128,8,256]{2,1,0:T(8,128)(2,1)}), bf16[128,8,256]{2,1,0:T(8,128)(2,1)S(1)}, u32[]{:S(2)}, u32[]{:S(2)}) async-start(bf16[128,8,256]{2,1,0:T(8,128)(2,1)} %bitcast.52), calls=%async_computation | async-start | bytes 1048576 | tf_op jit(solution)/shard_map/all_to_all | solution.py:168
  24.7 13.0 %all-to-all-done = bf16[128,8,256]{2,1,0:T(8,128)(2,1)S(1)} async-done(((bf16[128,8,256]{2,1,0:T(8,128)(2,1)}), bf16[128,8,256]{2,1,0:T(8,128)(2,1)S(1)}, u32[]{:S(2)}, u32[]{:S(2)}) %all-to-all-start) | async-done | bytes 524320 | tf_op jit(solution)/shard_map/all_to_all | solution.py:168
  42.7 13.6 %while.76 = (s32[]{:T(128)}, bf16[2,256,256]{1,2,0:T(8,128)(2,1)}, bf16[2,4,256,256]{2,3,1,0:T(8,128)(2,1)S(1)}, bf16[2,256,768]{1,2,0:T(8,128)(2,1)S(1)}, pred[...) while((s32[]{:T(128)}, bf16[2,256,256]{1,2,0:T(8,128)(2,1)}, ...), condition=%wide.region_11.12_spmd, body=%wide.region_6.11_spmd.sunk | while | flops 17513984 | bytes 4204822 | solution.py:108
  43.5 5.3 %while.81 = (s32[]{:T(128)}, bf16[4,256,64]{1,2,0:T(8,128)(2,1)S(1)}, bf16[4,256,256]{1,2,0:T(8,128)(2,1)S(1)}, pred[256]{0:T(512)(128)(4,1)S(1)}, bf16[4,256,64...) while((s32[]{:T(128)}, ...), condition=%wide.region_10.10_spmd, body=%wide.region_7.9_spmd.sunk | while | flops 17513984 | bytes 1320545 | solution.py:64
  50.3 5.3 %while.81 = (s32[]{:T(128)}, bf16[4,256,64]{1,2,0:T(8,128)(2,1)S(1)}, bf16[4,256,256]{1,2,0:T(8,128)(2,1)S(1)}, pred[256]{0:T(512)(128)(4,1)S(1)}, bf16[4,256,64...) while((s32[]{:T(128)}, ...), condition=%wide.region_10.10_spmd, body=%wide.region_7.9_spmd.sunk | while | flops 17513984 | bytes 1320545 | solution.py:64
  58.0 3.3 scatter_custom_fusion.1
  61.3 4.6 %all-to-all-start.1 = ((bf16[128,8,256]{2,1,0:T(8,128)(2,1)}), bf16[128,8,256]{2,1,0:T(8,128)(2,1)S(1)}, u32[]{:S(2)}, u32[]{:S(2)}) async-start(bf16[128,8,256]{2,1,0:T(8,128)(2,1)} %bitcast.368), calls=%async_computation.1 | async-start | bytes 1048576 | tf_op jit(solution)/shard_map/all_to_all | solution.py:174
  66.0 13.7 %all-to-all-done.1 = bf16[128,8,256]{2,1,0:T(8,128)(2,1)S(1)} async-done(((bf16[128,8,256]{2,1,0:T(8,128)(2,1)}), bf16[128,8,256]{2,1,0:T(8,128)(2,1)S(1)}, u32[]{:S(2)}, u32[]{:S(2)}) %all-to-all-start.1) | async-done | bytes 524320 | tf_op jit(solution)/shard_map/all_to_all | solution.py:174
  79.7 2.6 gather_fusion.1
  91.6 3.0 all-gather.2.cloned.1.call-done
  94.6 2.1 fusion.108
  101.2 2.4 copy.65
  103.6 32.8 %while.77 = (s32[]{:T(128)}, bf16[8,256,64]{1,2,0:T(8,128)(2,1)}, bf16[8,256,512]{2,1,0:T(8,128)(2,1)}, bf16[8,256,64]{2,1,0:T(8,128)(2,1)}, bf16[8,512,64]{2,1,...) while((s32[]{:T(128)}, bf16[8,256,64]{1,2,0:T(8,128)(2,1)}, bf16[8,256,512]{2,1,0:T(8,128)(2,1)}, ...), condition=%wide.region_18.19_spmd, body=%wide.region_15.18_spmd.sunk | while | flops 34881024 | bytes 2729049 | solution.py:64
  136.4 54.1 %while.78 = (s32[]{:T(128)}, bf16[8,256,64]{1,2,0:T(8,128)(2,1)}, bf16[8,512,64]{1,2,0:T(8,128)(2,1)}, bf16[8,512,64]{1,2,0:T(8,128)(2,1)}, bf16[8,256,512]{2,1,...) while((s32[]{:T(128)}, bf16[8,256,64]{1,2,0:T(8,128)(2,1)}, ...), condition=%wide.region_21.22_spmd, body=%wide.region_19.21_spmd.sunk | while | flops 68157184 | bytes 3349617 | solution.py:75
  194.4 8.3 %reduce-scatter.5.cloned.1.call-done = bf16[256,512]{0,1:T(8,128)(2,1)} async-done(((bf16[512,512]{0,1:T(8,128)(2,1)}), bf16[256,512]{0,1:T(8,128)(2,1)}) %reduce-scatter.5.cloned.1.call-update) | async-done | bytes 262160 | tf_op jit(solution)/shard_map/reduce_scatter | solution.py:250
  202.7 14.5 %reduce-scatter.3.cloned.1.call-done = bf16[256,512]{0,1:T(8,128)(2,1)} async-done(((bf16[512,512]{0,1:T(8,128)(2,1)}), bf16[256,512]{0,1:T(8,128)(2,1)}) %reduce-scatter.3.cloned.1.call-update) | async-done | bytes 262160 | tf_op jit(solution)/shard_map/reduce_scatter | solution.py:247
  217.2 2.3 fusion.103
  220.2 3.1 scatter_custom_fusion.2
  223.3 9.2 %all-to-all-start.2 = ((bf16[128,8,256]{2,1,0:T(8,128)(2,1)}), bf16[128,8,256]{2,1,0:T(8,128)(2,1)S(1)}, u32[]{:S(2)}, u32[]{:S(2)}) async-start(bf16[128,8,256]{2,1,0:T(8,128)(2,1)} %bitcast.367), calls=%async_computation.4 | async-start | bytes 1048576 | tf_op jit(solution)/shard_map/all_to_all | solution.py:168
  234.1 2.3 convolution_multiply_fusion.2
  236.4 9.8 %all-to-all-done.2 = bf16[128,8,256]{2,1,0:T(8,128)(2,1)S(1)} async-done(((bf16[128,8,256]{2,1,0:T(8,128)(2,1)}), bf16[128,8,256]{2,1,0:T(8,128)(2,1)S(1)}, u32[]{:S(2)}, u32[]{:S(2)}) %all-to-all-start.2) | async-done | bytes 524320 | tf_op jit(solution)/shard_map/all_to_all | solution.py:168
  249.1 24.5 %while.80 = (s32[]{:T(128)}, bf16[2,256,768]{1,2,0:T(8,128)(2,1)}, bf16[2,256,768]{1,2,0:T(8,128)(2,1)S(1)}, bf16[2,4,256,256]{2,3,1,0:T(8,128)(2,1)}, bf16[2,25...) while((s32[]{:T(128)}, bf16[2,256,768]{1,2,0:T(8,128)(2,1)}, ...), condition=%wide.region_31.32_spmd, body=%wide.region_27.31_spmd.sunk | while | flops 35258112 | bytes 5610806 | solution.py:145
  251.3 8.3 %while.82 = (s32[]{:T(128)}, bf16[4,256,64]{1,2,0:T(8,128)(2,1)S(1)}, bf16[4,256,64]{1,2,0:T(8,128)(2,1)}, bf16[4,256,64]{1,2,0:T(8,128)(2,1)}, bf16[4,256,256]{...) while((s32[]{:T(128)}, ...), condition=%wide.region_30.30_spmd, body=%wide.region_28.29_spmd.sunk | while | flops 34078464 | bytes 1678449 | solution.py:75
  263.5 8.3 %while.82 = (s32[]{:T(128)}, bf16[4,256,64]{1,2,0:T(8,128)(2,1)S(1)}, bf16[4,256,64]{1,2,0:T(8,128)(2,1)}, bf16[4,256,64]{1,2,0:T(8,128)(2,1)}, bf16[4,256,256]{...) while((s32[]{:T(128)}, ...), condition=%wide.region_30.30_spmd, body=%wide.region_28.29_spmd.sunk | while | flops 34078464 | bytes 1678449 | solution.py:75
  275.5 2.6 fusion.69
  280.4 3.3 scatter_custom_fusion.3
  283.7 4.6 %all-to-all-start.3 = ((bf16[128,8,256]{2,1,0:T(8,128)(2,1)}), bf16[128,8,256]{2,1,0:T(8,128)(2,1)S(1)}, u32[]{:S(2)}, u32[]{:S(2)}) async-start(bf16[128,8,256]{2,1,0:T(8,128)(2,1)} %bitcast.85), calls=%async_computation.5 | async-start | bytes 1048576 | tf_op jit(solution)/shard_map/all_to_all | solution.py:174
  289.3 13.7 %all-to-all-done.3 = bf16[128,8,256]{2,1,0:T(8,128)(2,1)S(1)} async-done(((bf16[128,8,256]{2,1,0:T(8,128)(2,1)}), bf16[128,8,256]{2,1,0:T(8,128)(2,1)S(1)}, u32[]{:S(2)}, u32[]{:S(2)}) %all-to-all-start.3) | async-done | bytes 524320 | tf_op jit(solution)/shard_map/all_to_all | solution.py:174
  303.0 2.6 gather_fusion.3
  305.6 132.2 %all-reduce.3.cloned.1.call-done = (f32[256,768]{1,0:T(8,128)}, f32[256,256]{1,0:T(8,128)}, f32[512,512]{1,0:T(8,128)}, f32[512,1536]{1,0:T(8,128)}, f32[512,512]{1,0:T(8,128)}) async-done(((f32[256,768]{1,0:T(8,128)}, f32[256,256]{1,0:T(8,128)}, f32[512,512]{1,0:T(8,128)}, f32[512,1536]{1,0:T(8,128)}, f32[512,512]{1,0:T(8,128)}), (f32[256,768]{1,0:T(8,128)}, f32[256,256]{1,0:T(8,128)}, ...) | async-done | bytes 6291472 | tf_op jit(solution)/shard_map/psum | solution.py:288
  437.8 2.2 copy.171
  (309 shorter events, 167.1 us)
Async XLA Ops:
  7.2 76.1 %copy-start = (bf16[512,512]{1,0:T(8,128)(2,1)S(1)}, bf16[512,512]{1,0:T(8,128)(2,1)}, u32[]{:S(2)}) copy-start(bf16[512,512]{1,0:T(8,128)(2,1)} %param.28) | copy-start | bytes 1572868
  7.2 16.8 %copy-start.21 = (s32[512]{0:T(512)S(1)}, s32[512]{0:T(512)}, u32[]{:S(2)}) copy-start(s32[512]{0:T(512)} %param.24) | copy-start | bytes 6148
  7.2 16.8 %copy-start.29 = (s32[256]{0:T(256)S(1)}, s32[256]{0:T(256)}, u32[]{:S(2)}) copy-start(s32[256]{0:T(256)} %param.25) | copy-start | bytes 3076
  8.9 3.5 copy-start.27
  12.4 25.2 %all-to-all-start = ((bf16[128,8,256]{2,1,0:T(8,128)(2,1)}), bf16[128,8,256]{2,1,0:T(8,128)(2,1)S(1)}, u32[]{:S(2)}, u32[]{:S(2)}) async-start(bf16[128,8,256]{2,1,0:T(8,128)(2,1)} %bitcast.52), calls=%async_computation | async-start | bytes 1048576 | tf_op jit(solution)/shard_map/all_to_all | solution.py:168
  24.0 16.0 %copy-start.15 = (bf16[256,768]{1,0:T(8,128)(2,1)S(1)}, bf16[256,768]{1,0:T(8,128)(2,1)}, u32[]{:S(2)}) copy-start(bf16[256,768]{1,0:T(8,128)(2,1)} %param.26) | copy-start | bytes 1179652
  24.6 13.0 %copy-start.26 = (s32[512]{0:T(512)}, s32[512]{0:T(512)S(1)}, u32[]{:S(2)}) copy-start(s32[512]{0:T(512)S(1)} %compare_select_fusion.1) | copy-start | bytes 6148
  24.7 16.7 %copy-start.24 = (s32[1024]{0:T(1024)}, s32[1024]{0:T(1024)S(1)}, u32[]{:S(2)}) copy-start(s32[1024]{0:T(1024)S(1)} %pad_clamp_fusion.1) | copy-start | bytes 12292
  56.4 25.9 %copy-start.1 = (bf16[2,4,256,256]{2,3,1,0:T(8,128)(2,1)}, bf16[2,4,256,256]{2,3,1,0:T(8,128)(2,1)S(1)}, u32[]{:S(2)}) copy-start(bf16[2,4,256,256]{2,3,1,0:T(8,128)(2,1)S(1)} %get-tuple-element.915) | copy-start | bytes 3145732
  56.4 9.6 %copy-start.28 = (s32[512]{0:T(512)S(1)}, s32[512]{0:T(512)}, u32[]{:S(2)}) copy-start(s32[512]{0:T(512)} %copy-done.27) | copy-start | bytes 6148
  61.3 18.4 %all-to-all-start.1 = ((bf16[128,8,256]{2,1,0:T(8,128)(2,1)}), bf16[128,8,256]{2,1,0:T(8,128)(2,1)S(1)}, u32[]{:S(2)}, u32[]{:S(2)}) async-start(bf16[128,8,256]{2,1,0:T(8,128)(2,1)} %bitcast.368), calls=%async_computation.1 | async-start | bytes 1048576 | tf_op jit(solution)/shard_map/all_to_all | solution.py:174
  65.9 28.7 %all-gather.2.cloned.1.call-start = ((), (), s32[]{:S(2)}) async-start(), calls=%async_computation.6 | async-start | bytes 1572864 | tf_op jit(solution)/shard_map/all_gather | solution.py:235
  66.0 17.7 %copy-start.22 = (s32[1024]{0:T(1024)}, s32[1024]{0:T(1024)S(1)}, u32[]{:S(2)}) copy-start(s32[1024]{0:T(1024)S(1)} %pad_clamp_fusion) | copy-start | bytes 12292
  83.9 2.3 copy-start.3
  84.0 2.3 copy-start.5
  84.7 4.4 copy-start.7
  86.0 116.7 %reduce-scatter.5.cloned.1.call-start = ((), (), s32[]{:S(2)}) async-start(), calls=%async_computation.8 | async-start | bytes 786432 | tf_op jit(solution)/shard_map/reduce_scatter | solution.py:250
  190.5 2.6 copy-start.4
  190.5 2.6 copy-start.11
  190.5 26.6 %copy-start.17 = (bf16[8,256,64]{1,2,0:T(8,128)(2,1)S(1)}, bf16[8,256,64]{1,2,0:T(8,128)(2,1)}, u32[]{:S(2)}) copy-start(bf16[8,256,64]{1,2,0:T(8,128)(2,1)} %get-tuple-element.257) | copy-start | bytes 786436
  190.5 26.6 %reduce-scatter.3.cloned.1.call-start = ((), (), s32[]{:S(2)}) async-start(), calls=%async_computation.7 | async-start | bytes 786432 | tf_op jit(solution)/shard_map/reduce_scatter | solution.py:247
  220.2 13.9 %copy-start.8 = (bf16[256,512]{1,0:T(8,128)(2,1)S(1)}, bf16[256,512]{1,0:T(8,128)(2,1)}, u32[]{:S(2)}) copy-start(bf16[256,512]{1,0:T(8,128)(2,1)} %copy-done.7) | copy-start | bytes 786436
  223.3 22.9 %all-to-all-start.2 = ((bf16[128,8,256]{2,1,0:T(8,128)(2,1)}), bf16[128,8,256]{2,1,0:T(8,128)(2,1)S(1)}, u32[]{:S(2)}, u32[]{:S(2)}) async-start(bf16[128,8,256]{2,1,0:T(8,128)(2,1)} %bitcast.367), calls=%async_computation.4 | async-start | bytes 1048576 | tf_op jit(solution)/shard_map/all_to_all | solution.py:168
  232.5 205.3 %all-reduce.3.cloned.1.call-start = ((), (), s32[]{:S(2)}) async-start(), calls=%async_computation.9 | async-start | bytes 12582912 | tf_op jit(solution)/shard_map/psum | solution.py:288
  234.1 12.1 %copy-start.25 = (s32[1024]{0:T(1024)S(1)}, s32[1024]{0:T(1024)}, u32[]{:S(2)}) copy-start(s32[1024]{0:T(1024)} %copy-done.24) | copy-start | bytes 12292
  236.4 11.7 %copy-start.14 = (bf16[256,256]{1,0:T(8,128)(2,1)S(1)}, bf16[256,256]{1,0:T(8,128)(2,1)}, u32[]{:S(2)}) copy-start(bf16[256,256]{1,0:T(8,128)(2,1)} %param.27) | copy-start | bytes 393220
  280.0 8.3 %copy-start.6 = (bf16[512,512]{1,0:T(8,128)(2,1)S(1)}, bf16[512,512]{1,0:T(8,128)(2,1)}, u32[]{:S(2)}) copy-start(bf16[512,512]{1,0:T(8,128)(2,1)} %param.30) | copy-start | bytes 1572868
  280.0 8.3 %copy-start.12 = (bf16[8,256,64]{1,2,0:T(8,128)(2,1)S(1)}, bf16[8,256,64]{1,2,0:T(8,128)(2,1)}, u32[]{:S(2)}) copy-start(bf16[8,256,64]{1,2,0:T(8,128)(2,1)} %get-tuple-element.255) | copy-start | bytes 786436
  280.4 22.6 %copy-start.23 = (s32[1024]{0:T(1024)S(1)}, s32[1024]{0:T(1024)}, u32[]{:S(2)}) copy-start(s32[1024]{0:T(1024)} %copy-done.22) | copy-start | bytes 12292
  283.7 19.4 %all-to-all-start.3 = ((bf16[128,8,256]{2,1,0:T(8,128)(2,1)}), bf16[128,8,256]{2,1,0:T(8,128)(2,1)S(1)}, u32[]{:S(2)}, u32[]{:S(2)}) async-start(bf16[128,8,256]{2,1,0:T(8,128)(2,1)} %bitcast.85), calls=%async_computation.5 | async-start | bytes 1048576 | tf_op jit(solution)/shard_map/all_to_all | solution.py:174
  437.8 3.9 copy-start.10
  437.8 4.9 %copy-start.2 = (f32[512,1536]{1,0:T(8,128)S(1)}, f32[512,1536]{1,0:T(8,128)}, u32[]{:S(2)}) copy-start(f32[512,1536]{1,0:T(8,128)} %get-tuple-element.941) | copy-start | bytes 9437188
  (7 other events, 9.7 us)
Sparse Core Ops, SparseCore 0:
  86.1 8.4 all-gather.1
  190.7 11.9 reduce-scatter.4
  205.1 11.9 reduce-scatter.2
  278.3 159.4 all-reduce.2
where the time goes:
time: 455 us; the launch traced here: 452 us
  waiting for transfers between devices  209 us (46%)
  matrix products  116 us (25%)
  local copies, waits for them, and re-layouts  55.4 us (12%)
  starting transfers between devices  30.5 us (7%)
  other arithmetic  26.2 us (6%)
  between operations  14.3 us (3%)
    psum x1, waiting for transfers between devices, on_device(): lax.psum((fine_projection_term * scaling, fine_output_term * scaling, poo...  132 us
    all_to_all x2, waiting for transfers between devices, route_back(): lax.all_to_all(values, ('pts', 'grp'), split_axis=0, concat_axis=0, tiled...  27.4 us
    all_to_all x2, waiting for transfers between devices, route_out(): lax.all_to_all(values, ('pts', 'grp'), split_axis=0, concat_axis=0, tiled...  22.7 us
    dot_general x16, matrix products, head_forward(): jnp.dot(weights, value_rows, preferred_element_type=jnp.float32)  22.1 us
    all_to_all x2, starting transfers between devices, route_out(): lax.all_to_all(values, ('pts', 'grp'), split_axis=0, concat_axis=0, tiled...  20.7 us
    dot_general x16, matrix products, head_backward(): jnp.dot(weights.T, incoming, preferred_element_type=jnp.float32)  20.5 us
    dot_general x16, matrix products, head_backward(): key_grad = jnp.dot(slopes.T, query_rows, preferred_element_type=jnp.float32)  20 us
    reduce_scatter x1, waiting for transfers between devices, on_device(): lax.psum_scatter(key_grad.astype(jnp.bfloat16), 'grp', scatter_dimension=...  14.5 us
  transfers between devices with their start and end apart: 8, of which 8 were waited for; matrix products, arithmetic and copies ran while one was open for 5% of the time, Pallas kernels for 0%

commit v1 on v0

v1 whole, which is shorter than its diff:
```python
import math

import jax
import jax.numpy as jnp
from jax import lax
from jax.experimental import pallas as pl
from jax.experimental.pallas import tpu as pltpu
from jax.sharding import PartitionSpec as P

HD = 64
BALL = 256
PAIR = 2 * HD
EPSILON = 1e-05
BF = jnp.bfloat16
F32 = jnp.float32


def mm(a, b, contract=(1, 0)):
    return lax.dot_general(
        a, b, (((contract[0],), (contract[1],)), ((), ())), preferred_element_type=F32
    )


def normalize(values):
    floats = values.astype(F32)
    center = floats - jnp.mean(floats, axis=-1, keepdims=True)
    inverse = lax.rsqrt(jnp.mean(center * center, axis=-1, keepdims=True) + EPSILON)
    return center * inverse, inverse


def norm_backward(incoming, normed, inverse):
    first_mean = jnp.mean(incoming, axis=-1, keepdims=True)
    second_mean = jnp.mean(incoming * normed, axis=-1, keepdims=True)
    return inverse * (incoming - first_mean - normed * second_mean)


def one_hot(slots, total):
    shape = (total, slots.shape[1])
    return (lax.broadcasted_iota(jnp.int32, shape, 0) == slots).astype(BF)


def head_half(shape, half):
    lanes = lax.broadcasted_iota(jnp.int32, shape, 1)
    return (lanes < HD) if half == 0 else (lanes >= HD)


def keep_half(rows, half):
    return jnp.where(head_half(rows.shape, half), rows, jnp.zeros_like(rows))


def softmax_rows(scores):
    raised = jnp.exp(scores - jnp.max(scores, axis=-1, keepdims=True))
    return (raised / jnp.sum(raised, axis=-1, keepdims=True)).astype(BF)


def slopes_of(weights, against):
    wide = weights.astype(F32)
    diagonal = jnp.sum(wide * against, axis=-1, keepdims=True)
    return (wide * (against - diagonal) * HD ** (-0.5)).astype(BF)


def column_of(row):
    count = row.shape[1]
    turned = jnp.broadcast_to(row.astype(F32), (128, count)).T
    return jnp.concatenate([turned] * (count // 128), axis=1)


def route_kernel(place, source, counts, points, send, send_slot, receive_slot, live):
    count = place.shape[1]
    shift = count.bit_length() - 1
    capacity = send.shape[0] * count // (counts.shape[1] * BALL)
    to_row = place[...] >> shift
    rows = lax.broadcasted_iota(jnp.int32, (count, count), 0)
    columns = lax.broadcasted_iota(jnp.int32, (count, count), 1)
    earlier = (column_of(to_row) == to_row.astype(F32)) & (rows < columns)
    rank = jnp.sum(jnp.where(earlier, 1.0, 0.0), axis=0, keepdims=True)
    slot = to_row * capacity + rank.astype(jnp.int32)
    send_slot[...] = slot
    source_row = source[...]
    from_row = source_row >> shift
    earlier = (column_of(from_row) == from_row.astype(F32)) & (
        column_of(source_row) < source_row.astype(F32)
    )
    rank = jnp.sum(jnp.where(earlier, 1.0, 0.0), axis=0, keepdims=True)
    receive_slot[...] = from_row * capacity + rank.astype(jnp.int32)
    balls = counts.shape[1]
    own_ball = one_hot(source_row >> (BALL.bit_length() - 1), balls)
    filled = mm(jnp.broadcast_to(counts[...].astype(F32), (8, balls)).astype(BF), own_ball)
    inside = (source_row & (BALL - 1)).astype(F32)
    live[...] = jnp.where(inside < filled[:1], 1.0, 0.0)
    send[...] = mm(one_hot(slot, send.shape[0]), points[...]).astype(BF)


def fine_forward_kernel(
    arrived, receive_slot, live, projection, output, send, rotated, projected, mixture, weights
):
    place = one_hot(receive_slot[...], arrived.shape[0])
    rows_in = mm(place, arrived[...], (0, 0))
    rotated[...] = rows_in.astype(BF)
    features = rows_in.shape[1]
    normed, _ = normalize(rows_in)
    projected[...] = mm(normed.astype(BF), projection[...]).astype(BF)
    balls = rows_in.shape[0] // BALL
    pairs = features // PAIR
    for ball in range(balls):
        rows = slice(ball * BALL, (ball + 1) * BALL)
        alive = live[:, rows] > 0.5
        for pair in range(pairs):
            lanes = slice(pair * PAIR, (pair + 1) * PAIR)
            query = projected[rows, lanes]
            key = projected[rows, features + pair * PAIR : features + (pair + 1) * PAIR]
            value = projected[rows, 2 * features + pair * PAIR : 2 * features + (pair + 1) * PAIR]
            halves = []
            for half in range(2):
                scores = mm(keep_half(query, half), key, (1, 1)) * HD ** (-0.5)
                head_weights = softmax_rows(jnp.where(alive, scores, -1e30))
                weights[(ball * pairs + pair) * 2 + half] = head_weights
                halves.append(mm(head_weights, value))
            mixed = jnp.where(head_half(halves[0].shape, 0), halves[0], halves[1])
            mixture[rows, lanes] = mixed.astype(BF)
    result = (rows_in + mm(mixture[...], output[...])).astype(BF)
    send[...] = mm(place, result).astype(BF)


def join_kernel(arrived, slots, joined):
    half = joined.shape[1] // 2
    for side in range(2):
        place = one_hot(slots[side : side + 1, :], arrived.shape[0])
        joined[:, side * half : (side + 1) * half] = mm(place, arrived[...], (0, 0)).astype(BF)


def coarse_kernel(
    group,
    own_joined,
    other_joined,
    own_cotangent,
    other_cotangent,
    pool,
    projection,
    output,
    coarse,
    unit,
    keep,
    give,
):
    half_rows, wide = own_joined.shape
    part = wide // 2
    first = pl.multiple_of(group[0] * part, part)
    joined = jnp.concatenate([own_joined[...], other_joined[...]], axis=0)
    cotangent = jnp.concatenate([own_cotangent[...], other_cotangent[...]], axis=0)
    tokens = mm(joined, pool[...]).astype(BF)
    coarse[...] = tokens[:half_rows]
    normed, _ = normalize(tokens)
    unit_rows = normed.astype(BF)
    unit[...] = unit_rows
    queries = mm(unit_rows, projection[:, pl.ds(first, part)]).astype(BF)
    keys = mm(unit_rows, projection[:, pl.ds(wide + first, part)]).astype(BF)
    values = mm(unit_rows, projection[:, pl.ds(2 * wide + first, part)]).astype(BF)
    incoming = mm(cotangent, output[pl.ds(first, part), :], (1, 1)).astype(BF)
    for pair in range(part // PAIR):
        lanes = slice(pair * PAIR, (pair + 1) * PAIR)
        query, key, value = queries[:, lanes], keys[:, lanes], values[:, lanes]
        entering = incoming[:, lanes]
        parts = ([], [], [], [])
        for half in range(2):
            scores = mm(keep_half(query, half), key, (1, 1)) * HD ** (-0.5)
            head_weights = softmax_rows(scores)
            parts[0].append(mm(head_weights, value))
            against = mm(keep_half(entering, half), value, (1, 1))
            slopes = slopes_of(head_weights, against)
            parts[1].append(mm(slopes, key))
            parts[2].append(mm(slopes, query, (0, 0)))
            parts[3].append(mm(head_weights, entering, (0, 0)))
        for at, (low, high) in enumerate(parts):
            both = jnp.where(head_half(low.shape, 0), low, high).astype(BF)
            target = slice(at * part + pair * PAIR, at * part + (pair + 1) * PAIR)
            keep[:, target] = both[:half_rows]
            give[:, target] = both[half_rows:]


def coarse_finish_kernel(
    group,
    coarse,
    keep,
    got,
    cotangent,
    pool,
    projection,
    output,
    slots,
    result,
    gradient,
    send,
):
    half_rows, wide = coarse.shape
    part = wide // 2
    mixed = coarse[...].astype(F32)
    back = jnp.zeros((half_rows, wide), F32)
    for source, index in ((keep, group[0]), (got, 1 - group[0])):
        first = pl.multiple_of(index * part, part)
        mixed = mixed + mm(source[:, :part], output[pl.ds(first, part), :])
        for at in range(3):
            back = back + mm(
                source[:, (at + 1) * part : (at + 2) * part],
                projection[:, pl.ds(at * wide + first, part)],
                (1, 1),
            )
    result[...] = mixed.astype(BF)
    normed, inverse = normalize(coarse[...])
    gradient_rows = (
        cotangent[...].astype(F32) + norm_backward(back, normed, inverse)
    ).astype(BF)
    gradient[...] = gradient_rows
    fine = mm(gradient_rows, pool[...], (1, 1)).astype(BF)
    features = send.shape[1]
    total = mm(one_hot(slots[0:1, :], send.shape[0]), fine[:, :features])
    total = total + mm(one_hot(slots[1:2, :], send.shape[0]), fine[:, features:])
    send[...] = total.astype(BF)


def coarse_weights_kernel(
    unit, keep, give, own_cotangent, other_cotangent, projection_term, output_term
):
    part = keep.shape[1] // 4
    stacked = jnp.concatenate([keep[...], give[...]], axis=0)
    cotangent = jnp.concatenate([own_cotangent[...], other_cotangent[...]], axis=0)
    projection_term[...] = mm(unit[...], stacked[:, part:], (0, 0))
    output_term[...] = mm(stacked[:, :part], cotangent, (0, 0))


def pool_weights_kernel(group, own_joined, other_joined, own_gradient, other_gradient, term):
    part = term.shape[0]
    first = pl.multiple_of(group[0] * part, part)
    term[...] = mm(own_joined[:, pl.ds(first, part)], own_gradient[...], (0, 0)) + mm(
        other_joined[:, pl.ds(first, part)], other_gradient[...], (0, 0)
    )


def fine_backward_kernel(
    arrived,
    receive_slot,
    rotated,
    projected,
    mixture,
    weights,
    projection,
    output,
    send,
    projection_term,
    output_term,
    grad_projected,
):
    place = one_hot(receive_slot[...], arrived.shape[0])
    gradient_in = mm(place, arrived[...], (0, 0))
    gradient_rows = gradient_in.astype(BF)
    features = rotated.shape[1]
    entering = mm(gradient_rows, output[...], (1, 1)).astype(BF)
    output_term[...] = mm(mixture[...], gradient_rows, (0, 0))
    balls = rotated.shape[0] // BALL
    pairs = features // PAIR
    for ball in range(balls):
        rows = slice(ball * BALL, (ball + 1) * BALL)
        for pair in range(pairs):
            lanes = slice(pair * PAIR, (pair + 1) * PAIR)
            query = projected[rows, lanes]
            key = projected[rows, features + pair * PAIR : features + (pair + 1) * PAIR]
            value = projected[rows, 2 * features + pair * PAIR : 2 * features + (pair + 1) * PAIR]
            enters = entering[rows, lanes]
            parts = ([], [], [])
            for half in range(2):
                head_weights = weights[(ball * pairs + pair) * 2 + half]
                against = mm(keep_half(enters, half), value, (1, 1))
                slopes = slopes_of(head_weights, against)
                parts[0].append(mm(slopes, key))
                parts[1].append(mm(slopes, query, (0, 0)))
                parts[2].append(mm(head_weights, enters, (0, 0)))
            for at, (low, high) in enumerate(parts):
                both = jnp.where(head_half(low.shape, 0), low, high).astype(BF)
                target = at * features + pair * PAIR
                grad_projected[rows, target : target + PAIR] = both
    normed, inverse = normalize(rotated[...])
    projection_term[...] = mm(normed.astype(BF), grad_projected[...], (0, 0))
    back = mm(grad_projected[...], projection[...], (1, 1))
    result = (gradient_in + norm_backward(back, normed, inverse)).astype(BF)
    send[...] = mm(place, result).astype(BF)


def take_kernel(arrived, slots, rows_out):
    place = one_hot(slots[...], arrived.shape[0])
    rows_out[...] = mm(place, arrived[...], (0, 0)).astype(BF)


VMEM = pl.BlockSpec(memory_space=pltpu.VMEM)
SMEM = pl.BlockSpec(memory_space=pltpu.SMEM)


def call(kernel, inputs, outputs, scalar=False, scratch=()):
    in_specs = [VMEM] * len(inputs)
    if scalar:
        in_specs[0] = SMEM
    shapes = [jax.ShapeDtypeStruct(shape, dtype) for shape, dtype in outputs]
    return pl.pallas_call(
        kernel,
        out_shape=shapes,
        in_specs=in_specs,
        out_specs=[VMEM] * len(shapes),
        scratch_shapes=list(scratch),
        compiler_params=pltpu.CompilerParams(vmem_limit_bytes=56 * 1024 * 1024),
    )(*inputs)


def exchange(values):
    return lax.ppermute(values, "grp", [(0, 1), (1, 0)])


def route(values, devices):
    rows, features = values.shape
    arrived = lax.all_to_all(
        values.reshape(devices, rows // devices, features),
        ("pts", "grp"),
        split_axis=0,
        concat_axis=0,
        tiled=True,
    )
    return arrived.reshape(rows, features)


def on_device(
    points,
    rotated_place,
    rotated_source,
    ball_counts,
    fine_projection,
    fine_output,
    pool_weight,
    coarse_projection,
    coarse_output,
    coarse_cotangent,
):
    count, features = points.shape
    devices = lax.axis_size(("pts", "grp"))
    slots = 2 * count
    scaling = 1.0 / math.sqrt(count * devices)
    group = lax.axis_index("grp").astype(jnp.int32).reshape(1)
    wide = 2 * features
    half_rows = count // 2

    send, send_slot, receive_slot, live = call(
        route_kernel,
        (
            rotated_place.reshape(1, count),
            rotated_source.reshape(1, count),
            ball_counts.reshape(1, -1),
            points,
        ),
        (
            ((slots, features), BF),
            ((1, count), jnp.int32),
            ((1, count), jnp.int32),
            ((1, count), F32),
        ),
    )
    other_cotangent = exchange(coarse_cotangent)
    arrived = route(send, devices)
    pair_slots = send_slot.reshape(half_rows, 2).T
    heads = features // HD * (count // BALL)
    send, rotated, projected, mixture, weights = call(
        fine_forward_kernel,
        (arrived, receive_slot, live, fine_projection, fine_output),
        (
            ((slots, features), BF),
            ((count, features), BF),
            ((count, 3 * features), BF),
            ((count, features), BF),
            ((heads, BALL, BALL), BF),
        ),
    )
    arrived = route(send, devices)
    (own_joined,) = call(join_kernel, (arrived, pair_slots), (((half_rows, wide), BF),))
    other_joined = exchange(own_joined)
    coarse, unit, keep, give = call(
        coarse_kernel,
        (
            group,
            own_joined,
            other_joined,
            coarse_cotangent,
            other_cotangent,
            pool_weight,
            coarse_projection,
            coarse_output,
        ),
        (
            ((half_rows, wide), BF),
            ((count, wide), BF),
            ((half_rows, 2 * wide), BF),
            ((half_rows, 2 * wide), BF),
        ),
        scalar=True,
    )
    got = exchange(give)
    coarse_result, coarse_gradient, send = call(
        coarse_finish_kernel,
        (
            group,
            coarse,
            keep,
            got,
            coarse_cotangent,
            pool_weight,
            coarse_projection,
            coarse_output,
            pair_slots,
        ),
        (((half_rows, wide), BF), ((half_rows, wide), BF), ((slots, features), BF)),
        scalar=True,
    )
    arrived = route(send, devices)
    projection_term, output_term = call(
        coarse_weights_kernel,
        (unit, keep, give, coarse_cotangent, other_cotangent),
        (((wide, 3 * wide // 2), F32), ((wide // 2, wide), F32)),
    )
    other_gradient = exchange(coarse_gradient)
    (pool_term,) = call(
        pool_weights_kernel,
        (group, own_joined, other_joined, coarse_gradient, other_gradient),
        (((wide // 2, wide), F32),),
        scalar=True,
    )
    send, fine_projection_term, fine_output_term = call(
        fine_backward_kernel,
        (
            arrived,
            receive_slot,
            rotated,
            projected,
            mixture,
            weights,
            fine_projection,
            fine_output,
        ),
        (
            ((slots, features), BF),
            ((features, 3 * features), F32),
            ((features, features), F32),
        ),
        scratch=(pltpu.VMEM((count, 3 * features), BF),),
    )
    arrived = route(send, devices)
    (points_gradient,) = call(take_kernel, (arrived, send_slot), (((count, features), BF),))

    sums = lax.psum(
        (fine_projection_term, fine_output_term, pool_term, projection_term, output_term), "pts"
    )
    fine_projection_sum, fine_output_sum = lax.psum(sums[:2], "grp")
    pool_sum, projection_sum, output_sum = lax.all_gather(sums[2:], "grp", axis=0, tiled=False)
    projection_sum = projection_sum.reshape(2, wide, 3, wide // 2).transpose(1, 2, 0, 3)
    return (
        coarse_result,
        points_gradient,
        fine_projection_sum * scaling,
        fine_output_sum * scaling,
        pool_sum.reshape(wide, wide) * scaling,
        projection_sum.reshape(wide, 3 * wide) * scaling,
        output_sum.reshape(wide, wide) * scaling,
    )


def solution(mesh):
    tokens = P(("pts", "grp"), None)
    in_specs = (
        tokens,
        P(("pts", "grp")),
        P(("pts", "grp")),
        P(),
        P(),
        P(),
        P(),
        P(),
        P(),
        tokens,
    )
    out_specs = (tokens, tokens, P(), P(), P(), P(), P())
    return jax.shard_map(
        on_device, mesh=mesh, in_specs=in_specs, out_specs=out_specs, check_vma=False
    )
```

time: 455 us -> 329 us (0.72)
  matrix products: 116 us -> 0 us
  blocking collectives: 0 us -> 46.7 us
  local copies, waits for them, and re-layouts: 55.4 us -> 10.2 us
  Pallas kernels: 0 us -> 39.3 us
  starting transfers between devices: 30.5 us -> 12.7 us
  other arithmetic: 26.2 us -> 9.34 us
  waiting for transfers between devices: 209 us -> 196 us
    dot_general x112 -> x0, matrix products: 116 us -> none  [the longest x16 22.1 us: head_forward(): jnp.dot(weights, value_rows, preferred_element_type=jnp.float32)]
    all_to_all x0 -> x2, blocking collectives: none -> 46.7 us  [route(): lax.all_to_all(values.reshape(devices, rows // devices, features), ('pts'...]
    pallas_call x0 -> x9, Pallas kernels: none -> 39.3 us  [call(): pl.pallas_call(kernel, out_shape=shapes, in_specs=in_specs, out_specs=[VM...]
    all_gather x1 -> x3, waiting for transfers between devices: 3.01 us -> 39.1 us  [on_device(): lax.all_gather(sums[2:], 'grp', axis=0, tiled=False)]
    all_to_all x4 -> x2, waiting for transfers between devices: 50.1 us -> 16.4 us  [route(): lax.all_to_all(values.reshape(devices, rows // devices, features), ('pts'...]
    reduce_scatter x2 -> x0, waiting for transfers between devices: 22.8 us -> none  [the longest x1 14.5 us: on_device(): lax.psum_scatter(key_grad.astype(jnp.bfloat16), 'grp', scatter_dimension=...]
    all_to_all x4 -> x2, starting transfers between devices: 29.9 us -> 8.45 us  [route(): lax.all_to_all(values.reshape(devices, rows // devices, features), ('pts'...]
    scatter x4 -> x0, local copies, waits for them, and re-layouts: 13.2 us -> none  [the longest x2 6.66 us: to_owners(): jnp.zeros((devices * capacity, features), jnp.bfloat16).at[send_slot]]
  transfers between devices with their start and end apart: 8 -> 11, of which waited for: 8 -> 9; matrix products, arithmetic and copies ran while one was open for 5% -> 3% of each run, Pallas kernels for 0% -> 3%
where the time goes in v1:
time: 329 us; the launch traced here: 328 us
  waiting for transfers between devices  196 us (60%)
  blocking collectives  46.7 us (14%)
  Pallas kernels  39.3 us (12%)
  between operations  13.9 us (4%)
  starting transfers between devices  12.7 us (4%)
  local copies, waits for them, and re-layouts  10.2 us (3%)
  other arithmetic  9.34 us (3%)
    psum x1, waiting for transfers between devices, on_device(): lax.psum((fine_projection_term, fine_output_term, pool_term, projection_t...  134 us
    all_to_all x2, blocking collectives, route(): lax.all_to_all(values.reshape(devices, rows // devices, features), ('pts'...  46.7 us
    pallas_call x9, Pallas kernels, call(): pl.pallas_call(kernel, out_shape=shapes, in_specs=in_specs, out_specs=[VM...  39.3 us
    all_gather x3, waiting for transfers between devices, on_device(): lax.all_gather(sums[2:], 'grp', axis=0, tiled=False)  39.1 us
    all_to_all x2, waiting for transfers between devices, route(): lax.all_to_all(values.reshape(devices, rows // devices, features), ('pts'...  16.4 us
    all_to_all x2, starting transfers between devices, route(): lax.all_to_all(values.reshape(devices, rows // devices, features), ('pts'...  8.45 us
  transfers between devices with their start and end apart: 11, of which 9 were waited for; matrix products, arithmetic and copies ran while one was open for 3% of the time, Pallas kernels for 3%

profile of v1, /device:TPU:1, one launch (start us, length us, event | category | flops | bytes accessed | tf_op | source)
XLA Modules:
  0.0 328.1 jit_solution(18299444464571837710)
XLA Ops:
  7.2 2.5 shard_map.153
  9.7 25.3 %all_to_all.20 = bf16[128,8,256]{2,1,0:T(8,128)(2,1)} all-to-all(bf16[128,8,256]{2,1,0:T(8,128)(2,1)} %bitcast.36), channel_id=1, replica_groups=mesh['pts'=64,'grp'=2] {'pts','grp'}, dimensions={0} | all-to-all | bytes 1048576 | tf_op jit(solution)/shard_map/all_to_all | solution.py:318
  35.0 5.2 %shard_map.154 = (bf16[1024,256]{1,0:T(8,128)(2,1)}, bf16[512,256]{1,0:T(8,128)(2,1)}, bf16[512,768]{1,0:T(8,128)(2,1)}, bf16[512,256]{1,0:T(8,128)(2,1)}, bf16[8,256,256]{2,1,0:T(8,128)(2,1)}) custom-call(bf16[1024,256]{1,0:T(8,128)(2,1)} %bitcast.26, s32[1,512]{1,0:T(1,128)} %get-tuple-element.29.receive_slot, f32[1,512]{1,0:T(1,128)} %get-tuple-element.30.live, ...), custom_call_target="tpu_custom_call" | custom-call | tf_op jit(solution)/shard_map/pallas_call | solution.py:302
  40.3 4.6 %all-to-all-start.1 = ((bf16[128,8,256]{2,1,0:T(8,128)(2,1)}), bf16[128,8,256]{2,1,0:T(8,128)(2,1)S(1)}, u32[]{:S(2)}, u32[]{:S(2)}) async-start(bf16[128,8,256]{2,1,0:T(8,128)(2,1)} %bitcast.35), calls=%async_computation.1 | async-start | bytes 1048576 | tf_op jit(solution)/shard_map/all_to_all | solution.py:318
  44.9 1.2 collective-permute-start.1
  48.1 10.5 %all-to-all-done.1 = bf16[128,8,256]{2,1,0:T(8,128)(2,1)S(1)} async-done(((bf16[128,8,256]{2,1,0:T(8,128)(2,1)}), bf16[128,8,256]{2,1,0:T(8,128)(2,1)S(1)}, u32[]{:S(2)}, u32[]{:S(2)}) %all-to-all-start.1) | async-done | bytes 524320 | tf_op jit(solution)/shard_map/all_to_all | solution.py:318
  59.4 2.2 shard_map.155.own_joined
  61.7 1.1 collective-permute-start
  62.8 1.4 collective-permute-done.other_joined
  64.9 9.0 %shard_map.156 = (bf16[256,512]{1,0:T(8,128)(2,1)}, bf16[512,512]{1,0:T(8,128)(2,1)}, bf16[256,1024]{1,0:T(8,128)(2,1)}, bf16[256,1024]{1,0:T(8,128)(2,1)}) custom-call(s32[1]{0:T(128)} %bitcast.group, bf16[256,512]{1,0:T(8,128)(2,1)} %shard_map.155.own_joined, bf16[256,512]{1,0:T(8,128)(2,1)} %copy-done.3, bf16[256,512]{1,0:T(8,128)(2,1)} %own_cotangent.3, ...), custom_call_target="tpu_custom_call" | custom-call | tf_op jit(solution)/shard_map/pallas_call | solution.py:302
  74.3 1.7 collective-permute-done.2.got
  76.8 4.4 %shard_map.157 = (bf16[256,512]{1,0:T(8,128)(2,1)}, bf16[256,512]{1,0:T(8,128)(2,1)}, bf16[1024,256]{1,0:T(8,128)(2,1)}) custom-call(s32[1]{0:T(128)} %bitcast.group, bf16[256,512]{1,0:T(8,128)(2,1)} %get-tuple-element.33.coarse, bf16[256,1024]{1,0:T(8,128)(2,1)} %get-tuple-element.34.keep, bf16[256,1024]{1,0:T(8,128)(2,1)} %copy-done.6, ...), custom_call_target="tpu_custom_call" | custom-call | tf_op jit(solution)/shard_map/pallas_call | solution.py:302
  81.2 3.8 %all-to-all-start.2 = ((bf16[128,8,256]{2,1,0:T(8,128)(2,1)}), bf16[128,8,256]{2,1,0:T(8,128)(2,1)S(1)}, u32[]{:S(2)}, u32[]{:S(2)}) async-start(bf16[128,8,256]{2,1,0:T(8,128)(2,1)} %bitcast.34), calls=%async_computation.2 | async-start | bytes 1048576 | tf_op jit(solution)/shard_map/all_to_all | solution.py:318
  85.1 1.3 collective-permute-start.3
  86.4 3.6 %shard_map.161 = (f32[512,768]{1,0:T(8,128)}, f32[256,512]{1,0:T(8,128)}) custom-call(bf16[512,512]{1,0:T(8,128)(2,1)} %get-tuple-element.46.unit, bf16[256,1024]{1,0:T(8,128)(2,1)} %get-tuple-element.34.keep, bf16[256,1024]{1,0:T(8,128)(2,1)} %get-tuple-element.35.give, bf16[256,512]{1,0:T(8,128)(2,1)} %own_cotangent.3, bf16[256,512]{1,0:T(8,128)(2,1)} %copy-done.4), custom_call_target="tpu_custom_call" | custom-call | tf_op jit(solution)/shard_map/pallas_call | solution.py:302
  90.7 2.3 shard_map.160
  93.0 5.8 %all-to-all-done.2 = bf16[128,8,256]{2,1,0:T(8,128)(2,1)S(1)} async-done(((bf16[128,8,256]{2,1,0:T(8,128)(2,1)}), bf16[128,8,256]{2,1,0:T(8,128)(2,1)S(1)}, u32[]{:S(2)}, u32[]{:S(2)}) %all-to-all-start.2) | async-done | bytes 524320 | tf_op jit(solution)/shard_map/all_to_all | solution.py:318
  98.9 0.8 copy-done.2
  99.7 7.7 %shard_map.158 = (bf16[1024,256]{1,0:T(8,128)(2,1)}, f32[256,768]{1,0:T(8,128)}, f32[256,256]{1,0:T(8,128)}) custom-call(bf16[1024,256]{1,0:T(8,128)(2,1)} %bitcast.28, s32[1,512]{1,0:T(1,128)} %get-tuple-element.29.receive_slot, bf16[512,256]{1,0:T(8,128)(2,1)} %get-tuple-element.38.rotated, bf16[512,768]{1,0:T(8,128)(2,1)} %get-tuple-element.39.projected, ...), custom_call_target="tpu_custom_call" | custom-call | tf_op jit(solution)/shard_map/pallas_call | solution.py:302
  107.5 133.6 %all-reduce.5.cloned.1.call-done = (f32[256,768]{1,0:T(8,128)}, f32[256,256]{1,0:T(8,128)}, f32[1,256,512]{2,1,0:T(8,128)}, f32[1,512,768]{2,1,0:T(8,128)}, f32[1,256,512]{2,1,0:T(8,128)}) async-done(((f32[256,768]{1,0:T(8,128)}, f32[256,256]{1,0:T(8,128)}, f32[1,256,512]{2,1,0:T(8,128)}, f32[1,512,768]{2,1,0:T(8,128)}, f32[1,256,512]{2,1,0:T(8,128)}), (f32[256,768]{1,0:T(8,128)}, f32[256,256]{1,0:T(8,128)}, ...) | async-done | bytes 3670032 | tf_op jit(solution)/shard_map/psum | solution.py:453
  243.0 21.4 %all_to_all.21 = bf16[128,8,256]{2,1,0:T(8,128)(2,1)} all-to-all(bf16[128,8,256]{2,1,0:T(8,128)(2,1)S(1)} %bitcast.33), channel_id=1, replica_groups=mesh['pts'=64,'grp'=2] {'pts','grp'}, dimensions={0} | all-to-all | bytes 1048576 | tf_op jit(solution)/shard_map/all_to_all | solution.py:318
  264.3 2.3 shard_map.159
  266.6 2.1 all-reduce.7.cloned.1.call-done
  268.7 1.7 broadcast_multiply_fusion.4
  270.4 2.1 broadcast_multiply_fusion.3
  272.5 11.2 %all-gather.4.cloned.1.call-done = f32[2,256,512]{2,1,0:T(8,128)} async-done(((f32[1,256,512]{2,1,0:T(8,128)}), f32[2,256,512]{2,1,0:T(8,128)}) %all-gather.4.cloned.1.call-update) | async-done | bytes 1048592 | tf_op jit(solution)/shard_map/all_gather | solution.py:457
  283.6 2.3 broadcast_multiply_fusion.2
  285.9 12.4 %all-gather.8.cloned.1.call-done = f32[2,256,512]{2,1,0:T(8,128)} async-done(((f32[1,256,512]{2,1,0:T(8,128)}), f32[2,256,512]{2,1,0:T(8,128)}) %all-gather.8.cloned.1.call-update) | async-done | bytes 1048592 | tf_op jit(solution)/shard_map/all_gather | solution.py:457
  298.3 2.3 broadcast_multiply_fusion.1
  300.6 15.5 %all-gather.6.cloned.1.call-done = f32[2,512,768]{2,1,0:T(8,128)} async-done(((f32[1,512,768]{2,1,0:T(8,128)}), f32[2,512,768]{2,1,0:T(8,128)}) %all-gather.6.cloned.1.call-update) | async-done | bytes 3145744 | tf_op jit(solution)/shard_map/all_gather | solution.py:457
  316.1 2.4 copy.25
  319.2 2.4 copy.27
  (36 shorter events, 8.0 us)
Async XLA Ops:
  7.2 37.7 %copy-start = (bf16[256,512]{1,0:T(8,128)(2,1)S(1)}, bf16[256,512]{1,0:T(8,128)(2,1)}, u32[]{:S(2)}) copy-start(bf16[256,512]{1,0:T(8,128)(2,1)} %own_cotangent.3) | copy-start | bytes 786436
  9.7 36.9 %copy-start.8 = (s32[1,512]{1,0:T(1,128)S(1)}, s32[1,512]{1,0:T(1,128)}, u32[]{:S(2)}) copy-start(s32[1,512]{1,0:T(1,128)} %get-tuple-element.32.slots) | copy-start | bytes 6148
  40.3 18.4 %all-to-all-start.1 = ((bf16[128,8,256]{2,1,0:T(8,128)(2,1)}), bf16[128,8,256]{2,1,0:T(8,128)(2,1)S(1)}, u32[]{:S(2)}, u32[]{:S(2)}) async-start(bf16[128,8,256]{2,1,0:T(8,128)(2,1)} %bitcast.35), calls=%async_computation.1 | async-start | bytes 1048576 | tf_op jit(solution)/shard_map/all_to_all | solution.py:318
  44.9 18.0 %collective-permute-start.1 = (bf16[256,512]{1,0:T(8,128)(2,1)S(1)}, bf16[256,512]{1,0:T(8,128)(2,1)S(1)}, u32[]{:S(2)}, u32[]{:S(2)}) collective-permute-start(bf16[256,512]{1,0:T(8,128)(2,1)S(1)} %copy-done), channel_id=1, source_target_pairs={{0,1},{1,0},{2,3},{3,2},{4,5},{5,4},{6,7},{7,6},{8,9},{9,8},{10,11... | collective-permute-start | bytes 786440 | tf_op jit(solution)/shard_map/ppermute | solution.py:313
  58.7 0.8 copy-start.1
  61.7 2.5 collective-permute-start
  62.8 1.4 copy-start.4
  64.2 0.7 copy-start.3
  73.9 2.1 collective-permute-start.2
  76.0 0.8 copy-start.6
  81.2 17.6 %all-to-all-start.2 = ((bf16[128,8,256]{2,1,0:T(8,128)(2,1)}), bf16[128,8,256]{2,1,0:T(8,128)(2,1)S(1)}, u32[]{:S(2)}, u32[]{:S(2)}) async-start(bf16[128,8,256]{2,1,0:T(8,128)(2,1)} %bitcast.34), calls=%async_computation.2 | async-start | bytes 1048576 | tf_op jit(solution)/shard_map/all_to_all | solution.py:318
  85.1 155.9 %all-reduce.5.cloned.1.call-start = ((), (), s32[]{:S(2)}) async-start(), calls=%async_computation.7 | async-start | bytes 7340032 | tf_op jit(solution)/shard_map/psum | solution.py:453
  85.1 4.9 %collective-permute-start.3 = (bf16[256,512]{1,0:T(8,128)(2,1)}, bf16[256,512]{1,0:T(8,128)(2,1)S(1)}, u32[]{:S(2)}, u32[]{:S(2)}) collective-permute-start(bf16[256,512]{1,0:T(8,128)(2,1)} %get-tuple-element.45.own_gradient), channel_id=1, source_target_pairs={{0,1},{1,0},{2,3},{3,2},{4,5},{5,4},{6,7},{7,6},{8,9},{9,8},{10,11... | collective-permute-start | bytes 786440 | tf_op jit(solution)/shard_map/ppermute | solution.py:313
  90.0 0.7 copy-start.7
  98.9 0.8 copy-start.2
  107.4 135.6 %copy-start.5 = (bf16[1024,256]{1,0:T(8,128)(2,1)S(1)}, bf16[1024,256]{1,0:T(8,128)(2,1)}, u32[]{:S(2)}) copy-start(bf16[1024,256]{1,0:T(8,128)(2,1)} %get-tuple-element.42) | copy-start | bytes 1572868
  107.4 161.3 %all-reduce.7.cloned.1.call-start = ((), (), s32[]{:S(2)}) async-start(), calls=%async_computation.8 | async-start | bytes 2097152 | tf_op jit(solution)/shard_map/psum | solution.py:456
  241.1 42.6 %all-gather.4.cloned.1.call-start = ((), (), s32[]{:S(2)}) async-start(), calls=%async_computation.4 | async-start | bytes 1572864 | tf_op jit(solution)/shard_map/all_gather | solution.py:457
  241.8 56.5 %all-gather.8.cloned.1.call-start = ((), (), s32[]{:S(2)}) async-start(), calls=%async_computation.6 | async-start | bytes 1572864 | tf_op jit(solution)/shard_map/all_gather | solution.py:457
  242.4 73.8 %all-gather.6.cloned.1.call-start = ((), (), s32[]{:S(2)}) async-start(), calls=%async_computation.5 | async-start | bytes 4718592 | tf_op jit(solution)/shard_map/all_gather | solution.py:457
Sparse Core Ops, SparseCore 0:
  107.5 133.4 all-reduce.4
  243.5 25.1 all-reduce.6
  270.5 13.0 all-gather.3
  285.2 13.0 all-gather.7
  299.9 16.1 all-gather.5

commit v2 on v1

--- a/solution.py
+++ b/solution.py
@@ -1,3 +1,4 @@
+import functools
 import math
 
 import jax
@@ -219,21 +220,63 @@
 
 
 def coarse_weights_kernel(
-    unit, keep, give, own_cotangent, other_cotangent, projection_term, output_term
+    group,
+    unit,
+    keep,
+    give,
+    own_cotangent,
+    other_cotangent,
+    own_joined,
+    other_joined,
+    own_gradient,
+    other_gradient,
+    terms,
 ):
     part = keep.shape[1] // 4
+    first = pl.multiple_of(group[0] * part, part)
     stacked = jnp.concatenate([keep[...], give[...]], axis=0)
     cotangent = jnp.concatenate([own_cotangent[...], other_cotangent[...]], axis=0)
-    projection_term[...] = mm(unit[...], stacked[:, part:], (0, 0))
-    output_term[...] = mm(stacked[:, :part], cotangent, (0, 0))
-
-
-def pool_weights_kernel(group, own_joined, other_joined, own_gradient, other_gradient, term):
-    part = term.shape[0]
-    first = pl.multiple_of(group[0] * part, part)
-    term[...] = mm(own_joined[:, pl.ds(first, part)], own_gradient[...], (0, 0)) + mm(
+    terms[:, : 3 * part] = mm(unit[...], stacked[:, part:], (0, 0)).astype(BF)
+    output_term = mm(stacked[:, :part], cotangent, (0, 0)).astype(BF)
+    pool_term = mm(own_joined[:, pl.ds(first, part)], own_gradient[...], (0, 0)) + mm(
         other_joined[:, pl.ds(first, part)], other_gradient[...], (0, 0)
     )
+    pool_term = pool_term.astype(BF)
+    for side in range(2):
+        rows, columns = slice(side * part, (side + 1) * part), slice(side * part, (side + 1) * part)
+        terms[rows, 3 * part : 4 * part] = output_term[:, columns]
+        terms[rows, 4 * part :] = pool_term[:, columns]
+
+
+def sum_kernel(arrived, spread):
+    total = jnp.sum(arrived[...].astype(F32), axis=0, keepdims=True).astype(BF)
+    spread[...] = jnp.broadcast_to(total, spread.shape)
+
+
+def coarse_sums_kernel(group, own, other, pool, projection, output, *, scaling):
+    wide = pool.shape[1]
+    part = wide // 2
+    for terms, index in ((own, group[0]), (other, 1 - group[0])):
+        first = pl.multiple_of(index * part, part)
+        for at in range(3):
+            projection[:, pl.ds(at * wide + first, part)] = (
+                terms[:, at * part : (at + 1) * part].astype(F32) * scaling
+            )
+        for side in range(2):
+            rows, columns = slice(side * part, (side + 1) * part), slice(side * part, (side + 1) * part)
+            output[pl.ds(first, part), columns] = (
+                terms[rows, 3 * part : 4 * part].astype(F32) * scaling
+            )
+            pool[pl.ds(first, part), columns] = terms[rows, 4 * part :].astype(F32) * scaling
+
+
+def fine_sums_kernel(terms, projection, output, *, scaling):
+    features = output.shape[0]
+    for at in range(3):
+        projection[:, at * features : (at + 1) * features] = (
+            terms[at * features : (at + 1) * features, :].astype(F32) * scaling
+        )
+    output[...] = terms[3 * features :, :].astype(F32) * scaling
 
 
 def fine_backward_kernel(
@@ -246,8 +289,7 @@
     projection,
     output,
     send,
-    projection_term,
-    output_term,
+    terms,
     grad_projected,
 ):
     place = one_hot(receive_slot[...], arrived.shape[0])
@@ -255,7 +297,7 @@
     gradient_rows = gradient_in.astype(BF)
     features = rotated.shape[1]
     entering = mm(gradient_rows, output[...], (1, 1)).astype(BF)
-    output_term[...] = mm(mixture[...], gradient_rows, (0, 0))
+    terms[3 * features :, :] = mm(mixture[...], gradient_rows, (0, 0)).astype(BF)
     balls = rotated.shape[0] // BALL
     pairs = features // PAIR
     for ball in range(balls):
@@ -279,7 +321,10 @@
                 target = at * features + pair * PAIR
                 grad_projected[rows, target : target + PAIR] = both
     normed, inverse = normalize(rotated[...])
-    projection_term[...] = mm(normed.astype(BF), grad_projected[...], (0, 0))
+    unit_rows = normed.astype(BF)
+    for at in range(3):
+        columns = slice(at * features, (at + 1) * features)
+        terms[columns, :] = mm(unit_rows, grad_projected[:, columns], (0, 0)).astype(BF)
     back = mm(grad_projected[...], projection[...], (1, 1))
     result = (gradient_in + norm_backward(back, normed, inverse)).astype(BF)
     send[...] = mm(place, result).astype(BF)
@@ -313,16 +358,23 @@
     return lax.ppermute(values, "grp", [(0, 1), (1, 0)])
 
 
+def spread_blocks(values, axes):
+    return lax.all_to_all(values, axes, split_axis=0, concat_axis=0, tiled=True)
+
+
 def route(values, devices):
     rows, features = values.shape
-    arrived = lax.all_to_all(
-        values.reshape(devices, rows // devices, features),
-        ("pts", "grp"),
-        split_axis=0,
-        concat_axis=0,
-        tiled=True,
-    )
-    return arrived.reshape(rows, features)
+    blocks = values.reshape(devices, rows // devices, features)
+    return spread_blocks(blocks, ("pts", "grp")).reshape(rows, features)
+
+
+def sum_over(terms, axes):
+    rows, columns = terms.shape
+    owners = lax.axis_size(axes)
+    blocks = (owners, rows // owners, columns)
+    arrived = spread_blocks(terms.reshape(blocks), axes)
+    (spread,) = call(sum_kernel, (arrived,), ((blocks, BF),))
+    return spread_blocks(spread, axes).reshape(rows, columns)
 
 
 def on_device(
@@ -416,19 +468,27 @@
         scalar=True,
     )
     arrived = route(send, devices)
-    projection_term, output_term = call(
+    other_gradient = exchange(coarse_gradient)
+    (coarse_terms,) = call(
         coarse_weights_kernel,
-        (unit, keep, give, coarse_cotangent, other_cotangent),
-        (((wide, 3 * wide // 2), F32), ((wide // 2, wide), F32)),
-    )
-    other_gradient = exchange(coarse_gradient)
-    (pool_term,) = call(
-        pool_weights_kernel,
-        (group, own_joined, other_joined, coarse_gradient, other_gradient),
-        (((wide // 2, wide), F32),),
+        (
+            group,
+            unit,
+            keep,
+            give,
+            coarse_cotangent,
+            other_cotangent,
+            own_joined,
+            other_joined,
+            coarse_gradient,
+            other_gradient,
+        ),
+        (((wide, 5 * wide // 2), BF),),
         scalar=True,
     )
-    send, fine_projection_term, fine_output_term = call(
+    own_sums = sum_over(coarse_terms, "pts")
+    other_sums = exchange(own_sums)
+    send, fine_terms = call(
         fine_backward_kernel,
         (
             arrived,
@@ -440,30 +500,31 @@
             fine_projection,
             fine_output,
         ),
-        (
-            ((slots, features), BF),
-            ((features, 3 * features), F32),
-            ((features, features), F32),
-        ),
+        (((slots, features), BF), ((4 * features, features), BF)),
         scratch=(pltpu.VMEM((count, 3 * features), BF),),
     )
+    fine_sums = sum_over(fine_terms, ("pts", "grp"))
     arrived = route(send, devices)
     (points_gradient,) = call(take_kernel, (arrived, send_slot), (((count, features), BF),))
-
-    sums = lax.psum(
-        (fine_projection_term, fine_output_term, pool_term, projection_term, output_term), "pts"
-    )
-    fine_projection_sum, fine_output_sum = lax.psum(sums[:2], "grp")
-    pool_sum, projection_sum, output_sum = lax.all_gather(sums[2:], "grp", axis=0, tiled=False)
-    projection_sum = projection_sum.reshape(2, wide, 3, wide // 2).transpose(1, 2, 0, 3)
+    pool_sum, projection_sum, output_sum = call(
+        functools.partial(coarse_sums_kernel, scaling=scaling),
+        (group, own_sums, other_sums),
+        (((wide, wide), F32), ((wide, 3 * wide), F32), ((wide, wide), F32)),
+        scalar=True,
+    )
+    fine_projection_sum, fine_output_sum = call(
+        functools.partial(fine_sums_kernel, scaling=scaling),
+        (fine_sums,),
+        (((features, 3 * features), F32), ((features, features), F32)),
+    )
     return (
         coarse_result,
         points_gradient,
-        fine_projection_sum * scaling,
-        fine_output_sum * scaling,
-        pool_sum.reshape(wide, wide) * scaling,
-        projection_sum.reshape(wide, 3 * wide) * scaling,
-        output_sum.reshape(wide, wide) * scaling,
+        fine_projection_sum,
+        fine_output_sum,
+        pool_sum,
+        projection_sum,
+        output_sum,
     )
 
 

time: 329 us -> 216 us (0.66)
  waiting for transfers between devices: 196 us -> 73.5 us
  starting transfers between devices: 12.7 us -> 35.9 us
  between operations: 13.9 us -> 0.74 us
  Pallas kernels: 39.3 us -> 48.1 us
  other arithmetic: 9.34 us -> 0.66 us
  local copies, waits for them, and re-layouts: 10.2 us -> 5.92 us
  blocking collectives: 46.7 us -> 50.5 us
    psum x2 -> x0, waiting for transfers between devices: 136 us -> none  [the longest x1 134 us: on_device(): lax.psum((fine_projection_term, fine_output_term, pool_term, projection_t...]
    all_to_all x2 -> x6, waiting for transfers between devices: 16.4 us -> 69 us  [spread_blocks(): return lax.all_to_all(values, axes, split_axis=0, concat_axis=0, tiled=True)]
    all_gather x3 -> x0, waiting for transfers between devices: 39.1 us -> none  [on_device(): lax.all_gather(sums[2:], 'grp', axis=0, tiled=False)]
    all_to_all x2 -> x6, starting transfers between devices: 8.45 us -> 31.4 us  [spread_blocks(): return lax.all_to_all(values, axes, split_axis=0, concat_axis=0, tiled=True)]
    pallas_call x9 -> x12, Pallas kernels: 39.3 us -> 48.1 us  [call(): pl.pallas_call(kernel, out_shape=shapes, in_specs=in_specs, out_specs=[VM...]
    mul x5 -> x0, other arithmetic: 8.68 us -> none  [the longest x1 2.29 us: on_device(): pool_sum.reshape(wide, wide) * scaling]
    all_to_all x2, blocking collectives: 46.7 us -> 50.5 us  [spread_blocks(): return lax.all_to_all(values, axes, split_axis=0, concat_axis=0, tiled=True)]
  transfers between devices with their start and end apart: 11 -> 11, of which waited for: 9 -> 9; matrix products, arithmetic and copies ran while one was open for 3% -> 1% of each run, Pallas kernels for 3% -> 9%
where the time goes in v2:
time: 216 us; the launch traced here: 215 us
  waiting for transfers between devices  73.5 us (34%)
  blocking collectives  50.5 us (23%)
  Pallas kernels  48.1 us (22%)
  starting transfers between devices  35.9 us (17%)
  local copies, waits for them, and re-layouts  5.92 us (3%)
    all_to_all x6, waiting for transfers between devices, spread_blocks(): return lax.all_to_all(values, axes, split_axis=0, concat_axis=0, tiled=True)  69 us
    all_to_all x2, blocking collectives, spread_blocks(): return lax.all_to_all(values, axes, split_axis=0, concat_axis=0, tiled=True)  50.5 us
    pallas_call x12, Pallas kernels, call(): pl.pallas_call(kernel, out_shape=shapes, in_specs=in_specs, out_specs=[VM...  48.1 us
    all_to_all x6, starting transfers between devices, spread_blocks(): return lax.all_to_all(values, axes, split_axis=0, concat_axis=0, tiled=True)  31.4 us
    unnamed x24, local copies, waits for them, and re-layouts  4.6 us
    ppermute x5, waiting for transfers between devices, exchange(): return lax.ppermute(values, 'grp', [(0, 1), (1, 0)])  4.49 us
    ppermute x5, starting transfers between devices, exchange(): return lax.ppermute(values, 'grp', [(0, 1), (1, 0)])  4.45 us
  transfers between devices with their start and end apart: 11, of which 9 were waited for; matrix products, arithmetic and copies ran while one was open for 1% of the time, Pallas kernels for 9%

profile of v2, /device:TPU:1, one launch (start us, length us, event | category | flops | bytes accessed | tf_op | source)
XLA Modules:
  0.0 215.3 jit_solution(18089275451911933622)
XLA Ops:
  0.6 2.5 %shard_map.153 = (bf16[1024,256]{1,0:T(8,128)(2,1)}, s32[1,512]{1,0:T(1,128)}, s32[1,512]{1,0:T(1,128)}, f32[1,512]{1,0:T(1,128)}) custom-call(s32[1,512]{1,0:T(1,128)} %bitcast.31, s32[1,512]{1,0:T(1,128)} %bitcast.32, s32[1,256]{1,0:T(1,128)} %bitcast.33, bf16[512,256]{1,0:T(8,128)(2,1)} %points.1), custom_call_target="tpu_custom_call" | custom-call | tf_op jit(solution)/shard_map/pallas_call | solution.py:347
  3.1 25.3 %all_to_all.40 = bf16[128,8,256]{2,1,0:T(8,128)(2,1)} all-to-all(bf16[128,8,256]{2,1,0:T(8,128)(2,1)} %bitcast.28), channel_id=1, replica_groups=mesh['pts'=64,'grp'=2] {'pts','grp'}, dimensions={0} | all-to-all | bytes 1048576 | tf_op jit(solution)/shard_map/all_to_all | solution.py:362
  28.4 5.3 %shard_map.154 = (bf16[1024,256]{1,0:T(8,128)(2,1)}, bf16[512,256]{1,0:T(8,128)(2,1)}, bf16[512,768]{1,0:T(8,128)(2,1)}, bf16[512,256]{1,0:T(8,128)(2,1)}, bf16[8,256,256]{2,1,0:T(8,128)(2,1)}) custom-call(bf16[1024,256]{1,0:T(8,128)(2,1)} %bitcast.23, s32[1,512]{1,0:T(1,128)} %get-tuple-element.31.receive_slot, f32[1,512]{1,0:T(1,128)} %get-tuple-element.32.live, ...), custom_call_target="tpu_custom_call" | custom-call | tf_op jit(solution)/shard_map/pallas_call | solution.py:347
  33.7 4.6 %all-to-all-start.1 = ((bf16[128,8,256]{2,1,0:T(8,128)(2,1)}), bf16[128,8,256]{2,1,0:T(8,128)(2,1)S(1)}, u32[]{:S(2)}, u32[]{:S(2)}) async-start(bf16[128,8,256]{2,1,0:T(8,128)(2,1)} %bitcast.26), calls=%async_computation.1 | async-start | bytes 1048576 | tf_op jit(solution)/shard_map/all_to_all | solution.py:362
  38.3 1.2 collective-permute-start.1
  41.6 10.5 %all-to-all-done.1 = bf16[128,8,256]{2,1,0:T(8,128)(2,1)S(1)} async-done(((bf16[128,8,256]{2,1,0:T(8,128)(2,1)}), bf16[128,8,256]{2,1,0:T(8,128)(2,1)S(1)}, u32[]{:S(2)}, u32[]{:S(2)}) %all-to-all-start.1) | async-done | bytes 524320 | tf_op jit(solution)/shard_map/all_to_all | solution.py:362
  52.9 2.2 %shard_map.155.own_joined = bf16[256,512]{1,0:T(8,128)(2,1)} custom-call(bf16[1024,256]{1,0:T(8,128)(2,1)} %bitcast.20, s32[2,256]{1,0:T(2,128)} %bitcast.29), custom_call_target="tpu_custom_call" | custom-call | tf_op jit(solution)/shard_map/pallas_call | solution.py:347
  55.1 1.1 collective-permute-start
  56.3 1.4 collective-permute-done.other_joined
  58.4 8.9 %shard_map.156 = (bf16[256,512]{1,0:T(8,128)(2,1)}, bf16[512,512]{1,0:T(8,128)(2,1)}, bf16[256,1024]{1,0:T(8,128)(2,1)}, bf16[256,1024]{1,0:T(8,128)(2,1)}) custom-call(s32[1]{0:T(128)} %bitcast.group, bf16[256,512]{1,0:T(8,128)(2,1)} %shard_map.155.own_joined, bf16[256,512]{1,0:T(8,128)(2,1)} %copy-done.8, bf16[256,512]{1,0:T(8,128)(2,1)} %own_cotangent.3, ...), custom_call_target="tpu_custom_call" | custom-call | tf_op jit(solution)/shard_map/pallas_call | solution.py:347
  67.7 1.7 collective-permute-done.2.got
  70.2 4.5 %shard_map.157 = (bf16[256,512]{1,0:T(8,128)(2,1)}, bf16[256,512]{1,0:T(8,128)(2,1)}, bf16[1024,256]{1,0:T(8,128)(2,1)}) custom-call(s32[1]{0:T(128)} %bitcast.group, bf16[256,512]{1,0:T(8,128)(2,1)} %get-tuple-element.35.coarse, bf16[256,1024]{1,0:T(8,128)(2,1)} %get-tuple-element.36.keep, bf16[256,1024]{1,0:T(8,128)(2,1)} %copy-done.9, ...), custom_call_target="tpu_custom_call" | custom-call | tf_op jit(solution)/shard_map/pallas_call | solution.py:347
  75.1 1.4 collective-permute-done.3.other_gradient
  77.1 3.8 %shard_map.162 = bf16[512,1280]{1,0:T(8,128)(2,1)} custom-call(s32[1]{0:T(128)} %bitcast.group, bf16[512,512]{1,0:T(8,128)(2,1)} %get-tuple-element.48.unit, bf16[256,1024]{1,0:T(8,128)(2,1)} %get-tuple-element.36.keep, bf16[256,1024]{1,0:T(8,128)(2,1)} %get-tuple-element.37.give, bf16[256,512]{1,0:T(8,128)(2,1)} %own_cotangent.3, ...), custom_call_target="tpu_custom_call" | custom-call | tf_op jit(solution)/shard_map/pallas_call | solution.py:347
  80.9 25.2 %all_to_all.41.arrived = bf16[64,8,1280]{2,1,0:T(8,128)(2,1)} all-to-all(bf16[64,8,1280]{2,1,0:T(8,128)(2,1)} %bitcast.17), channel_id=1, replica_groups=mesh['pts'=64,'grp'=2] {'pts'}, dimensions={0} | all-to-all | bytes 2621440 | tf_op jit(solution)/shard_map/all_to_all | solution.py:362
  106.1 6.0 %all-to-all-start.2 = ((bf16[128,8,256]{2,1,0:T(8,128)(2,1)}), bf16[128,8,256]{2,1,0:T(8,128)(2,1)S(1)}, u32[]{:S(2)}, u32[]{:S(2)}) async-start(bf16[128,8,256]{2,1,0:T(8,128)(2,1)} %bitcast.9), calls=%async_computation.2 | async-start | bytes 1048576 | tf_op jit(solution)/shard_map/all_to_all | solution.py:362
  112.2 2.6 %shard_map.163 = bf16[64,8,1280]{2,1,0:T(8,128)(2,1)} custom-call(bf16[64,8,1280]{2,1,0:T(8,128)(2,1)} %all_to_all.41.arrived), custom_call_target="tpu_custom_call" | custom-call | tf_op jit(solution)/shard_map/pallas_call | solution.py:347
  114.8 11.2 %all-to-all-done.2 = bf16[128,8,256]{2,1,0:T(8,128)(2,1)S(1)} async-done(((bf16[128,8,256]{2,1,0:T(8,128)(2,1)}), bf16[128,8,256]{2,1,0:T(8,128)(2,1)S(1)}, u32[]{:S(2)}, u32[]{:S(2)}) %all-to-all-start.2) | async-done | bytes 524320 | tf_op jit(solution)/shard_map/all_to_all | solution.py:362
  126.8 4.9 %all-to-all-start.7 = ((bf16[64,8,1280]{2,1,0:T(8,128)(2,1)}), bf16[64,8,1280]{2,1,0:T(8,128)(2,1)S(1)}, u32[]{:S(2)}, u32[]{:S(2)}) async-start(bf16[64,8,1280]{2,1,0:T(8,128)(2,1)} %shard_map.163), calls=%async_computation.7 | async-start | bytes 2621440 | tf_op jit(solution)/shard_map/all_to_all | solution.py:362
  131.7 7.7 %shard_map.158 = (bf16[1024,256]{1,0:T(8,128)(2,1)}, bf16[1024,256]{1,0:T(8,128)(2,1)}) custom-call(bf16[1024,256]{1,0:T(8,128)(2,1)} %bitcast.24, s32[1,512]{1,0:T(1,128)} %get-tuple-element.31.receive_slot, bf16[512,256]{1,0:T(8,128)(2,1)} %get-tuple-element.40.rotated, bf16[512,768]{1,0:T(8,128)(2,1)} %get-tuple-element.41.projected, ...), custom_call_target="tpu_custom_call" | custom-call | tf_op jit(solution)/shard_map/pallas_call | solution.py:347
  139.4 11.4 %all-to-all-done.7 = bf16[64,8,1280]{2,1,0:T(8,128)(2,1)S(1)} async-done(((bf16[64,8,1280]{2,1,0:T(8,128)(2,1)}), bf16[64,8,1280]{2,1,0:T(8,128)(2,1)S(1)}, u32[]{:S(2)}, u32[]{:S(2)}) %all-to-all-start.7) | async-done | bytes 1310752 | tf_op jit(solution)/shard_map/all_to_all | solution.py:362
  150.8 6.7 %all-to-all-start.4 = ((bf16[128,8,256]{2,1,0:T(8,128)(2,1)}), bf16[128,8,256]{2,1,0:T(8,128)(2,1)S(1)}, u32[]{:S(2)}, u32[]{:S(2)}) async-start(bf16[128,8,256]{2,1,0:T(8,128)(2,1)} %bitcast.27), calls=%async_computation.4 | async-start | bytes 1048576 | tf_op jit(solution)/shard_map/all_to_all | solution.py:362
  157.5 1.3 collective-permute-start.4
  158.8 12.5 %all-to-all-done.4.arrived = bf16[128,8,256]{2,1,0:T(8,128)(2,1)S(1)} async-done(((bf16[128,8,256]{2,1,0:T(8,128)(2,1)}), bf16[128,8,256]{2,1,0:T(8,128)(2,1)S(1)}, u32[]{:S(2)}, u32[]{:S(2)}) %all-to-all-start.4) | async-done | bytes 524320 | tf_op jit(solution)/shard_map/all_to_all | solution.py:362
  171.4 4.6 %all-to-all-start.3 = ((bf16[128,8,256]{2,1,0:T(8,128)(2,1)}), bf16[128,8,256]{2,1,0:T(8,128)(2,1)S(1)}, u32[]{:S(2)}, u32[]{:S(2)}) async-start(bf16[128,8,256]{2,1,0:T(8,128)(2,1)} %bitcast.25), calls=%async_computation.3 | async-start | bytes 1048576 | tf_op jit(solution)/shard_map/all_to_all | solution.py:362
  176.0 2.0 shard_map.160
  178.0 11.8 %all-to-all-done.3 = bf16[128,8,256]{2,1,0:T(8,128)(2,1)S(1)} async-done(((bf16[128,8,256]{2,1,0:T(8,128)(2,1)}), bf16[128,8,256]{2,1,0:T(8,128)(2,1)S(1)}, u32[]{:S(2)}, u32[]{:S(2)}) %all-to-all-start.3) | async-done | bytes 524320 | tf_op jit(solution)/shard_map/all_to_all | solution.py:362
  189.7 4.6 %all-to-all-start.5 = ((bf16[128,8,256]{2,1,0:T(8,128)(2,1)}), bf16[128,8,256]{2,1,0:T(8,128)(2,1)S(1)}, u32[]{:S(2)}, u32[]{:S(2)}) async-start(bf16[128,8,256]{2,1,0:T(8,128)(2,1)} %shard_map.160), calls=%async_computation.5 | async-start | bytes 1048576 | tf_op jit(solution)/shard_map/all_to_all | solution.py:362
  194.4 2.2 %shard_map.159 = bf16[512,256]{1,0:T(8,128)(2,1)} custom-call(bf16[1024,256]{1,0:T(8,128)(2,1)} %bitcast.21, s32[1,512]{1,0:T(1,128)} %get-tuple-element.34.slots), custom_call_target="tpu_custom_call" | custom-call | tf_op jit(solution)/shard_map/pallas_call | solution.py:347
  196.6 11.5 %all-to-all-done.5 = bf16[128,8,256]{2,1,0:T(8,128)(2,1)S(1)} async-done(((bf16[128,8,256]{2,1,0:T(8,128)(2,1)}), bf16[128,8,256]{2,1,0:T(8,128)(2,1)S(1)}, u32[]{:S(2)}, u32[]{:S(2)}) %all-to-all-start.5) | async-done | bytes 524320 | tf_op jit(solution)/shard_map/all_to_all | solution.py:362
  208.9 2.1 shard_map.161
  211.0 4.4 %shard_map.164 = (f32[512,512]{1,0:T(8,128)}, f32[512,1536]{1,0:T(8,128)}, f32[512,512]{1,0:T(8,128)}) custom-call(s32[1]{0:T(128)} %bitcast.group, bf16[512,1280]{1,0:T(8,128)(2,1)} %bitcast.19, bf16[512,1280]{1,0:T(8,128)(2,1)} %collective-permute-done.4.other), custom_call_target="tpu_custom_call" | custom-call | tf_op jit(solution)/shard_map/pallas_call | solution.py:347
  (32 shorter events, 7.4 us)
Async XLA Ops:
  28.4 9.9 %copy-start.1 = (bf16[256,512]{1,0:T(8,128)(2,1)S(1)}, bf16[256,512]{1,0:T(8,128)(2,1)}, u32[]{:S(2)}) copy-start(bf16[256,512]{1,0:T(8,128)(2,1)} %own_cotangent.3) | copy-start | bytes 786436
  28.4 11.7 %copy-start.11 = (s32[1,512]{1,0:T(1,128)S(1)}, s32[1,512]{1,0:T(1,128)}, u32[]{:S(2)}) copy-start(s32[1,512]{1,0:T(1,128)} %get-tuple-element.34.slots) | copy-start | bytes 6148
  33.7 18.4 %all-to-all-start.1 = ((bf16[128,8,256]{2,1,0:T(8,128)(2,1)}), bf16[128,8,256]{2,1,0:T(8,128)(2,1)S(1)}, u32[]{:S(2)}, u32[]{:S(2)}) async-start(bf16[128,8,256]{2,1,0:T(8,128)(2,1)} %bitcast.26), calls=%async_computation.1 | async-start | bytes 1048576 | tf_op jit(solution)/shard_map/all_to_all | solution.py:362
  38.3 18.0 %collective-permute-start.1 = (bf16[256,512]{1,0:T(8,128)(2,1)S(1)}, bf16[256,512]{1,0:T(8,128)(2,1)S(1)}, u32[]{:S(2)}, u32[]{:S(2)}) collective-permute-start(bf16[256,512]{1,0:T(8,128)(2,1)S(1)} %copy-done.1), channel_id=1, source_target_pairs={{0,1},{1,0},{2,3},{3,2},{4,5},{5,4},{6,7},{7,6},{8,9},{9,8},{10,11... | collective-permute-start | bytes 786440 | tf_op jit(solution)/shard_map/ppermute | solution.py:358
  52.1 0.8 copy-start.2
  55.1 2.5 %collective-permute-start = (bf16[256,512]{1,0:T(8,128)(2,1)}, bf16[256,512]{1,0:T(8,128)(2,1)S(1)}, u32[]{:S(2)}, u32[]{:S(2)}) collective-permute-start(bf16[256,512]{1,0:T(8,128)(2,1)} %shard_map.155.own_joined), channel_id=1, source_target_pairs={{0,1},{1,0},{2,3},{3,2},{4,5},{5,4},{6,7},{7,6},{8,9},{9,8},{10,11... | collective-permute-start | bytes 786440 | tf_op jit(solution)/shard_map/ppermute | solution.py:358
  56.3 1.4 copy-start.7
  57.7 0.7 copy-start.8
  67.3 2.1 collective-permute-start.2
  69.5 0.8 copy-start.9
  74.7 1.7 collective-permute-start.3
  76.4 0.7 copy-start.10
  106.1 19.8 %all-to-all-start.2 = ((bf16[128,8,256]{2,1,0:T(8,128)(2,1)}), bf16[128,8,256]{2,1,0:T(8,128)(2,1)S(1)}, u32[]{:S(2)}, u32[]{:S(2)}) async-start(bf16[128,8,256]{2,1,0:T(8,128)(2,1)} %bitcast.9), calls=%async_computation.2 | async-start | bytes 1048576 | tf_op jit(solution)/shard_map/all_to_all | solution.py:362
  126.0 0.8 copy-start.6
  126.8 24.0 %all-to-all-start.7 = ((bf16[64,8,1280]{2,1,0:T(8,128)(2,1)}), bf16[64,8,1280]{2,1,0:T(8,128)(2,1)S(1)}, u32[]{:S(2)}, u32[]{:S(2)}) async-start(bf16[64,8,1280]{2,1,0:T(8,128)(2,1)} %shard_map.163), calls=%async_computation.7 | async-start | bytes 2621440 | tf_op jit(solution)/shard_map/all_to_all | solution.py:362
  150.8 27.2 %copy-start = (bf16[64,8,1280]{2,1,0:T(8,128)(2,1)}, bf16[64,8,1280]{2,1,0:T(8,128)(2,1)S(1)}, u32[]{:S(2)}) copy-start(bf16[64,8,1280]{2,1,0:T(8,128)(2,1)S(1)} %all-to-all-done.7) | copy-start | bytes 3932164
  150.8 20.5 %all-to-all-start.4 = ((bf16[128,8,256]{2,1,0:T(8,128)(2,1)}), bf16[128,8,256]{2,1,0:T(8,128)(2,1)S(1)}, u32[]{:S(2)}, u32[]{:S(2)}) async-start(bf16[128,8,256]{2,1,0:T(8,128)(2,1)} %bitcast.27), calls=%async_computation.4 | async-start | bytes 1048576 | tf_op jit(solution)/shard_map/all_to_all | solution.py:362
  157.5 53.4 %collective-permute-start.4 = (bf16[512,1280]{1,0:T(8,128)(2,1)S(1)}, bf16[512,1280]{1,0:T(8,128)(2,1)}, u32[]{:S(2)}, u32[]{:S(2)}) collective-permute-start(bf16[512,1280]{1,0:T(8,128)(2,1)S(1)} %bitcast.18), channel_id=1, source_target_pairs={{0,1},{1,0},{2,3},{3,2},{4,5},{5,4},{6,7},{7,6},{8,9},{9,8},{10,11... | collective-permute-start | bytes 3932168 | tf_op jit(solution)/shard_map/ppermute | solution.py:358
  171.4 4.6 %copy-start.3 = (bf16[128,8,256]{2,1,0:T(8,128)(2,1)}, bf16[128,8,256]{2,1,0:T(8,128)(2,1)S(1)}, u32[]{:S(2)}) copy-start(bf16[128,8,256]{2,1,0:T(8,128)(2,1)S(1)} %all-to-all-done.4.arrived) | copy-start | bytes 1572868
  171.4 18.4 %all-to-all-start.3 = ((bf16[128,8,256]{2,1,0:T(8,128)(2,1)}), bf16[128,8,256]{2,1,0:T(8,128)(2,1)S(1)}, u32[]{:S(2)}, u32[]{:S(2)}) async-start(bf16[128,8,256]{2,1,0:T(8,128)(2,1)} %bitcast.25), calls=%async_computation.3 | async-start | bytes 1048576 | tf_op jit(solution)/shard_map/all_to_all | solution.py:362
  189.7 4.6 %copy-start.4 = (bf16[128,8,256]{2,1,0:T(8,128)(2,1)}, bf16[128,8,256]{2,1,0:T(8,128)(2,1)S(1)}, u32[]{:S(2)}) copy-start(bf16[128,8,256]{2,1,0:T(8,128)(2,1)S(1)} %all-to-all-done.3) | copy-start | bytes 1572868
  189.7 18.4 %all-to-all-start.5 = ((bf16[128,8,256]{2,1,0:T(8,128)(2,1)}), bf16[128,8,256]{2,1,0:T(8,128)(2,1)S(1)}, u32[]{:S(2)}, u32[]{:S(2)}) async-start(bf16[128,8,256]{2,1,0:T(8,128)(2,1)} %shard_map.160), calls=%async_computation.5 | async-start | bytes 1048576 | tf_op jit(solution)/shard_map/all_to_all | solution.py:362
  208.1 0.8 copy-start.5

commit v3 on v2

--- a/solution.py
+++ b/solution.py
@@ -236,47 +236,83 @@
     first = pl.multiple_of(group[0] * part, part)
     stacked = jnp.concatenate([keep[...], give[...]], axis=0)
     cotangent = jnp.concatenate([own_cotangent[...], other_cotangent[...]], axis=0)
-    terms[:, : 3 * part] = mm(unit[...], stacked[:, part:], (0, 0)).astype(BF)
-    output_term = mm(stacked[:, :part], cotangent, (0, 0)).astype(BF)
+    projection_term = mm(unit[...], stacked[:, part:], (0, 0))
+    output_term = mm(stacked[:, :part], cotangent, (0, 0))
     pool_term = mm(own_joined[:, pl.ds(first, part)], own_gradient[...], (0, 0)) + mm(
         other_joined[:, pl.ds(first, part)], other_gradient[...], (0, 0)
     )
-    pool_term = pool_term.astype(BF)
+    across = projection_term.shape[1] // 2
     for side in range(2):
-        rows, columns = slice(side * part, (side + 1) * part), slice(side * part, (side + 1) * part)
-        terms[rows, 3 * part : 4 * part] = output_term[:, columns]
-        terms[rows, 4 * part :] = pool_term[:, columns]
-
-
-def sum_kernel(arrived, spread):
-    total = jnp.sum(arrived[...].astype(F32), axis=0, keepdims=True).astype(BF)
-    spread[...] = jnp.broadcast_to(total, spread.shape)
-
-
-def coarse_sums_kernel(group, own, other, pool, projection, output, *, scaling):
-    wide = pool.shape[1]
+        columns = projection_term[:, side * across : (side + 1) * across]
+        put_blocks(terms, side, 0, columns)
+        for at, term in enumerate((output_term, pool_term)):
+            width = term.shape[1] // 4
+            stack = [term[:, (2 * side + k) * width : (2 * side + k + 1) * width] for k in range(2)]
+            put_blocks(terms, side, across + at * width, jnp.concatenate(stack, axis=0))
+
+
+def put_blocks(blocks, side, lane, rows):
+    owners, width = blocks.shape[0], rows.shape[1]
+    pieces = rows.reshape(owners, rows.shape[0] // owners, width)
+    blocks[:, side, :, lane : lane + width] = pieces.astype(BF)
+
+
+def sum_kernel(arrived, spread, *, tokens, fine):
+    fine_part = jnp.sum(arrived[:, :, :, tokens : tokens + fine].astype(F32), axis=0)
+    coarse_part = jnp.sum(arrived[:, :, :, tokens + fine :].astype(F32), axis=0)
+    total = [fine_part[0] + fine_part[1], coarse_part[0], coarse_part[1]]
+    total = jnp.concatenate(total, axis=1).astype(BF)
+    spread[...] = jnp.broadcast_to(total[None], spread.shape)
+
+
+def sums_kernel(
+    group, own, other, fine_projection, fine_output, pool, projection, output, *, scaling
+):
+    features = fine_output.shape[0]
+    wide = pool.shape[0]
     part = wide // 2
-    for terms, index in ((own, group[0]), (other, 1 - group[0])):
-        first = pl.multiple_of(index * part, part)
-        for at in range(3):
-            projection[:, pl.ds(at * wide + first, part)] = (
-                terms[:, at * part : (at + 1) * part].astype(F32) * scaling
-            )
-        for side in range(2):
-            rows, columns = slice(side * part, (side + 1) * part), slice(side * part, (side + 1) * part)
-            output[pl.ds(first, part), columns] = (
-                terms[rows, 3 * part : 4 * part].astype(F32) * scaling
-            )
-            pool[pl.ds(first, part), columns] = terms[rows, 4 * part :].astype(F32) * scaling
-
-
-def fine_sums_kernel(terms, projection, output, *, scaling):
-    features = output.shape[0]
-    for at in range(3):
-        projection[:, at * features : (at + 1) * features] = (
-            terms[at * features : (at + 1) * features, :].astype(F32) * scaling
-        )
-    output[...] = terms[3 * features :, :].astype(F32) * scaling
+    width = wide // 4
+    across = 3 * part // 2
+
+    def write(low, high):
+        for side, terms in enumerate((low, high)):
+            rows = terms.shape[0] * terms.shape[1]
+
+            def lanes(start, count):
+                values = terms[:, :, start : start + count].astype(F32) * scaling
+                return values.reshape(rows, count)
+
+            fine = lanes(0, features)
+            for k in range(2):
+                at = 2 * side + k
+                block = fine[k * features : (k + 1) * features]
+                if at < 3:
+                    fine_projection[:, at * features : (at + 1) * features] = block
+                else:
+                    fine_output[...] = block
+            for heads in range(2):
+                start = features + heads * (across + 2 * width)
+                place = heads * part
+                for k in range(3):
+                    column = side * across + k * width
+                    at, inner = column // part, column % part
+                    target = at * wide + place + inner
+                    projection[:, target : target + width] = lanes(start + k * width, width)
+                for at, ref in enumerate((output, pool)):
+                    block = lanes(start + across + at * width, width)
+                    for k in range(2):
+                        column = (2 * side + k) * width
+                        ref[place : place + part, column : column + width] = block[
+                            k * part : (k + 1) * part
+                        ]
+
+    @pl.when(group[0] == 0)
+    def _():
+        write(own, other)
+
+    @pl.when(group[0] != 0)
+    def _():
+        write(other, own)
 
 
 def fine_backward_kernel(
@@ -288,8 +324,8 @@
     weights,
     projection,
     output,
+    coarse_terms,
     send,
-    terms,
     grad_projected,
 ):
     place = one_hot(receive_slot[...], arrived.shape[0])
@@ -297,7 +333,7 @@
     gradient_rows = gradient_in.astype(BF)
     features = rotated.shape[1]
     entering = mm(gradient_rows, output[...], (1, 1)).astype(BF)
-    terms[3 * features :, :] = mm(mixture[...], gradient_rows, (0, 0)).astype(BF)
+    terms = [mm(mixture[...], gradient_rows, (0, 0))]
     balls = rotated.shape[0] // BALL
     pairs = features // PAIR
     for ball in range(balls):
@@ -324,15 +360,20 @@
     unit_rows = normed.astype(BF)
     for at in range(3):
         columns = slice(at * features, (at + 1) * features)
-        terms[columns, :] = mm(unit_rows, grad_projected[:, columns], (0, 0)).astype(BF)
+        terms.insert(at, mm(unit_rows, grad_projected[:, columns], (0, 0)))
     back = mm(grad_projected[...], projection[...], (1, 1))
     result = (gradient_in + norm_backward(back, normed, inverse)).astype(BF)
-    send[...] = mm(place, result).astype(BF)
+    tokens = mm(place, result)
+    send[:, :, :, :features] = tokens.reshape(send.shape[:3] + (features,)).astype(BF)
+    for side in range(2):
+        put_blocks(send, side, features, jnp.concatenate(terms[2 * side : 2 * side + 2], axis=0))
+    send[:, :, :, 2 * features :] = coarse_terms[...]
 
 
 def take_kernel(arrived, slots, rows_out):
-    place = one_hot(slots[...], arrived.shape[0])
-    rows_out[...] = mm(place, arrived[...], (0, 0)).astype(BF)
+    place = one_hot(slots[...], slots.shape[1] * 2)
+    rows = arrived[...].reshape(place.shape[0], arrived.shape[-1])
+    rows_out[...] = mm(place, rows, (0, 0)).astype(BF)
 
 
 VMEM = pl.BlockSpec(memory_space=pltpu.VMEM)
@@ -350,7 +391,7 @@
         in_specs=in_specs,
         out_specs=[VMEM] * len(shapes),
         scratch_shapes=list(scratch),
-        compiler_params=pltpu.CompilerParams(vmem_limit_bytes=56 * 1024 * 1024),
+        compiler_params=pltpu.CompilerParams(vmem_limit_bytes=16 * 1024 * 1024),
     )(*inputs)
 
 
@@ -366,15 +407,6 @@
     rows, features = values.shape
     blocks = values.reshape(devices, rows // devices, features)
     return spread_blocks(blocks, ("pts", "grp")).reshape(rows, features)
-
-
-def sum_over(terms, axes):
-    rows, columns = terms.shape
-    owners = lax.axis_size(axes)
-    blocks = (owners, rows // owners, columns)
-    arrived = spread_blocks(terms.reshape(blocks), axes)
-    (spread,) = call(sum_kernel, (arrived,), ((blocks, BF),))
-    return spread_blocks(spread, axes).reshape(rows, columns)
 
 
 def on_device(
@@ -469,6 +501,7 @@
     )
     arrived = route(send, devices)
     other_gradient = exchange(coarse_gradient)
+    owners = lax.axis_size("pts")
     (coarse_terms,) = call(
         coarse_weights_kernel,
         (
@@ -483,12 +516,11 @@
             coarse_gradient,
             other_gradient,
         ),
-        (((wide, 5 * wide // 2), BF),),
+        (((owners, 2, slots // devices, 5 * wide // 4), BF),),
         scalar=True,
     )
-    own_sums = sum_over(coarse_terms, "pts")
-    other_sums = exchange(own_sums)
-    send, fine_terms = call(
+    across = 2 * features + 5 * wide // 4
+    (send,) = call(
         fine_backward_kernel,
         (
             arrived,
@@ -499,33 +531,35 @@
             weights,
             fine_projection,
             fine_output,
-        ),
-        (((slots, features), BF), ((4 * features, features), BF)),
+            coarse_terms,
+        ),
+        (((owners, 2, slots // devices, across), BF),),
         scratch=(pltpu.VMEM((count, 3 * features), BF),),
     )
-    fine_sums = sum_over(fine_terms, ("pts", "grp"))
-    arrived = route(send, devices)
-    (points_gradient,) = call(take_kernel, (arrived, send_slot), (((count, features), BF),))
-    pool_sum, projection_sum, output_sum = call(
-        functools.partial(coarse_sums_kernel, scaling=scaling),
+    arrived = spread_blocks(send.reshape(devices, slots // devices, across), ("pts", "grp"))
+    (spread,) = call(
+        functools.partial(sum_kernel, tokens=features, fine=features),
+        (arrived.reshape(send.shape),),
+        (((owners, slots // devices, features + 5 * wide // 2), BF),),
+    )
+    own_sums = spread_blocks(spread, "pts")
+    (points_gradient,) = call(
+        take_kernel, (arrived[:, :, :features], send_slot), (((count, features), BF),)
+    )
+    other_sums = exchange(own_sums)
+    sums = call(
+        functools.partial(sums_kernel, scaling=scaling),
         (group, own_sums, other_sums),
-        (((wide, wide), F32), ((wide, 3 * wide), F32), ((wide, wide), F32)),
+        (
+            ((features, 3 * features), F32),
+            ((features, features), F32),
+            ((wide, wide), F32),
+            ((wide, 3 * wide), F32),
+            ((wide, wide), F32),
+        ),
         scalar=True,
     )
-    fine_projection_sum, fine_output_sum = call(
-        functools.partial(fine_sums_kernel, scaling=scaling),
-        (fine_sums,),
-        (((features, 3 * features), F32), ((features, features), F32)),
-    )
-    return (
-        coarse_result,
-        points_gradient,
-        fine_projection_sum,
-        fine_output_sum,
-        pool_sum,
-        projection_sum,
-        output_sum,
-    )
+    return (coarse_result, points_gradient, *sums)
 
 
 def solution(mesh):

time: 216 us -> 177 us (0.82)
  waiting for transfers between devices: 73.5 us -> 21.5 us
  blocking collectives: 50.5 us -> 88.4 us
  Pallas kernels: 48.1 us -> 25 us
  starting transfers between devices: 35.9 us -> 16.4 us
  local copies, waits for them, and re-layouts: 5.92 us -> 22.9 us
    all_to_all x6 -> x2, waiting for transfers between devices: 69 us -> 16.5 us  [spread_blocks(): return lax.all_to_all(values, axes, split_axis=0, concat_axis=0, tiled=True)]
    all_to_all x2 -> x3, blocking collectives: 50.5 us -> 88.4 us  [spread_blocks(): return lax.all_to_all(values, axes, split_axis=0, concat_axis=0, tiled=True)]
    pallas_call x12 -> x10, Pallas kernels: 48.1 us -> 25 us  [call(): pl.pallas_call(kernel, out_shape=shapes, in_specs=in_specs, out_specs=[VM...]
    all_to_all x6 -> x2, starting transfers between devices: 31.4 us -> 8.44 us  [spread_blocks(): return lax.all_to_all(values, axes, split_axis=0, concat_axis=0, tiled=True)]
    unnamed x24 -> x62, local copies, waits for them, and re-layouts: 4.6 us -> 22.1 us
    ppermute x5, starting transfers between devices: 4.45 us -> 7.97 us  [exchange(): return lax.ppermute(values, 'grp', [(0, 1), (1, 0)])]
  transfers between devices with their start and end apart: 11 -> 7, of which waited for: 9 -> 6; matrix products, arithmetic and copies ran while one was open for 1% -> 1% of each run, Pallas kernels for 9% -> 2%
where the time goes in v3:
time: 177 us; the launch traced here: 176 us
  blocking collectives  88.4 us (50%)
  Pallas kernels  25 us (14%)
  local copies, waits for them, and re-layouts  22.9 us (13%)
  waiting for transfers between devices  21.5 us (12%)
  starting transfers between devices  16.4 us (9%)
    all_to_all x3, blocking collectives, spread_blocks(): return lax.all_to_all(values, axes, split_axis=0, concat_axis=0, tiled=True)  88.4 us
    pallas_call x10, Pallas kernels, call(): pl.pallas_call(kernel, out_shape=shapes, in_specs=in_specs, out_specs=[VM...  25 us
    unnamed x62, local copies, waits for them, and re-layouts  22.1 us
    all_to_all x2, waiting for transfers between devices, spread_blocks(): return lax.all_to_all(values, axes, split_axis=0, concat_axis=0, tiled=True)  16.5 us
    all_to_all x2, starting transfers between devices, spread_blocks(): return lax.all_to_all(values, axes, split_axis=0, concat_axis=0, tiled=True)  8.44 us
    ppermute x5, starting transfers between devices, exchange(): return lax.ppermute(values, 'grp', [(0, 1), (1, 0)])  7.97 us
    ppermute x5, waiting for transfers between devices, exchange(): return lax.ppermute(values, 'grp', [(0, 1), (1, 0)])  5.09 us
  transfers between devices with their start and end apart: 7, of which 6 were waited for; matrix products, arithmetic and copies ran while one was open for 1% of the time, Pallas kernels for 2%

profile of v3, /device:TPU:1, one launch (start us, length us, event | category | flops | bytes accessed | tf_op | source)
XLA Modules:
  0.0 175.7 jit_solution(2281316380625931670)
XLA Ops:
  0.7 1.0 copy-done.23
  4.4 25.0 %all_to_all.25 = bf16[128,8,256]{2,1,0:T(8,128)(2,1)S(1)} all-to-all(bf16[128,8,256]{2,1,0:T(8,128)(2,1)S(1)} %bitcast.20), channel_id=1, replica_groups=mesh['pts'=64,'grp'=2] {'pts','grp'}, dimensions={0} | all-to-all | bytes 1048576 | tf_op jit(solution)/shard_map/all_to_all | solution.py:403
  30.3 3.2 %shard_map.154 = (bf16[1024,256]{1,0:T(8,128)(2,1)S(1)}, bf16[512,256]{1,0:T(8,128)(2,1)S(1)}, bf16[512,768]{1,0:T(8,128)(2,1)S(1)}, bf16[512,256]{1,0:T(8,128)(2,1)S(1)}, bf16[8,256,256]{2,1,0:T(8,128)(2,1)S(1)}) custom-call(bf16[1024,256]{1,0:T(8,128)(2,1)S(1)} %bitcast.16, s32[1,512]{1,0:T(1,128)S(1)} %get-tuple-element.29.receive_slot, ...), custom_call_target="tpu_custom_call" | custom-call | tf_op jit(solution)/shard_map/pallas_call | solution.py:388
  33.6 1.0 copy-done.6
  37.6 4.6 %all-to-all-start.1 = ((bf16[128,8,256]{2,1,0:T(8,128)(2,1)}), bf16[128,8,256]{2,1,0:T(8,128)(2,1)S(1)}, u32[]{:S(2)}, u32[]{:S(2)}) async-start(bf16[128,8,256]{2,1,0:T(8,128)(2,1)} %bitcast.19), calls=%async_computation.1 | async-start | bytes 1048576 | tf_op jit(solution)/shard_map/all_to_all | solution.py:403
  42.2 1.2 collective-permute-start.1
  44.9 11.1 %all-to-all-done.1 = bf16[128,8,256]{2,1,0:T(8,128)(2,1)S(1)} async-done(((bf16[128,8,256]{2,1,0:T(8,128)(2,1)}), bf16[128,8,256]{2,1,0:T(8,128)(2,1)S(1)}, u32[]{:S(2)}, u32[]{:S(2)}) %all-to-all-start.1) | async-done | bytes 524320 | tf_op jit(solution)/shard_map/all_to_all | solution.py:403
  56.5 1.2 collective-permute-start
  57.7 1.2 collective-permute-done.other_joined
  59.6 1.0 copy-done.3
  60.6 0.9 copy-done.9
  61.6 7.1 %shard_map.156 = (bf16[256,512]{1,0:T(8,128)(2,1)S(1)}, bf16[512,512]{1,0:T(8,128)(2,1)S(1)}, bf16[256,1024]{1,0:T(8,128)(2,1)S(1)}, bf16[256,1024]{1,0:T(8,128)(2,1)S(1)}) custom-call(s32[1]{0:T(128)} %bitcast.group, bf16[256,512]{1,0:T(8,128)(2,1)S(1)} %shard_map.155.own_joined, bf16[256,512]{1,0:T(8,128)(2,1)S(1)} %copy-done.9, ...), custom_call_target="tpu_custom_call" | custom-call | tf_op jit(solution)/shard_map/pallas_call | solution.py:388
  70.8 1.6 shard_map.157
  74.0 3.8 %all-to-all-start.2 = ((bf16[128,8,256]{2,1,0:T(8,128)(2,1)}), bf16[128,8,256]{2,1,0:T(8,128)(2,1)S(1)}, u32[]{:S(2)}, u32[]{:S(2)}) async-start(bf16[128,8,256]{2,1,0:T(8,128)(2,1)} %bitcast.18), calls=%async_computation.2 | async-start | bytes 1048576 | tf_op jit(solution)/shard_map/all_to_all | solution.py:403
  77.8 1.3 collective-permute-start.3
  79.1 1.4 collective-permute-done.3.other_gradient
  80.5 0.9 copy-done.10
  81.4 1.0 copy-done.14
  82.4 1.0 copy-done.16
  83.5 0.9 copy-done.22
  84.4 1.8 %shard_map.158.coarse_terms = bf16[64,2,8,640]{3,2,1,0:T(8,128)(2,1)S(1)} custom-call(s32[1]{0:T(128)} %bitcast.group, bf16[512,512]{1,0:T(8,128)(2,1)S(1)} %copy-done.14, bf16[256,1024]{1,0:T(8,128)(2,1)S(1)} %get-tuple-element.34.keep, bf16[256,1024]{1,0:T(8,128)(2,1)S(1)} %copy-done.16, bf16[256,512]{1,0:T(8,128)(2,1)S(1)} %copy-done.1, ...), custom_call_target="tpu_custom_call" | custom-call | tf_op jit(solution)/shard_map/pallas_call | solution.py:388
  86.3 5.3 %all-to-all-done.2 = bf16[128,8,256]{2,1,0:T(8,128)(2,1)S(1)} async-done(((bf16[128,8,256]{2,1,0:T(8,128)(2,1)}), bf16[128,8,256]{2,1,0:T(8,128)(2,1)S(1)}, u32[]{:S(2)}, u32[]{:S(2)}) %all-to-all-start.2) | async-done | bytes 524320 | tf_op jit(solution)/shard_map/all_to_all | solution.py:403
  91.6 1.2 copy-done.7
  92.8 1.1 copy-done.12
  94.9 0.9 copy-done.25
  96.8 5.0 %shard_map.159 = bf16[64,2,8,1152]{3,2,1,0:T(8,128)(2,1)S(1)} custom-call(bf16[1024,256]{1,0:T(8,128)(2,1)S(1)} %bitcast.17, s32[1,512]{1,0:T(1,128)S(1)} %get-tuple-element.29.receive_slot, bf16[512,256]{1,0:T(8,128)(2,1)S(1)} %copy-done.25, bf16[512,768]{1,0:T(8,128)(2,1)S(1)} %copy-done.12, bf16[512,256]{1,0:T(8,128)(2,1)S(1)} %copy-done.27, ...), custom_call_target="tpu_custom_call" | custom-call | tf_op jit(solution)/shard_map/pallas_call | solution.py:388
  101.8 37.7 %all_to_all.26 = bf16[128,8,1152]{2,1,0:T(8,128)(2,1)S(1)} all-to-all(bf16[128,8,1152]{2,1,0:T(8,128)(2,1)S(1)} %bitcast.14), channel_id=1, replica_groups=mesh['pts'=64,'grp'=2] {'pts','grp'}, dimensions={0} | all-to-all | bytes 4718592 | tf_op jit(solution)/shard_map/all_to_all | solution.py:403
  139.9 25.7 %all_to_all.27.own = bf16[64,8,1536]{2,1,0:T(8,128)(2,1)S(1)} all-to-all(bf16[64,8,1536]{2,1,0:T(8,128)(2,1)S(1)} %shard_map.161), channel_id=1, replica_groups=mesh['pts'=64,'grp'=2] {'pts'}, dimensions={0} | all-to-all | bytes 3145728 | tf_op jit(solution)/shard_map/all_to_all | solution.py:403
  165.6 3.6 %collective-permute-start.4 = (bf16[64,8,1536]{2,1,0:T(8,128)(2,1)S(1)}, bf16[64,8,1536]{2,1,0:T(8,128)(2,1)S(1)}, u32[]{:S(2)}, u32[]{:S(2)}) collective-permute-start(bf16[64,8,1536]{2,1,0:T(8,128)(2,1)S(1)} %all_to_all.27.own), channel_id=1, source_target_pairs={{0,1},{1,0},{2,3},{3,2},{4,5},{5,4},{6,7},{7,6},{8,9},{9,8},{10,11... | collective-permute-start | bytes 4718600 | tf_op jit(solution)/shard_map/ppermute | solution.py:399
  169.2 1.2 shard_map.160
  170.4 1.8 %collective-permute-done.4.other = bf16[64,8,1536]{2,1,0:T(8,128)(2,1)S(1)} collective-permute-done((bf16[64,8,1536]{2,1,0:T(8,128)(2,1)S(1)}, bf16[64,8,1536]{2,1,0:T(8,128)(2,1)S(1)}, u32[]{:S(2)}, u32[]{:S(2)}) %collective-permute-start.4) | collective-permute-done | bytes 1572896 | tf_op jit(solution)/shard_map/ppermute | solution.py:399
  172.2 3.4 %shard_map.162 = (f32[256,768]{1,0:T(8,128)}, f32[256,256]{1,0:T(8,128)}, f32[512,512]{1,0:T(8,128)}, f32[512,1536]{1,0:T(8,128)}, f32[512,512]{1,0:T(8,128)}) custom-call(s32[1]{0:T(128)} %bitcast.group, bf16[64,8,1536]{2,1,0:T(8,128)(2,1)S(1)} %all_to_all.27.own, bf16[64,8,1536]{2,1,0:T(8,128)(2,1)S(1)} %collective-permute-done.4.other), custom_call_target="tpu_custom_call" | custom-call | tf_op jit(solution)/shard_map/pallas_call | solution.py:388
  (62 shorter events, 15.3 us)
Async XLA Ops:
  0.6 28.8 %copy-start.5 = (bf16[256,768]{1,0:T(8,128)(2,1)S(1)}, bf16[256,768]{1,0:T(8,128)(2,1)}, u32[]{:S(2)}) copy-start(bf16[256,768]{1,0:T(8,128)(2,1)} %projection.7) | copy-start | bytes 1179652
  0.6 1.0 copy-start.23
  4.4 37.8 %copy-start.1 = (bf16[256,512]{1,0:T(8,128)(2,1)S(1)}, bf16[256,512]{1,0:T(8,128)(2,1)}, u32[]{:S(2)}) copy-start(bf16[256,512]{1,0:T(8,128)(2,1)} %own_cotangent.3) | copy-start | bytes 786436
  29.4 0.9 copy-start.19
  30.3 29.3 %copy-start = (bf16[512,1536]{1,0:T(8,128)(2,1)S(1)}, bf16[512,1536]{1,0:T(8,128)(2,1)}, u32[]{:S(2)}) copy-start(bf16[512,1536]{1,0:T(8,128)(2,1)} %projection.6) | copy-start | bytes 4718596
  30.3 29.3 %copy-start.2 = (bf16[512,512]{1,0:T(8,128)(2,1)S(1)}, bf16[512,512]{1,0:T(8,128)(2,1)}, u32[]{:S(2)}) copy-start(bf16[512,512]{1,0:T(8,128)(2,1)} %pool.3) | copy-start | bytes 1572868
  33.6 1.0 copy-start.6
  34.5 0.9 copy-start.11
  35.4 0.8 copy-start.18
  36.9 0.7 copy-start.26
  37.6 18.4 %all-to-all-start.1 = ((bf16[128,8,256]{2,1,0:T(8,128)(2,1)}), bf16[128,8,256]{2,1,0:T(8,128)(2,1)S(1)}, u32[]{:S(2)}, u32[]{:S(2)}) async-start(bf16[128,8,256]{2,1,0:T(8,128)(2,1)} %bitcast.19), calls=%async_computation.1 | async-start | bytes 1048576 | tf_op jit(solution)/shard_map/all_to_all | solution.py:403
  42.2 15.5 %collective-permute-start.1 = (bf16[256,512]{1,0:T(8,128)(2,1)S(1)}, bf16[256,512]{1,0:T(8,128)(2,1)}, u32[]{:S(2)}, u32[]{:S(2)}) collective-permute-start(bf16[256,512]{1,0:T(8,128)(2,1)S(1)} %copy-done.1), channel_id=1, source_target_pairs={{0,1},{1,0},{2,3},{3,2},{4,5},{5,4},{6,7},{7,6},{8,9},{9,8},{10,11... | collective-permute-start | bytes 786440 | tf_op jit(solution)/shard_map/ppermute | solution.py:399
  56.5 2.4 %collective-permute-start = (bf16[256,512]{1,0:T(8,128)(2,1)S(1)}, bf16[256,512]{1,0:T(8,128)(2,1)S(1)}, u32[]{:S(2)}, u32[]{:S(2)}) collective-permute-start(bf16[256,512]{1,0:T(8,128)(2,1)S(1)} %shard_map.155.own_joined), channel_id=1, source_target_pairs={{0,1},{1,0},{2,3},{3,2},{4,5},{5,4},{6,7},{7,6},{8,9},{9,8},{10,11... | collective-permute-start | bytes 786440 | tf_op jit(solution)/shard_map/ppermute | solution.py:399
  59.6 1.0 copy-start.3
  60.6 0.9 copy-start.9
  61.6 9.3 %copy-start.4 = (bf16[512,512]{1,0:T(8,128)(2,1)S(1)}, bf16[512,512]{1,0:T(8,128)(2,1)}, u32[]{:S(2)}) copy-start(bf16[512,512]{1,0:T(8,128)(2,1)} %output.6) | copy-start | bytes 1572868
  68.7 3.8 %copy-start.13 = (bf16[512,512]{1,0:T(8,128)(2,1)}, bf16[512,512]{1,0:T(8,128)(2,1)S(1)}, u32[]{:S(2)}) copy-start(bf16[512,512]{1,0:T(8,128)(2,1)S(1)} %get-tuple-element.42.unit) | copy-start | bytes 1572868
  68.7 2.2 %collective-permute-start.2 = (bf16[256,1024]{1,0:T(8,128)(2,1)S(1)}, bf16[256,1024]{1,0:T(8,128)(2,1)S(1)}, u32[]{:S(2)}, u32[]{:S(2)}) collective-permute-start(bf16[256,1024]{1,0:T(8,128)(2,1)S(1)} %get-tuple-element.35.give), channel_id=1, source_target_pairs={{0,1},{1,0},{2,3},{3,2},{4,5},{5,4},{6,7},{7,6},{8,9},{9,8},{10,11... | collective-permute-start | bytes 1572872 | tf_op jit(solution)/shard_map/ppermute | solution.py:399
  69.3 0.8 copy-start.15
  72.5 0.8 copy-start.17
  74.0 17.6 %all-to-all-start.2 = ((bf16[128,8,256]{2,1,0:T(8,128)(2,1)}), bf16[128,8,256]{2,1,0:T(8,128)(2,1)S(1)}, u32[]{:S(2)}, u32[]{:S(2)}) async-start(bf16[128,8,256]{2,1,0:T(8,128)(2,1)} %bitcast.18), calls=%async_computation.2 | async-start | bytes 1048576 | tf_op jit(solution)/shard_map/all_to_all | solution.py:403
  77.8 2.6 %collective-permute-start.3 = (bf16[256,512]{1,0:T(8,128)(2,1)}, bf16[256,512]{1,0:T(8,128)(2,1)S(1)}, u32[]{:S(2)}, u32[]{:S(2)}) collective-permute-start(bf16[256,512]{1,0:T(8,128)(2,1)} %copy-done.21), channel_id=1, source_target_pairs={{0,1},{1,0},{2,3},{3,2},{4,5},{5,4},{6,7},{7,6},{8,9},{9,8},{10,11... | collective-permute-start | bytes 786440 | tf_op jit(solution)/shard_map/ppermute | solution.py:399
  80.5 0.9 copy-start.10
  81.4 1.0 copy-start.14
  82.4 1.0 copy-start.16
  83.5 0.9 copy-start.22
  91.6 1.2 copy-start.7
  92.8 1.1 copy-start.12
  94.0 0.9 copy-start.20
  94.9 0.9 copy-start.25
  95.8 0.9 copy-start.27
  165.6 6.7 %collective-permute-start.4 = (bf16[64,8,1536]{2,1,0:T(8,128)(2,1)S(1)}, bf16[64,8,1536]{2,1,0:T(8,128)(2,1)S(1)}, u32[]{:S(2)}, u32[]{:S(2)}) collective-permute-start(bf16[64,8,1536]{2,1,0:T(8,128)(2,1)S(1)} %all_to_all.27.own), channel_id=1, source_target_pairs={{0,1},{1,0},{2,3},{3,2},{4,5},{5,4},{6,7},{7,6},{8,9},{9,8},{10,11... | collective-permute-start | bytes 4718600 | tf_op jit(solution)/shard_map/ppermute | solution.py:399
  (6 other events, 4.2 us)

commit v4 on v3

--- a/solution.py
+++ b/solution.py
@@ -1,5 +1,6 @@
 import functools
 import math
+from typing import NamedTuple
 
 import jax
 import jax.numpy as jnp
@@ -98,9 +99,11 @@
     place = one_hot(receive_slot[...], arrived.shape[0])
     rows_in = mm(place, arrived[...], (0, 0))
     rotated[...] = rows_in.astype(BF)
+    rotated.flush()
     features = rows_in.shape[1]
     normed, _ = normalize(rows_in)
     projected[...] = mm(normed.astype(BF), projection[...]).astype(BF)
+    projected.flush()
     balls = rows_in.shape[0] // BALL
     pairs = features // PAIR
     for ball in range(balls):
@@ -119,6 +122,8 @@
                 halves.append(mm(head_weights, value))
             mixed = jnp.where(head_half(halves[0].shape, 0), halves[0], halves[1])
             mixture[rows, lanes] = mixed.astype(BF)
+    weights.flush()
+    mixture.flush()
     result = (rows_in + mm(mixture[...], output[...])).astype(BF)
     send[...] = mm(place, result).astype(BF)
 
@@ -140,23 +145,28 @@
     projection,
     output,
     coarse,
-    unit,
     keep,
     give,
+    both_joined,
+    unit,
+    stacked,
 ):
     half_rows, wide = own_joined.shape
     part = wide // 2
     first = pl.multiple_of(group[0] * part, part)
     joined = jnp.concatenate([own_joined[...], other_joined[...]], axis=0)
-    cotangent = jnp.concatenate([own_cotangent[...], other_cotangent[...]], axis=0)
+    both_joined[...] = joined
+    both_joined.flush()
     tokens = mm(joined, pool[...]).astype(BF)
     coarse[...] = tokens[:half_rows]
     normed, _ = normalize(tokens)
     unit_rows = normed.astype(BF)
     unit[...] = unit_rows
+    unit.flush()
     queries = mm(unit_rows, projection[:, pl.ds(first, part)]).astype(BF)
     keys = mm(unit_rows, projection[:, pl.ds(wide + first, part)]).astype(BF)
     values = mm(unit_rows, projection[:, pl.ds(2 * wide + first, part)]).astype(BF)
+    cotangent = jnp.concatenate([own_cotangent[...], other_cotangent[...]], axis=0)
     incoming = mm(cotangent, output[pl.ds(first, part), :], (1, 1)).astype(BF)
     for pair in range(part // PAIR):
         lanes = slice(pair * PAIR, (pair + 1) * PAIR)
@@ -177,6 +187,7 @@
             target = slice(at * part + pair * PAIR, at * part + (pair + 1) * PAIR)
             keep[:, target] = both[:half_rows]
             give[:, target] = both[half_rows:]
+            stacked[:, target] = both
 
 
 def coarse_finish_kernel(
@@ -207,6 +218,7 @@
                 (1, 1),
             )
     result[...] = mixed.astype(BF)
+    result.flush()
     normed, inverse = normalize(coarse[...])
     gradient_rows = (
         cotangent[...].astype(F32) + norm_backward(back, normed, inverse)
@@ -222,25 +234,21 @@
 def coarse_weights_kernel(
     group,
     unit,
-    keep,
-    give,
+    stacked,
     own_cotangent,
     other_cotangent,
-    own_joined,
-    other_joined,
+    joined,
     own_gradient,
     other_gradient,
     terms,
 ):
-    part = keep.shape[1] // 4
+    part = stacked.shape[1] // 4
     first = pl.multiple_of(group[0] * part, part)
-    stacked = jnp.concatenate([keep[...], give[...]], axis=0)
+    projection_term = mm(unit[...], stacked[:, part:], (0, 0))
     cotangent = jnp.concatenate([own_cotangent[...], other_cotangent[...]], axis=0)
-    projection_term = mm(unit[...], stacked[:, part:], (0, 0))
     output_term = mm(stacked[:, :part], cotangent, (0, 0))
-    pool_term = mm(own_joined[:, pl.ds(first, part)], own_gradient[...], (0, 0)) + mm(
-        other_joined[:, pl.ds(first, part)], other_gradient[...], (0, 0)
-    )
+    gradient = jnp.concatenate([own_gradient[...], other_gradient[...]], axis=0)
+    pool_term = mm(joined[:, pl.ds(first, part)], gradient, (0, 0))
     across = projection_term.shape[1] // 2
     for side in range(2):
         columns = projection_term[:, side * across : (side + 1) * across]
@@ -274,45 +282,46 @@
     width = wide // 4
     across = 3 * part // 2
 
-    def write(low, high):
-        for side, terms in enumerate((low, high)):
-            rows = terms.shape[0] * terms.shape[1]
-
-            def lanes(start, count):
-                values = terms[:, :, start : start + count].astype(F32) * scaling
-                return values.reshape(rows, count)
-
-            fine = lanes(0, features)
-            for k in range(2):
-                at = 2 * side + k
-                block = fine[k * features : (k + 1) * features]
-                if at < 3:
-                    fine_projection[:, at * features : (at + 1) * features] = block
-                else:
-                    fine_output[...] = block
+    owns_low = group[0] == 0
+
+    def lanes(side, start, count):
+        here, there = own[:, :, start : start + count], other[:, :, start : start + count]
+        low = owns_low if side == 0 else jnp.logical_not(owns_low)
+        values = jnp.where(low, here, there).astype(F32) * scaling
+        return values.reshape(own.shape[0] * own.shape[1], count)
+
+    def start_of(heads):
+        return features + heads * (across + 2 * width)
+
+    for side in range(2):
+        for heads in range(2):
+            for k in range(3):
+                column = side * across + k * width
+                at, inner = column // part, column % part
+                target = at * wide + heads * part + inner
+                projection[:, target : target + width] = lanes(
+                    side, start_of(heads) + k * width, width
+                )
+    projection.flush()
+    for at, ref in enumerate((output, pool)):
+        for side in range(2):
             for heads in range(2):
-                start = features + heads * (across + 2 * width)
-                place = heads * part
-                for k in range(3):
-                    column = side * across + k * width
-                    at, inner = column // part, column % part
-                    target = at * wide + place + inner
-                    projection[:, target : target + width] = lanes(start + k * width, width)
-                for at, ref in enumerate((output, pool)):
-                    block = lanes(start + across + at * width, width)
-                    for k in range(2):
-                        column = (2 * side + k) * width
-                        ref[place : place + part, column : column + width] = block[
-                            k * part : (k + 1) * part
-                        ]
-
-    @pl.when(group[0] == 0)
-    def _():
-        write(own, other)
-
-    @pl.when(group[0] != 0)
-    def _():
-        write(other, own)
+                block = lanes(side, start_of(heads) + across + at * width, width)
+                for k in range(2):
+                    column = (2 * side + k) * width
+                    ref[heads * part : (heads + 1) * part, column : column + width] = block[
+                        k * part : (k + 1) * part
+                    ]
+        ref.flush()
+    for side in range(2):
+        fine = lanes(side, 0, features)
+        for k in range(2):
+            at = 2 * side + k
+            block = fine[k * features : (k + 1) * features]
+            if at < 3:
+                fine_projection[:, at * features : (at + 1) * features] = block
+            else:
+                fine_output[...] = block
 
 
 def fine_backward_kernel(
@@ -327,7 +336,12 @@
     coarse_terms,
     send,
     grad_projected,
+    arriving,
 ):
+    filling = pltpu.make_async_copy(
+        coarse_terms, send.at[:, :, :, 2 * rotated.shape[1] :], arriving
+    )
+    filling.start()
     place = one_hot(receive_slot[...], arrived.shape[0])
     gradient_in = mm(place, arrived[...], (0, 0))
     gradient_rows = gradient_in.astype(BF)
@@ -367,7 +381,7 @@
     send[:, :, :, :features] = tokens.reshape(send.shape[:3] + (features,)).astype(BF)
     for side in range(2):
         put_blocks(send, side, features, jnp.concatenate(terms[2 * side : 2 * side + 2], axis=0))
-    send[:, :, :, 2 * features :] = coarse_terms[...]
+    filling.wait()
 
 
 def take_kernel(arrived, slots, rows_out):
@@ -378,21 +392,97 @@
 
 VMEM = pl.BlockSpec(memory_space=pltpu.VMEM)
 SMEM = pl.BlockSpec(memory_space=pltpu.SMEM)
+HBM = pl.BlockSpec(memory_space=pltpu.HBM)
+
+
+class Far(NamedTuple):
+    value: jax.Array
+
+
+class Direct(NamedTuple):
+    value: jax.Array
+
+
+class Near(NamedTuple):
+    shape: tuple
+    dtype: jnp.dtype = BF
+    far: bool = False
+
+
+class Fetched:
+    def __init__(self, source, buffer, semaphore):
+        self.buffer, self.shape, self.waited = buffer, buffer.shape, False
+        self.copy = pltpu.make_async_copy(source, buffer, semaphore)
+        self.copy.start()
+
+    def wait(self):
+        if not self.waited:
+            self.copy.wait()
+            self.waited = True
+
+    def __getitem__(self, index):
+        self.wait()
+        return self.buffer[index]
+
+
+class Stored:
+    def __init__(self, target, buffer, semaphore):
+        self.buffer, self.shape, self.dtype, self.started = buffer, buffer.shape, buffer.dtype, False
+        self.copy = pltpu.make_async_copy(buffer, target, semaphore)
+
+    def __setitem__(self, index, values):
+        self.buffer[index] = values
+
+    def __getitem__(self, index):
+        return self.buffer[index]
+
+    def flush(self):
+        if not self.started:
+            self.copy.start()
+            self.started = True
 
 
 def call(kernel, inputs, outputs, scalar=False, scratch=()):
-    in_specs = [VMEM] * len(inputs)
-    if scalar:
-        in_specs[0] = SMEM
-    shapes = [jax.ShapeDtypeStruct(shape, dtype) for shape, dtype in outputs]
+    in_specs, arrays, buffers = [], [], []
+    for at, value in enumerate(inputs):
+        far, direct = isinstance(value, Far), isinstance(value, Direct)
+        in_specs.append(SMEM if scalar and at == 0 else HBM if far or direct else VMEM)
+        arrays.append(value.value if far or direct else value)
+        if far:
+            buffers.append(pltpu.VMEM(value.value.shape, value.value.dtype))
+    buffers.extend(pltpu.VMEM(out.shape, out.dtype) for out in outputs if out.far)
+    flags = [isinstance(value, Far) for value in inputs] + [out.far for out in outputs]
+    sizes = len(inputs), len(flags), len(flags) + len(buffers)
+
+    def body(*refs):
+        semaphores = refs[sizes[2]] if buffers else None
+        given, views = 0, []
+        for at, far in enumerate(flags):
+            if far:
+                kind = Fetched if at < sizes[0] else Stored
+                views.append(kind(refs[at], refs[sizes[1] + given], semaphores.at[given]))
+                given += 1
+            else:
+                views.append(refs[at])
+        kernel(*views, *refs[sizes[2] + (1 if buffers else 0) :])
+        for view in views:
+            if isinstance(view, Stored):
+                view.flush()
+        for view in views:
+            if isinstance(view, Fetched):
+                view.wait()
+            if isinstance(view, Stored):
+                view.copy.wait()
+
+    own = [pltpu.SemaphoreType.DMA((len(buffers),))] if buffers else []
     return pl.pallas_call(
-        kernel,
-        out_shape=shapes,
+        body,
+        out_shape=[jax.ShapeDtypeStruct(out.shape, out.dtype) for out in outputs],
         in_specs=in_specs,
-        out_specs=[VMEM] * len(shapes),
-        scratch_shapes=list(scratch),
-        compiler_params=pltpu.CompilerParams(vmem_limit_bytes=16 * 1024 * 1024),
-    )(*inputs)
+        out_specs=[HBM if out.far else VMEM for out in outputs],
+        scratch_shapes=buffers + own + list(scratch),
+        compiler_params=pltpu.CompilerParams(vmem_limit_bytes=20 * 1024 * 1024),
+    )(*arrays)
 
 
 def exchange(values):
@@ -432,16 +522,16 @@
     send, send_slot, receive_slot, live = call(
         route_kernel,
         (
-            rotated_place.reshape(1, count),
-            rotated_source.reshape(1, count),
-            ball_counts.reshape(1, -1),
-            points,
-        ),
-        (
-            ((slots, features), BF),
-            ((1, count), jnp.int32),
-            ((1, count), jnp.int32),
-            ((1, count), F32),
+            Far(rotated_place.reshape(1, count)),
+            Far(rotated_source.reshape(1, count)),
+            Far(ball_counts.reshape(1, -1)),
+            Far(points),
+        ),
+        (
+            Near((slots, features)),
+            Near((1, count), jnp.int32),
+            Near((1, count), jnp.int32),
+            Near((1, count), F32),
         ),
     )
     other_cotangent = exchange(coarse_cotangent)
@@ -450,35 +540,37 @@
     heads = features // HD * (count // BALL)
     send, rotated, projected, mixture, weights = call(
         fine_forward_kernel,
-        (arrived, receive_slot, live, fine_projection, fine_output),
-        (
-            ((slots, features), BF),
-            ((count, features), BF),
-            ((count, 3 * features), BF),
-            ((count, features), BF),
-            ((heads, BALL, BALL), BF),
+        (arrived, receive_slot, live, Far(fine_projection), Far(fine_output)),
+        (
+            Near((slots, features)),
+            Near((count, features), far=True),
+            Near((count, 3 * features), far=True),
+            Near((count, features), far=True),
+            Near((heads, BALL, BALL), far=True),
         ),
     )
     arrived = route(send, devices)
-    (own_joined,) = call(join_kernel, (arrived, pair_slots), (((half_rows, wide), BF),))
+    (own_joined,) = call(join_kernel, (arrived, pair_slots), (Near((half_rows, wide)),))
     other_joined = exchange(own_joined)
-    coarse, unit, keep, give = call(
+    coarse, keep, give, joined, unit, stacked = call(
         coarse_kernel,
         (
             group,
             own_joined,
             other_joined,
-            coarse_cotangent,
-            other_cotangent,
-            pool_weight,
-            coarse_projection,
-            coarse_output,
-        ),
-        (
-            ((half_rows, wide), BF),
-            ((count, wide), BF),
-            ((half_rows, 2 * wide), BF),
-            ((half_rows, 2 * wide), BF),
+            Far(coarse_cotangent),
+            Far(other_cotangent),
+            Far(pool_weight),
+            Far(coarse_projection),
+            Far(coarse_output),
+        ),
+        (
+            Near((half_rows, wide)),
+            Near((half_rows, 2 * wide)),
+            Near((half_rows, 2 * wide)),
+            Near((count, wide), far=True),
+            Near((count, wide), far=True),
+            Near((count, 2 * wide), far=True),
         ),
         scalar=True,
     )
@@ -490,13 +582,17 @@
             coarse,
             keep,
             got,
-            coarse_cotangent,
-            pool_weight,
-            coarse_projection,
-            coarse_output,
+            Far(coarse_cotangent),
+            Far(pool_weight),
+            Far(coarse_projection),
+            Far(coarse_output),
             pair_slots,
         ),
-        (((half_rows, wide), BF), ((half_rows, wide), BF), ((slots, features), BF)),
+        (
+            Near((half_rows, wide), far=True),
+            Near((half_rows, wide)),
+            Near((slots, features)),
+        ),
         scalar=True,
     )
     arrived = route(send, devices)
@@ -506,17 +602,15 @@
         coarse_weights_kernel,
         (
             group,
-            unit,
-            keep,
-            give,
-            coarse_cotangent,
-            other_cotangent,
-            own_joined,
-            other_joined,
+            Far(unit),
+            Far(stacked),
+            Far(coarse_cotangent),
+            Far(other_cotangent),
+            Far(joined),
             coarse_gradient,
             other_gradient,
         ),
-        (((owners, 2, slots // devices, 5 * wide // 4), BF),),
+        (Near((owners, 2, slots // devices, 5 * wide // 4), far=True),),
         scalar=True,
     )
     across = 2 * features + 5 * wide // 4
@@ -525,37 +619,37 @@
         (
             arrived,
             receive_slot,
-            rotated,
-            projected,
-            mixture,
-            weights,
-            fine_projection,
-            fine_output,
-            coarse_terms,
-        ),
-        (((owners, 2, slots // devices, across), BF),),
-        scratch=(pltpu.VMEM((count, 3 * features), BF),),
+            Far(rotated),
+            Far(projected),
+            Far(mixture),
+            Far(weights),
+            Far(fine_projection),
+            Far(fine_output),
+            Direct(coarse_terms),
+        ),
+        (Near((owners, 2, slots // devices, across)),),
+        scratch=(pltpu.VMEM((count, 3 * features), BF), pltpu.SemaphoreType.DMA),
     )
     arrived = spread_blocks(send.reshape(devices, slots // devices, across), ("pts", "grp"))
     (spread,) = call(
         functools.partial(sum_kernel, tokens=features, fine=features),
         (arrived.reshape(send.shape),),
-        (((owners, slots // devices, features + 5 * wide // 2), BF),),
+        (Near((owners, slots // devices, features + 5 * wide // 2)),),
     )
     own_sums = spread_blocks(spread, "pts")
     (points_gradient,) = call(
-        take_kernel, (arrived[:, :, :features], send_slot), (((count, features), BF),)
+        take_kernel, (arrived[:, :, :features], send_slot), (Near((count, features)),)
     )
     other_sums = exchange(own_sums)
     sums = call(
         functools.partial(sums_kernel, scaling=scaling),
         (group, own_sums, other_sums),
         (
-            ((features, 3 * features), F32),
-            ((features, features), F32),
-            ((wide, wide), F32),
-            ((wide, 3 * wide), F32),
-            ((wide, wide), F32),
+            Near((features, 3 * features), F32, far=True),
+            Near((features, features), F32, far=True),
+            Near((wide, wide), F32, far=True),
+            Near((wide, 3 * wide), F32, far=True),
+            Near((wide, wide), F32, far=True),
         ),
         scalar=True,
     )

time: 177 us -> 177 us (level)
  Pallas kernels: 25 us -> 31.4 us
  local copies, waits for them, and re-layouts: 22.9 us -> 16.9 us
    pallas_call x10, Pallas kernels: 25 us -> 31.4 us  [call(): pl.pallas_call(body, out_shape=[jax.ShapeDtypeStruct(out.shape, out.dtype...]
    unnamed x62 -> x58, local copies, waits for them, and re-layouts: 22.1 us -> 16.2 us
  transfers between devices with their start and end apart: 7 -> 7, of which waited for: 6 -> 6; matrix products, arithmetic and copies ran while one was open for 1% -> 1% of each run, Pallas kernels for 2% -> 3%
where the time goes in v4:
time: 177 us; the launch traced here: 176 us
  blocking collectives  88.4 us (50%)
  Pallas kernels  31.4 us (18%)
  waiting for transfers between devices  21.6 us (12%)
  local copies, waits for them, and re-layouts  16.9 us (10%)
  starting transfers between devices  16.3 us (9%)
    all_to_all x3, blocking collectives, spread_blocks(): return lax.all_to_all(values, axes, split_axis=0, concat_axis=0, tiled=True)  88.4 us
    pallas_call x10, Pallas kernels, call(): pl.pallas_call(body, out_shape=[jax.ShapeDtypeStruct(out.shape, out.dtype...  31.4 us
    unnamed x58, local copies, waits for them, and re-layouts  16.2 us
    all_to_all x2, waiting for transfers between devices, spread_blocks(): return lax.all_to_all(values, axes, split_axis=0, concat_axis=0, tiled=True)  15.8 us
    all_to_all x2, starting transfers between devices, spread_blocks(): return lax.all_to_all(values, axes, split_axis=0, concat_axis=0, tiled=True)  8.46 us
    ppermute x5, starting transfers between devices, exchange(): return lax.ppermute(values, 'grp', [(0, 1), (1, 0)])  7.88 us
    ppermute x5, waiting for transfers between devices, exchange(): return lax.ppermute(values, 'grp', [(0, 1), (1, 0)])  5.87 us
  transfers between devices with their start and end apart: 7, of which 6 were waited for; matrix products, arithmetic and copies ran while one was open for 1% of the time, Pallas kernels for 3%

profile of v4, /device:TPU:1, one launch (start us, length us, event | category | flops | bytes accessed | tf_op | source)
XLA Modules:
  0.0 176.5 jit_solution(5824264512892642486)
XLA Ops:
  0.7 1.0 copy-done.21
  3.7 1.3 shard_map.153
  5.0 25.0 %all_to_all.25 = bf16[128,8,256]{2,1,0:T(8,128)(2,1)S(1)} all-to-all(bf16[128,8,256]{2,1,0:T(8,128)(2,1)S(1)} %bitcast.19), channel_id=1, replica_groups=mesh['pts'=64,'grp'=2] {'pts','grp'}, dimensions={0} | all-to-all | bytes 1048576 | tf_op jit(solution)/shard_map/all_to_all | solution.py:493
  30.9 4.3 %shard_map.154 = (bf16[1024,256]{1,0:T(8,128)(2,1)S(1)}, bf16[512,256]{1,0:T(8,128)(2,1)S(1)}, bf16[512,768]{1,0:T(8,128)(2,1)S(1)}, bf16[512,256]{1,0:T(8,128)(2,1)S(1)}, bf16[8,256,256]{2,1,0:T(8,128)(2,1)S(1)}) custom-call(bf16[1024,256]{1,0:T(8,128)(2,1)S(1)} %bitcast.16, s32[1,512]{1,0:T(1,128)S(1)} %get-tuple-element.31.refs_1_, ...), custom_call_target="tpu_custom_call" | custom-call | tf_op jit(solution)/shard_map/pallas_call | solution.py:478
  35.2 1.0 copy-done.8
  39.2 4.6 %all-to-all-start.1 = ((bf16[128,8,256]{2,1,0:T(8,128)(2,1)}), bf16[128,8,256]{2,1,0:T(8,128)(2,1)S(1)}, u32[]{:S(2)}, u32[]{:S(2)}) async-start(bf16[128,8,256]{2,1,0:T(8,128)(2,1)} %bitcast.18), calls=%async_computation.1 | async-start | bytes 1048576 | tf_op jit(solution)/shard_map/all_to_all | solution.py:493
  43.8 1.2 collective-permute-start.1
  46.5 11.1 %all-to-all-done.1 = bf16[128,8,256]{2,1,0:T(8,128)(2,1)S(1)} async-done(((bf16[128,8,256]{2,1,0:T(8,128)(2,1)}), bf16[128,8,256]{2,1,0:T(8,128)(2,1)S(1)}, u32[]{:S(2)}, u32[]{:S(2)}) %all-to-all-start.1) | async-done | bytes 524320 | tf_op jit(solution)/shard_map/all_to_all | solution.py:493
  57.6 1.2 shard_map.155.refs_1_
  58.8 1.1 collective-permute-start
  59.9 1.4 collective-permute-done.refs_2_
  61.3 8.1 %shard_map.156 = (bf16[256,512]{1,0:T(8,128)(2,1)S(1)}, bf16[256,1024]{1,0:T(8,128)(2,1)S(1)}, bf16[256,1024]{1,0:T(8,128)(2,1)S(1)}, bf16[512,512]{1,0:T(8,128)...) custom-call(s32[1]{0:T(128)} %bitcast.refs_0_, bf16[256,512]{1,0:T(8,128)(2,1)} %shard_map.155.refs_1_, ...), custom_call_target="tpu_custom_call" | custom-call | tf_op jit(solution)/shard_map/pallas_call | solution.py:478
  70.6 1.5 collective-permute-done.2.refs_3_
  72.1 2.9 %shard_map.157 = (bf16[256,512]{1,0:T(8,128)(2,1)}, bf16[256,512]{1,0:T(8,128)(2,1)S(1)}, bf16[1024,256]{1,0:T(8,128)(2,1)}) custom-call(s32[1]{0:T(128)} %bitcast.refs_0_, bf16[256,512]{1,0:T(8,128)(2,1)S(1)} %get-tuple-element.35.refs_1_, bf16[256,1024]{1,0:T(8,128)(2,1)S(1)} %get-tuple-element.36.refs_2_, ...), custom_call_target="tpu_custom_call" | custom-call | tf_op jit(solution)/shard_map/pallas_call | solution.py:478
  75.1 3.9 %all-to-all-start.2 = ((bf16[128,8,256]{2,1,0:T(8,128)(2,1)}), bf16[128,8,256]{2,1,0:T(8,128)(2,1)S(1)}, u32[]{:S(2)}, u32[]{:S(2)}) async-start(bf16[128,8,256]{2,1,0:T(8,128)(2,1)} %bitcast.9), calls=%async_computation.2 | async-start | bytes 1048576 | tf_op jit(solution)/shard_map/all_to_all | solution.py:493
  78.9 1.5 collective-permute-start.3
  80.4 1.2 collective-permute-done.3.refs_7_
  81.6 1.2 copy-done.7
  82.8 1.0 copy-done.13
  83.8 1.0 copy-done.15
  85.8 2.2 %shard_map.158.refs_8_ = bf16[64,2,8,640]{3,2,1,0:T(8,128)(2,1)S(1)} custom-call(s32[1]{0:T(128)} %bitcast.refs_0_, bf16[512,512]{1,0:T(8,128)(2,1)S(1)} %copy-done.15, bf16[512,1024]{1,0:T(8,128)(2,1)S(1)} %copy-done.7, bf16[256,512]{1,0:T(8,128)(2,1)S(1)} %copy-done.1, bf16[256,512]{1,0:T(8,128)(2,1)} %collective-permute-done.1.refs_4_, ...), custom_call_target="tpu_custom_call" | custom-call | tf_op jit(solution)/shard_map/pallas_call | solution.py:478
  88.1 4.6 %all-to-all-done.2 = bf16[128,8,256]{2,1,0:T(8,128)(2,1)S(1)} async-done(((bf16[128,8,256]{2,1,0:T(8,128)(2,1)}), bf16[128,8,256]{2,1,0:T(8,128)(2,1)S(1)}, u32[]{:S(2)}, u32[]{:S(2)}) %all-to-all-start.2) | async-done | bytes 524320 | tf_op jit(solution)/shard_map/all_to_all | solution.py:493
  92.7 1.2 copy-done.9
  94.0 0.9 copy-done.23
  94.9 0.9 copy-done.25
  95.9 6.8 %shard_map.159 = bf16[64,2,8,1152]{3,2,1,0:T(8,128)(2,1)S(1)} custom-call(bf16[1024,256]{1,0:T(8,128)(2,1)S(1)} %bitcast.17, s32[1,512]{1,0:T(1,128)S(1)} %get-tuple-element.31.refs_1_, bf16[512,256]{1,0:T(8,128)(2,1)S(1)} %copy-done.23, bf16[512,768]{1,0:T(8,128)(2,1)S(1)} %copy-done.11, bf16[512,256]{1,0:T(8,128)(2,1)S(1)} %copy-done.25, ...), custom_call_target="tpu_custom_call" | custom-call | tf_op jit(solution)/shard_map/pallas_call | solution.py:478
  102.7 37.7 %all_to_all.26 = bf16[128,8,1152]{2,1,0:T(8,128)(2,1)S(1)} all-to-all(bf16[128,8,1152]{2,1,0:T(8,128)(2,1)S(1)} %bitcast.14), channel_id=1, replica_groups=mesh['pts'=64,'grp'=2] {'pts','grp'}, dimensions={0} | all-to-all | bytes 4718592 | tf_op jit(solution)/shard_map/all_to_all | solution.py:493
  140.8 25.7 %all_to_all.27.refs_1_ = bf16[64,8,1536]{2,1,0:T(8,128)(2,1)S(1)} all-to-all(bf16[64,8,1536]{2,1,0:T(8,128)(2,1)S(1)} %shard_map.161), channel_id=1, replica_groups=mesh['pts'=64,'grp'=2] {'pts'}, dimensions={0} | all-to-all | bytes 3145728 | tf_op jit(solution)/shard_map/all_to_all | solution.py:493
  166.5 3.6 %collective-permute-start.4 = (bf16[64,8,1536]{2,1,0:T(8,128)(2,1)S(1)}, bf16[64,8,1536]{2,1,0:T(8,128)(2,1)S(1)}, u32[]{:S(2)}, u32[]{:S(2)}) collective-permute-start(bf16[64,8,1536]{2,1,0:T(8,128)(2,1)S(1)} %all_to_all.27.refs_1_), channel_id=1, source_target_pairs={{0,1},{1,0},{2,3},{3,2},{4,5},{5,4},{6,7},{7,6},{8,9},{9,8},{10,11... | collective-permute-start | bytes 4718600 | tf_op jit(solution)/shard_map/ppermute | solution.py:489
  170.1 1.2 shard_map.160
  171.3 1.8 %collective-permute-done.4.refs_2_ = bf16[64,8,1536]{2,1,0:T(8,128)(2,1)S(1)} collective-permute-done((bf16[64,8,1536]{2,1,0:T(8,128)(2,1)S(1)}, bf16[64,8,1536]{2,1,0:T(8,128)(2,1)S(1)}, u32[]{:S(2)}, u32[]{:S(2)}) %collective-permute-start.4) | collective-permute-done | bytes 1572896 | tf_op jit(solution)/shard_map/ppermute | solution.py:489
  173.1 3.1 %shard_map.162 = (f32[256,768]{1,0:T(8,128)}, f32[256,256]{1,0:T(8,128)}, f32[512,512]{1,0:T(8,128)}, f32[512,1536]{1,0:T(8,128)}, f32[512,512]{1,0:T(8,128)}) custom-call(s32[1]{0:T(128)} %bitcast.refs_0_, bf16[64,8,1536]{2,1,0:T(8,128)(2,1)S(1)} %all_to_all.27.refs_1_, bf16[64,8,1536]{2,1,0:T(8,128)(2,1)S(1)} %collective-permute-done.4.refs_2_), custom_call_target="tpu_custom_call" | custom-call | tf_op jit(solution)/shard_map/pallas_call | solution.py:478
  (58 shorter events, 10.0 us)
Async XLA Ops:
  0.6 29.3 %copy-start.4 = (bf16[256,768]{1,0:T(8,128)(2,1)S(1)}, bf16[256,768]{1,0:T(8,128)(2,1)}, u32[]{:S(2)}) copy-start(bf16[256,768]{1,0:T(8,128)(2,1)} %refs_6_.5) | copy-start | bytes 1179652
  0.6 1.0 copy-start.21
  5.0 38.8 %copy-start.1 = (bf16[256,512]{1,0:T(8,128)(2,1)S(1)}, bf16[256,512]{1,0:T(8,128)(2,1)}, u32[]{:S(2)}) copy-start(bf16[256,512]{1,0:T(8,128)(2,1)} %refs_3_.7) | copy-start | bytes 786436
  30.0 0.9 copy-start.17
  30.9 30.4 %copy-start = (bf16[512,1536]{1,0:T(8,128)(2,1)S(1)}, bf16[512,1536]{1,0:T(8,128)(2,1)}, u32[]{:S(2)}) copy-start(bf16[512,1536]{1,0:T(8,128)(2,1)} %refs_6_.4) | copy-start | bytes 4718596
  30.9 30.4 %copy-start.2 = (bf16[512,512]{1,0:T(8,128)(2,1)S(1)}, bf16[512,512]{1,0:T(8,128)(2,1)}, u32[]{:S(2)}) copy-start(bf16[512,512]{1,0:T(8,128)(2,1)} %refs_5_.3) | copy-start | bytes 1572868
  30.9 30.4 %copy-start.3 = (bf16[512,512]{1,0:T(8,128)(2,1)S(1)}, bf16[512,512]{1,0:T(8,128)(2,1)}, u32[]{:S(2)}) copy-start(bf16[512,512]{1,0:T(8,128)(2,1)} %refs_7_.4) | copy-start | bytes 1572868
  35.2 1.0 copy-start.8
  36.1 0.9 copy-start.10
  37.0 0.8 copy-start.16
  37.8 0.7 copy-start.22
  39.2 18.4 %all-to-all-start.1 = ((bf16[128,8,256]{2,1,0:T(8,128)(2,1)}), bf16[128,8,256]{2,1,0:T(8,128)(2,1)S(1)}, u32[]{:S(2)}, u32[]{:S(2)}) async-start(bf16[128,8,256]{2,1,0:T(8,128)(2,1)} %bitcast.18), calls=%async_computation.1 | async-start | bytes 1048576 | tf_op jit(solution)/shard_map/all_to_all | solution.py:493
  43.8 16.1 %collective-permute-start.1 = (bf16[256,512]{1,0:T(8,128)(2,1)S(1)}, bf16[256,512]{1,0:T(8,128)(2,1)}, u32[]{:S(2)}, u32[]{:S(2)}) collective-permute-start(bf16[256,512]{1,0:T(8,128)(2,1)S(1)} %copy-done.1), channel_id=1, source_target_pairs={{0,1},{1,0},{2,3},{3,2},{4,5},{5,4},{6,7},{7,6},{8,9},{9,8},{10,11... | collective-permute-start | bytes 786440 | tf_op jit(solution)/shard_map/ppermute | solution.py:489
  58.8 2.5 %collective-permute-start = (bf16[256,512]{1,0:T(8,128)(2,1)}, bf16[256,512]{1,0:T(8,128)(2,1)S(1)}, u32[]{:S(2)}, u32[]{:S(2)}) collective-permute-start(bf16[256,512]{1,0:T(8,128)(2,1)} %shard_map.155.refs_1_), channel_id=1, source_target_pairs={{0,1},{1,0},{2,3},{3,2},{4,5},{5,4},{6,7},{7,6},{8,9},{9,8},{10,11... | collective-permute-start | bytes 786440 | tf_op jit(solution)/shard_map/ppermute | solution.py:489
  69.4 0.8 copy-start.12
  70.2 4.8 %copy-start.6 = (bf16[512,1024]{1,0:T(8,128)(2,1)}, bf16[512,1024]{1,0:T(8,128)(2,1)S(1)}, u32[]{:S(2)}) copy-start(bf16[512,1024]{1,0:T(8,128)(2,1)S(1)} %get-tuple-element.45.refs_2_) | copy-start | bytes 3145732
  70.2 4.8 %copy-start.14 = (bf16[512,512]{1,0:T(8,128)(2,1)}, bf16[512,512]{1,0:T(8,128)(2,1)S(1)}, u32[]{:S(2)}) copy-start(bf16[512,512]{1,0:T(8,128)(2,1)S(1)} %get-tuple-element.44.refs_1_) | copy-start | bytes 1572868
  70.2 1.9 %collective-permute-start.2 = (bf16[256,1024]{1,0:T(8,128)(2,1)S(1)}, bf16[256,1024]{1,0:T(8,128)(2,1)S(1)}, u32[]{:S(2)}, u32[]{:S(2)}) collective-permute-start(bf16[256,1024]{1,0:T(8,128)(2,1)S(1)} %get-tuple-element.37), channel_id=1, source_target_pairs={{0,1},{1,0},{2,3},{3,2},{4,5},{5,4},{6,7},{7,6},{8,9},{9,8},{10,11... | collective-permute-start | bytes 1572872 | tf_op jit(solution)/shard_map/ppermute | solution.py:489
  75.0 6.5 %copy-start.19 = (bf16[256,512]{1,0:T(8,128)(2,1)}, bf16[256,512]{1,0:T(8,128)(2,1)S(1)}, u32[]{:S(2)}) copy-start(bf16[256,512]{1,0:T(8,128)(2,1)S(1)} %get-tuple-element.47.refs_6_) | copy-start | bytes 786436
  75.1 17.7 %all-to-all-start.2 = ((bf16[128,8,256]{2,1,0:T(8,128)(2,1)}), bf16[128,8,256]{2,1,0:T(8,128)(2,1)S(1)}, u32[]{:S(2)}, u32[]{:S(2)}) async-start(bf16[128,8,256]{2,1,0:T(8,128)(2,1)} %bitcast.9), calls=%async_computation.2 | async-start | bytes 1048576 | tf_op jit(solution)/shard_map/all_to_all | solution.py:493
  78.9 2.6 %collective-permute-start.3 = (bf16[256,512]{1,0:T(8,128)(2,1)S(1)}, bf16[256,512]{1,0:T(8,128)(2,1)S(1)}, u32[]{:S(2)}, u32[]{:S(2)}) collective-permute-start(bf16[256,512]{1,0:T(8,128)(2,1)S(1)} %get-tuple-element.47.refs_6_), channel_id=1, source_target_pairs={{0,1},{1,0},{2,3},{3,2},{4,5},{5,4},{6,7},{7,6},{8,9},{9,8},{10,11... | collective-permute-start | bytes 786440 | tf_op jit(solution)/shard_map/ppermute | solution.py:489
  81.6 1.2 copy-start.7
  82.8 1.0 copy-start.13
  83.8 1.0 copy-start.15
  84.9 0.9 copy-start.20
  85.8 6.9 %copy-start.5 = (bf16[256,768]{1,0:T(8,128)(2,1)S(1)}, bf16[256,768]{1,0:T(8,128)(2,1)}, u32[]{:S(2)}) copy-start(bf16[256,768]{1,0:T(8,128)(2,1)} %refs_6_.5) | copy-start | bytes 1179652
  85.8 6.9 %copy-start.11 = (bf16[512,768]{1,0:T(8,128)(2,1)S(1)}, bf16[512,768]{1,0:T(8,128)(2,1)}, u32[]{:S(2)}) copy-start(bf16[512,768]{1,0:T(8,128)(2,1)} %copy-done.10) | copy-start | bytes 2359300
  85.8 6.9 %copy-start.18 = (bf16[256,256]{1,0:T(8,128)(2,1)S(1)}, bf16[256,256]{1,0:T(8,128)(2,1)}, u32[]{:S(2)}) copy-start(bf16[256,256]{1,0:T(8,128)(2,1)} %refs_7_.5) | copy-start | bytes 393220
  92.7 1.2 copy-start.9
  94.0 0.9 copy-start.23
  94.9 0.9 copy-start.25
  166.5 6.7 %collective-permute-start.4 = (bf16[64,8,1536]{2,1,0:T(8,128)(2,1)S(1)}, bf16[64,8,1536]{2,1,0:T(8,128)(2,1)S(1)}, u32[]{:S(2)}, u32[]{:S(2)}) collective-permute-start(bf16[64,8,1536]{2,1,0:T(8,128)(2,1)S(1)} %all_to_all.27.refs_1_), channel_id=1, source_target_pairs={{0,1},{1,0},{2,3},{3,2},{4,5},{5,4},{6,7},{7,6},{8,9},{9,8},{10,11... | collective-permute-start | bytes 4718600 | tf_op jit(solution)/shard_map/ppermute | solution.py:489
  (4 other events, 2.7 us)

commit v5 on v4

--- a/solution.py
+++ b/solution.py
@@ -67,7 +67,9 @@
     return jnp.concatenate([turned] * (count // 128), axis=1)
 
 
-def route_kernel(place, source, counts, points, send, send_slot, receive_slot, live):
+def route_kernel(
+    place, source, counts, points, send, send_slot, pair_slot, receive_slot, live
+):
     count = place.shape[1]
     shift = count.bit_length() - 1
     capacity = send.shape[0] * count // (counts.shape[1] * BALL)
@@ -78,6 +80,10 @@
     rank = jnp.sum(jnp.where(earlier, 1.0, 0.0), axis=0, keepdims=True)
     slot = to_row * capacity + rank.astype(jnp.int32)
     send_slot[...] = slot
+    even_first = jnp.where(columns < count // 2, 2 * columns, 2 * columns + 1 - count)
+    digits = jnp.concatenate([slot >> 5, slot & 31] + [jnp.zeros_like(slot)] * 6, axis=0)
+    moved = mm(digits.astype(F32).astype(BF), (rows == even_first).astype(BF)).astype(jnp.int32)
+    pair_slot[...] = moved[0:1] * 32 + moved[1:2]
     source_row = source[...]
     from_row = source_row >> shift
     earlier = (column_of(from_row) == from_row.astype(F32)) & (
@@ -99,11 +105,9 @@
     place = one_hot(receive_slot[...], arrived.shape[0])
     rows_in = mm(place, arrived[...], (0, 0))
     rotated[...] = rows_in.astype(BF)
-    rotated.flush()
     features = rows_in.shape[1]
     normed, _ = normalize(rows_in)
     projected[...] = mm(normed.astype(BF), projection[...]).astype(BF)
-    projected.flush()
     balls = rows_in.shape[0] // BALL
     pairs = features // PAIR
     for ball in range(balls):
@@ -122,51 +126,35 @@
                 halves.append(mm(head_weights, value))
             mixed = jnp.where(head_half(halves[0].shape, 0), halves[0], halves[1])
             mixture[rows, lanes] = mixed.astype(BF)
-    weights.flush()
-    mixture.flush()
     result = (rows_in + mm(mixture[...], output[...])).astype(BF)
     send[...] = mm(place, result).astype(BF)
 
 
-def join_kernel(arrived, slots, joined):
-    half = joined.shape[1] // 2
-    for side in range(2):
-        place = one_hot(slots[side : side + 1, :], arrived.shape[0])
-        joined[:, side * half : (side + 1) * half] = mm(place, arrived[...], (0, 0)).astype(BF)
+def join_kernel(arrived, pair_slot, cotangent, pack):
+    half_rows, wide = cotangent.shape
+    place = one_hot(pair_slot[...], arrived.shape[0])
+    rows = mm(place, arrived[...], (0, 0)).astype(BF)
+    pack[:, : wide // 2] = rows[:half_rows]
+    pack[:, wide // 2 : wide] = rows[half_rows:]
+    pack[:, wide:] = cotangent[...]
 
 
 def coarse_kernel(
-    group,
-    own_joined,
-    other_joined,
-    own_cotangent,
-    other_cotangent,
-    pool,
-    projection,
-    output,
-    coarse,
-    keep,
-    give,
-    both_joined,
-    unit,
-    stacked,
-):
-    half_rows, wide = own_joined.shape
+    group, own_pack, other_pack, pool, projection, output, coarse, keep, give, unit
+):
+    half_rows, wide = coarse.shape
     part = wide // 2
     first = pl.multiple_of(group[0] * part, part)
-    joined = jnp.concatenate([own_joined[...], other_joined[...]], axis=0)
-    both_joined[...] = joined
-    both_joined.flush()
+    joined = jnp.concatenate([own_pack[:, :wide], other_pack[:, :wide]], axis=0)
     tokens = mm(joined, pool[...]).astype(BF)
     coarse[...] = tokens[:half_rows]
     normed, _ = normalize(tokens)
     unit_rows = normed.astype(BF)
     unit[...] = unit_rows
-    unit.flush()
     queries = mm(unit_rows, projection[:, pl.ds(first, part)]).astype(BF)
     keys = mm(unit_rows, projection[:, pl.ds(wide + first, part)]).astype(BF)
     values = mm(unit_rows, projection[:, pl.ds(2 * wide + first, part)]).astype(BF)
-    cotangent = jnp.concatenate([own_cotangent[...], other_cotangent[...]], axis=0)
+    cotangent = jnp.concatenate([own_pack[:, wide:], other_pack[:, wide:]], axis=0)
     incoming = mm(cotangent, output[pl.ds(first, part), :], (1, 1)).astype(BF)
     for pair in range(part // PAIR):
         lanes = slice(pair * PAIR, (pair + 1) * PAIR)
@@ -187,7 +175,6 @@
             target = slice(at * part + pair * PAIR, at * part + (pair + 1) * PAIR)
             keep[:, target] = both[:half_rows]
             give[:, target] = both[half_rows:]
-            stacked[:, target] = both
 
 
 def coarse_finish_kernel(
@@ -199,7 +186,7 @@
     pool,
     projection,
     output,
-    slots,
+    pair_slot,
     result,
     gradient,
     send,
@@ -226,37 +213,31 @@
     gradient[...] = gradient_rows
     fine = mm(gradient_rows, pool[...], (1, 1)).astype(BF)
     features = send.shape[1]
-    total = mm(one_hot(slots[0:1, :], send.shape[0]), fine[:, :features])
-    total = total + mm(one_hot(slots[1:2, :], send.shape[0]), fine[:, features:])
-    send[...] = total.astype(BF)
+    stacked = jnp.concatenate([fine[:, :features], fine[:, features:]], axis=0)
+    send[...] = mm(one_hot(pair_slot[...], send.shape[0]), stacked).astype(BF)
 
 
 def coarse_weights_kernel(
-    group,
-    unit,
-    stacked,
-    own_cotangent,
-    other_cotangent,
-    joined,
-    own_gradient,
-    other_gradient,
-    terms,
-):
-    part = stacked.shape[1] // 4
-    first = pl.multiple_of(group[0] * part, part)
+    arrived, unit, keep, give, own_pack, other_pack, gradient, terms, gradient_out
+):
+    gradient_out[...] = gradient[...]
+    wide = unit.shape[1]
+    part = wide // 2
+    stacked = jnp.concatenate([keep[...], give[...]], axis=0)
+    cotangent = jnp.concatenate([own_pack[:, wide:], other_pack[:, wide:]], axis=0)
     projection_term = mm(unit[...], stacked[:, part:], (0, 0))
-    cotangent = jnp.concatenate([own_cotangent[...], other_cotangent[...]], axis=0)
-    output_term = mm(stacked[:, :part], cotangent, (0, 0))
-    gradient = jnp.concatenate([own_gradient[...], other_gradient[...]], axis=0)
-    pool_term = mm(joined[:, pl.ds(first, part)], gradient, (0, 0))
     across = projection_term.shape[1] // 2
     for side in range(2):
         columns = projection_term[:, side * across : (side + 1) * across]
         put_blocks(terms, side, 0, columns)
-        for at, term in enumerate((output_term, pool_term)):
-            width = term.shape[1] // 4
-            stack = [term[:, (2 * side + k) * width : (2 * side + k + 1) * width] for k in range(2)]
-            put_blocks(terms, side, across + at * width, jnp.concatenate(stack, axis=0))
+    put_quarters(terms, across, mm(stacked[:, :part], cotangent, (0, 0)))
+
+
+def put_quarters(blocks, lane, term):
+    width = term.shape[1] // 4
+    for side in range(2):
+        stack = [term[:, (2 * side + k) * width : (2 * side + k + 1) * width] for k in range(2)]
+        put_blocks(blocks, side, lane, jnp.concatenate(stack, axis=0))
 
 
 def put_blocks(blocks, side, lane, rows):
@@ -325,6 +306,7 @@
 
 
 def fine_backward_kernel(
+    group,
     arrived,
     receive_slot,
     rotated,
@@ -334,14 +316,13 @@
     projection,
     output,
     coarse_terms,
+    own_pack,
+    other_pack,
+    own_gradient,
+    other_gradient,
     send,
     grad_projected,
-    arriving,
-):
-    filling = pltpu.make_async_copy(
-        coarse_terms, send.at[:, :, :, 2 * rotated.shape[1] :], arriving
-    )
-    filling.start()
+):
     place = one_hot(receive_slot[...], arrived.shape[0])
     gradient_in = mm(place, arrived[...], (0, 0))
     gradient_rows = gradient_in.astype(BF)
@@ -381,7 +362,13 @@
     send[:, :, :, :features] = tokens.reshape(send.shape[:3] + (features,)).astype(BF)
     for side in range(2):
         put_blocks(send, side, features, jnp.concatenate(terms[2 * side : 2 * side + 2], axis=0))
-    filling.wait()
+    settled = 2 * features + coarse_terms.shape[3]
+    send[:, :, :, 2 * features : settled] = coarse_terms[...]
+    part = own_gradient.shape[1] // 2
+    first = pl.multiple_of(group[0] * part, part)
+    pool_term = mm(own_pack[:, pl.ds(first, part)], own_gradient[...], (0, 0))
+    pool_term = pool_term + mm(other_pack[:, pl.ds(first, part)], other_gradient[...], (0, 0))
+    put_quarters(send, settled, pool_term)
 
 
 def take_kernel(arrived, slots, rows_out):
@@ -396,10 +383,6 @@
 
 
 class Far(NamedTuple):
-    value: jax.Array
-
-
-class Direct(NamedTuple):
     value: jax.Array
 
 
@@ -442,12 +425,12 @@
             self.started = True
 
 
-def call(kernel, inputs, outputs, scalar=False, scratch=()):
+def call(kernel, inputs, outputs, scalar=False, scratch=(), mebibytes=16):
     in_specs, arrays, buffers = [], [], []
     for at, value in enumerate(inputs):
-        far, direct = isinstance(value, Far), isinstance(value, Direct)
-        in_specs.append(SMEM if scalar and at == 0 else HBM if far or direct else VMEM)
-        arrays.append(value.value if far or direct else value)
+        far = isinstance(value, Far)
+        in_specs.append(SMEM if scalar and at == 0 else HBM if far else VMEM)
+        arrays.append(value.value if far else value)
         if far:
             buffers.append(pltpu.VMEM(value.value.shape, value.value.dtype))
     buffers.extend(pltpu.VMEM(out.shape, out.dtype) for out in outputs if out.far)
@@ -481,7 +464,7 @@
         in_specs=in_specs,
         out_specs=[HBM if out.far else VMEM for out in outputs],
         scratch_shapes=buffers + own + list(scratch),
-        compiler_params=pltpu.CompilerParams(vmem_limit_bytes=20 * 1024 * 1024),
+        compiler_params=pltpu.CompilerParams(vmem_limit_bytes=mebibytes * 1024 * 1024),
     )(*arrays)
 
 
@@ -519,7 +502,7 @@
     wide = 2 * features
     half_rows = count // 2
 
-    send, send_slot, receive_slot, live = call(
+    send, send_slot, pair_slot, receive_slot, live = call(
         route_kernel,
         (
             Far(rotated_place.reshape(1, count)),
@@ -531,46 +514,37 @@
             Near((slots, features)),
             Near((1, count), jnp.int32),
             Near((1, count), jnp.int32),
+            Near((1, count), jnp.int32),
             Near((1, count), F32),
         ),
-    )
-    other_cotangent = exchange(coarse_cotangent)
+        mebibytes=56,
+    )
     arrived = route(send, devices)
-    pair_slots = send_slot.reshape(half_rows, 2).T
     heads = features // HD * (count // BALL)
     send, rotated, projected, mixture, weights = call(
         fine_forward_kernel,
-        (arrived, receive_slot, live, Far(fine_projection), Far(fine_output)),
+        (arrived, receive_slot, live, fine_projection, fine_output),
         (
             Near((slots, features)),
-            Near((count, features), far=True),
-            Near((count, 3 * features), far=True),
-            Near((count, features), far=True),
-            Near((heads, BALL, BALL), far=True),
+            Near((count, features)),
+            Near((count, 3 * features)),
+            Near((count, features)),
+            Near((heads, BALL, BALL)),
         ),
     )
     arrived = route(send, devices)
-    (own_joined,) = call(join_kernel, (arrived, pair_slots), (Near((half_rows, wide)),))
-    other_joined = exchange(own_joined)
-    coarse, keep, give, joined, unit, stacked = call(
+    (own_pack,) = call(
+        join_kernel, (arrived, pair_slot, coarse_cotangent), (Near((half_rows, 2 * wide)),)
+    )
+    other_pack = exchange(own_pack)
+    coarse, keep, give, unit = call(
         coarse_kernel,
-        (
-            group,
-            own_joined,
-            other_joined,
-            Far(coarse_cotangent),
-            Far(other_cotangent),
-            Far(pool_weight),
-            Far(coarse_projection),
-            Far(coarse_output),
-        ),
+        (group, own_pack, other_pack, pool_weight, coarse_projection, coarse_output),
         (
             Near((half_rows, wide)),
             Near((half_rows, 2 * wide)),
             Near((half_rows, 2 * wide)),
-            Near((count, wide), far=True),
-            Near((count, wide), far=True),
-            Near((count, 2 * wide), far=True),
+            Near((count, wide)),
         ),
         scalar=True,
     )
@@ -582,11 +556,11 @@
             coarse,
             keep,
             got,
-            Far(coarse_cotangent),
-            Far(pool_weight),
-            Far(coarse_projection),
-            Far(coarse_output),
-            pair_slots,
+            coarse_cotangent,
+            pool_weight,
+            coarse_projection,
+            coarse_output,
+            pair_slot,
         ),
         (
             Near((half_rows, wide), far=True),
@@ -596,39 +570,35 @@
         scalar=True,
     )
     arrived = route(send, devices)
-    other_gradient = exchange(coarse_gradient)
     owners = lax.axis_size("pts")
-    (coarse_terms,) = call(
+    coarse_terms, own_gradient = call(
         coarse_weights_kernel,
-        (
-            group,
-            Far(unit),
-            Far(stacked),
-            Far(coarse_cotangent),
-            Far(other_cotangent),
-            Far(joined),
-            coarse_gradient,
-            other_gradient,
-        ),
-        (Near((owners, 2, slots // devices, 5 * wide // 4), far=True),),
-        scalar=True,
-    )
+        (arrived, unit, keep, give, own_pack, other_pack, coarse_gradient),
+        (Near((owners, 2, slots // devices, wide)), Near((half_rows, wide))),
+    )
+    other_gradient = exchange(own_gradient)
     across = 2 * features + 5 * wide // 4
     (send,) = call(
         fine_backward_kernel,
         (
+            group,
             arrived,
             receive_slot,
-            Far(rotated),
-            Far(projected),
-            Far(mixture),
-            Far(weights),
-            Far(fine_projection),
-            Far(fine_output),
-            Direct(coarse_terms),
+            rotated,
+            projected,
+            mixture,
+            weights,
+            fine_projection,
+            fine_output,
+            coarse_terms,
+            own_pack,
+            other_pack,
+            own_gradient,
+            other_gradient,
         ),
         (Near((owners, 2, slots // devices, across)),),
-        scratch=(pltpu.VMEM((count, 3 * features), BF), pltpu.SemaphoreType.DMA),
+        scalar=True,
+        scratch=(pltpu.VMEM((count, 3 * features), BF),),
     )
     arrived = spread_blocks(send.reshape(devices, slots // devices, across), ("pts", "grp"))
     (spread,) = call(

time: 177 us -> 166 us (0.938)
  blocking collectives: 88.4 us -> 123 us
  waiting for transfers between devices: 21.6 us -> 6.03 us
  local copies, waits for them, and re-layouts: 16.9 us -> 3.43 us
  starting transfers between devices: 16.3 us -> 6.93 us
  Pallas kernels: 31.4 us -> 24.8 us
    all_to_all x3 -> x5, blocking collectives: 88.4 us -> 123 us  [spread_blocks(): return lax.all_to_all(values, axes, split_axis=0, concat_axis=0, tiled=True)]
    all_to_all x2 -> x0, waiting for transfers between devices: 15.8 us -> none  [spread_blocks(): return lax.all_to_all(values, axes, split_axis=0, concat_axis=0, tiled=True)]
    unnamed x58 -> x44, local copies, waits for them, and re-layouts: 16.2 us -> 3.4 us
    all_to_all x2 -> x0, starting transfers between devices: 8.46 us -> none  [spread_blocks(): return lax.all_to_all(values, axes, split_axis=0, concat_axis=0, tiled=True)]
    pallas_call x10, Pallas kernels: 31.4 us -> 24.8 us  [call(): pl.pallas_call(body, out_shape=[jax.ShapeDtypeStruct(out.shape, out.dtype...]
    ppermute x5 -> x4, starting transfers between devices: 7.88 us -> 6.93 us  [exchange(): return lax.ppermute(values, 'grp', [(0, 1), (1, 0)])]
    ppermute x5 -> x4, waiting for transfers between devices: 5.87 us -> 6.03 us  [exchange(): return lax.ppermute(values, 'grp', [(0, 1), (1, 0)])]
  transfers between devices with their start and end apart: 7 -> 4, of which waited for: 6 -> 4; matrix products, arithmetic and copies ran while one was open for 1% -> 0% of each run, Pallas kernels for 3% -> 1%
where the time goes in v5:
time: 166 us; the launch traced here: 165 us
  blocking collectives  123 us (74%)
  Pallas kernels  24.8 us (15%)
  starting transfers between devices  6.93 us (4%)
  waiting for transfers between devices  6.03 us (4%)
  local copies, waits for them, and re-layouts  3.43 us (2%)
    all_to_all x5, blocking collectives, spread_blocks(): return lax.all_to_all(values, axes, split_axis=0, concat_axis=0, tiled=True)  123 us
    pallas_call x10, Pallas kernels, call(): pl.pallas_call(body, out_shape=[jax.ShapeDtypeStruct(out.shape, out.dtype...  24.8 us
    ppermute x4, starting transfers between devices, exchange(): return lax.ppermute(values, 'grp', [(0, 1), (1, 0)])  6.93 us
    ppermute x4, waiting for transfers between devices, exchange(): return lax.ppermute(values, 'grp', [(0, 1), (1, 0)])  6.03 us
    unnamed x44, local copies, waits for them, and re-layouts  3.4 us
  transfers between devices with their start and end apart: 4, of which 4 were waited for; matrix products, arithmetic and copies ran while one was open for 0% of the time, Pallas kernels for 1%

profile of v5, /device:TPU:1, one launch (start us, length us, event | category | flops | bytes accessed | tf_op | source)
XLA Modules:
  0.0 165.5 jit_solution(1489643408604800373)
XLA Ops:
  0.6 3.0 %shard_map.153 = (bf16[1024,256]{1,0:T(8,128)(2,1)}, s32[1,512]{1,0:T(1,128)}, s32[1,512]{1,0:T(1,128)}, s32[1,512]{1,0:T(1,128)}, f32[1,512]{1,0:T(1,128)}) custom-call(s32[1,512]{1,0:T(1,128)} %bitcast.21, s32[1,512]{1,0:T(1,128)} %bitcast.22, s32[1,256]{1,0:T(1,128)} %bitcast.23, bf16[512,256]{1,0:T(8,128)(2,1)} %refs_3_.3), custom_call_target="tpu_custom_call" | custom-call | tf_op jit(solution)/shard_map/pallas_call | solution.py:461
  3.6 0.0 copy-start.7
  3.6 0.0 copy-start.19
  3.6 25.2 %all_to_all.25 = bf16[128,8,256]{2,1,0:T(8,128)(2,1)S(1)} all-to-all(bf16[128,8,256]{2,1,0:T(8,128)(2,1)} %bitcast.20), channel_id=1, replica_groups=mesh['pts'=64,'grp'=2] {'pts','grp'}, dimensions={0} | all-to-all | bytes 1048576 | tf_op jit(solution)/shard_map/all_to_all | solution.py:476
  28.8 0.9 copy-done.11
  29.7 0.7 copy-done.17
  30.4 0.7 copy-done.21
  31.1 3.3 %shard_map.154 = (bf16[1024,256]{1,0:T(8,128)(2,1)S(1)}, bf16[512,256]{1,0:T(8,128)(2,1)S(1)}, bf16[512,768]{1,0:T(8,128)(2,1)S(1)}, bf16[512,256]{1,0:T(8,128)(2,1)S(1)}, bf16[8,256,256]{2,1,0:T(8,128)(2,1)S(1)}) custom-call(bf16[1024,256]{1,0:T(8,128)(2,1)S(1)} %bitcast.17, s32[1,512]{1,0:T(1,128)S(1)} %copy-done.17, f32[1,512]{1,0:T(1,128)S(1)} %copy-done.21, ...), custom_call_target="tpu_custom_call" | custom-call | tf_op jit(solution)/shard_map/pallas_call | solution.py:461
  34.4 0.0 copy-start.5
  34.4 0.0 copy-start.9
  34.4 18.1 %all_to_all.26 = bf16[128,8,256]{2,1,0:T(8,128)(2,1)S(1)} all-to-all(bf16[128,8,256]{2,1,0:T(8,128)(2,1)S(1)} %bitcast.18), channel_id=1, replica_groups=mesh['pts'=64,'grp'=2] {'pts','grp'}, dimensions={0} | all-to-all | bytes 1048576 | tf_op jit(solution)/shard_map/all_to_all | solution.py:476
  52.5 0.5 shard_map.155.refs_1_.refs_4_.refs_10_
  53.0 1.4 collective-permute-start
  54.4 1.5 collective-permute-done.refs_2_.refs_5_.refs_11_
  56.0 1.0 copy-done.2
  57.0 6.1 %shard_map.156 = (bf16[256,512]{1,0:T(8,128)(2,1)S(1)}, bf16[256,1024]{1,0:T(8,128)(2,1)S(1)}, bf16[256,1024]{1,0:T(8,128)(2,1)S(1)}, bf16[512,512]{1,0:T(8,128)(2,1)S(1)}) custom-call(s32[1]{0:T(128)} %bitcast.refs_0_, bf16[256,1024]{1,0:T(8,128)(2,1)S(1)} %shard_map.155.refs_1_.refs_4_.refs_10_, ...), custom_call_target="tpu_custom_call" | custom-call | tf_op jit(solution)/shard_map/pallas_call | solution.py:461
  63.1 0.4 collective-permute-start.1
  63.5 1.5 collective-permute-done.1.refs_3_
  65.1 1.5 shard_map.157
  66.6 17.3 %all_to_all.27 = bf16[128,8,256]{2,1,0:T(8,128)(2,1)S(1)} all-to-all(bf16[128,8,256]{2,1,0:T(8,128)(2,1)S(1)} %bitcast.19), channel_id=1, replica_groups=mesh['pts'=64,'grp'=2] {'pts','grp'}, dimensions={0} | all-to-all | bytes 1048576 | tf_op jit(solution)/shard_map/all_to_all | solution.py:476
  83.9 0.0 copy-start.16
  84.0 0.7 shard_map.158
  84.7 1.5 collective-permute-start.2
  86.2 1.2 collective-permute-done.2.refs_13_
  87.4 5.1 %shard_map.159 = bf16[64,2,8,1152]{3,2,1,0:T(8,128)(2,1)S(1)} custom-call(s32[1]{0:T(128)} %bitcast.refs_0_, bf16[1024,256]{1,0:T(8,128)(2,1)S(1)} %bitcast.15, s32[1,512]{1,0:T(1,128)S(1)} %copy-done.18, bf16[512,256]{1,0:T(8,128)(2,1)S(1)} %copy-done.14, bf16[512,768]{1,0:T(8,128)(2,1)S(1)} %copy-done.10, bf16[512,256]{1,0:T(8,128)(2,1)S(1)} %copy-done.16, ...), custom_call_target="tpu_custom_call" | custom-call | tf_op jit(solution)/shard_map/pallas_call | solution.py:461
  92.5 37.0 %all_to_all.28 = bf16[128,8,1152]{2,1,0:T(8,128)(2,1)S(1)} all-to-all(bf16[128,8,1152]{2,1,0:T(8,128)(2,1)S(1)} %bitcast.13), channel_id=1, replica_groups=mesh['pts'=64,'grp'=2] {'pts','grp'}, dimensions={0} | all-to-all | bytes 4718592 | tf_op jit(solution)/shard_map/all_to_all | solution.py:476
  129.4 0.3 shard_map.161
  129.8 25.7 %all_to_all.29.refs_1_ = bf16[64,8,1536]{2,1,0:T(8,128)(2,1)S(1)} all-to-all(bf16[64,8,1536]{2,1,0:T(8,128)(2,1)S(1)} %shard_map.161), channel_id=1, replica_groups=mesh['pts'=64,'grp'=2] {'pts'}, dimensions={0} | all-to-all | bytes 3145728 | tf_op jit(solution)/shard_map/all_to_all | solution.py:476
  155.5 3.6 %collective-permute-start.3 = (bf16[64,8,1536]{2,1,0:T(8,128)(2,1)S(1)}, bf16[64,8,1536]{2,1,0:T(8,128)(2,1)S(1)}, u32[]{:S(2)}, u32[]{:S(2)}) collective-permute-start(bf16[64,8,1536]{2,1,0:T(8,128)(2,1)S(1)} %all_to_all.29.refs_1_), channel_id=1, source_target_pairs={{0,1},{1,0},{2,3},{3,2},{4,5},{5,4},{6,7},{7,6},{8,9},{9,8},{10,11... | collective-permute-start | bytes 4718600 | tf_op jit(solution)/shard_map/ppermute | solution.py:472
  159.2 1.2 shard_map.160
  160.4 1.8 %collective-permute-done.3.refs_2_ = bf16[64,8,1536]{2,1,0:T(8,128)(2,1)S(1)} collective-permute-done((bf16[64,8,1536]{2,1,0:T(8,128)(2,1)S(1)}, bf16[64,8,1536]{2,1,0:T(8,128)(2,1)S(1)}, u32[]{:S(2)}, u32[]{:S(2)}) %collective-permute-start.3) | collective-permute-done | bytes 1572896 | tf_op jit(solution)/shard_map/ppermute | solution.py:472
  162.2 3.1 %shard_map.162 = (f32[256,768]{1,0:T(8,128)}, f32[256,256]{1,0:T(8,128)}, f32[512,512]{1,0:T(8,128)}, f32[512,1536]{1,0:T(8,128)}, f32[512,512]{1,0:T(8,128)}) custom-call(s32[1]{0:T(128)} %bitcast.refs_0_, bf16[64,8,1536]{2,1,0:T(8,128)(2,1)S(1)} %all_to_all.29.refs_1_, bf16[64,8,1536]{2,1,0:T(8,128)(2,1)S(1)} %collective-permute-done.3.refs_2_), custom_call_target="tpu_custom_call" | custom-call | tf_op jit(solution)/shard_map/pallas_call | solution.py:461
  (36 shorter events, 0.1 us)
Async XLA Ops:
  0.6 28.2 %copy-start.4 = (bf16[256,768]{1,0:T(8,128)(2,1)S(1)}, bf16[256,768]{1,0:T(8,128)(2,1)}, u32[]{:S(2)}) copy-start(bf16[256,768]{1,0:T(8,128)(2,1)} %refs_7_.3) | copy-start | bytes 1179652
  3.6 48.9 %copy-start.7 = (bf16[256,512]{1,0:T(8,128)(2,1)S(1)}, bf16[256,512]{1,0:T(8,128)(2,1)}, u32[]{:S(2)}) copy-start(bf16[256,512]{1,0:T(8,128)(2,1)} %refs_4_.5) | copy-start | bytes 786436
  3.6 48.9 %copy-start.19 = (s32[1,512]{1,0:T(1,128)S(1)}, s32[1,512]{1,0:T(1,128)}, u32[]{:S(2)}) copy-start(s32[1,512]{1,0:T(1,128)} %get-tuple-element.35.refs_1_.refs_8_) | copy-start | bytes 6148
  28.8 0.9 copy-start.11
  29.7 0.7 copy-start.17
  30.4 0.7 copy-start.21
  31.1 24.9 %copy-start = (bf16[512,1536]{1,0:T(8,128)(2,1)S(1)}, bf16[512,1536]{1,0:T(8,128)(2,1)}, u32[]{:S(2)}) copy-start(bf16[512,1536]{1,0:T(8,128)(2,1)} %refs_6_.1) | copy-start | bytes 4718596
  31.1 24.9 %copy-start.1 = (bf16[512,512]{1,0:T(8,128)(2,1)S(1)}, bf16[512,512]{1,0:T(8,128)(2,1)}, u32[]{:S(2)}) copy-start(bf16[512,512]{1,0:T(8,128)(2,1)} %refs_5_.3) | copy-start | bytes 1572868
  34.4 18.6 %copy-start.5 = (bf16[8,256,256]{2,1,0:T(8,128)(2,1)}, bf16[8,256,256]{2,1,0:T(8,128)(2,1)S(1)}, u32[]{:S(2)}) copy-start(bf16[8,256,256]{2,1,0:T(8,128)(2,1)S(1)} %get-tuple-element.44.refs_6_) | copy-start | bytes 3145732
  34.4 20.0 %copy-start.9 = (bf16[512,768]{1,0:T(8,128)(2,1)}, bf16[512,768]{1,0:T(8,128)(2,1)S(1)}, u32[]{:S(2)}) copy-start(bf16[512,768]{1,0:T(8,128)(2,1)S(1)} %get-tuple-element.42.refs_4_) | copy-start | bytes 2359300
  34.4 20.0 %copy-start.13 = (bf16[512,256]{1,0:T(8,128)(2,1)}, bf16[512,256]{1,0:T(8,128)(2,1)S(1)}, u32[]{:S(2)}) copy-start(bf16[512,256]{1,0:T(8,128)(2,1)S(1)} %get-tuple-element.41.refs_3_) | copy-start | bytes 786436
  34.4 20.0 %copy-start.15 = (bf16[512,256]{1,0:T(8,128)(2,1)}, bf16[512,256]{1,0:T(8,128)(2,1)S(1)}, u32[]{:S(2)}) copy-start(bf16[512,256]{1,0:T(8,128)(2,1)S(1)} %get-tuple-element.43.refs_5_) | copy-start | bytes 786436
  53.0 2.9 %collective-permute-start = (bf16[256,1024]{1,0:T(8,128)(2,1)S(1)}, bf16[256,1024]{1,0:T(8,128)(2,1)S(1)}, u32[]{:S(2)}, u32[]{:S(2)}) collective-permute-start(bf16[256,1024]{1,0:T(8,128)(2,1)S(1)} %shard_map.155.refs_1_.refs_4_.refs_10_), channel_id=1, source_target_pairs={{0,1},{1,0},{2,3},{3,2},{4,5},{5,4},{6,7},{7,6},{8,9},{9,8},{10,11... | collective-permute-start | bytes 1572872 | tf_op jit(solution)/shard_map/ppermute | solution.py:472
  56.0 1.0 copy-start.2
  57.0 8.1 %copy-start.3 = (bf16[512,512]{1,0:T(8,128)(2,1)S(1)}, bf16[512,512]{1,0:T(8,128)(2,1)}, u32[]{:S(2)}) copy-start(bf16[512,512]{1,0:T(8,128)(2,1)} %refs_7_.2) | copy-start | bytes 1572868
  57.0 8.1 %copy-start.8 = (bf16[256,512]{1,0:T(8,128)(2,1)S(1)}, bf16[256,512]{1,0:T(8,128)(2,1)}, u32[]{:S(2)}) copy-start(bf16[256,512]{1,0:T(8,128)(2,1)} %refs_4_.5) | copy-start | bytes 786436
  63.1 2.0 %collective-permute-start.1 = (bf16[256,1024]{1,0:T(8,128)(2,1)S(1)}, bf16[256,1024]{1,0:T(8,128)(2,1)S(1)}, u32[]{:S(2)}, u32[]{:S(2)}) collective-permute-start(bf16[256,1024]{1,0:T(8,128)(2,1)S(1)} %get-tuple-element.38.refs_3_), channel_id=1, source_target_pairs={{0,1},{1,0},{2,3},{3,2},{4,5},{5,4},{6,7},{7,6},{8,9},{9,8},{10,11... | collective-permute-start | bytes 1572872 | tf_op jit(solution)/shard_map/ppermute | solution.py:472
  83.9 3.4 %copy-start.6 = (bf16[8,256,256]{2,1,0:T(8,128)(2,1)S(1)}, bf16[8,256,256]{2,1,0:T(8,128)(2,1)}, u32[]{:S(2)}) copy-start(bf16[8,256,256]{2,1,0:T(8,128)(2,1)} %copy-done.5) | copy-start | bytes 3145732
  83.9 3.4 %copy-start.10 = (bf16[512,768]{1,0:T(8,128)(2,1)S(1)}, bf16[512,768]{1,0:T(8,128)(2,1)}, u32[]{:S(2)}) copy-start(bf16[512,768]{1,0:T(8,128)(2,1)} %copy-done.9) | copy-start | bytes 2359300
  83.9 3.4 %copy-start.12 = (bf16[256,256]{1,0:T(8,128)(2,1)S(1)}, bf16[256,256]{1,0:T(8,128)(2,1)}, u32[]{:S(2)}) copy-start(bf16[256,256]{1,0:T(8,128)(2,1)} %refs_8_.1) | copy-start | bytes 393220
  83.9 3.4 %copy-start.14 = (bf16[512,256]{1,0:T(8,128)(2,1)S(1)}, bf16[512,256]{1,0:T(8,128)(2,1)}, u32[]{:S(2)}) copy-start(bf16[512,256]{1,0:T(8,128)(2,1)} %copy-done.13) | copy-start | bytes 786436
  83.9 3.4 %copy-start.16 = (bf16[512,256]{1,0:T(8,128)(2,1)S(1)}, bf16[512,256]{1,0:T(8,128)(2,1)}, u32[]{:S(2)}) copy-start(bf16[512,256]{1,0:T(8,128)(2,1)} %copy-done.15) | copy-start | bytes 786436
  83.9 3.4 %copy-start.18 = (s32[1,512]{1,0:T(1,128)S(1)}, s32[1,512]{1,0:T(1,128)}, u32[]{:S(2)}) copy-start(s32[1,512]{1,0:T(1,128)} %get-tuple-element.32.refs_1_.refs_2_) | copy-start | bytes 6148
  84.7 2.6 %collective-permute-start.2 = (bf16[256,512]{1,0:T(8,128)(2,1)S(1)}, bf16[256,512]{1,0:T(8,128)(2,1)S(1)}, u32[]{:S(2)}, u32[]{:S(2)}) collective-permute-start(bf16[256,512]{1,0:T(8,128)(2,1)S(1)} %get-tuple-element.48.refs_12_), channel_id=1, source_target_pairs={{0,1},{1,0},{2,3},{3,2},{4,5},{5,4},{6,7},{7,6},{8,9},{9,8},{10,11... | collective-permute-start | bytes 786440 | tf_op jit(solution)/shard_map/ppermute | solution.py:472
  129.8 29.4 %copy-start.20 = (s32[1,512]{1,0:T(1,128)S(1)}, s32[1,512]{1,0:T(1,128)}, u32[]{:S(2)}) copy-start(s32[1,512]{1,0:T(1,128)} %get-tuple-element.49.refs_1_) | copy-start | bytes 6148
  155.5 6.7 %collective-permute-start.3 = (bf16[64,8,1536]{2,1,0:T(8,128)(2,1)S(1)}, bf16[64,8,1536]{2,1,0:T(8,128)(2,1)S(1)}, u32[]{:S(2)}, u32[]{:S(2)}) collective-permute-start(bf16[64,8,1536]{2,1,0:T(8,128)(2,1)S(1)} %all_to_all.29.refs_1_), channel_id=1, source_target_pairs={{0,1},{1,0},{2,3},{3,2},{4,5},{5,4},{6,7},{7,6},{8,9},{9,8},{10,11... | collective-permute-start | bytes 4718600 | tf_op jit(solution)/shard_map/ppermute | solution.py:472

commit v6 on v5

--- a/solution.py
+++ b/solution.py
@@ -140,12 +140,14 @@
 
 
 def coarse_kernel(
-    group, own_pack, other_pack, pool, projection, output, coarse, keep, give, unit
+    group, own_pack, other_pack, pool, projection, output, coarse, keep, give, unit, both_joined
 ):
     half_rows, wide = coarse.shape
     part = wide // 2
     first = pl.multiple_of(group[0] * part, part)
     joined = jnp.concatenate([own_pack[:, :wide], other_pack[:, :wide]], axis=0)
+    both_joined[...] = joined
+    both_joined.flush()
     tokens = mm(joined, pool[...]).astype(BF)
     coarse[...] = tokens[:half_rows]
     normed, _ = normalize(tokens)
@@ -187,6 +189,7 @@
     projection,
     output,
     pair_slot,
+    mark,
     result,
     gradient,
     send,
@@ -218,19 +221,27 @@
 
 
 def coarse_weights_kernel(
-    arrived, unit, keep, give, own_pack, other_pack, gradient, terms, gradient_out
-):
-    gradient_out[...] = gradient[...]
+    parity, unit, keep, give, own_pack, other_pack, kept, first_half, second_half, mark
+):
     wide = unit.shape[1]
     part = wide // 2
     stacked = jnp.concatenate([keep[...], give[...]], axis=0)
     cotangent = jnp.concatenate([own_pack[:, wide:], other_pack[:, wide:]], axis=0)
     projection_term = mm(unit[...], stacked[:, part:], (0, 0))
+    output_term = mm(stacked[:, :part], cotangent, (0, 0))
     across = projection_term.shape[1] // 2
+    width = wide // 4
     for side in range(2):
+        stack = [output_term[:, (2 * side + k) * width : (2 * side + k + 1) * width] for k in range(2)]
         columns = projection_term[:, side * across : (side + 1) * across]
-        put_blocks(terms, side, 0, columns)
-    put_quarters(terms, across, mm(stacked[:, :part], cotangent, (0, 0)))
+        terms = jnp.concatenate([columns, jnp.concatenate(stack, axis=0)], axis=1)
+        for at, passed in enumerate((first_half, second_half)):
+            low = terms[:, 2 * at * width : (2 * at + 1) * width]
+            high = terms[:, (2 * at + 1) * width : (2 * at + 2) * width]
+            upper = parity[at] == 1
+            put_blocks(kept, side, at * width, jnp.where(upper, high, low))
+            put_blocks(passed, side, 0, jnp.where(upper, low, high))
+    mark[...] = jnp.zeros_like(mark)
 
 
 def put_quarters(blocks, lane, term):
@@ -246,10 +257,19 @@
     blocks[:, side, :, lane : lane + width] = pieces.astype(BF)
 
 
-def sum_kernel(arrived, spread, *, tokens, fine):
-    fine_part = jnp.sum(arrived[:, :, :, tokens : tokens + fine].astype(F32), axis=0)
-    coarse_part = jnp.sum(arrived[:, :, :, tokens + fine :].astype(F32), axis=0)
-    total = [fine_part[0] + fine_part[1], coarse_part[0], coarse_part[1]]
+def sum_kernel(arrived, spread, *, tokens, fine, run, step):
+    senders, _, rows, across = arrived.shape
+    start = tokens + fine
+    width = (across - start) // 3
+    fine_part = jnp.sum(arrived[:, :, :, tokens:start].astype(F32), axis=0)
+    total = [fine_part[0] + fine_part[1]]
+    for side in range(2):
+        for at, block in enumerate((run, step)):
+            values = arrived[:, side, :, start + at * width : start + (at + 1) * width]
+            split = values.astype(F32).reshape(senders // (2 * block), 2, block, rows, width)
+            halves = jnp.sum(jnp.sum(split, axis=2), axis=0)
+            total.extend([halves[0], halves[1]])
+        total.append(jnp.sum(arrived[:, side, :, start + 2 * width :].astype(F32), axis=0))
     total = jnp.concatenate(total, axis=1).astype(BF)
     spread[...] = jnp.broadcast_to(total[None], spread.shape)
 
@@ -315,9 +335,10 @@
     weights,
     projection,
     output,
-    coarse_terms,
-    own_pack,
-    other_pack,
+    kept,
+    got_first,
+    got_second,
+    joined,
     own_gradient,
     other_gradient,
     send,
@@ -362,13 +383,16 @@
     send[:, :, :, :features] = tokens.reshape(send.shape[:3] + (features,)).astype(BF)
     for side in range(2):
         put_blocks(send, side, features, jnp.concatenate(terms[2 * side : 2 * side + 2], axis=0))
-    settled = 2 * features + coarse_terms.shape[3]
-    send[:, :, :, 2 * features : settled] = coarse_terms[...]
+    width = got_first.shape[3]
+    for at, got in enumerate((got_first, got_second)):
+        mine = kept[:, :, :, at * width : (at + 1) * width].astype(F32)
+        start = 2 * features + at * width
+        send[:, :, :, start : start + width] = (mine + got[...].astype(F32)).astype(BF)
     part = own_gradient.shape[1] // 2
     first = pl.multiple_of(group[0] * part, part)
-    pool_term = mm(own_pack[:, pl.ds(first, part)], own_gradient[...], (0, 0))
-    pool_term = pool_term + mm(other_pack[:, pl.ds(first, part)], other_gradient[...], (0, 0))
-    put_quarters(send, settled, pool_term)
+    gradient = jnp.concatenate([own_gradient[...], other_gradient[...]], axis=0)
+    pool_term = mm(joined[:, pl.ds(first, part)], gradient, (0, 0))
+    put_quarters(send, 2 * features + 2 * width, pool_term)
 
 
 def take_kernel(arrived, slots, rows_out):
@@ -430,7 +454,9 @@
     for at, value in enumerate(inputs):
         far = isinstance(value, Far)
         in_specs.append(SMEM if scalar and at == 0 else HBM if far else VMEM)
-        arrays.append(value.value if far else value)
+        arrays.append(
+            pltpu.with_memory_space_constraint(value.value, pltpu.HBM) if far else value
+        )
         if far:
             buffers.append(pltpu.VMEM(value.value.shape, value.value.dtype))
     buffers.extend(pltpu.VMEM(out.shape, out.dtype) for out in outputs if out.far)
@@ -460,7 +486,10 @@
     own = [pltpu.SemaphoreType.DMA((len(buffers),))] if buffers else []
     return pl.pallas_call(
         body,
-        out_shape=[jax.ShapeDtypeStruct(out.shape, out.dtype) for out in outputs],
+        out_shape=[
+            (pltpu.HBM if out.far else jax.ShapeDtypeStruct)(out.shape, out.dtype)
+            for out in outputs
+        ],
         in_specs=in_specs,
         out_specs=[HBM if out.far else VMEM for out in outputs],
         scratch_shapes=buffers + own + list(scratch),
@@ -517,13 +546,12 @@
             Near((1, count), jnp.int32),
             Near((1, count), F32),
         ),
-        mebibytes=56,
     )
     arrived = route(send, devices)
     heads = features // HD * (count // BALL)
     send, rotated, projected, mixture, weights = call(
         fine_forward_kernel,
-        (arrived, receive_slot, live, fine_projection, fine_output),
+        (arrived, receive_slot, live, Far(fine_projection), Far(fine_output)),
         (
             Near((slots, features)),
             Near((count, features)),
@@ -537,18 +565,37 @@
         join_kernel, (arrived, pair_slot, coarse_cotangent), (Near((half_rows, 2 * wide)),)
     )
     other_pack = exchange(own_pack)
-    coarse, keep, give, unit = call(
+    coarse, keep, give, unit, joined = call(
         coarse_kernel,
-        (group, own_pack, other_pack, pool_weight, coarse_projection, coarse_output),
+        (group, own_pack, other_pack, pool_weight, coarse_projection, Far(coarse_output)),
         (
             Near((half_rows, wide)),
             Near((half_rows, 2 * wide)),
             Near((half_rows, 2 * wide)),
             Near((count, wide)),
+            Near((count, wide), far=True),
         ),
         scalar=True,
     )
     got = exchange(give)
+    owners = lax.axis_size("pts")
+    run, step = owners // 4, owners // 16
+    place = lax.axis_index("pts").astype(jnp.int32)
+    parity = jnp.stack([place // run % 2, place // step % 2])
+    blocks = (owners, 2, slots // devices)
+    kept, first_half, second_half, mark = call(
+        coarse_weights_kernel,
+        (parity, unit, keep, give, own_pack, other_pack),
+        (
+            Near((*blocks, wide // 2), far=True),
+            Near((*blocks, wide // 4), far=True),
+            Near((*blocks, wide // 4), far=True),
+            Near((8, 128), F32),
+        ),
+        scalar=True,
+    )
+    got_first = lax.ppermute(first_half, "pts", [(i, i ^ run) for i in range(owners)])
+    got_second = lax.ppermute(second_half, "pts", [(i, i ^ step) for i in range(owners)])
     coarse_result, coarse_gradient, send = call(
         coarse_finish_kernel,
         (
@@ -561,6 +608,7 @@
             coarse_projection,
             coarse_output,
             pair_slot,
+            mark,
         ),
         (
             Near((half_rows, wide), far=True),
@@ -570,14 +618,8 @@
         scalar=True,
     )
     arrived = route(send, devices)
-    owners = lax.axis_size("pts")
-    coarse_terms, own_gradient = call(
-        coarse_weights_kernel,
-        (arrived, unit, keep, give, own_pack, other_pack, coarse_gradient),
-        (Near((owners, 2, slots // devices, wide)), Near((half_rows, wide))),
-    )
-    other_gradient = exchange(own_gradient)
-    across = 2 * features + 5 * wide // 4
+    other_gradient = exchange(coarse_gradient)
+    across = 2 * features + 3 * wide // 4
     (send,) = call(
         fine_backward_kernel,
         (
@@ -590,19 +632,20 @@
             weights,
             fine_projection,
             fine_output,
-            coarse_terms,
-            own_pack,
-            other_pack,
-            own_gradient,
+            Far(kept),
+            got_first,
+            got_second,
+            Far(joined),
+            coarse_gradient,
             other_gradient,
         ),
-        (Near((owners, 2, slots // devices, across)),),
+        (Near((*blocks, across)),),
         scalar=True,
         scratch=(pltpu.VMEM((count, 3 * features), BF),),
     )
     arrived = spread_blocks(send.reshape(devices, slots // devices, across), ("pts", "grp"))
     (spread,) = call(
-        functools.partial(sum_kernel, tokens=features, fine=features),
+        functools.partial(sum_kernel, tokens=features, fine=features, run=run, step=step),
         (arrived.reshape(send.shape),),
         (Near((owners, slots // devices, features + 5 * wide // 2)),),
     )

time: 166 us -> 177 us (1.066)
  blocking collectives: 123 us -> 105 us
  local copies, waits for them, and re-layouts: 3.43 us -> 13.4 us
  waiting for transfers between devices: 6.03 us -> 13.2 us
  starting transfers between devices: 6.93 us -> 13 us
  Pallas kernels: 24.8 us -> 30.8 us
    all_to_all x5 -> x4, blocking collectives: 123 us -> 105 us  [spread_blocks(): return lax.all_to_all(values, axes, split_axis=0, concat_axis=0, tiled=True)]
    unnamed x44 -> x56, local copies, waits for them, and re-layouts: 3.4 us -> 13.4 us
    ppermute x0 -> x2, waiting for transfers between devices: none -> 9.85 us  [the longest x1 9.09 us: on_device(): lax.ppermute(first_half, 'pts', [(i, i ^ run) for i in range(owners)])]
    pallas_call x10, Pallas kernels: 24.8 us -> 30.8 us  [call(): pl.pallas_call(body, out_shape=[(pltpu.HBM if out.far else jax.ShapeDtype...]
    all_to_all x0 -> x1, starting transfers between devices: none -> 3.69 us  [spread_blocks(): return lax.all_to_all(values, axes, split_axis=0, concat_axis=0, tiled=True)]
    ppermute x0 -> x2, starting transfers between devices: none -> 2.71 us  [the longest x1 1.46 us: on_device(): lax.ppermute(first_half, 'pts', [(i, i ^ run) for i in range(owners)])]
    ppermute x4, waiting for transfers between devices: 6.03 us -> 3.34 us  [exchange(): return lax.ppermute(values, 'grp', [(0, 1), (1, 0)])]
  transfers between devices with their start and end apart: 4 -> 7, of which waited for: 4 -> 4; matrix products, arithmetic and copies ran while one was open for 0% -> 0% of each run, Pallas kernels for 1% -> 2%
where the time goes in v6:
time: 177 us
  blocking collectives  105 us (59%)
  Pallas kernels  30.8 us (17%)
  local copies, waits for them, and re-layouts  13.4 us (8%)
  waiting for transfers between devices  13.2 us (7%)
  starting transfers between devices  13 us (7%)
    all_to_all x4, blocking collectives, spread_blocks(): return lax.all_to_all(values, axes, split_axis=0, concat_axis=0, tiled=True)  105 us
    pallas_call x10, Pallas kernels, call(): pl.pallas_call(body, out_shape=[(pltpu.HBM if out.far else jax.ShapeDtype...  30.8 us
    unnamed x56, local copies, waits for them, and re-layouts  13.4 us
    ppermute x1, waiting for transfers between devices, on_device(): lax.ppermute(first_half, 'pts', [(i, i ^ run) for i in range(owners)])  9.09 us
    ppermute x4, starting transfers between devices, exchange(): return lax.ppermute(values, 'grp', [(0, 1), (1, 0)])  6.59 us
    all_to_all x1, starting transfers between devices, spread_blocks(): return lax.all_to_all(values, axes, split_axis=0, concat_axis=0, tiled=True)  3.69 us
  transfers between devices with their start and end apart: 7, of which 4 were waited for; matrix products, arithmetic and copies ran while one was open for 0% of the time, Pallas kernels for 2%

profile of v6, /device:TPU:1, one launch (start us, length us, event | category | flops | bytes accessed | tf_op | source)
XLA Modules:
  0.0 176.5 jit_solution(6013057212601696507)
XLA Ops:
  0.6 2.1 %shard_map.153 = (bf16[1024,256]{1,0:T(8,128)(2,1)S(1)}, s32[1,512]{1,0:T(1,128)S(1)}, s32[1,512]{1,0:T(1,128)S(1)}, s32[1,512]{1,0:T(1,128)S(1)}, f32[1,512]{1,0:T(1,128)S(1)}) custom-call(s32[1,512]{1,0:T(1,128)} %bitcast.22, s32[1,512]{1,0:T(1,128)} %bitcast.23, s32[1,256]{1,0:T(1,128)} %bitcast.24, bf16[512,256]{1,0:T(8,128)(2,1)} %refs_3_.3), custom_call_target="tpu_custom_call" | custom-call | tf_op jit(solution)/shard_map/pallas_call | solution.py:487
  2.8 25.0 %all_to_all.25 = bf16[128,8,256]{2,1,0:T(8,128)(2,1)S(1)} all-to-all(bf16[128,8,256]{2,1,0:T(8,128)(2,1)S(1)} %bitcast.21), channel_id=1, replica_groups=mesh['pts'=64,'grp'=2] {'pts','grp'}, dimensions={0} | all-to-all | bytes 1048576 | tf_op jit(solution)/shard_map/all_to_all | solution.py:505
  27.8 4.4 %shard_map.154 = (bf16[1024,256]{1,0:T(8,128)(2,1)S(1)}, bf16[512,256]{1,0:T(8,128)(2,1)S(1)}, bf16[512,768]{1,0:T(8,128)(2,1)S(1)}, bf16[512,256]{1,0:T(8,128)(2,1)S(1)}, bf16[8,256,256]{2,1,0:T(8,128)(2,1)S(1)}) custom-call(bf16[1024,256]{1,0:T(8,128)(2,1)S(1)} %bitcast.17, s32[1,512]{1,0:T(1,128)S(1)} %get-tuple-element.35.refs_1_.refs_2_, ...), custom_call_target="tpu_custom_call" | custom-call | tf_op jit(solution)/shard_map/pallas_call | solution.py:487
  32.2 18.1 %all_to_all.26 = bf16[128,8,256]{2,1,0:T(8,128)(2,1)S(1)} all-to-all(bf16[128,8,256]{2,1,0:T(8,128)(2,1)S(1)} %bitcast.20), channel_id=1, replica_groups=mesh['pts'=64,'grp'=2] {'pts','grp'}, dimensions={0} | all-to-all | bytes 1048576 | tf_op jit(solution)/shard_map/all_to_all | solution.py:505
  50.8 1.4 collective-permute-start
  52.2 1.5 collective-permute-done.refs_2_.refs_5_
  53.7 8.0 %shard_map.156 = (bf16[256,512]{1,0:T(8,128)(2,1)S(1)}, bf16[256,1024]{1,0:T(8,128)(2,1)S(1)}, bf16[256,1024]{1,0:T(8,128)(2,1)}, bf16[512,512]{1,0:T(8,128)(2,1)S(1)}, bf16[512,512]{1,0:T(8,128)(2,1)}) custom-call(s32[1]{0:T(128)} %bitcast.refs_0_, bf16[256,1024]{1,0:T(8,128)(2,1)S(1)} %shard_map.155.refs_1_.refs_4_, ...), custom_call_target="tpu_custom_call" | custom-call | tf_op jit(solution)/shard_map/pallas_call | solution.py:487
  62.5 0.8 copy-done.6
  63.3 0.8 copy-done.16
  65.2 1.0 copy-done.4
  66.3 1.0 copy-done.7
  67.3 1.0 copy-done.17
  68.4 2.8 %shard_map.157 = (bf16[64,2,8,256]{3,2,1,0:T(8,128)(2,1)}, bf16[64,2,8,128]{3,2,1,0:T(8,128)(2,1)}, bf16[64,2,8,128]{3,2,1,0:T(8,128)(2,1)}, f32[8,128]{1,0:T(8,128)S(1)}) custom-call(s32[2]{0:T(128)S(1)} %pad_add_fusion.refs_0_, bf16[512,512]{1,0:T(8,128)(2,1)S(1)} %copy-done.17, bf16[256,1024]{1,0:T(8,128)(2,1)S(1)} %copy-done.4, ...), custom_call_target="tpu_custom_call" | custom-call | tf_op jit(solution)/shard_map/pallas_call | solution.py:487
  71.3 2.6 %shard_map.158 = (bf16[256,512]{1,0:T(8,128)(2,1)}, bf16[256,512]{1,0:T(8,128)(2,1)S(1)}, bf16[1024,256]{1,0:T(8,128)(2,1)S(1)}) custom-call(s32[1]{0:T(128)} %bitcast.refs_0_, bf16[256,512]{1,0:T(8,128)(2,1)S(1)} %copy-done.23, bf16[256,1024]{1,0:T(8,128)(2,1)S(1)} %copy-done.5, bf16[256,1024]{1,0:T(8,128)(2,1)} %collective-permute-done.1.refs_3_, ...), custom_call_target="tpu_custom_call" | custom-call | tf_op jit(solution)/shard_map/pallas_call | solution.py:487
  73.9 0.8 copy-done.15
  75.4 3.7 %all-to-all-start.2 = ((bf16[128,8,256]{2,1,0:T(8,128)(2,1)}), bf16[128,8,256]{2,1,0:T(8,128)(2,1)S(1)}, u32[]{:S(2)}, u32[]{:S(2)}) async-start(bf16[128,8,256]{2,1,0:T(8,128)(2,1)} %bitcast.19), calls=%async_computation.2 | async-start | bytes 1048576 | tf_op jit(solution)/shard_map/all_to_all | solution.py:505
  79.1 1.5 collective-permute-start.2
  80.6 1.2 collective-permute-start.3
  81.8 0.9 collective-permute-start.4
  82.7 9.1 %collective-permute-done.2.refs_10_ = bf16[64,2,8,128]{3,2,1,0:T(8,128)(2,1)S(1)} collective-permute-done((bf16[64,2,8,128]{3,2,1,0:T(8,128)(2,1)}, bf16[64,2,8,128]{3,2,1,0:T(8,128)(2,1)S(1)}, u32[]{:S(2)}, u32[]{:S(2)}) %collective-permute-start.2) | collective-permute-done | bytes 262176 | tf_op jit(solution)/shard_map/ppermute | solution.py:597
  93.3 1.1 copy-done.13
  94.5 0.9 copy-done.19
  95.4 0.9 copy-done.21
  96.4 0.9 copy-done.25
  97.3 0.9 copy-done.27
  98.3 5.7 %shard_map.159 = bf16[64,2,8,896]{3,2,1,0:T(8,128)(2,1)S(1)} custom-call(s32[1]{0:T(128)} %bitcast.refs_0_, bf16[1024,256]{1,0:T(8,128)(2,1)S(1)} %bitcast.18, s32[1,512]{1,0:T(1,128)S(1)} %get-tuple-element.35.refs_1_.refs_2_, bf16[512,256]{1,0:T(8,128)(2,1)S(1)} %copy-done.19, bf16[512,768]{1,0:T(8,128)(2,1)S(1)} %copy-done.13, ...), custom_call_target="tpu_custom_call" | custom-call | tf_op jit(solution)/shard_map/pallas_call | solution.py:487
  104.0 36.7 %all_to_all.27 = bf16[128,8,896]{2,1,0:T(8,128)(2,1)S(1)} all-to-all(bf16[128,8,896]{2,1,0:T(8,128)(2,1)S(1)} %bitcast.15), channel_id=1, replica_groups=mesh['pts'=64,'grp'=2] {'pts','grp'}, dimensions={0} | all-to-all | bytes 3670016 | tf_op jit(solution)/shard_map/all_to_all | solution.py:505
  141.0 25.3 %all_to_all.28.refs_1_ = bf16[64,8,1536]{2,1,0:T(8,128)(2,1)S(1)} all-to-all(bf16[64,8,1536]{2,1,0:T(8,128)(2,1)S(1)} %shard_map.161), channel_id=1, replica_groups=mesh['pts'=64,'grp'=2] {'pts'}, dimensions={0} | all-to-all | bytes 3145728 | tf_op jit(solution)/shard_map/all_to_all | solution.py:505
  166.3 3.9 %collective-permute-start.5 = (bf16[64,8,1536]{2,1,0:T(8,128)(2,1)S(1)}, bf16[64,8,1536]{2,1,0:T(8,128)(2,1)S(1)}, u32[]{:S(2)}, u32[]{:S(2)}) collective-permute-start(bf16[64,8,1536]{2,1,0:T(8,128)(2,1)S(1)} %all_to_all.28.refs_1_), channel_id=1, source_target_pairs={{0,1},{1,0},{2,3},{3,2},{4,5},{5,4},{6,7},{7,6},{8,9},{9,8},{10,11... | collective-permute-start | bytes 4718600 | tf_op jit(solution)/shard_map/ppermute | solution.py:501
  170.2 1.2 shard_map.160
  171.4 1.8 %collective-permute-done.5.refs_2_ = bf16[64,8,1536]{2,1,0:T(8,128)(2,1)S(1)} collective-permute-done((bf16[64,8,1536]{2,1,0:T(8,128)(2,1)S(1)}, bf16[64,8,1536]{2,1,0:T(8,128)(2,1)S(1)}, u32[]{:S(2)}, u32[]{:S(2)}) %collective-permute-start.5) | collective-permute-done | bytes 1572896 | tf_op jit(solution)/shard_map/ppermute | solution.py:501
  173.2 3.2 %shard_map.162 = (f32[256,768]{1,0:T(8,128)}, f32[256,256]{1,0:T(8,128)}, f32[512,512]{1,0:T(8,128)}, f32[512,1536]{1,0:T(8,128)}, f32[512,512]{1,0:T(8,128)}) custom-call(s32[1]{0:T(128)} %bitcast.refs_0_, bf16[64,8,1536]{2,1,0:T(8,128)(2,1)S(1)} %all_to_all.28.refs_1_, bf16[64,8,1536]{2,1,0:T(8,128)(2,1)S(1)} %collective-permute-done.5.refs_2_), custom_call_target="tpu_custom_call" | custom-call | tf_op jit(solution)/shard_map/pallas_call | solution.py:487
  (54 shorter events, 5.0 us)
Async XLA Ops:
  2.8 47.5 %copy-start.9 = (bf16[256,512]{1,0:T(8,128)(2,1)S(1)}, bf16[256,512]{1,0:T(8,128)(2,1)}, u32[]{:S(2)}) copy-start(bf16[256,512]{1,0:T(8,128)(2,1)} %refs_4_.5) | copy-start | bytes 786436
  27.8 26.0 %copy-start = (bf16[512,1536]{1,0:T(8,128)(2,1)S(1)}, bf16[512,1536]{1,0:T(8,128)(2,1)}, u32[]{:S(2)}) copy-start(bf16[512,1536]{1,0:T(8,128)(2,1)} %refs_6_.1) | copy-start | bytes 4718596
  27.8 26.0 %copy-start.1 = (bf16[512,512]{1,0:T(8,128)(2,1)S(1)}, bf16[512,512]{1,0:T(8,128)(2,1)}, u32[]{:S(2)}) copy-start(bf16[512,512]{1,0:T(8,128)(2,1)} %refs_5_.3) | copy-start | bytes 1572868
  32.1 18.6 %copy-start.10 = (bf16[8,256,256]{2,1,0:T(8,128)(2,1)}, bf16[8,256,256]{2,1,0:T(8,128)(2,1)S(1)}, u32[]{:S(2)}) copy-start(bf16[8,256,256]{2,1,0:T(8,128)(2,1)S(1)} %get-tuple-element.49.refs_6_) | copy-start | bytes 3145732
  32.2 20.0 %copy-start.12 = (bf16[512,768]{1,0:T(8,128)(2,1)}, bf16[512,768]{1,0:T(8,128)(2,1)S(1)}, u32[]{:S(2)}) copy-start(bf16[512,768]{1,0:T(8,128)(2,1)S(1)} %get-tuple-element.47.refs_4_) | copy-start | bytes 2359300
  32.2 20.0 %copy-start.18 = (bf16[512,256]{1,0:T(8,128)(2,1)}, bf16[512,256]{1,0:T(8,128)(2,1)S(1)}, u32[]{:S(2)}) copy-start(bf16[512,256]{1,0:T(8,128)(2,1)S(1)} %get-tuple-element.46.refs_3_) | copy-start | bytes 786436
  32.2 20.0 %copy-start.20 = (bf16[512,256]{1,0:T(8,128)(2,1)}, bf16[512,256]{1,0:T(8,128)(2,1)S(1)}, u32[]{:S(2)}) copy-start(bf16[512,256]{1,0:T(8,128)(2,1)S(1)} %get-tuple-element.48.refs_5_) | copy-start | bytes 786436
  50.8 2.9 %collective-permute-start = (bf16[256,1024]{1,0:T(8,128)(2,1)S(1)}, bf16[256,1024]{1,0:T(8,128)(2,1)S(1)}, u32[]{:S(2)}, u32[]{:S(2)}) collective-permute-start(bf16[256,1024]{1,0:T(8,128)(2,1)S(1)} %shard_map.155.refs_1_.refs_4_), channel_id=1, source_target_pairs={{0,1},{1,0},{2,3},{3,2},{4,5},{5,4},{6,7},{7,6},{8,9},{9,8},{10,11... | collective-permute-start | bytes 1572872 | tf_op jit(solution)/shard_map/ppermute | solution.py:501
  61.7 0.8 copy-start.3
  62.5 0.8 copy-start.6
  63.3 0.8 copy-start.16
  64.8 6.5 %copy-start.2 = (bf16[512,512]{1,0:T(8,128)(2,1)S(1)}, bf16[512,512]{1,0:T(8,128)(2,1)}, u32[]{:S(2)}) copy-start(bf16[512,512]{1,0:T(8,128)(2,1)} %refs_7_.2) | copy-start | bytes 1572868
  64.8 6.4 %collective-permute-start.1 = (bf16[256,1024]{1,0:T(8,128)(2,1)}, bf16[256,1024]{1,0:T(8,128)(2,1)}, u32[]{:S(2)}, u32[]{:S(2)}) collective-permute-start(bf16[256,1024]{1,0:T(8,128)(2,1)} %get-tuple-element.41.refs_3_), channel_id=1, source_target_pairs={{0,1},{1,0},{2,3},{3,2},{4,5},{5,4},{6,7},{7,6},{8,9},{9,8},{10,11... | collective-permute-start | bytes 1572872 | tf_op jit(solution)/shard_map/ppermute | solution.py:501
  65.2 1.0 copy-start.4
  66.3 1.0 copy-start.7
  67.3 1.0 copy-start.17
  68.4 2.9 %copy-start.5 = (bf16[256,1024]{1,0:T(8,128)(2,1)S(1)}, bf16[256,1024]{1,0:T(8,128)(2,1)}, u32[]{:S(2)}) copy-start(bf16[256,1024]{1,0:T(8,128)(2,1)} %copy-done.3) | copy-start | bytes 1572868
  68.4 2.9 %copy-start.23 = (bf16[256,512]{1,0:T(8,128)(2,1)S(1)}, bf16[256,512]{1,0:T(8,128)(2,1)}, u32[]{:S(2)}) copy-start(bf16[256,512]{1,0:T(8,128)(2,1)} %copy-done.22) | copy-start | bytes 786436
  71.3 22.0 %copy-start.8 = (bf16[256,768]{1,0:T(8,128)(2,1)S(1)}, bf16[256,768]{1,0:T(8,128)(2,1)}, u32[]{:S(2)}) copy-start(bf16[256,768]{1,0:T(8,128)(2,1)} %refs_7_.3) | copy-start | bytes 1179652
  71.3 22.0 %copy-start.14 = (bf16[256,256]{1,0:T(8,128)(2,1)S(1)}, bf16[256,256]{1,0:T(8,128)(2,1)}, u32[]{:S(2)}) copy-start(bf16[256,256]{1,0:T(8,128)(2,1)} %refs_8_.1) | copy-start | bytes 393220
  73.9 0.8 copy-start.15
  75.4 17.9 %copy-start.11 = (bf16[8,256,256]{2,1,0:T(8,128)(2,1)S(1)}, bf16[8,256,256]{2,1,0:T(8,128)(2,1)}, u32[]{:S(2)}) copy-start(bf16[8,256,256]{2,1,0:T(8,128)(2,1)} %copy-done.10) | copy-start | bytes 3145732
  75.4 17.9 %all-to-all-start.2 = ((bf16[128,8,256]{2,1,0:T(8,128)(2,1)}), bf16[128,8,256]{2,1,0:T(8,128)(2,1)S(1)}, u32[]{:S(2)}, u32[]{:S(2)}) async-start(bf16[128,8,256]{2,1,0:T(8,128)(2,1)} %bitcast.19), calls=%async_computation.2 | async-start | bytes 1048576 | tf_op jit(solution)/shard_map/all_to_all | solution.py:505
  79.1 12.7 %collective-permute-start.2 = (bf16[64,2,8,128]{3,2,1,0:T(8,128)(2,1)}, bf16[64,2,8,128]{3,2,1,0:T(8,128)(2,1)S(1)}, u32[]{:S(2)}, u32[]{:S(2)}) collective-permute-start(bf16[64,2,8,128]{3,2,1,0:T(8,128)(2,1)} %get-tuple-element.51), channel_id=1, source_target_pairs={{0,32},{2,34},{4,36},{6,38},{8,40},{10,42},{12,44},{14,46},{16,48}... | collective-permute-start | bytes 786440 | tf_op jit(solution)/shard_map/ppermute | solution.py:597
  80.6 12.0 %collective-permute-start.3 = (bf16[64,2,8,128]{3,2,1,0:T(8,128)(2,1)}, bf16[64,2,8,128]{3,2,1,0:T(8,128)(2,1)S(1)}, u32[]{:S(2)}, u32[]{:S(2)}) collective-permute-start(bf16[64,2,8,128]{3,2,1,0:T(8,128)(2,1)} %get-tuple-element.52), channel_id=1, source_target_pairs={{0,8},{2,10},{4,12},{6,14},{8,0},{10,2},{12,4},{14,6},{16,24},{18,... | collective-permute-start | bytes 786440 | tf_op jit(solution)/shard_map/ppermute | solution.py:598
  81.8 10.8 %collective-permute-start.4 = (bf16[256,512]{1,0:T(8,128)(2,1)}, bf16[256,512]{1,0:T(8,128)(2,1)S(1)}, u32[]{:S(2)}, u32[]{:S(2)}) collective-permute-start(bf16[256,512]{1,0:T(8,128)(2,1)} %copy-done.24), channel_id=1, source_target_pairs={{0,1},{1,0},{2,3},{3,2},{4,5},{5,4},{6,7},{7,6},{8,9},{9,8},{10,11... | collective-permute-start | bytes 786440 | tf_op jit(solution)/shard_map/ppermute | solution.py:501
  93.3 1.1 copy-start.13
  94.5 0.9 copy-start.19
  95.4 0.9 copy-start.21
  96.4 0.9 copy-start.25
  97.3 0.9 copy-start.27
  166.3 6.9 %collective-permute-start.5 = (bf16[64,8,1536]{2,1,0:T(8,128)(2,1)S(1)}, bf16[64,8,1536]{2,1,0:T(8,128)(2,1)S(1)}, u32[]{:S(2)}, u32[]{:S(2)}) collective-permute-start(bf16[64,8,1536]{2,1,0:T(8,128)(2,1)S(1)} %all_to_all.28.refs_1_), channel_id=1, source_target_pairs={{0,1},{1,0},{2,3},{3,2},{4,5},{5,4},{6,7},{7,6},{8,9},{9,8},{10,11... | collective-permute-start | bytes 4718600 | tf_op jit(solution)/shard_map/ppermute | solution.py:501
  (3 other events, 2.1 us)

commit v7 on v6

--- a/solution.py
+++ b/solution.py
@@ -52,13 +52,17 @@
 
 def softmax_rows(scores):
     raised = jnp.exp(scores - jnp.max(scores, axis=-1, keepdims=True))
-    return (raised / jnp.sum(raised, axis=-1, keepdims=True)).astype(BF)
+    return (raised * (1.0 / jnp.sum(raised, axis=-1, keepdims=True))).astype(BF)
 
 
 def slopes_of(weights, against):
     wide = weights.astype(F32)
     diagonal = jnp.sum(wide * against, axis=-1, keepdims=True)
-    return (wide * (against - diagonal) * HD ** (-0.5)).astype(BF)
+    return (wide * (against - diagonal)).astype(BF)
+
+
+def scaled_half(rows, half):
+    return keep_half(rows * jnp.asarray(HD ** (-0.5), BF), half)
 
 
 def column_of(row):
@@ -120,7 +124,7 @@
             value = projected[rows, 2 * features + pair * PAIR : 2 * features + (pair + 1) * PAIR]
             halves = []
             for half in range(2):
-                scores = mm(keep_half(query, half), key, (1, 1)) * HD ** (-0.5)
+                scores = mm(scaled_half(query, half), key, (1, 1))
                 head_weights = softmax_rows(jnp.where(alive, scores, -1e30))
                 weights[(ball * pairs + pair) * 2 + half] = head_weights
                 halves.append(mm(head_weights, value))
@@ -140,14 +144,12 @@
 
 
 def coarse_kernel(
-    group, own_pack, other_pack, pool, projection, output, coarse, keep, give, unit, both_joined
+    group, own_pack, other_pack, pool, projection, output, coarse, keep, give, unit
 ):
     half_rows, wide = coarse.shape
     part = wide // 2
     first = pl.multiple_of(group[0] * part, part)
     joined = jnp.concatenate([own_pack[:, :wide], other_pack[:, :wide]], axis=0)
-    both_joined[...] = joined
-    both_joined.flush()
     tokens = mm(joined, pool[...]).astype(BF)
     coarse[...] = tokens[:half_rows]
     normed, _ = normalize(tokens)
@@ -164,13 +166,13 @@
         entering = incoming[:, lanes]
         parts = ([], [], [], [])
         for half in range(2):
-            scores = mm(keep_half(query, half), key, (1, 1)) * HD ** (-0.5)
+            scores = mm(scaled_half(query, half), key, (1, 1))
             head_weights = softmax_rows(scores)
             parts[0].append(mm(head_weights, value))
             against = mm(keep_half(entering, half), value, (1, 1))
             slopes = slopes_of(head_weights, against)
-            parts[1].append(mm(slopes, key))
-            parts[2].append(mm(slopes, query, (0, 0)))
+            parts[1].append(mm(slopes, key) * HD ** (-0.5))
+            parts[2].append(mm(slopes, query, (0, 0)) * HD ** (-0.5))
             parts[3].append(mm(head_weights, entering, (0, 0)))
         for at, (low, high) in enumerate(parts):
             both = jnp.where(head_half(low.shape, 0), low, high).astype(BF)
@@ -189,7 +191,6 @@
     projection,
     output,
     pair_slot,
-    mark,
     result,
     gradient,
     send,
@@ -221,7 +222,18 @@
 
 
 def coarse_weights_kernel(
-    parity, unit, keep, give, own_pack, other_pack, kept, first_half, second_half, mark
+    parity,
+    arrived,
+    unit,
+    keep,
+    give,
+    own_pack,
+    other_pack,
+    gradient,
+    kept,
+    first_half,
+    second_half,
+    gradient_out,
 ):
     wide = unit.shape[1]
     part = wide // 2
@@ -241,7 +253,7 @@
             upper = parity[at] == 1
             put_blocks(kept, side, at * width, jnp.where(upper, high, low))
             put_blocks(passed, side, 0, jnp.where(upper, low, high))
-    mark[...] = jnp.zeros_like(mark)
+    gradient_out[...] = gradient[...]
 
 
 def put_quarters(blocks, lane, term):
@@ -326,7 +338,6 @@
 
 
 def fine_backward_kernel(
-    group,
     arrived,
     receive_slot,
     rotated,
@@ -335,12 +346,6 @@
     weights,
     projection,
     output,
-    kept,
-    got_first,
-    got_second,
-    joined,
-    own_gradient,
-    other_gradient,
     send,
     grad_projected,
 ):
@@ -365,8 +370,8 @@
                 head_weights = weights[(ball * pairs + pair) * 2 + half]
                 against = mm(keep_half(enters, half), value, (1, 1))
                 slopes = slopes_of(head_weights, against)
-                parts[0].append(mm(slopes, key))
-                parts[1].append(mm(slopes, query, (0, 0)))
+                parts[0].append(mm(slopes, key) * HD ** (-0.5))
+                parts[1].append(mm(slopes, query, (0, 0)) * HD ** (-0.5))
                 parts[2].append(mm(head_weights, enters, (0, 0)))
             for at, (low, high) in enumerate(parts):
                 both = jnp.where(head_half(low.shape, 0), low, high).astype(BF)
@@ -383,16 +388,21 @@
     send[:, :, :, :features] = tokens.reshape(send.shape[:3] + (features,)).astype(BF)
     for side in range(2):
         put_blocks(send, side, features, jnp.concatenate(terms[2 * side : 2 * side + 2], axis=0))
-    width = got_first.shape[3]
+
+def assemble_kernel(
+    group, fine, kept, got_first, got_second, own_pack, other_pack, own_gradient, other_gradient, send
+):
+    start, width = fine.shape[3], got_first.shape[3]
+    send[:, :, :, :start] = fine[...]
     for at, got in enumerate((got_first, got_second)):
         mine = kept[:, :, :, at * width : (at + 1) * width].astype(F32)
-        start = 2 * features + at * width
         send[:, :, :, start : start + width] = (mine + got[...].astype(F32)).astype(BF)
+        start += width
     part = own_gradient.shape[1] // 2
     first = pl.multiple_of(group[0] * part, part)
-    gradient = jnp.concatenate([own_gradient[...], other_gradient[...]], axis=0)
-    pool_term = mm(joined[:, pl.ds(first, part)], gradient, (0, 0))
-    put_quarters(send, 2 * features + 2 * width, pool_term)
+    pool_term = mm(own_pack[:, pl.ds(first, part)], own_gradient[...], (0, 0))
+    pool_term = pool_term + mm(other_pack[:, pl.ds(first, part)], other_gradient[...], (0, 0))
+    put_quarters(send, start, pool_term)
 
 
 def take_kernel(arrived, slots, rows_out):
@@ -565,37 +575,18 @@
         join_kernel, (arrived, pair_slot, coarse_cotangent), (Near((half_rows, 2 * wide)),)
     )
     other_pack = exchange(own_pack)
-    coarse, keep, give, unit, joined = call(
+    coarse, keep, give, unit = call(
         coarse_kernel,
-        (group, own_pack, other_pack, pool_weight, coarse_projection, Far(coarse_output)),
+        (group, own_pack, other_pack, pool_weight, coarse_projection, coarse_output),
         (
             Near((half_rows, wide)),
             Near((half_rows, 2 * wide)),
             Near((half_rows, 2 * wide)),
             Near((count, wide)),
-            Near((count, wide), far=True),
         ),
         scalar=True,
     )
     got = exchange(give)
-    owners = lax.axis_size("pts")
-    run, step = owners // 4, owners // 16
-    place = lax.axis_index("pts").astype(jnp.int32)
-    parity = jnp.stack([place // run % 2, place // step % 2])
-    blocks = (owners, 2, slots // devices)
-    kept, first_half, second_half, mark = call(
-        coarse_weights_kernel,
-        (parity, unit, keep, give, own_pack, other_pack),
-        (
-            Near((*blocks, wide // 2), far=True),
-            Near((*blocks, wide // 4), far=True),
-            Near((*blocks, wide // 4), far=True),
-            Near((8, 128), F32),
-        ),
-        scalar=True,
-    )
-    got_first = lax.ppermute(first_half, "pts", [(i, i ^ run) for i in range(owners)])
-    got_second = lax.ppermute(second_half, "pts", [(i, i ^ step) for i in range(owners)])
     coarse_result, coarse_gradient, send = call(
         coarse_finish_kernel,
         (
@@ -608,7 +599,6 @@
             coarse_projection,
             coarse_output,
             pair_slot,
-            mark,
         ),
         (
             Near((half_rows, wide), far=True),
@@ -618,12 +608,28 @@
         scalar=True,
     )
     arrived = route(send, devices)
-    other_gradient = exchange(coarse_gradient)
-    across = 2 * features + 3 * wide // 4
-    (send,) = call(
+    owners = lax.axis_size("pts")
+    run, step = owners // 4, owners // 16
+    place = lax.axis_index("pts").astype(jnp.int32)
+    parity = jnp.stack([place // run % 2, place // step % 2])
+    blocks = (owners, 2, slots // devices)
+    kept, first_half, second_half, own_gradient = call(
+        coarse_weights_kernel,
+        (parity, arrived, unit, keep, give, own_pack, other_pack, coarse_gradient),
+        (
+            Near((*blocks, wide // 2)),
+            Near((*blocks, wide // 4)),
+            Near((*blocks, wide // 4)),
+            Near((half_rows, wide)),
+        ),
+        scalar=True,
+    )
+    got_first = lax.ppermute(first_half, "pts", [(i, i ^ run) for i in range(owners)])
+    got_second = lax.ppermute(second_half, "pts", [(i, i ^ step) for i in range(owners)])
+    other_gradient = exchange(own_gradient)
+    (fine,) = call(
         fine_backward_kernel,
         (
-            group,
             arrived,
             receive_slot,
             rotated,
@@ -632,16 +638,26 @@
             weights,
             fine_projection,
             fine_output,
-            Far(kept),
+        ),
+        (Near((*blocks, 2 * features)),),
+        scratch=(pltpu.VMEM((count, 3 * features), BF),),
+    )
+    across = 2 * features + 3 * wide // 4
+    (send,) = call(
+        assemble_kernel,
+        (
+            group,
+            fine,
+            kept,
             got_first,
             got_second,
-            Far(joined),
-            coarse_gradient,
+            own_pack,
+            other_pack,
+            own_gradient,
             other_gradient,
         ),
         (Near((*blocks, across)),),
         scalar=True,
-        scratch=(pltpu.VMEM((count, 3 * features), BF),),
     )
     arrived = spread_blocks(send.reshape(devices, slots // devices, across), ("pts", "grp"))
     (spread,) = call(

time: 177 us -> 168 us (0.949)
  local copies, waits for them, and re-layouts: 13.4 us -> 8.3 us
  Pallas kernels: 30.8 us -> 26 us
  waiting for transfers between devices: 13.2 us -> 17.7 us
  blocking collectives: 105 us -> 102 us
    all_to_all x1, waiting for transfers between devices: 0.01 us -> 13.6 us  [spread_blocks(): return lax.all_to_all(values, axes, split_axis=0, concat_axis=0, tiled=True)]
    ppermute x1, waiting for transfers between devices: 9.09 us -> 0.01 us  [on_device(): lax.ppermute(first_half, 'pts', [(i, i ^ run) for i in range(owners)])]
    unnamed x56 -> x48, local copies, waits for them, and re-layouts: 13.4 us -> 8.26 us
    pallas_call x10 -> x11, Pallas kernels: 30.8 us -> 26 us  [call(): pl.pallas_call(body, out_shape=[(pltpu.HBM if out.far else jax.ShapeDtype...]
    all_to_all x4, blocking collectives: 105 us -> 102 us  [spread_blocks(): return lax.all_to_all(values, axes, split_axis=0, concat_axis=0, tiled=True)]
  transfers between devices with their start and end apart: 7 -> 7, of which waited for: 4 -> 4; matrix products, arithmetic and copies ran while one was open for 0% -> 0% of each run, Pallas kernels for 2% -> 4%
where the time goes in v7:
time: 168 us; the launch traced here: 167 us
  blocking collectives  102 us (61%)
  Pallas kernels  26 us (15%)
  waiting for transfers between devices  17.7 us (11%)
  starting transfers between devices  11.9 us (7%)
  local copies, waits for them, and re-layouts  8.3 us (5%)
    all_to_all x4, blocking collectives, spread_blocks(): return lax.all_to_all(values, axes, split_axis=0, concat_axis=0, tiled=True)  102 us
    pallas_call x11, Pallas kernels, call(): pl.pallas_call(body, out_shape=[(pltpu.HBM if out.far else jax.ShapeDtype...  26 us
    all_to_all x1, waiting for transfers between devices, spread_blocks(): return lax.all_to_all(values, axes, split_axis=0, concat_axis=0, tiled=True)  13.6 us
    unnamed x48, local copies, waits for them, and re-layouts  8.26 us
    ppermute x4, starting transfers between devices, exchange(): return lax.ppermute(values, 'grp', [(0, 1), (1, 0)])  7.38 us
    ppermute x4, waiting for transfers between devices, exchange(): return lax.ppermute(values, 'grp', [(0, 1), (1, 0)])  4.08 us
    all_to_all x1, starting transfers between devices, spread_blocks(): return lax.all_to_all(values, axes, split_axis=0, concat_axis=0, tiled=True)  3.8 us
  transfers between devices with their start and end apart: 7, of which 4 were waited for; matrix products, arithmetic and copies ran while one was open for 0% of the time, Pallas kernels for 4%

profile of v7, /device:TPU:1, one launch (start us, length us, event | category | flops | bytes accessed | tf_op | source)
XLA Modules:
  0.0 167.3 jit_solution(12382409022868281449)
XLA Ops:
  0.6 2.1 %shard_map.153 = (bf16[1024,256]{1,0:T(8,128)(2,1)S(1)}, s32[1,512]{1,0:T(1,128)S(1)}, s32[1,512]{1,0:T(1,128)S(1)}, s32[1,512]{1,0:T(1,128)S(1)}, f32[1,512]{1,0:T(1,128)S(1)}) custom-call(s32[1,512]{1,0:T(1,128)} %bitcast.23, s32[1,512]{1,0:T(1,128)} %bitcast.24, s32[1,256]{1,0:T(1,128)} %bitcast.25, bf16[512,256]{1,0:T(8,128)(2,1)} %refs_3_.3), custom_call_target="tpu_custom_call" | custom-call | tf_op jit(solution)/shard_map/pallas_call | solution.py:497
  2.8 25.0 %all_to_all.25 = bf16[128,8,256]{2,1,0:T(8,128)(2,1)S(1)} all-to-all(bf16[128,8,256]{2,1,0:T(8,128)(2,1)S(1)} %bitcast.22), channel_id=1, replica_groups=mesh['pts'=64,'grp'=2] {'pts','grp'}, dimensions={0} | all-to-all | bytes 1048576 | tf_op jit(solution)/shard_map/all_to_all | solution.py:515
  27.8 4.4 %shard_map.154 = (bf16[1024,256]{1,0:T(8,128)(2,1)S(1)}, bf16[512,256]{1,0:T(8,128)(2,1)S(1)}, bf16[512,768]{1,0:T(8,128)(2,1)S(1)}, bf16[512,256]{1,0:T(8,128)(2,1)S(1)}, bf16[8,256,256]{2,1,0:T(8,128)(2,1)S(1)}) custom-call(bf16[1024,256]{1,0:T(8,128)(2,1)S(1)} %bitcast.19, s32[1,512]{1,0:T(1,128)S(1)} %get-tuple-element.34.refs_1_, ...), custom_call_target="tpu_custom_call" | custom-call | tf_op jit(solution)/shard_map/pallas_call | solution.py:497
  32.2 18.1 %all_to_all.26 = bf16[128,8,256]{2,1,0:T(8,128)(2,1)S(1)} all-to-all(bf16[128,8,256]{2,1,0:T(8,128)(2,1)S(1)} %bitcast.21), channel_id=1, replica_groups=mesh['pts'=64,'grp'=2] {'pts','grp'}, dimensions={0} | all-to-all | bytes 1048576 | tf_op jit(solution)/shard_map/all_to_all | solution.py:515
  50.3 0.5 shard_map.155.refs_1_.refs_5_
  50.8 1.4 collective-permute-start
  52.2 1.5 collective-permute-done.refs_2_.refs_6_
  53.7 1.0 copy-done.2
  54.8 6.0 %shard_map.156 = (bf16[256,512]{1,0:T(8,128)(2,1)S(1)}, bf16[256,1024]{1,0:T(8,128)(2,1)S(1)}, bf16[256,1024]{1,0:T(8,128)(2,1)S(1)}, bf16[512,512]{1,0:T(8,128)(2,1)S(1)}) custom-call(s32[1]{0:T(128)} %bitcast.refs_0_, bf16[256,1024]{1,0:T(8,128)(2,1)S(1)} %shard_map.155.refs_1_.refs_5_, bf16[256,1024]{1,0:T(8,128)(2,1)S(1)} %collective-permute-done.refs_2_.refs_6_, ...), custom_call_target="tpu_custom_call" | custom-call | tf_op jit(solution)/shard_map/pallas_call | solution.py:497
  60.8 0.8 copy-done.15
  61.6 0.4 collective-permute-start.1
  61.9 0.8 copy-done.13
  62.7 0.7 collective-permute-done.1.refs_3_
  63.5 1.5 shard_map.157
  65.0 0.7 copy-done.22
  65.7 0.8 copy-done.12
  66.5 3.8 %all-to-all-start.2 = ((bf16[128,8,256]{2,1,0:T(8,128)(2,1)}), bf16[128,8,256]{2,1,0:T(8,128)(2,1)S(1)}, u32[]{:S(2)}, u32[]{:S(2)}) async-start(bf16[128,8,256]{2,1,0:T(8,128)(2,1)} %bitcast.20), calls=%async_computation.2 | async-start | bytes 1048576 | tf_op jit(solution)/shard_map/all_to_all | solution.py:515
  70.4 13.6 %all-to-all-done.2 = bf16[128,8,256]{2,1,0:T(8,128)(2,1)S(1)} async-done(((bf16[128,8,256]{2,1,0:T(8,128)(2,1)}), bf16[128,8,256]{2,1,0:T(8,128)(2,1)S(1)}, u32[]{:S(2)}, u32[]{:S(2)}) %all-to-all-start.2) | async-done | bytes 524320 | tf_op jit(solution)/shard_map/all_to_all | solution.py:515
  84.1 1.0 copy-done.5
  85.1 1.0 copy-done.14
  86.2 1.0 copy-done.16
  87.2 0.9 copy-done.23
  88.2 1.3 shard_map.159
  90.2 1.7 %collective-permute-start.4 = (bf16[256,512]{1,0:T(8,128)(2,1)S(1)}, bf16[256,512]{1,0:T(8,128)(2,1)S(1)}, u32[]{:S(2)}, u32[]{:S(2)}) collective-permute-start(bf16[256,512]{1,0:T(8,128)(2,1)S(1)} %get-tuple-element.52.refs_7_), channel_id=1, source_target_pairs={{0,1},{1,0},{2,3},{3,2},{4,5},{5,4},{6,7},{7,6},{8,9},{9,8},{10,11... | collective-permute-start | bytes 786440 | tf_op jit(solution)/shard_map/ppermute | solution.py:511
  92.0 5.0 %shard_map.158.refs_1_ = bf16[64,2,8,512]{3,2,1,0:T(8,128)(2,1)S(1)} custom-call(bf16[1024,256]{1,0:T(8,128)(2,1)S(1)} %bitcast.17, s32[1,512]{1,0:T(1,128)S(1)} %get-tuple-element.34.refs_1_, bf16[512,256]{1,0:T(8,128)(2,1)S(1)} %copy-done.19, bf16[512,768]{1,0:T(8,128)(2,1)S(1)} %copy-done.11, bf16[512,256]{1,0:T(8,128)(2,1)S(1)} %copy-done.21, ...), custom_call_target="tpu_custom_call" | custom-call | tf_op jit(solution)/shard_map/pallas_call | solution.py:497
  97.0 0.7 shard_map.160
  97.6 33.8 %all_to_all.27 = bf16[128,8,896]{2,1,0:T(8,128)(2,1)S(1)} all-to-all(bf16[128,8,896]{2,1,0:T(8,128)(2,1)S(1)} %bitcast.15), channel_id=1, replica_groups=mesh['pts'=64,'grp'=2] {'pts','grp'}, dimensions={0} | all-to-all | bytes 3670016 | tf_op jit(solution)/shard_map/all_to_all | solution.py:515
  131.8 25.3 %all_to_all.28.refs_1_ = bf16[64,8,1536]{2,1,0:T(8,128)(2,1)S(1)} all-to-all(bf16[64,8,1536]{2,1,0:T(8,128)(2,1)S(1)} %shard_map.162), channel_id=1, replica_groups=mesh['pts'=64,'grp'=2] {'pts'}, dimensions={0} | all-to-all | bytes 3145728 | tf_op jit(solution)/shard_map/all_to_all | solution.py:515
  157.1 3.9 %collective-permute-start.5 = (bf16[64,8,1536]{2,1,0:T(8,128)(2,1)S(1)}, bf16[64,8,1536]{2,1,0:T(8,128)(2,1)S(1)}, u32[]{:S(2)}, u32[]{:S(2)}) collective-permute-start(bf16[64,8,1536]{2,1,0:T(8,128)(2,1)S(1)} %all_to_all.28.refs_1_), channel_id=1, source_target_pairs={{0,1},{1,0},{2,3},{3,2},{4,5},{5,4},{6,7},{7,6},{8,9},{9,8},{10,11... | collective-permute-start | bytes 4718600 | tf_op jit(solution)/shard_map/ppermute | solution.py:511
  161.0 1.2 shard_map.161
  162.2 1.8 %collective-permute-done.5.refs_2_ = bf16[64,8,1536]{2,1,0:T(8,128)(2,1)S(1)} collective-permute-done((bf16[64,8,1536]{2,1,0:T(8,128)(2,1)S(1)}, bf16[64,8,1536]{2,1,0:T(8,128)(2,1)S(1)}, u32[]{:S(2)}, u32[]{:S(2)}) %collective-permute-start.5) | collective-permute-done | bytes 1572896 | tf_op jit(solution)/shard_map/ppermute | solution.py:511
  164.0 3.1 %shard_map.163 = (f32[256,768]{1,0:T(8,128)}, f32[256,256]{1,0:T(8,128)}, f32[512,512]{1,0:T(8,128)}, f32[512,1536]{1,0:T(8,128)}, f32[512,512]{1,0:T(8,128)}) custom-call(s32[1]{0:T(128)} %bitcast.refs_0_, bf16[64,8,1536]{2,1,0:T(8,128)(2,1)S(1)} %all_to_all.28.refs_1_, bf16[64,8,1536]{2,1,0:T(8,128)(2,1)S(1)} %collective-permute-done.5.refs_2_), custom_call_target="tpu_custom_call" | custom-call | tf_op jit(solution)/shard_map/pallas_call | solution.py:497
  (47 shorter events, 1.2 us)
Async XLA Ops:
  2.8 47.5 %copy-start.7 = (bf16[256,512]{1,0:T(8,128)(2,1)S(1)}, bf16[256,512]{1,0:T(8,128)(2,1)}, u32[]{:S(2)}) copy-start(bf16[256,512]{1,0:T(8,128)(2,1)} %refs_4_.5) | copy-start | bytes 786436
  27.8 26.0 %copy-start = (bf16[512,1536]{1,0:T(8,128)(2,1)S(1)}, bf16[512,1536]{1,0:T(8,128)(2,1)}, u32[]{:S(2)}) copy-start(bf16[512,1536]{1,0:T(8,128)(2,1)} %refs_6_.2) | copy-start | bytes 4718596
  27.8 26.0 %copy-start.1 = (bf16[512,512]{1,0:T(8,128)(2,1)S(1)}, bf16[512,512]{1,0:T(8,128)(2,1)}, u32[]{:S(2)}) copy-start(bf16[512,512]{1,0:T(8,128)(2,1)} %refs_5_.3) | copy-start | bytes 1572868
  32.1 18.6 %copy-start.8 = (bf16[8,256,256]{2,1,0:T(8,128)(2,1)}, bf16[8,256,256]{2,1,0:T(8,128)(2,1)S(1)}, u32[]{:S(2)}) copy-start(bf16[8,256,256]{2,1,0:T(8,128)(2,1)S(1)} %get-tuple-element.46.refs_5_) | copy-start | bytes 3145732
  32.2 20.0 %copy-start.10 = (bf16[512,768]{1,0:T(8,128)(2,1)}, bf16[512,768]{1,0:T(8,128)(2,1)S(1)}, u32[]{:S(2)}) copy-start(bf16[512,768]{1,0:T(8,128)(2,1)S(1)} %get-tuple-element.44.refs_3_) | copy-start | bytes 2359300
  32.2 20.0 %copy-start.18 = (bf16[512,256]{1,0:T(8,128)(2,1)}, bf16[512,256]{1,0:T(8,128)(2,1)S(1)}, u32[]{:S(2)}) copy-start(bf16[512,256]{1,0:T(8,128)(2,1)S(1)} %get-tuple-element.43.refs_2_) | copy-start | bytes 786436
  32.2 20.0 %copy-start.20 = (bf16[512,256]{1,0:T(8,128)(2,1)}, bf16[512,256]{1,0:T(8,128)(2,1)S(1)}, u32[]{:S(2)}) copy-start(bf16[512,256]{1,0:T(8,128)(2,1)S(1)} %get-tuple-element.45.refs_4_) | copy-start | bytes 786436
  50.8 2.9 %collective-permute-start = (bf16[256,1024]{1,0:T(8,128)(2,1)S(1)}, bf16[256,1024]{1,0:T(8,128)(2,1)S(1)}, u32[]{:S(2)}, u32[]{:S(2)}) collective-permute-start(bf16[256,1024]{1,0:T(8,128)(2,1)S(1)} %shard_map.155.refs_1_.refs_5_), channel_id=1, source_target_pairs={{0,1},{1,0},{2,3},{3,2},{4,5},{5,4},{6,7},{7,6},{8,9},{9,8},{10,11... | collective-permute-start | bytes 1572872 | tf_op jit(solution)/shard_map/ppermute | solution.py:511
  53.7 1.0 copy-start.2
  54.8 8.7 %copy-start.3 = (bf16[512,512]{1,0:T(8,128)(2,1)S(1)}, bf16[512,512]{1,0:T(8,128)(2,1)}, u32[]{:S(2)}) copy-start(bf16[512,512]{1,0:T(8,128)(2,1)} %refs_7_.2) | copy-start | bytes 1572868
  60.8 0.8 copy-start.15
  61.6 3.4 %copy-start.4 = (bf16[256,1024]{1,0:T(8,128)(2,1)}, bf16[256,1024]{1,0:T(8,128)(2,1)S(1)}, u32[]{:S(2)}) copy-start(bf16[256,1024]{1,0:T(8,128)(2,1)S(1)} %get-tuple-element.39.refs_2_.refs_3_) | copy-start | bytes 1572868
  61.6 1.9 %collective-permute-start.1 = (bf16[256,1024]{1,0:T(8,128)(2,1)S(1)}, bf16[256,1024]{1,0:T(8,128)(2,1)S(1)}, u32[]{:S(2)}, u32[]{:S(2)}) collective-permute-start(bf16[256,1024]{1,0:T(8,128)(2,1)S(1)} %get-tuple-element.40.refs_4_), channel_id=1, source_target_pairs={{0,1},{1,0},{2,3},{3,2},{4,5},{5,4},{6,7},{7,6},{8,9},{9,8},{10,11... | collective-permute-start | bytes 1572872 | tf_op jit(solution)/shard_map/ppermute | solution.py:511
  61.9 0.8 copy-start.13
  65.0 0.7 copy-start.22
  65.7 0.8 copy-start.12
  66.5 17.6 %all-to-all-start.2 = ((bf16[128,8,256]{2,1,0:T(8,128)(2,1)}), bf16[128,8,256]{2,1,0:T(8,128)(2,1)S(1)}, u32[]{:S(2)}, u32[]{:S(2)}) async-start(bf16[128,8,256]{2,1,0:T(8,128)(2,1)} %bitcast.20), calls=%async_computation.2 | async-start | bytes 1048576 | tf_op jit(solution)/shard_map/all_to_all | solution.py:515
  84.1 1.0 copy-start.5
  85.1 1.0 copy-start.14
  86.2 1.0 copy-start.16
  87.2 0.9 copy-start.23
  88.2 3.8 %copy-start.6 = (bf16[256,768]{1,0:T(8,128)(2,1)S(1)}, bf16[256,768]{1,0:T(8,128)(2,1)}, u32[]{:S(2)}) copy-start(bf16[256,768]{1,0:T(8,128)(2,1)} %refs_6_.3) | copy-start | bytes 1179652
  88.2 3.8 %copy-start.9 = (bf16[8,256,256]{2,1,0:T(8,128)(2,1)S(1)}, bf16[8,256,256]{2,1,0:T(8,128)(2,1)}, u32[]{:S(2)}) copy-start(bf16[8,256,256]{2,1,0:T(8,128)(2,1)} %copy-done.8) | copy-start | bytes 3145732
  88.2 3.8 %copy-start.11 = (bf16[512,768]{1,0:T(8,128)(2,1)S(1)}, bf16[512,768]{1,0:T(8,128)(2,1)}, u32[]{:S(2)}) copy-start(bf16[512,768]{1,0:T(8,128)(2,1)} %copy-done.10) | copy-start | bytes 2359300
  88.2 3.8 %copy-start.17 = (bf16[256,256]{1,0:T(8,128)(2,1)S(1)}, bf16[256,256]{1,0:T(8,128)(2,1)}, u32[]{:S(2)}) copy-start(bf16[256,256]{1,0:T(8,128)(2,1)} %refs_7_.3) | copy-start | bytes 393220
  88.2 3.8 %copy-start.19 = (bf16[512,256]{1,0:T(8,128)(2,1)S(1)}, bf16[512,256]{1,0:T(8,128)(2,1)}, u32[]{:S(2)}) copy-start(bf16[512,256]{1,0:T(8,128)(2,1)} %copy-done.18) | copy-start | bytes 786436
  88.2 3.8 %copy-start.21 = (bf16[512,256]{1,0:T(8,128)(2,1)S(1)}, bf16[512,256]{1,0:T(8,128)(2,1)}, u32[]{:S(2)}) copy-start(bf16[512,256]{1,0:T(8,128)(2,1)} %copy-done.20) | copy-start | bytes 786436
  89.5 7.4 %collective-permute-start.2 = (bf16[64,2,8,128]{3,2,1,0:T(8,128)(2,1)S(1)}, bf16[64,2,8,128]{3,2,1,0:T(8,128)(2,1)S(1)}, u32[]{:S(2)}, u32[]{:S(2)}) collective-permute-start(bf16[64,2,8,128]{3,2,1,0:T(8,128)(2,1)S(1)} %get-tuple-element.50), channel_id=1, source_target_pairs={{0,32},{2,34},{4,36},{6,38},{8,40},{10,42},{12,44},{14,46},{16,48}... | collective-permute-start | bytes 786440 | tf_op jit(solution)/shard_map/ppermute | solution.py:627
  89.9 7.1 %collective-permute-start.3 = (bf16[64,2,8,128]{3,2,1,0:T(8,128)(2,1)S(1)}, bf16[64,2,8,128]{3,2,1,0:T(8,128)(2,1)S(1)}, u32[]{:S(2)}, u32[]{:S(2)}) collective-permute-start(bf16[64,2,8,128]{3,2,1,0:T(8,128)(2,1)S(1)} %get-tuple-element.51), channel_id=1, source_target_pairs={{0,8},{2,10},{4,12},{6,14},{8,0},{10,2},{12,4},{14,6},{16,24},{18,... | collective-permute-start | bytes 786440 | tf_op jit(solution)/shard_map/ppermute | solution.py:628
  90.2 6.8 %collective-permute-start.4 = (bf16[256,512]{1,0:T(8,128)(2,1)S(1)}, bf16[256,512]{1,0:T(8,128)(2,1)S(1)}, u32[]{:S(2)}, u32[]{:S(2)}) collective-permute-start(bf16[256,512]{1,0:T(8,128)(2,1)S(1)} %get-tuple-element.52.refs_7_), channel_id=1, source_target_pairs={{0,1},{1,0},{2,3},{3,2},{4,5},{5,4},{6,7},{7,6},{8,9},{9,8},{10,11... | collective-permute-start | bytes 786440 | tf_op jit(solution)/shard_map/ppermute | solution.py:511
  157.1 6.9 %collective-permute-start.5 = (bf16[64,8,1536]{2,1,0:T(8,128)(2,1)S(1)}, bf16[64,8,1536]{2,1,0:T(8,128)(2,1)S(1)}, u32[]{:S(2)}, u32[]{:S(2)}) collective-permute-start(bf16[64,8,1536]{2,1,0:T(8,128)(2,1)S(1)} %all_to_all.28.refs_1_), channel_id=1, source_target_pairs={{0,1},{1,0},{2,3},{3,2},{4,5},{5,4},{6,7},{7,6},{8,9},{9,8},{10,11... | collective-permute-start | bytes 4718600 | tf_op jit(solution)/shard_map/ppermute | solution.py:511

commit v8 on v7

--- a/solution.py
+++ b/solution.py
@@ -50,15 +50,38 @@
     return jnp.where(head_half(rows.shape, half), rows, jnp.zeros_like(rows))
 
 
-def softmax_rows(scores):
-    raised = jnp.exp(scores - jnp.max(scores, axis=-1, keepdims=True))
-    return (raised * (1.0 / jnp.sum(raised, axis=-1, keepdims=True))).astype(BF)
+def softmax_columns(scores):
+    raised = jnp.exp(scores - jnp.max(scores, axis=0, keepdims=True))
+    return (raised * (1.0 / jnp.sum(raised, axis=0, keepdims=True))).astype(BF)
 
 
 def slopes_of(weights, against):
     wide = weights.astype(F32)
-    diagonal = jnp.sum(wide * against, axis=-1, keepdims=True)
+    diagonal = jnp.sum(wide * against, axis=0, keepdims=True)
     return (wide * (against - diagonal)).astype(BF)
+
+
+def attend(query, key, value_turned, half, alive=None):
+    scores = mm(key, scaled_half(query, half), (1, 1))
+    if alive is not None:
+        scores = jnp.where(alive, scores, -1e30)
+    weights = softmax_columns(scores)
+    return weights, mm(value_turned[half * HD : (half + 1) * HD], weights)
+
+
+def attend_backward(query, key_turned, value, entering, weights, half):
+    slopes = slopes_of(weights, mm(value, keep_half(entering, half), (1, 1)))
+    query_part = mm(key_turned[half * HD : (half + 1) * HD], slopes) * HD ** (-0.5)
+    key_part = mm(slopes, query) * HD ** (-0.5)
+    return query_part, key_part, mm(weights, entering)
+
+
+def pick_halves(low, high):
+    return jnp.where(head_half(low.shape, 0), low, high).astype(BF)
+
+
+def turned(rows):
+    return rows.astype(F32).T.astype(BF)
 
 
 def scaled_half(rows, half):
@@ -72,7 +95,7 @@
 
 
 def route_kernel(
-    place, source, counts, points, send, send_slot, pair_slot, receive_slot, live
+    where, place, source, counts, points, send, send_slot, pair_slot, receive_slot, live
 ):
     count = place.shape[1]
     shift = count.bit_length() - 1
@@ -114,22 +137,25 @@
     projected[...] = mm(normed.astype(BF), projection[...]).astype(BF)
     balls = rows_in.shape[0] // BALL
     pairs = features // PAIR
+    alive = jnp.broadcast_to(live[...], (128, rows_in.shape[0])).T
+    alive = jnp.concatenate([alive] * (BALL // 128), axis=1) > 0.5
+    value_turned = turned(projected[:, 2 * features :])
+    mixed = []
     for ball in range(balls):
         rows = slice(ball * BALL, (ball + 1) * BALL)
-        alive = live[:, rows] > 0.5
+        pieces = []
         for pair in range(pairs):
             lanes = slice(pair * PAIR, (pair + 1) * PAIR)
             query = projected[rows, lanes]
             key = projected[rows, features + pair * PAIR : features + (pair + 1) * PAIR]
-            value = projected[rows, 2 * features + pair * PAIR : 2 * features + (pair + 1) * PAIR]
-            halves = []
             for half in range(2):
-                scores = mm(scaled_half(query, half), key, (1, 1))
-                head_weights = softmax_rows(jnp.where(alive, scores, -1e30))
+                head_weights, piece = attend(
+                    query, key, value_turned[lanes, rows], half, alive[rows]
+                )
                 weights[(ball * pairs + pair) * 2 + half] = head_weights
-                halves.append(mm(head_weights, value))
-            mixed = jnp.where(head_half(halves[0].shape, 0), halves[0], halves[1])
-            mixture[rows, lanes] = mixed.astype(BF)
+                pieces.append(piece)
+        mixed.append(jnp.concatenate(pieces, axis=0))
+    mixture[...] = jnp.concatenate(mixed, axis=1).T.astype(BF)
     result = (rows_in + mm(mixture[...], output[...])).astype(BF)
     send[...] = mm(place, result).astype(BF)
 
@@ -160,25 +186,32 @@
     values = mm(unit_rows, projection[:, pl.ds(2 * wide + first, part)]).astype(BF)
     cotangent = jnp.concatenate([own_pack[:, wide:], other_pack[:, wide:]], axis=0)
     incoming = mm(cotangent, output[pl.ds(first, part), :], (1, 1)).astype(BF)
+    keys_turned, values_turned = turned(keys), turned(values)
+    mixed, query_grads = [], []
+
+    def put(at, rows):
+        target = slice(at, at + rows.shape[1])
+        keep[:, target] = rows[:half_rows]
+        give[:, target] = rows[half_rows:]
+
     for pair in range(part // PAIR):
         lanes = slice(pair * PAIR, (pair + 1) * PAIR)
         query, key, value = queries[:, lanes], keys[:, lanes], values[:, lanes]
         entering = incoming[:, lanes]
-        parts = ([], [], [], [])
+        key_parts, value_parts = [], []
         for half in range(2):
-            scores = mm(scaled_half(query, half), key, (1, 1))
-            head_weights = softmax_rows(scores)
-            parts[0].append(mm(head_weights, value))
-            against = mm(keep_half(entering, half), value, (1, 1))
-            slopes = slopes_of(head_weights, against)
-            parts[1].append(mm(slopes, key) * HD ** (-0.5))
-            parts[2].append(mm(slopes, query, (0, 0)) * HD ** (-0.5))
-            parts[3].append(mm(head_weights, entering, (0, 0)))
-        for at, (low, high) in enumerate(parts):
-            both = jnp.where(head_half(low.shape, 0), low, high).astype(BF)
-            target = slice(at * part + pair * PAIR, at * part + (pair + 1) * PAIR)
-            keep[:, target] = both[:half_rows]
-            give[:, target] = both[half_rows:]
+            head_weights, piece = attend(query, key, values_turned[lanes], half)
+            mixed.append(piece)
+            query_part, key_part, value_part = attend_backward(
+                query, keys_turned[lanes], value, entering, head_weights, half
+            )
+            query_grads.append(query_part)
+            key_parts.append(key_part)
+            value_parts.append(value_part)
+        put(2 * part + pair * PAIR, pick_halves(*key_parts))
+        put(3 * part + pair * PAIR, pick_halves(*value_parts))
+    put(0, jnp.concatenate(mixed, axis=0).T.astype(BF))
+    put(part, jnp.concatenate(query_grads, axis=0).T.astype(BF))
 
 
 def coarse_finish_kernel(
@@ -222,7 +255,7 @@
 
 
 def coarse_weights_kernel(
-    parity,
+    where,
     arrived,
     unit,
     keep,
@@ -250,7 +283,7 @@
         for at, passed in enumerate((first_half, second_half)):
             low = terms[:, 2 * at * width : (2 * at + 1) * width]
             high = terms[:, (2 * at + 1) * width : (2 * at + 2) * width]
-            upper = parity[at] == 1
+            upper = where[1 + at] == 1
             put_blocks(kept, side, at * width, jnp.where(upper, high, low))
             put_blocks(passed, side, 0, jnp.where(upper, low, high))
     gradient_out[...] = gradient[...]
@@ -357,26 +390,33 @@
     terms = [mm(mixture[...], gradient_rows, (0, 0))]
     balls = rotated.shape[0] // BALL
     pairs = features // PAIR
+    key_turned = turned(projected[:, features : 2 * features])
+    query_grads = []
     for ball in range(balls):
         rows = slice(ball * BALL, (ball + 1) * BALL)
+        pieces = []
         for pair in range(pairs):
             lanes = slice(pair * PAIR, (pair + 1) * PAIR)
             query = projected[rows, lanes]
-            key = projected[rows, features + pair * PAIR : features + (pair + 1) * PAIR]
             value = projected[rows, 2 * features + pair * PAIR : 2 * features + (pair + 1) * PAIR]
-            enters = entering[rows, lanes]
-            parts = ([], [], [])
+            key_parts, value_parts = [], []
             for half in range(2):
-                head_weights = weights[(ball * pairs + pair) * 2 + half]
-                against = mm(keep_half(enters, half), value, (1, 1))
-                slopes = slopes_of(head_weights, against)
-                parts[0].append(mm(slopes, key) * HD ** (-0.5))
-                parts[1].append(mm(slopes, query, (0, 0)) * HD ** (-0.5))
-                parts[2].append(mm(head_weights, enters, (0, 0)))
-            for at, (low, high) in enumerate(parts):
-                both = jnp.where(head_half(low.shape, 0), low, high).astype(BF)
+                query_part, key_part, value_part = attend_backward(
+                    query,
+                    key_turned[lanes, rows],
+                    value,
+                    entering[rows, lanes],
+                    weights[(ball * pairs + pair) * 2 + half],
+                    half,
+                )
+                pieces.append(query_part)
+                key_parts.append(key_part)
+                value_parts.append(value_part)
+            for at, halves in ((1, key_parts), (2, value_parts)):
                 target = at * features + pair * PAIR
-                grad_projected[rows, target : target + PAIR] = both
+                grad_projected[rows, target : target + PAIR] = pick_halves(*halves)
+        query_grads.append(jnp.concatenate(pieces, axis=0))
+    grad_projected[:, :features] = jnp.concatenate(query_grads, axis=1).T.astype(BF)
     normed, inverse = normalize(rotated[...])
     unit_rows = normed.astype(BF)
     for at in range(3):
@@ -537,13 +577,17 @@
     devices = lax.axis_size(("pts", "grp"))
     slots = 2 * count
     scaling = 1.0 / math.sqrt(count * devices)
-    group = lax.axis_index("grp").astype(jnp.int32).reshape(1)
+    owners = lax.axis_size("pts")
+    run, step = owners // 4, owners // 16
+    chip = lax.axis_index("pts")
+    group = jnp.stack([lax.axis_index("grp"), chip // run % 2, chip // step % 2]).astype(jnp.int32)
     wide = 2 * features
     half_rows = count // 2
 
     send, send_slot, pair_slot, receive_slot, live = call(
         route_kernel,
         (
+            group,
             Far(rotated_place.reshape(1, count)),
             Far(rotated_source.reshape(1, count)),
             Far(ball_counts.reshape(1, -1)),
@@ -556,12 +600,13 @@
             Near((1, count), jnp.int32),
             Near((1, count), F32),
         ),
+        scalar=True,
     )
     arrived = route(send, devices)
     heads = features // HD * (count // BALL)
     send, rotated, projected, mixture, weights = call(
         fine_forward_kernel,
-        (arrived, receive_slot, live, Far(fine_projection), Far(fine_output)),
+        (arrived, receive_slot, live, fine_projection, Far(fine_output)),
         (
             Near((slots, features)),
             Near((count, features)),
@@ -577,7 +622,7 @@
     other_pack = exchange(own_pack)
     coarse, keep, give, unit = call(
         coarse_kernel,
-        (group, own_pack, other_pack, pool_weight, coarse_projection, coarse_output),
+        (group, own_pack, other_pack, pool_weight, coarse_projection, Far(coarse_output)),
         (
             Near((half_rows, wide)),
             Near((half_rows, 2 * wide)),
@@ -608,14 +653,10 @@
         scalar=True,
     )
     arrived = route(send, devices)
-    owners = lax.axis_size("pts")
-    run, step = owners // 4, owners // 16
-    place = lax.axis_index("pts").astype(jnp.int32)
-    parity = jnp.stack([place // run % 2, place // step % 2])
     blocks = (owners, 2, slots // devices)
     kept, first_half, second_half, own_gradient = call(
         coarse_weights_kernel,
-        (parity, arrived, unit, keep, give, own_pack, other_pack, coarse_gradient),
+        (group, arrived, unit, keep, give, own_pack, other_pack, coarse_gradient),
         (
             Near((*blocks, wide // 2)),
             Near((*blocks, wide // 4)),

time: 168 us -> 164 us (0.976)
  blocking collectives: 102 us -> 119 us
  waiting for transfers between devices: 17.7 us -> 4.91 us
  local copies, waits for them, and re-layouts: 8.3 us -> 0.06 us
  Pallas kernels: 26 us -> 30.1 us
  starting transfers between devices: 11.9 us -> 8.15 us
    all_to_all x4 -> x5, blocking collectives: 102 us -> 119 us  [spread_blocks(): return lax.all_to_all(values, axes, split_axis=0, concat_axis=0, tiled=True)]
    all_to_all x1 -> x0, waiting for transfers between devices: 13.6 us -> none  [spread_blocks(): return lax.all_to_all(values, axes, split_axis=0, concat_axis=0, tiled=True)]
    unnamed x48 -> x12, local copies, waits for them, and re-layouts: 8.26 us -> 0.03 us
    pallas_call x11, Pallas kernels: 26 us -> 30.1 us  [call(): pl.pallas_call(body, out_shape=[(pltpu.HBM if out.far else jax.ShapeDtype...]
    all_to_all x1 -> x0, starting transfers between devices: 3.8 us -> none  [spread_blocks(): return lax.all_to_all(values, axes, split_axis=0, concat_axis=0, tiled=True)]
  transfers between devices with their start and end apart: 7 -> 6, of which waited for: 4 -> 3; matrix products, arithmetic and copies ran while one was open for 0% -> 0% of each run, Pallas kernels for 4% -> 4%
where the time goes in v8:
time: 164 us
  blocking collectives  119 us (73%)
  Pallas kernels  30.1 us (18%)
  starting transfers between devices  8.15 us (5%)
  waiting for transfers between devices  4.91 us (3%)
    all_to_all x5, blocking collectives, spread_blocks(): return lax.all_to_all(values, axes, split_axis=0, concat_axis=0, tiled=True)  119 us
    pallas_call x11, Pallas kernels, call(): pl.pallas_call(body, out_shape=[(pltpu.HBM if out.far else jax.ShapeDtype...  30.1 us
    ppermute x4, starting transfers between devices, exchange(): return lax.ppermute(values, 'grp', [(0, 1), (1, 0)])  7.44 us
    ppermute x4, waiting for transfers between devices, exchange(): return lax.ppermute(values, 'grp', [(0, 1), (1, 0)])  4.9 us
  transfers between devices with their start and end apart: 6, of which 3 were waited for; matrix products, arithmetic and copies ran while one was open for 0% of the time, Pallas kernels for 4%

profile of v8, /device:TPU:1, one launch (start us, length us, event | category | flops | bytes accessed | tf_op | source)
XLA Modules:
  0.0 163.7 jit_solution(11738049670750590807)
XLA Ops:
  0.7 0.1 pad_add_fusion.refs_0_
  0.8 2.7 %shard_map.153 = (bf16[1024,256]{1,0:T(8,128)(2,1)S(1)}, s32[1,512]{1,0:T(1,128)S(1)}, s32[1,512]{1,0:T(1,128)S(1)}, s32[1,512]{1,0:T(1,128)S(1)}, f32[1,512]{1,0:T(1,128)S(1)}) custom-call(s32[3]{0:T(128)S(1)} %pad_add_fusion.refs_0_, s32[1,512]{1,0:T(1,128)} %bitcast.23, s32[1,512]{1,0:T(1,128)} %bitcast.24, s32[1,256]{1,0:T(1,128)} %bitcast.25, ...), custom_call_target="tpu_custom_call" | custom-call | tf_op jit(solution)/shard_map/pallas_call | solution.py:537
  3.4 0.0 copy-start.4
  3.5 25.0 %all_to_all.25 = bf16[128,8,256]{2,1,0:T(8,128)(2,1)S(1)} all-to-all(bf16[128,8,256]{2,1,0:T(8,128)(2,1)S(1)} %bitcast.22), channel_id=1, replica_groups=mesh['pts'=64,'grp'=2] {'pts','grp'}, dimensions={0} | all-to-all | bytes 1048576 | tf_op jit(solution)/shard_map/all_to_all | solution.py:555
  28.4 4.9 %shard_map.154 = (bf16[1024,256]{1,0:T(8,128)(2,1)S(1)}, bf16[512,256]{1,0:T(8,128)(2,1)S(1)}, bf16[512,768]{1,0:T(8,128)(2,1)S(1)}, bf16[512,256]{1,0:T(8,128)(2,1)S(1)}, bf16[8,256,256]{2,1,0:T(8,128)(2,1)S(1)}) custom-call(bf16[1024,256]{1,0:T(8,128)(2,1)S(1)} %bitcast.19, s32[1,512]{1,0:T(1,128)S(1)} %get-tuple-element.34.refs_1_, ...), custom_call_target="tpu_custom_call" | custom-call | tf_op jit(solution)/shard_map/pallas_call | solution.py:537
  33.3 18.1 %all_to_all.26 = bf16[128,8,256]{2,1,0:T(8,128)(2,1)S(1)} all-to-all(bf16[128,8,256]{2,1,0:T(8,128)(2,1)S(1)} %bitcast.20), channel_id=1, replica_groups=mesh['pts'=64,'grp'=2] {'pts','grp'}, dimensions={0} | all-to-all | bytes 1048576 | tf_op jit(solution)/shard_map/all_to_all | solution.py:555
  51.4 0.0 copy-done.4
  51.4 0.5 shard_map.155.refs_1_.refs_5_
  51.9 0.0 copy-start.2
  51.9 1.4 collective-permute-start
  53.3 1.5 collective-permute-done.refs_2_.refs_6_
  54.9 7.4 %shard_map.156 = (bf16[256,512]{1,0:T(8,128)(2,1)S(1)}, bf16[256,1024]{1,0:T(8,128)(2,1)S(1)}, bf16[256,1024]{1,0:T(8,128)(2,1)S(1)}, bf16[512,512]{1,0:T(8,128)(2,1)S(1)}) custom-call(s32[3]{0:T(128)S(1)} %pad_add_fusion.refs_0_, bf16[256,1024]{1,0:T(8,128)(2,1)S(1)} %shard_map.155.refs_1_.refs_5_, ...), custom_call_target="tpu_custom_call" | custom-call | tf_op jit(solution)/shard_map/pallas_call | solution.py:537
  62.3 0.4 collective-permute-start.1
  62.7 1.6 collective-permute-done.1.refs_3_
  64.3 2.1 %shard_map.157 = (bf16[256,512]{1,0:T(8,128)(2,1)}, bf16[256,512]{1,0:T(8,128)(2,1)S(1)}, bf16[1024,256]{1,0:T(8,128)(2,1)S(1)}) custom-call(s32[3]{0:T(128)S(1)} %pad_add_fusion.refs_0_, bf16[256,512]{1,0:T(8,128)(2,1)S(1)} %get-tuple-element.38.refs_1_, bf16[256,1024]{1,0:T(8,128)(2,1)S(1)} %get-tuple-element.39.refs_2_.refs_3_, ...), custom_call_target="tpu_custom_call" | custom-call | tf_op jit(solution)/shard_map/pallas_call | solution.py:537
  66.3 17.3 %all_to_all.27 = bf16[128,8,256]{2,1,0:T(8,128)(2,1)S(1)} all-to-all(bf16[128,8,256]{2,1,0:T(8,128)(2,1)S(1)} %bitcast.21), channel_id=1, replica_groups=mesh['pts'=64,'grp'=2] {'pts','grp'}, dimensions={0} | all-to-all | bytes 1048576 | tf_op jit(solution)/shard_map/all_to_all | solution.py:555
  83.6 1.3 shard_map.159
  84.9 0.4 collective-permute-start.2
  85.3 0.3 collective-permute-start.3
  85.6 1.7 %collective-permute-start.4 = (bf16[256,512]{1,0:T(8,128)(2,1)S(1)}, bf16[256,512]{1,0:T(8,128)(2,1)S(1)}, u32[]{:S(2)}, u32[]{:S(2)}) collective-permute-start(bf16[256,512]{1,0:T(8,128)(2,1)S(1)} %get-tuple-element.52.refs_7_), channel_id=1, source_target_pairs={{0,1},{1,0},{2,3},{3,2},{4,5},{5,4},{6,7},{7,6},{8,9},{9,8},{10,11... | collective-permute-start | bytes 786440 | tf_op jit(solution)/shard_map/ppermute | solution.py:551
  87.4 4.9 %shard_map.158.refs_1_ = bf16[64,2,8,512]{3,2,1,0:T(8,128)(2,1)S(1)} custom-call(bf16[1024,256]{1,0:T(8,128)(2,1)S(1)} %bitcast.17, s32[1,512]{1,0:T(1,128)S(1)} %get-tuple-element.34.refs_1_, bf16[512,256]{1,0:T(8,128)(2,1)S(1)} %get-tuple-element.43.refs_2_, bf16[512,768]{1,0:T(8,128)(2,1)S(1)} %get-tuple-element.44.refs_3_, ...), custom_call_target="tpu_custom_call" | custom-call | tf_op jit(solution)/shard_map/pallas_call | solution.py:537
  92.3 0.0 collective-permute-done.2.refs_3_
  92.3 0.0 collective-permute-done.3.refs_4_
  92.3 0.0 collective-permute-done.4.refs_8_
  92.3 1.1 shard_map.160
  93.5 33.8 %all_to_all.28 = bf16[128,8,896]{2,1,0:T(8,128)(2,1)S(1)} all-to-all(bf16[128,8,896]{2,1,0:T(8,128)(2,1)S(1)} %bitcast.15), channel_id=1, replica_groups=mesh['pts'=64,'grp'=2] {'pts','grp'}, dimensions={0} | all-to-all | bytes 3670016 | tf_op jit(solution)/shard_map/all_to_all | solution.py:555
  127.3 0.3 shard_map.162
  127.7 25.3 %all_to_all.29.refs_1_ = bf16[64,8,1536]{2,1,0:T(8,128)(2,1)S(1)} all-to-all(bf16[64,8,1536]{2,1,0:T(8,128)(2,1)S(1)} %shard_map.162), channel_id=1, replica_groups=mesh['pts'=64,'grp'=2] {'pts'}, dimensions={0} | all-to-all | bytes 3145728 | tf_op jit(solution)/shard_map/all_to_all | solution.py:555
  152.9 3.9 %collective-permute-start.5 = (bf16[64,8,1536]{2,1,0:T(8,128)(2,1)S(1)}, bf16[64,8,1536]{2,1,0:T(8,128)(2,1)S(1)}, u32[]{:S(2)}, u32[]{:S(2)}) collective-permute-start(bf16[64,8,1536]{2,1,0:T(8,128)(2,1)S(1)} %all_to_all.29.refs_1_), channel_id=1, source_target_pairs={{0,1},{1,0},{2,3},{3,2},{4,5},{5,4},{6,7},{7,6},{8,9},{9,8},{10,11... | collective-permute-start | bytes 4718600 | tf_op jit(solution)/shard_map/ppermute | solution.py:551
  156.9 1.2 shard_map.161
  158.1 1.8 %collective-permute-done.5.refs_2_ = bf16[64,8,1536]{2,1,0:T(8,128)(2,1)S(1)} collective-permute-done((bf16[64,8,1536]{2,1,0:T(8,128)(2,1)S(1)}, bf16[64,8,1536]{2,1,0:T(8,128)(2,1)S(1)}, u32[]{:S(2)}, u32[]{:S(2)}) %collective-permute-start.5) | collective-permute-done | bytes 1572896 | tf_op jit(solution)/shard_map/ppermute | solution.py:551
  159.9 3.7 %shard_map.163 = (f32[256,768]{1,0:T(8,128)}, f32[256,256]{1,0:T(8,128)}, f32[512,512]{1,0:T(8,128)}, f32[512,1536]{1,0:T(8,128)}, f32[512,512]{1,0:T(8,128)}) custom-call(s32[3]{0:T(128)S(1)} %pad_add_fusion.refs_0_, bf16[64,8,1536]{2,1,0:T(8,128)(2,1)S(1)} %all_to_all.29.refs_1_, bf16[64,8,1536]{2,1,0:T(8,128)(2,1)S(1)} %collective-permute-done.5.refs_2_), custom_call_target="tpu_custom_call" | custom-call | tf_op jit(solution)/shard_map/pallas_call | solution.py:537
  (10 shorter events, 0.1 us)
Async XLA Ops:
  0.6 27.8 %copy-start.3 = (bf16[256,768]{1,0:T(8,128)(2,1)S(1)}, bf16[256,768]{1,0:T(8,128)(2,1)}, u32[]{:S(2)}) copy-start(bf16[256,768]{1,0:T(8,128)(2,1)} %refs_6_.3) | copy-start | bytes 1179652
  3.4 48.0 %copy-start.4 = (bf16[256,512]{1,0:T(8,128)(2,1)S(1)}, bf16[256,512]{1,0:T(8,128)(2,1)}, u32[]{:S(2)}) copy-start(bf16[256,512]{1,0:T(8,128)(2,1)} %refs_4_.7) | copy-start | bytes 786436
  28.4 26.4 %copy-start = (bf16[512,1536]{1,0:T(8,128)(2,1)S(1)}, bf16[512,1536]{1,0:T(8,128)(2,1)}, u32[]{:S(2)}) copy-start(bf16[512,1536]{1,0:T(8,128)(2,1)} %refs_6_.2) | copy-start | bytes 4718596
  28.4 26.4 %copy-start.1 = (bf16[512,512]{1,0:T(8,128)(2,1)S(1)}, bf16[512,512]{1,0:T(8,128)(2,1)}, u32[]{:S(2)}) copy-start(bf16[512,512]{1,0:T(8,128)(2,1)} %refs_5_.3) | copy-start | bytes 1572868
  51.9 12.4 %copy-start.2 = (bf16[512,512]{1,0:T(8,128)(2,1)S(1)}, bf16[512,512]{1,0:T(8,128)(2,1)}, u32[]{:S(2)}) copy-start(bf16[512,512]{1,0:T(8,128)(2,1)} %refs_7_.2) | copy-start | bytes 1572868
  51.9 2.9 %collective-permute-start = (bf16[256,1024]{1,0:T(8,128)(2,1)S(1)}, bf16[256,1024]{1,0:T(8,128)(2,1)S(1)}, u32[]{:S(2)}, u32[]{:S(2)}) collective-permute-start(bf16[256,1024]{1,0:T(8,128)(2,1)S(1)} %shard_map.155.refs_1_.refs_5_), channel_id=1, source_target_pairs={{0,1},{1,0},{2,3},{3,2},{4,5},{5,4},{6,7},{7,6},{8,9},{9,8},{10,11... | collective-permute-start | bytes 1572872 | tf_op jit(solution)/shard_map/ppermute | solution.py:551
  62.3 2.0 %collective-permute-start.1 = (bf16[256,1024]{1,0:T(8,128)(2,1)S(1)}, bf16[256,1024]{1,0:T(8,128)(2,1)S(1)}, u32[]{:S(2)}, u32[]{:S(2)}) collective-permute-start(bf16[256,1024]{1,0:T(8,128)(2,1)S(1)} %get-tuple-element.40.refs_4_), channel_id=1, source_target_pairs={{0,1},{1,0},{2,3},{3,2},{4,5},{5,4},{6,7},{7,6},{8,9},{9,8},{10,11... | collective-permute-start | bytes 1572872 | tf_op jit(solution)/shard_map/ppermute | solution.py:551
  83.6 3.8 %copy-start.5 = (bf16[256,256]{1,0:T(8,128)(2,1)S(1)}, bf16[256,256]{1,0:T(8,128)(2,1)}, u32[]{:S(2)}) copy-start(bf16[256,256]{1,0:T(8,128)(2,1)} %refs_7_.3) | copy-start | bytes 393220
  84.9 7.4 %collective-permute-start.2 = (bf16[64,2,8,128]{3,2,1,0:T(8,128)(2,1)S(1)}, bf16[64,2,8,128]{3,2,1,0:T(8,128)(2,1)S(1)}, u32[]{:S(2)}, u32[]{:S(2)}) collective-permute-start(bf16[64,2,8,128]{3,2,1,0:T(8,128)(2,1)S(1)} %get-tuple-element.50), channel_id=1, source_target_pairs={{0,32},{2,34},{4,36},{6,38},{8,40},{10,42},{12,44},{14,46},{16,48}... | collective-permute-start | bytes 786440 | tf_op jit(solution)/shard_map/ppermute | solution.py:668
  85.3 7.0 %collective-permute-start.3 = (bf16[64,2,8,128]{3,2,1,0:T(8,128)(2,1)S(1)}, bf16[64,2,8,128]{3,2,1,0:T(8,128)(2,1)S(1)}, u32[]{:S(2)}, u32[]{:S(2)}) collective-permute-start(bf16[64,2,8,128]{3,2,1,0:T(8,128)(2,1)S(1)} %get-tuple-element.51), channel_id=1, source_target_pairs={{0,8},{2,10},{4,12},{6,14},{8,0},{10,2},{12,4},{14,6},{16,24},{18,... | collective-permute-start | bytes 786440 | tf_op jit(solution)/shard_map/ppermute | solution.py:669
  85.6 6.7 %collective-permute-start.4 = (bf16[256,512]{1,0:T(8,128)(2,1)S(1)}, bf16[256,512]{1,0:T(8,128)(2,1)S(1)}, u32[]{:S(2)}, u32[]{:S(2)}) collective-permute-start(bf16[256,512]{1,0:T(8,128)(2,1)S(1)} %get-tuple-element.52.refs_7_), channel_id=1, source_target_pairs={{0,1},{1,0},{2,3},{3,2},{4,5},{5,4},{6,7},{7,6},{8,9},{9,8},{10,11... | collective-permute-start | bytes 786440 | tf_op jit(solution)/shard_map/ppermute | solution.py:551
  152.9 6.9 %collective-permute-start.5 = (bf16[64,8,1536]{2,1,0:T(8,128)(2,1)S(1)}, bf16[64,8,1536]{2,1,0:T(8,128)(2,1)S(1)}, u32[]{:S(2)}, u32[]{:S(2)}) collective-permute-start(bf16[64,8,1536]{2,1,0:T(8,128)(2,1)S(1)} %all_to_all.29.refs_1_), channel_id=1, source_target_pairs={{0,1},{1,0},{2,3},{3,2},{4,5},{5,4},{6,7},{7,6},{8,9},{9,8},{10,11... | collective-permute-start | bytes 4718600 | tf_op jit(solution)/shard_map/ppermute | solution.py:551

commit v9 on v7

--- a/solution.py
+++ b/solution.py
@@ -144,11 +144,11 @@
 
 
 def coarse_kernel(
-    group, own_pack, other_pack, pool, projection, output, coarse, keep, give, unit
+    own_pack, other_pack, pool, projection, output, coarse, keep, give, unit
 ):
     half_rows, wide = coarse.shape
     part = wide // 2
-    first = pl.multiple_of(group[0] * part, part)
+    first = pl.multiple_of(lax.axis_index("grp") * part, part)
     joined = jnp.concatenate([own_pack[:, :wide], other_pack[:, :wide]], axis=0)
     tokens = mm(joined, pool[...]).astype(BF)
     coarse[...] = tokens[:half_rows]
@@ -182,7 +182,6 @@
 
 
 def coarse_finish_kernel(
-    group,
     coarse,
     keep,
     got,
@@ -199,7 +198,7 @@
     part = wide // 2
     mixed = coarse[...].astype(F32)
     back = jnp.zeros((half_rows, wide), F32)
-    for source, index in ((keep, group[0]), (got, 1 - group[0])):
+    for source, index in ((keep, lax.axis_index("grp")), (got, 1 - lax.axis_index("grp"))):
         first = pl.multiple_of(index * part, part)
         mixed = mixed + mm(source[:, :part], output[pl.ds(first, part), :])
         for at in range(3):
@@ -222,7 +221,6 @@
 
 
 def coarse_weights_kernel(
-    parity,
     arrived,
     unit,
     keep,
@@ -234,7 +232,10 @@
     first_half,
     second_half,
     gradient_out,
-):
+    *,
+    strides,
+):
+    chip = lax.axis_index("pts")
     wide = unit.shape[1]
     part = wide // 2
     stacked = jnp.concatenate([keep[...], give[...]], axis=0)
@@ -250,7 +251,7 @@
         for at, passed in enumerate((first_half, second_half)):
             low = terms[:, 2 * at * width : (2 * at + 1) * width]
             high = terms[:, (2 * at + 1) * width : (2 * at + 2) * width]
-            upper = parity[at] == 1
+            upper = chip // strides[at] % 2 == 1
             put_blocks(kept, side, at * width, jnp.where(upper, high, low))
             put_blocks(passed, side, 0, jnp.where(upper, low, high))
     gradient_out[...] = gradient[...]
@@ -287,7 +288,7 @@
 
 
 def sums_kernel(
-    group, own, other, fine_projection, fine_output, pool, projection, output, *, scaling
+    own, other, fine_projection, fine_output, pool, projection, output, *, scaling
 ):
     features = fine_output.shape[0]
     wide = pool.shape[0]
@@ -295,7 +296,7 @@
     width = wide // 4
     across = 3 * part // 2
 
-    owns_low = group[0] == 0
+    owns_low = lax.axis_index("grp") == 0
 
     def lanes(side, start, count):
         here, there = own[:, :, start : start + count], other[:, :, start : start + count]
@@ -390,7 +391,7 @@
         put_blocks(send, side, features, jnp.concatenate(terms[2 * side : 2 * side + 2], axis=0))
 
 def assemble_kernel(
-    group, fine, kept, got_first, got_second, own_pack, other_pack, own_gradient, other_gradient, send
+    fine, kept, got_first, got_second, own_pack, other_pack, own_gradient, other_gradient, send
 ):
     start, width = fine.shape[3], got_first.shape[3]
     send[:, :, :, :start] = fine[...]
@@ -399,7 +400,7 @@
         send[:, :, :, start : start + width] = (mine + got[...].astype(F32)).astype(BF)
         start += width
     part = own_gradient.shape[1] // 2
-    first = pl.multiple_of(group[0] * part, part)
+    first = pl.multiple_of(lax.axis_index("grp") * part, part)
     pool_term = mm(own_pack[:, pl.ds(first, part)], own_gradient[...], (0, 0))
     pool_term = pool_term + mm(other_pack[:, pl.ds(first, part)], other_gradient[...], (0, 0))
     put_quarters(send, start, pool_term)
@@ -412,7 +413,6 @@
 
 
 VMEM = pl.BlockSpec(memory_space=pltpu.VMEM)
-SMEM = pl.BlockSpec(memory_space=pltpu.SMEM)
 HBM = pl.BlockSpec(memory_space=pltpu.HBM)
 
 
@@ -459,11 +459,11 @@
             self.started = True
 
 
-def call(kernel, inputs, outputs, scalar=False, scratch=(), mebibytes=16):
+def call(kernel, inputs, outputs, scratch=(), mebibytes=16):
     in_specs, arrays, buffers = [], [], []
-    for at, value in enumerate(inputs):
+    for value in inputs:
         far = isinstance(value, Far)
-        in_specs.append(SMEM if scalar and at == 0 else HBM if far else VMEM)
+        in_specs.append(HBM if far else VMEM)
         arrays.append(
             pltpu.with_memory_space_constraint(value.value, pltpu.HBM) if far else value
         )
@@ -537,7 +537,8 @@
     devices = lax.axis_size(("pts", "grp"))
     slots = 2 * count
     scaling = 1.0 / math.sqrt(count * devices)
-    group = lax.axis_index("grp").astype(jnp.int32).reshape(1)
+    owners = lax.axis_size("pts")
+    run, step = owners // 4, owners // 16
     wide = 2 * features
     half_rows = count // 2
 
@@ -561,7 +562,7 @@
     heads = features // HD * (count // BALL)
     send, rotated, projected, mixture, weights = call(
         fine_forward_kernel,
-        (arrived, receive_slot, live, Far(fine_projection), Far(fine_output)),
+        (arrived, receive_slot, live, fine_projection, Far(fine_output)),
         (
             Near((slots, features)),
             Near((count, features)),
@@ -577,20 +578,18 @@
     other_pack = exchange(own_pack)
     coarse, keep, give, unit = call(
         coarse_kernel,
-        (group, own_pack, other_pack, pool_weight, coarse_projection, coarse_output),
+        (own_pack, other_pack, pool_weight, coarse_projection, Far(coarse_output)),
         (
             Near((half_rows, wide)),
             Near((half_rows, 2 * wide)),
             Near((half_rows, 2 * wide)),
             Near((count, wide)),
         ),
-        scalar=True,
     )
     got = exchange(give)
     coarse_result, coarse_gradient, send = call(
         coarse_finish_kernel,
         (
-            group,
             coarse,
             keep,
             got,
@@ -605,24 +604,18 @@
             Near((half_rows, wide)),
             Near((slots, features)),
         ),
-        scalar=True,
     )
     arrived = route(send, devices)
-    owners = lax.axis_size("pts")
-    run, step = owners // 4, owners // 16
-    place = lax.axis_index("pts").astype(jnp.int32)
-    parity = jnp.stack([place // run % 2, place // step % 2])
     blocks = (owners, 2, slots // devices)
     kept, first_half, second_half, own_gradient = call(
-        coarse_weights_kernel,
-        (parity, arrived, unit, keep, give, own_pack, other_pack, coarse_gradient),
+        functools.partial(coarse_weights_kernel, strides=(run, step)),
+        (arrived, unit, keep, give, own_pack, other_pack, coarse_gradient),
         (
             Near((*blocks, wide // 2)),
             Near((*blocks, wide // 4)),
             Near((*blocks, wide // 4)),
             Near((half_rows, wide)),
         ),
-        scalar=True,
     )
     got_first = lax.ppermute(first_half, "pts", [(i, i ^ run) for i in range(owners)])
     got_second = lax.ppermute(second_half, "pts", [(i, i ^ step) for i in range(owners)])
@@ -646,7 +639,6 @@
     (send,) = call(
         assemble_kernel,
         (
-            group,
             fine,
             kept,
             got_first,
@@ -657,7 +649,6 @@
             other_gradient,
         ),
         (Near((*blocks, across)),),
-        scalar=True,
     )
     arrived = spread_blocks(send.reshape(devices, slots // devices, across), ("pts", "grp"))
     (spread,) = call(
@@ -672,7 +663,7 @@
     other_sums = exchange(own_sums)
     sums = call(
         functools.partial(sums_kernel, scaling=scaling),
-        (group, own_sums, other_sums),
+        (own_sums, other_sums),
         (
             Near((features, 3 * features), F32, far=True),
             Near((features, features), F32, far=True),
@@ -680,7 +671,6 @@
             Near((wide, 3 * wide), F32, far=True),
             Near((wide, wide), F32, far=True),
         ),
-        scalar=True,
     )
     return (coarse_result, points_gradient, *sums)
 

time: 168 us -> 159 us (0.946)
  blocking collectives: 102 us -> 120 us
  waiting for transfers between devices: 17.7 us -> 4.88 us
  local copies, waits for them, and re-layouts: 8.3 us -> 0.06 us
  starting transfers between devices: 11.9 us -> 8.18 us
    all_to_all x4 -> x5, blocking collectives: 102 us -> 120 us  [spread_blocks(): return lax.all_to_all(values, axes, split_axis=0, concat_axis=0, tiled=True)]
    all_to_all x1 -> x0, waiting for transfers between devices: 13.6 us -> none  [spread_blocks(): return lax.all_to_all(values, axes, split_axis=0, concat_axis=0, tiled=True)]
    unnamed x48 -> x12, local copies, waits for them, and re-layouts: 8.26 us -> 0.03 us
    all_to_all x1 -> x0, starting transfers between devices: 3.8 us -> none  [spread_blocks(): return lax.all_to_all(values, axes, split_axis=0, concat_axis=0, tiled=True)]
  transfers between devices with their start and end apart: 7 -> 6, of which waited for: 4 -> 3; matrix products, arithmetic and copies ran while one was open for 0% -> 0% of each run, Pallas kernels for 4% -> 4%
where the time goes in v9:
time: 159 us
  blocking collectives  120 us (75%)
  Pallas kernels  25.1 us (16%)
  starting transfers between devices  8.18 us (5%)
  waiting for transfers between devices  4.88 us (3%)
    all_to_all x5, blocking collectives, spread_blocks(): return lax.all_to_all(values, axes, split_axis=0, concat_axis=0, tiled=True)  120 us
    pallas_call x11, Pallas kernels, call(): pl.pallas_call(body, out_shape=[(pltpu.HBM if out.far else jax.ShapeDtype...  25.1 us
    ppermute x4, starting transfers between devices, exchange(): return lax.ppermute(values, 'grp', [(0, 1), (1, 0)])  7.48 us
    ppermute x4, waiting for transfers between devices, exchange(): return lax.ppermute(values, 'grp', [(0, 1), (1, 0)])  4.88 us
  transfers between devices with their start and end apart: 6, of which 3 were waited for; matrix products, arithmetic and copies ran while one was open for 0% of the time, Pallas kernels for 4%

profile of v9, /device:TPU:1, one launch (start us, length us, event | category | flops | bytes accessed | tf_op | source)
XLA Modules:
  0.0 158.7 jit_solution(11205444352811951299)
XLA Ops:
  0.6 0.0 copy-start.3
  0.6 2.2 %shard_map.153 = (bf16[1024,256]{1,0:T(8,128)(2,1)S(1)}, s32[1,512]{1,0:T(1,128)S(1)}, s32[1,512]{1,0:T(1,128)S(1)}, s32[1,512]{1,0:T(1,128)S(1)}, f32[1,512]{1,0:T(1,128)S(1)}) custom-call(s32[1,512]{1,0:T(1,128)} %bitcast.20, s32[1,512]{1,0:T(1,128)} %bitcast.21, s32[1,256]{1,0:T(1,128)} %bitcast.22, bf16[512,256]{1,0:T(8,128)(2,1)} %refs_3_.4), custom_call_target="tpu_custom_call" | custom-call | tf_op jit(solution)/shard_map/pallas_call | solution.py:497
  2.8 0.0 copy-start.4
  2.8 25.0 %all_to_all.25 = bf16[128,8,256]{2,1,0:T(8,128)(2,1)S(1)} all-to-all(bf16[128,8,256]{2,1,0:T(8,128)(2,1)S(1)} %bitcast.19), channel_id=1, replica_groups=mesh['pts'=64,'grp'=2] {'pts','grp'}, dimensions={0} | all-to-all | bytes 1048576 | tf_op jit(solution)/shard_map/all_to_all | solution.py:515
  27.8 3.4 %shard_map.154 = (bf16[1024,256]{1,0:T(8,128)(2,1)S(1)}, bf16[512,256]{1,0:T(8,128)(2,1)S(1)}, bf16[512,768]{1,0:T(8,128)(2,1)S(1)}, bf16[512,256]{1,0:T(8,128)(2,1)S(1)}, bf16[8,256,256]{2,1,0:T(8,128)(2,1)S(1)}) custom-call(bf16[1024,256]{1,0:T(8,128)(2,1)S(1)} %bitcast.16, s32[1,512]{1,0:T(1,128)S(1)} %get-tuple-element.34.refs_1_, ...), custom_call_target="tpu_custom_call" | custom-call | tf_op jit(solution)/shard_map/pallas_call | solution.py:497
  31.3 18.1 %all_to_all.26 = bf16[128,8,256]{2,1,0:T(8,128)(2,1)S(1)} all-to-all(bf16[128,8,256]{2,1,0:T(8,128)(2,1)S(1)} %bitcast.17), channel_id=1, replica_groups=mesh['pts'=64,'grp'=2] {'pts','grp'}, dimensions={0} | all-to-all | bytes 1048576 | tf_op jit(solution)/shard_map/all_to_all | solution.py:515
  49.4 0.5 shard_map.155.refs_0_.refs_4_
  49.9 0.0 copy-start.2
  49.9 1.4 collective-permute-start
  51.3 1.5 collective-permute-done.refs_1_.refs_5_
  52.8 6.4 %shard_map.156 = (bf16[256,512]{1,0:T(8,128)(2,1)S(1)}, bf16[256,1024]{1,0:T(8,128)(2,1)S(1)}, bf16[256,1024]{1,0:T(8,128)(2,1)S(1)}, bf16[512,512]{1,0:T(8,128)(2,1)S(1)}) custom-call(bf16[256,1024]{1,0:T(8,128)(2,1)S(1)} %shard_map.155.refs_0_.refs_4_, bf16[256,1024]{1,0:T(8,128)(2,1)S(1)} %collective-permute-done.refs_1_.refs_5_, ...), custom_call_target="tpu_custom_call" | custom-call | tf_op jit(solution)/shard_map/pallas_call | solution.py:497
  59.3 0.5 collective-permute-start.1
  59.7 1.5 collective-permute-done.1.refs_2_
  61.3 0.0 copy-done.2
  61.3 1.5 shard_map.157
  62.8 17.3 %all_to_all.27 = bf16[128,8,256]{2,1,0:T(8,128)(2,1)S(1)} all-to-all(bf16[128,8,256]{2,1,0:T(8,128)(2,1)S(1)} %bitcast.18), channel_id=1, replica_groups=mesh['pts'=64,'grp'=2] {'pts','grp'}, dimensions={0} | all-to-all | bytes 1048576 | tf_op jit(solution)/shard_map/all_to_all | solution.py:515
  80.1 0.8 shard_map.159
  80.9 0.4 collective-permute-start.2
  81.2 0.3 collective-permute-start.3
  81.6 1.7 %collective-permute-start.4 = (bf16[256,512]{1,0:T(8,128)(2,1)S(1)}, bf16[256,512]{1,0:T(8,128)(2,1)S(1)}, u32[]{:S(2)}, u32[]{:S(2)}) collective-permute-start(bf16[256,512]{1,0:T(8,128)(2,1)S(1)} %get-tuple-element.52.refs_6_), channel_id=1, source_target_pairs={{0,1},{1,0},{2,3},{3,2},{4,5},{5,4},{6,7},{7,6},{8,9},{9,8},{10,11... | collective-permute-start | bytes 786440 | tf_op jit(solution)/shard_map/ppermute | solution.py:511
  83.3 4.9 %shard_map.158.refs_0_ = bf16[64,2,8,512]{3,2,1,0:T(8,128)(2,1)S(1)} custom-call(bf16[1024,256]{1,0:T(8,128)(2,1)S(1)} %bitcast.14, s32[1,512]{1,0:T(1,128)S(1)} %get-tuple-element.34.refs_1_, bf16[512,256]{1,0:T(8,128)(2,1)S(1)} %get-tuple-element.43.refs_2_, bf16[512,768]{1,0:T(8,128)(2,1)S(1)} %get-tuple-element.44.refs_3_, ...), custom_call_target="tpu_custom_call" | custom-call | tf_op jit(solution)/shard_map/pallas_call | solution.py:497
  88.2 0.0 collective-permute-done.2.refs_2_
  88.2 0.0 collective-permute-done.3.refs_3_
  88.3 0.0 collective-permute-done.4.refs_7_
  88.3 0.7 shard_map.160
  88.9 33.9 %all_to_all.28 = bf16[128,8,896]{2,1,0:T(8,128)(2,1)S(1)} all-to-all(bf16[128,8,896]{2,1,0:T(8,128)(2,1)S(1)} %bitcast.12), channel_id=1, replica_groups=mesh['pts'=64,'grp'=2] {'pts','grp'}, dimensions={0} | all-to-all | bytes 3670016 | tf_op jit(solution)/shard_map/all_to_all | solution.py:515
  122.8 0.3 shard_map.162
  123.1 25.3 %all_to_all.29.refs_0_ = bf16[64,8,1536]{2,1,0:T(8,128)(2,1)S(1)} all-to-all(bf16[64,8,1536]{2,1,0:T(8,128)(2,1)S(1)} %shard_map.162), channel_id=1, replica_groups=mesh['pts'=64,'grp'=2] {'pts'}, dimensions={0} | all-to-all | bytes 3145728 | tf_op jit(solution)/shard_map/all_to_all | solution.py:515
  148.4 3.9 %collective-permute-start.5 = (bf16[64,8,1536]{2,1,0:T(8,128)(2,1)S(1)}, bf16[64,8,1536]{2,1,0:T(8,128)(2,1)S(1)}, u32[]{:S(2)}, u32[]{:S(2)}) collective-permute-start(bf16[64,8,1536]{2,1,0:T(8,128)(2,1)S(1)} %all_to_all.29.refs_0_), channel_id=1, source_target_pairs={{0,1},{1,0},{2,3},{3,2},{4,5},{5,4},{6,7},{7,6},{8,9},{9,8},{10,11... | collective-permute-start | bytes 4718600 | tf_op jit(solution)/shard_map/ppermute | solution.py:511
  152.3 1.2 shard_map.161
  153.5 1.8 %collective-permute-done.5.refs_1_ = bf16[64,8,1536]{2,1,0:T(8,128)(2,1)S(1)} collective-permute-done((bf16[64,8,1536]{2,1,0:T(8,128)(2,1)S(1)}, bf16[64,8,1536]{2,1,0:T(8,128)(2,1)S(1)}, u32[]{:S(2)}, u32[]{:S(2)}) %collective-permute-start.5) | collective-permute-done | bytes 1572896 | tf_op jit(solution)/shard_map/ppermute | solution.py:511
  155.3 3.2 %shard_map.163 = (f32[256,768]{1,0:T(8,128)}, f32[256,256]{1,0:T(8,128)}, f32[512,512]{1,0:T(8,128)}, f32[512,1536]{1,0:T(8,128)}, f32[512,512]{1,0:T(8,128)}) custom-call(bf16[64,8,1536]{2,1,0:T(8,128)(2,1)S(1)} %all_to_all.29.refs_0_, bf16[64,8,1536]{2,1,0:T(8,128)(2,1)S(1)} %collective-permute-done.5.refs_1_), custom_call_target="tpu_custom_call" | custom-call | tf_op jit(solution)/shard_map/pallas_call | solution.py:497
  (9 shorter events, 0.0 us)
Async XLA Ops:
  0.6 27.2 %copy-start.3 = (bf16[256,768]{1,0:T(8,128)(2,1)S(1)}, bf16[256,768]{1,0:T(8,128)(2,1)}, u32[]{:S(2)}) copy-start(bf16[256,768]{1,0:T(8,128)(2,1)} %refs_6_.3) | copy-start | bytes 1179652
  2.8 46.5 %copy-start.4 = (bf16[256,512]{1,0:T(8,128)(2,1)S(1)}, bf16[256,512]{1,0:T(8,128)(2,1)}, u32[]{:S(2)}) copy-start(bf16[256,512]{1,0:T(8,128)(2,1)} %refs_3_.7) | copy-start | bytes 786436
  27.8 25.0 %copy-start = (bf16[512,1536]{1,0:T(8,128)(2,1)S(1)}, bf16[512,1536]{1,0:T(8,128)(2,1)}, u32[]{:S(2)}) copy-start(bf16[512,1536]{1,0:T(8,128)(2,1)} %refs_5_.1) | copy-start | bytes 4718596
  27.8 25.0 %copy-start.1 = (bf16[512,512]{1,0:T(8,128)(2,1)S(1)}, bf16[512,512]{1,0:T(8,128)(2,1)}, u32[]{:S(2)}) copy-start(bf16[512,512]{1,0:T(8,128)(2,1)} %refs_4_.5) | copy-start | bytes 1572868
  49.9 11.4 %copy-start.2 = (bf16[512,512]{1,0:T(8,128)(2,1)S(1)}, bf16[512,512]{1,0:T(8,128)(2,1)}, u32[]{:S(2)}) copy-start(bf16[512,512]{1,0:T(8,128)(2,1)} %refs_6_.2) | copy-start | bytes 1572868
  49.9 2.9 %collective-permute-start = (bf16[256,1024]{1,0:T(8,128)(2,1)S(1)}, bf16[256,1024]{1,0:T(8,128)(2,1)S(1)}, u32[]{:S(2)}, u32[]{:S(2)}) collective-permute-start(bf16[256,1024]{1,0:T(8,128)(2,1)S(1)} %shard_map.155.refs_0_.refs_4_), channel_id=1, source_target_pairs={{0,1},{1,0},{2,3},{3,2},{4,5},{5,4},{6,7},{7,6},{8,9},{9,8},{10,11... | collective-permute-start | bytes 1572872 | tf_op jit(solution)/shard_map/ppermute | solution.py:511
  59.3 2.0 %collective-permute-start.1 = (bf16[256,1024]{1,0:T(8,128)(2,1)S(1)}, bf16[256,1024]{1,0:T(8,128)(2,1)S(1)}, u32[]{:S(2)}, u32[]{:S(2)}) collective-permute-start(bf16[256,1024]{1,0:T(8,128)(2,1)S(1)} %get-tuple-element.40.refs_3_), channel_id=1, source_target_pairs={{0,1},{1,0},{2,3},{3,2},{4,5},{5,4},{6,7},{7,6},{8,9},{9,8},{10,11... | collective-permute-start | bytes 1572872 | tf_op jit(solution)/shard_map/ppermute | solution.py:511
  80.1 3.2 %copy-start.5 = (bf16[256,256]{1,0:T(8,128)(2,1)S(1)}, bf16[256,256]{1,0:T(8,128)(2,1)}, u32[]{:S(2)}) copy-start(bf16[256,256]{1,0:T(8,128)(2,1)} %refs_7_.1) | copy-start | bytes 393220
  80.9 7.4 %collective-permute-start.2 = (bf16[64,2,8,128]{3,2,1,0:T(8,128)(2,1)S(1)}, bf16[64,2,8,128]{3,2,1,0:T(8,128)(2,1)S(1)}, u32[]{:S(2)}, u32[]{:S(2)}) collective-permute-start(bf16[64,2,8,128]{3,2,1,0:T(8,128)(2,1)S(1)} %get-tuple-element.50), channel_id=1, source_target_pairs={{0,32},{2,34},{4,36},{6,38},{8,40},{10,42},{12,44},{14,46},{16,48}... | collective-permute-start | bytes 786440 | tf_op jit(solution)/shard_map/ppermute | solution.py:620
  81.2 7.0 %collective-permute-start.3 = (bf16[64,2,8,128]{3,2,1,0:T(8,128)(2,1)S(1)}, bf16[64,2,8,128]{3,2,1,0:T(8,128)(2,1)S(1)}, u32[]{:S(2)}, u32[]{:S(2)}) collective-permute-start(bf16[64,2,8,128]{3,2,1,0:T(8,128)(2,1)S(1)} %get-tuple-element.51), channel_id=1, source_target_pairs={{0,8},{2,10},{4,12},{6,14},{8,0},{10,2},{12,4},{14,6},{16,24},{18,... | collective-permute-start | bytes 786440 | tf_op jit(solution)/shard_map/ppermute | solution.py:621
  81.6 6.7 %collective-permute-start.4 = (bf16[256,512]{1,0:T(8,128)(2,1)S(1)}, bf16[256,512]{1,0:T(8,128)(2,1)S(1)}, u32[]{:S(2)}, u32[]{:S(2)}) collective-permute-start(bf16[256,512]{1,0:T(8,128)(2,1)S(1)} %get-tuple-element.52.refs_6_), channel_id=1, source_target_pairs={{0,1},{1,0},{2,3},{3,2},{4,5},{5,4},{6,7},{7,6},{8,9},{9,8},{10,11... | collective-permute-start | bytes 786440 | tf_op jit(solution)/shard_map/ppermute | solution.py:511
  148.4 6.9 %collective-permute-start.5 = (bf16[64,8,1536]{2,1,0:T(8,128)(2,1)S(1)}, bf16[64,8,1536]{2,1,0:T(8,128)(2,1)S(1)}, u32[]{:S(2)}, u32[]{:S(2)}) collective-permute-start(bf16[64,8,1536]{2,1,0:T(8,128)(2,1)S(1)} %all_to_all.29.refs_0_), channel_id=1, source_target_pairs={{0,1},{1,0},{2,3},{3,2},{4,5},{5,4},{6,7},{7,6},{8,9},{9,8},{10,11... | collective-permute-start | bytes 4718600 | tf_op jit(solution)/shard_map/ppermute | solution.py:511

commit v10 on v9

--- a/solution.py
+++ b/solution.py
@@ -63,6 +63,10 @@
 
 def scaled_half(rows, half):
     return keep_half(rows * jnp.asarray(HD ** (-0.5), BF), half)
+
+
+def turned(rows):
+    return rows.astype(F32).T.astype(BF)
 
 
 def column_of(row):
@@ -160,25 +164,34 @@
     values = mm(unit_rows, projection[:, pl.ds(2 * wide + first, part)]).astype(BF)
     cotangent = jnp.concatenate([own_pack[:, wide:], other_pack[:, wide:]], axis=0)
     incoming = mm(cotangent, output[pl.ds(first, part), :], (1, 1)).astype(BF)
+    queries_turned, incoming_turned = turned(queries), turned(incoming)
+    key_parts, value_parts = [], []
+
+    def put(at, rows):
+        target = slice(at, at + rows.shape[1])
+        keep[:, target] = rows[:half_rows]
+        give[:, target] = rows[half_rows:]
+
     for pair in range(part // PAIR):
         lanes = slice(pair * PAIR, (pair + 1) * PAIR)
         query, key, value = queries[:, lanes], keys[:, lanes], values[:, lanes]
         entering = incoming[:, lanes]
-        parts = ([], [], [], [])
+        parts = ([], [])
         for half in range(2):
+            band = slice(pair * PAIR + half * HD, pair * PAIR + (half + 1) * HD)
             scores = mm(scaled_half(query, half), key, (1, 1))
             head_weights = softmax_rows(scores)
             parts[0].append(mm(head_weights, value))
             against = mm(keep_half(entering, half), value, (1, 1))
             slopes = slopes_of(head_weights, against)
             parts[1].append(mm(slopes, key) * HD ** (-0.5))
-            parts[2].append(mm(slopes, query, (0, 0)) * HD ** (-0.5))
-            parts[3].append(mm(head_weights, entering, (0, 0)))
+            key_parts.append(mm(queries_turned[band], slopes) * HD ** (-0.5))
+            value_parts.append(mm(incoming_turned[band], head_weights))
         for at, (low, high) in enumerate(parts):
             both = jnp.where(head_half(low.shape, 0), low, high).astype(BF)
-            target = slice(at * part + pair * PAIR, at * part + (pair + 1) * PAIR)
-            keep[:, target] = both[:half_rows]
-            give[:, target] = both[half_rows:]
+            put(at * part + pair * PAIR, both)
+    put(2 * part, jnp.concatenate(key_parts, axis=0).T.astype(BF))
+    put(3 * part, jnp.concatenate(value_parts, axis=0).T.astype(BF))
 
 
 def coarse_finish_kernel(
@@ -221,19 +234,7 @@
 
 
 def coarse_weights_kernel(
-    arrived,
-    unit,
-    keep,
-    give,
-    own_pack,
-    other_pack,
-    gradient,
-    kept,
-    first_half,
-    second_half,
-    gradient_out,
-    *,
-    strides,
+    unit, keep, give, own_pack, other_pack, kept, first_half, second_half, *, strides
 ):
     chip = lax.axis_index("pts")
     wide = unit.shape[1]
@@ -254,7 +255,6 @@
             upper = chip // strides[at] % 2 == 1
             put_blocks(kept, side, at * width, jnp.where(upper, high, low))
             put_blocks(passed, side, 0, jnp.where(upper, low, high))
-    gradient_out[...] = gradient[...]
 
 
 def put_quarters(blocks, lane, term):
@@ -270,19 +270,21 @@
     blocks[:, side, :, lane : lane + width] = pieces.astype(BF)
 
 
-def sum_kernel(arrived, spread, *, tokens, fine, run, step):
+def sum_kernel(arrived, spread, *, tokens, run, step):
     senders, _, rows, across = arrived.shape
-    start = tokens + fine
-    width = (across - start) // 3
-    fine_part = jnp.sum(arrived[:, :, :, tokens:start].astype(F32), axis=0)
-    total = [fine_part[0] + fine_part[1]]
+    width = (across - tokens) // 4
+
+    def pieces(side, at):
+        start = tokens + at * width
+        return arrived[:, side, :, start : start + width].astype(F32)
+
+    total = [jnp.sum(pieces(side, 0), axis=0) for side in range(2)]
     for side in range(2):
         for at, block in enumerate((run, step)):
-            values = arrived[:, side, :, start + at * width : start + (at + 1) * width]
-            split = values.astype(F32).reshape(senders // (2 * block), 2, block, rows, width)
+            split = pieces(side, 1 + at).reshape(senders // (2 * block), 2, block, rows, width)
             halves = jnp.sum(jnp.sum(split, axis=2), axis=0)
             total.extend([halves[0], halves[1]])
-        total.append(jnp.sum(arrived[:, side, :, start + 2 * width :].astype(F32), axis=0))
+        total.append(jnp.sum(pieces(side, 3), axis=0))
     total = jnp.concatenate(total, axis=1).astype(BF)
     spread[...] = jnp.broadcast_to(total[None], spread.shape)
 
@@ -328,14 +330,15 @@
                     ]
         ref.flush()
     for side in range(2):
-        fine = lanes(side, 0, features)
-        for k in range(2):
-            at = 2 * side + k
-            block = fine[k * features : (k + 1) * features]
-            if at < 3:
-                fine_projection[:, at * features : (at + 1) * features] = block
-            else:
-                fine_output[...] = block
+        for heads in range(2):
+            block = lanes(side, heads * width, width)
+            for k in range(2):
+                column = (2 * heads + side) * features + k * width
+                piece = block[k * features : (k + 1) * features]
+                if column < 3 * features:
+                    fine_projection[:, column : column + width] = piece
+                else:
+                    fine_output[:, column - 3 * features : column - 3 * features + width] = piece
 
 
 def fine_backward_kernel(
@@ -347,63 +350,79 @@
     weights,
     projection,
     output,
-    send,
+    tokens,
+    kept,
+    passed,
     grad_projected,
 ):
     place = one_hot(receive_slot[...], arrived.shape[0])
-    gradient_in = mm(place, arrived[...], (0, 0))
-    gradient_rows = gradient_in.astype(BF)
+    gradient_rows = mm(place, arrived[...], (0, 0)).astype(BF)
     features = rotated.shape[1]
     entering = mm(gradient_rows, output[...], (1, 1)).astype(BF)
     terms = [mm(mixture[...], gradient_rows, (0, 0))]
     balls = rotated.shape[0] // BALL
     pairs = features // PAIR
+    query_turned, entering_turned = turned(projected[:, :features]), turned(entering)
+    turned_parts = ([], [])
     for ball in range(balls):
         rows = slice(ball * BALL, (ball + 1) * BALL)
+        pieces = ([], [])
         for pair in range(pairs):
             lanes = slice(pair * PAIR, (pair + 1) * PAIR)
-            query = projected[rows, lanes]
             key = projected[rows, features + pair * PAIR : features + (pair + 1) * PAIR]
             value = projected[rows, 2 * features + pair * PAIR : 2 * features + (pair + 1) * PAIR]
-            enters = entering[rows, lanes]
-            parts = ([], [], [])
+            query_parts = []
             for half in range(2):
+                band = slice(pair * PAIR + half * HD, pair * PAIR + (half + 1) * HD)
                 head_weights = weights[(ball * pairs + pair) * 2 + half]
-                against = mm(keep_half(enters, half), value, (1, 1))
+                against = mm(keep_half(entering[rows, lanes], half), value, (1, 1))
                 slopes = slopes_of(head_weights, against)
-                parts[0].append(mm(slopes, key) * HD ** (-0.5))
-                parts[1].append(mm(slopes, query, (0, 0)) * HD ** (-0.5))
-                parts[2].append(mm(head_weights, enters, (0, 0)))
-            for at, (low, high) in enumerate(parts):
-                both = jnp.where(head_half(low.shape, 0), low, high).astype(BF)
-                target = at * features + pair * PAIR
-                grad_projected[rows, target : target + PAIR] = both
+                query_parts.append(mm(slopes, key) * HD ** (-0.5))
+                pieces[0].append(mm(query_turned[band, rows], slopes) * HD ** (-0.5))
+                pieces[1].append(mm(entering_turned[band, rows], head_weights))
+            low, high = query_parts
+            both = jnp.where(head_half(low.shape, 0), low, high).astype(BF)
+            grad_projected[rows, lanes] = both
+        for at in range(2):
+            turned_parts[at].append(jnp.concatenate(pieces[at], axis=0))
+    for at in range(2):
+        whole = jnp.concatenate(turned_parts[at], axis=1).T.astype(BF)
+        grad_projected[:, (at + 1) * features : (at + 2) * features] = whole
     normed, inverse = normalize(rotated[...])
     unit_rows = normed.astype(BF)
     for at in range(3):
         columns = slice(at * features, (at + 1) * features)
         terms.insert(at, mm(unit_rows, grad_projected[:, columns], (0, 0)))
+    low = jnp.concatenate(terms[:2], axis=1)
+    high = jnp.concatenate(terms[2:], axis=1)
+    upper = lax.axis_index("grp") == 1
+    kept[...] = jnp.where(upper, high, low)
+    passed[...] = jnp.where(upper, low, high).astype(BF)
     back = mm(grad_projected[...], projection[...], (1, 1))
-    result = (gradient_in + norm_backward(back, normed, inverse)).astype(BF)
-    tokens = mm(place, result)
-    send[:, :, :, :features] = tokens.reshape(send.shape[:3] + (features,)).astype(BF)
-    for side in range(2):
-        put_blocks(send, side, features, jnp.concatenate(terms[2 * side : 2 * side + 2], axis=0))
-
-def assemble_kernel(
-    fine, kept, got_first, got_second, own_pack, other_pack, own_gradient, other_gradient, send
-):
-    start, width = fine.shape[3], got_first.shape[3]
-    send[:, :, :, :start] = fine[...]
+    result = gradient_rows.astype(F32) + norm_backward(back, normed, inverse)
+    tokens[...] = mm(place, result.astype(BF)).reshape(tokens.shape).astype(BF)
+
+
+def coarse_part_kernel(
+    kept, got_first, got_second, own_pack, other_pack, own_gradient, other_gradient, coarse
+):
+    width = got_first.shape[3]
     for at, got in enumerate((got_first, got_second)):
-        mine = kept[:, :, :, at * width : (at + 1) * width].astype(F32)
-        send[:, :, :, start : start + width] = (mine + got[...].astype(F32)).astype(BF)
-        start += width
+        lanes = slice(at * width, (at + 1) * width)
+        mine = kept[:, :, :, lanes].astype(F32)
+        coarse[:, :, :, lanes] = (mine + got[...].astype(F32)).astype(BF)
     part = own_gradient.shape[1] // 2
     first = pl.multiple_of(lax.axis_index("grp") * part, part)
     pool_term = mm(own_pack[:, pl.ds(first, part)], own_gradient[...], (0, 0))
     pool_term = pool_term + mm(other_pack[:, pl.ds(first, part)], other_gradient[...], (0, 0))
-    put_quarters(send, start, pool_term)
+    put_quarters(coarse, 2 * width, pool_term)
+
+
+def assemble_kernel(tokens, fine_kept, fine_got, coarse, send):
+    start = tokens.shape[3]
+    send[:, :, :, :start] = tokens[...]
+    put_quarters(send, start, fine_kept[...] + fine_got[...].astype(F32))
+    send[:, :, :, send.shape[3] - coarse.shape[3] :] = coarse[...]
 
 
 def take_kernel(arrived, slots, rows_out):
@@ -587,6 +606,19 @@
         ),
     )
     got = exchange(give)
+    blocks = (owners, 2, slots // devices)
+    kept, first_half, second_half = call(
+        functools.partial(coarse_weights_kernel, strides=(run, step)),
+        (unit, keep, give, own_pack, other_pack),
+        (
+            Near((*blocks, wide // 2)),
+            Near((*blocks, wide // 4)),
+            Near((*blocks, wide // 4)),
+        ),
+    )
+    got, kept, first_half, second_half = lax.optimization_barrier(
+        (got, kept, first_half, second_half)
+    )
     coarse_result, coarse_gradient, send = call(
         coarse_finish_kernel,
         (
@@ -606,21 +638,13 @@
         ),
     )
     arrived = route(send, devices)
-    blocks = (owners, 2, slots // devices)
-    kept, first_half, second_half, own_gradient = call(
-        functools.partial(coarse_weights_kernel, strides=(run, step)),
-        (arrived, unit, keep, give, own_pack, other_pack, coarse_gradient),
-        (
-            Near((*blocks, wide // 2)),
-            Near((*blocks, wide // 4)),
-            Near((*blocks, wide // 4)),
-            Near((half_rows, wide)),
-        ),
+    arrived, first_half, second_half, coarse_gradient = lax.optimization_barrier(
+        (arrived, first_half, second_half, coarse_gradient)
     )
     got_first = lax.ppermute(first_half, "pts", [(i, i ^ run) for i in range(owners)])
     got_second = lax.ppermute(second_half, "pts", [(i, i ^ step) for i in range(owners)])
-    other_gradient = exchange(own_gradient)
-    (fine,) = call(
+    other_gradient = exchange(coarse_gradient)
+    tokens, fine_kept, fine_passed = call(
         fine_backward_kernel,
         (
             arrived,
@@ -632,27 +656,36 @@
             fine_projection,
             fine_output,
         ),
-        (Near((*blocks, 2 * features)),),
+        (
+            Near((*blocks, features)),
+            Near((features, 2 * features), F32),
+            Near((features, 2 * features)),
+        ),
         scratch=(pltpu.VMEM((count, 3 * features), BF),),
     )
-    across = 2 * features + 3 * wide // 4
-    (send,) = call(
-        assemble_kernel,
-        (
-            fine,
+    fine_got = exchange(fine_passed)
+    (coarse_part,) = call(
+        coarse_part_kernel,
+        (
             kept,
             got_first,
             got_second,
             own_pack,
             other_pack,
-            own_gradient,
+            coarse_gradient,
             other_gradient,
         ),
+        (Near((*blocks, 3 * wide // 4)),),
+    )
+    across = features + wide
+    (send,) = call(
+        assemble_kernel,
+        (tokens, fine_kept, fine_got, coarse_part),
         (Near((*blocks, across)),),
     )
     arrived = spread_blocks(send.reshape(devices, slots // devices, across), ("pts", "grp"))
     (spread,) = call(
-        functools.partial(sum_kernel, tokens=features, fine=features, run=run, step=step),
+        functools.partial(sum_kernel, tokens=features, run=run, step=step),
         (arrived.reshape(send.shape),),
         (Near((owners, slots // devices, features + 5 * wide // 2)),),
     )

time: 159 us -> 155 us (0.975)
  blocking collectives: 120 us -> 116 us
    all_to_all x5, blocking collectives: 120 us -> 116 us  [spread_blocks(): return lax.all_to_all(values, axes, split_axis=0, concat_axis=0, tiled=True)]
    pallas_call x11 -> x12, Pallas kernels: 25.1 us -> 24.6 us  [call(): pl.pallas_call(body, out_shape=[(pltpu.HBM if out.far else jax.ShapeDtype...]
    ppermute x4 -> x5, waiting for transfers between devices: 4.88 us -> 5.01 us  [exchange(): return lax.ppermute(values, 'grp', [(0, 1), (1, 0)])]
    ppermute x4 -> x5, starting transfers between devices: 7.48 us -> 7.58 us  [exchange(): return lax.ppermute(values, 'grp', [(0, 1), (1, 0)])]
  transfers between devices with their start and end apart: 6 -> 7, of which waited for: 3 -> 4; matrix products, arithmetic and copies ran while one was open for 0% -> 0% of each run, Pallas kernels for 4% -> 5%
where the time goes in v10:
time: 155 us
  blocking collectives  116 us (75%)
  Pallas kernels  24.6 us (16%)
  starting transfers between devices  8.21 us (5%)
  waiting for transfers between devices  5.02 us (3%)
    all_to_all x5, blocking collectives, spread_blocks(): return lax.all_to_all(values, axes, split_axis=0, concat_axis=0, tiled=True)  116 us
    pallas_call x12, Pallas kernels, call(): pl.pallas_call(body, out_shape=[(pltpu.HBM if out.far else jax.ShapeDtype...  24.6 us
    ppermute x5, starting transfers between devices, exchange(): return lax.ppermute(values, 'grp', [(0, 1), (1, 0)])  7.58 us
    ppermute x5, waiting for transfers between devices, exchange(): return lax.ppermute(values, 'grp', [(0, 1), (1, 0)])  5.01 us
  transfers between devices with their start and end apart: 7, of which 4 were waited for; matrix products, arithmetic and copies ran while one was open for 0% of the time, Pallas kernels for 5%

profile of v10, /device:TPU:1, one launch (start us, length us, event | category | flops | bytes accessed | tf_op | source)
XLA Modules:
  0.0 154.5 jit_solution(15500115809010252625)
XLA Ops:
  0.6 2.2 %shard_map.153 = (bf16[1024,256]{1,0:T(8,128)(2,1)S(1)}, s32[1,512]{1,0:T(1,128)S(1)}, s32[1,512]{1,0:T(1,128)S(1)}, s32[1,512]{1,0:T(1,128)S(1)}, f32[1,512]{1,0:T(1,128)S(1)}) custom-call(s32[1,512]{1,0:T(1,128)} %bitcast.19, s32[1,512]{1,0:T(1,128)} %bitcast.20, s32[1,256]{1,0:T(1,128)} %bitcast.21, bf16[512,256]{1,0:T(8,128)(2,1)} %refs_3_.4), custom_call_target="tpu_custom_call" | custom-call | tf_op jit(solution)/shard_map/pallas_call | solution.py:516
  2.8 0.0 copy-start.4
  2.8 25.0 %all_to_all.25 = bf16[128,8,256]{2,1,0:T(8,128)(2,1)S(1)} all-to-all(bf16[128,8,256]{2,1,0:T(8,128)(2,1)S(1)} %bitcast.18), channel_id=1, replica_groups=mesh['pts'=64,'grp'=2] {'pts','grp'}, dimensions={0} | all-to-all | bytes 1048576 | tf_op jit(solution)/shard_map/all_to_all | solution.py:534
  27.8 3.4 %shard_map.154 = (bf16[1024,256]{1,0:T(8,128)(2,1)S(1)}, bf16[512,256]{1,0:T(8,128)(2,1)S(1)}, bf16[512,768]{1,0:T(8,128)(2,1)S(1)}, bf16[512,256]{1,0:T(8,128)(2,1)S(1)}, bf16[8,256,256]{2,1,0:T(8,128)(2,1)S(1)}) custom-call(bf16[1024,256]{1,0:T(8,128)(2,1)S(1)} %bitcast.14, s32[1,512]{1,0:T(1,128)S(1)} %get-tuple-element.44.refs_1_, ...), custom_call_target="tpu_custom_call" | custom-call | tf_op jit(solution)/shard_map/pallas_call | solution.py:516
  31.3 18.1 %all_to_all.26 = bf16[128,8,256]{2,1,0:T(8,128)(2,1)S(1)} all-to-all(bf16[128,8,256]{2,1,0:T(8,128)(2,1)S(1)} %bitcast.16), channel_id=1, replica_groups=mesh['pts'=64,'grp'=2] {'pts','grp'}, dimensions={0} | all-to-all | bytes 1048576 | tf_op jit(solution)/shard_map/all_to_all | solution.py:534
  49.4 0.5 shard_map.155.refs_0_.refs_3_
  49.9 1.2 collective-permute-start
  51.1 1.5 collective-permute-done.refs_1_.refs_4_
  52.6 5.9 %shard_map.156 = (bf16[256,512]{1,0:T(8,128)(2,1)S(1)}, bf16[256,1024]{1,0:T(8,128)(2,1)S(1)}, bf16[256,1024]{1,0:T(8,128)(2,1)S(1)}, bf16[512,512]{1,0:T(8,128)(2,1)S(1)}) custom-call(bf16[256,1024]{1,0:T(8,128)(2,1)S(1)} %shard_map.155.refs_0_.refs_3_, bf16[256,1024]{1,0:T(8,128)(2,1)S(1)} %collective-permute-done.refs_1_.refs_4_, ...), custom_call_target="tpu_custom_call" | custom-call | tf_op jit(solution)/shard_map/pallas_call | solution.py:516
  58.5 0.0 copy-start.2
  58.5 0.6 collective-permute-start.1
  59.2 0.8 shard_map.157
  59.9 0.8 collective-permute-done.1.refs_2_
  60.7 1.5 shard_map.158
  62.2 17.3 %all_to_all.27 = bf16[128,8,256]{2,1,0:T(8,128)(2,1)S(1)} all-to-all(bf16[128,8,256]{2,1,0:T(8,128)(2,1)S(1)} %bitcast.17), channel_id=1, replica_groups=mesh['pts'=64,'grp'=2] {'pts','grp'}, dimensions={0} | all-to-all | bytes 1048576 | tf_op jit(solution)/shard_map/all_to_all | solution.py:534
  79.5 0.3 collective-permute-start.3
  79.8 0.3 collective-permute-start.4
  80.2 1.7 %collective-permute-start.5 = (bf16[256,512]{1,0:T(8,128)(2,1)S(1)}, bf16[256,512]{1,0:T(8,128)(2,1)S(1)}, u32[]{:S(2)}, u32[]{:S(2)}) collective-permute-start(bf16[256,512]{1,0:T(8,128)(2,1)S(1)} %get-tuple-element.72.refs_5_), channel_id=1, source_target_pairs={{0,1},{1,0},{2,3},{3,2},{4,5},{5,4},{6,7},{7,6},{8,9},{9,8},{10,11... | collective-permute-start | bytes 786440 | tf_op jit(solution)/shard_map/ppermute | solution.py:530
  81.9 5.0 %shard_map.159 = (bf16[64,2,8,256]{3,2,1,0:T(8,128)(2,1)S(1)}, f32[256,512]{1,0:T(8,128)S(1)}, bf16[256,512]{1,0:T(8,128)(2,1)S(1)}) custom-call(bf16[1024,256]{1,0:T(8,128)(2,1)S(1)} %bitcast.15, s32[1,512]{1,0:T(1,128)S(1)} %get-tuple-element.44.refs_1_, bf16[512,256]{1,0:T(8,128)(2,1)S(1)} %get-tuple-element.62.refs_2_, ...), custom_call_target="tpu_custom_call" | custom-call | tf_op jit(solution)/shard_map/pallas_call | solution.py:516
  86.9 0.1 collective-permute-start.2
  87.0 0.0 collective-permute-done.3.refs_1_
  87.0 0.0 collective-permute-done.4.refs_2_
  87.0 0.6 shard_map.160.refs_3_
  87.6 0.9 collective-permute-done.2.refs_2_
  88.5 0.2 shard_map.161
  88.7 30.0 %all_to_all.28 = bf16[128,8,768]{2,1,0:T(8,128)(2,1)S(1)} all-to-all(bf16[128,8,768]{2,1,0:T(8,128)(2,1)S(1)} %bitcast.12), channel_id=1, replica_groups=mesh['pts'=64,'grp'=2] {'pts','grp'}, dimensions={0} | all-to-all | bytes 3145728 | tf_op jit(solution)/shard_map/all_to_all | solution.py:534
  118.7 0.3 shard_map.163
  119.0 25.3 %all_to_all.29.refs_0_ = bf16[64,8,1536]{2,1,0:T(8,128)(2,1)S(1)} all-to-all(bf16[64,8,1536]{2,1,0:T(8,128)(2,1)S(1)} %shard_map.163), channel_id=1, replica_groups=mesh['pts'=64,'grp'=2] {'pts'}, dimensions={0} | all-to-all | bytes 3145728 | tf_op jit(solution)/shard_map/all_to_all | solution.py:534
  144.3 3.9 %collective-permute-start.6 = (bf16[64,8,1536]{2,1,0:T(8,128)(2,1)S(1)}, bf16[64,8,1536]{2,1,0:T(8,128)(2,1)S(1)}, u32[]{:S(2)}, u32[]{:S(2)}) collective-permute-start(bf16[64,8,1536]{2,1,0:T(8,128)(2,1)S(1)} %all_to_all.29.refs_0_), channel_id=1, source_target_pairs={{0,1},{1,0},{2,3},{3,2},{4,5},{5,4},{6,7},{7,6},{8,9},{9,8},{10,11... | collective-permute-start | bytes 4718600 | tf_op jit(solution)/shard_map/ppermute | solution.py:530
  148.2 1.2 shard_map.162
  149.4 1.8 %collective-permute-done.6.refs_1_ = bf16[64,8,1536]{2,1,0:T(8,128)(2,1)S(1)} collective-permute-done((bf16[64,8,1536]{2,1,0:T(8,128)(2,1)S(1)}, bf16[64,8,1536]{2,1,0:T(8,128)(2,1)S(1)}, u32[]{:S(2)}, u32[]{:S(2)}) %collective-permute-start.6) | collective-permute-done | bytes 1572896 | tf_op jit(solution)/shard_map/ppermute | solution.py:530
  151.2 3.2 %shard_map.164 = (f32[256,768]{1,0:T(8,128)}, f32[256,256]{1,0:T(8,128)}, f32[512,512]{1,0:T(8,128)}, f32[512,1536]{1,0:T(8,128)}, f32[512,512]{1,0:T(8,128)}) custom-call(bf16[64,8,1536]{2,1,0:T(8,128)(2,1)S(1)} %all_to_all.29.refs_0_, bf16[64,8,1536]{2,1,0:T(8,128)(2,1)S(1)} %collective-permute-done.6.refs_1_), custom_call_target="tpu_custom_call" | custom-call | tf_op jit(solution)/shard_map/pallas_call | solution.py:516
  (12 shorter events, 0.1 us)
Async XLA Ops:
  0.6 27.2 %copy-start.3 = (bf16[256,768]{1,0:T(8,128)(2,1)S(1)}, bf16[256,768]{1,0:T(8,128)(2,1)}, u32[]{:S(2)}) copy-start(bf16[256,768]{1,0:T(8,128)(2,1)} %refs_6_.3) | copy-start | bytes 1179652
  2.8 46.5 %copy-start.4 = (bf16[256,512]{1,0:T(8,128)(2,1)S(1)}, bf16[256,512]{1,0:T(8,128)(2,1)}, u32[]{:S(2)}) copy-start(bf16[256,512]{1,0:T(8,128)(2,1)} %refs_3_.7) | copy-start | bytes 786436
  27.8 24.8 %copy-start = (bf16[512,1536]{1,0:T(8,128)(2,1)S(1)}, bf16[512,1536]{1,0:T(8,128)(2,1)}, u32[]{:S(2)}) copy-start(bf16[512,1536]{1,0:T(8,128)(2,1)} %refs_5_.1) | copy-start | bytes 4718596
  27.8 24.8 %copy-start.1 = (bf16[512,512]{1,0:T(8,128)(2,1)S(1)}, bf16[512,512]{1,0:T(8,128)(2,1)}, u32[]{:S(2)}) copy-start(bf16[512,512]{1,0:T(8,128)(2,1)} %refs_4_.5) | copy-start | bytes 1572868
  49.9 2.8 %collective-permute-start = (bf16[256,1024]{1,0:T(8,128)(2,1)S(1)}, bf16[256,1024]{1,0:T(8,128)(2,1)S(1)}, u32[]{:S(2)}, u32[]{:S(2)}) collective-permute-start(bf16[256,1024]{1,0:T(8,128)(2,1)S(1)} %shard_map.155.refs_0_.refs_3_), channel_id=1, source_target_pairs={{0,1},{1,0},{2,3},{3,2},{4,5},{5,4},{6,7},{7,6},{8,9},{9,8},{10,11... | collective-permute-start | bytes 1572872 | tf_op jit(solution)/shard_map/ppermute | solution.py:530
  58.5 2.2 %copy-start.2 = (bf16[512,512]{1,0:T(8,128)(2,1)S(1)}, bf16[512,512]{1,0:T(8,128)(2,1)}, u32[]{:S(2)}) copy-start(bf16[512,512]{1,0:T(8,128)(2,1)} %refs_6_.2) | copy-start | bytes 1572868
  58.5 2.2 %collective-permute-start.1 = (bf16[256,1024]{1,0:T(8,128)(2,1)S(1)}, bf16[256,1024]{1,0:T(8,128)(2,1)S(1)}, u32[]{:S(2)}, u32[]{:S(2)}) collective-permute-start(bf16[256,1024]{1,0:T(8,128)(2,1)S(1)} %get-tuple-element.50.refs_2_), channel_id=1, source_target_pairs={{0,1},{1,0},{2,3},{3,2},{4,5},{5,4},{6,7},{7,6},{8,9},{9,8},{10,11... | collective-permute-start | bytes 1572872 | tf_op jit(solution)/shard_map/ppermute | solution.py:530
  60.7 21.2 %copy-start.5 = (bf16[256,256]{1,0:T(8,128)(2,1)S(1)}, bf16[256,256]{1,0:T(8,128)(2,1)}, u32[]{:S(2)}) copy-start(bf16[256,256]{1,0:T(8,128)(2,1)} %refs_7_.1) | copy-start | bytes 393220
  79.5 7.5 %collective-permute-start.3 = (bf16[64,2,8,128]{3,2,1,0:T(8,128)(2,1)S(1)}, bf16[64,2,8,128]{3,2,1,0:T(8,128)(2,1)S(1)}, u32[]{:S(2)}, u32[]{:S(2)}) collective-permute-start(bf16[64,2,8,128]{3,2,1,0:T(8,128)(2,1)S(1)} %get-tuple-element.70), channel_id=1, source_target_pairs={{0,32},{2,34},{4,36},{6,38},{8,40},{10,42},{12,44},{14,46},{16,48}... | collective-permute-start | bytes 786440 | tf_op jit(solution)/shard_map/ppermute | solution.py:644
  79.8 7.2 %collective-permute-start.4 = (bf16[64,2,8,128]{3,2,1,0:T(8,128)(2,1)S(1)}, bf16[64,2,8,128]{3,2,1,0:T(8,128)(2,1)S(1)}, u32[]{:S(2)}, u32[]{:S(2)}) collective-permute-start(bf16[64,2,8,128]{3,2,1,0:T(8,128)(2,1)S(1)} %get-tuple-element.71), channel_id=1, source_target_pairs={{0,8},{2,10},{4,12},{6,14},{8,0},{10,2},{12,4},{14,6},{16,24},{18,... | collective-permute-start | bytes 786440 | tf_op jit(solution)/shard_map/ppermute | solution.py:645
  80.2 6.9 %collective-permute-start.5 = (bf16[256,512]{1,0:T(8,128)(2,1)S(1)}, bf16[256,512]{1,0:T(8,128)(2,1)S(1)}, u32[]{:S(2)}, u32[]{:S(2)}) collective-permute-start(bf16[256,512]{1,0:T(8,128)(2,1)S(1)} %get-tuple-element.72.refs_5_), channel_id=1, source_target_pairs={{0,1},{1,0},{2,3},{3,2},{4,5},{5,4},{6,7},{7,6},{8,9},{9,8},{10,11... | collective-permute-start | bytes 786440 | tf_op jit(solution)/shard_map/ppermute | solution.py:530
  86.9 1.6 %collective-permute-start.2 = (bf16[256,512]{1,0:T(8,128)(2,1)S(1)}, bf16[256,512]{1,0:T(8,128)(2,1)S(1)}, u32[]{:S(2)}, u32[]{:S(2)}) collective-permute-start(bf16[256,512]{1,0:T(8,128)(2,1)S(1)} %get-tuple-element.68), channel_id=1, source_target_pairs={{0,1},{1,0},{2,3},{3,2},{4,5},{5,4},{6,7},{7,6},{8,9},{9,8},{10,11... | collective-permute-start | bytes 786440 | tf_op jit(solution)/shard_map/ppermute | solution.py:530
  144.3 6.9 %collective-permute-start.6 = (bf16[64,8,1536]{2,1,0:T(8,128)(2,1)S(1)}, bf16[64,8,1536]{2,1,0:T(8,128)(2,1)S(1)}, u32[]{:S(2)}, u32[]{:S(2)}) collective-permute-start(bf16[64,8,1536]{2,1,0:T(8,128)(2,1)S(1)} %all_to_all.29.refs_0_), channel_id=1, source_target_pairs={{0,1},{1,0},{2,3},{3,2},{4,5},{5,4},{6,7},{7,6},{8,9},{9,8},{10,11... | collective-permute-start | bytes 4718600 | tf_op jit(solution)/shard_map/ppermute | solution.py:530

commit v11 on v10

--- a/solution.py
+++ b/solution.py
@@ -63,6 +63,21 @@
 
 def scaled_half(rows, half):
     return keep_half(rows * jnp.asarray(HD ** (-0.5), BF), half)
+
+
+def stack_heads(rows, heads):
+    lanes = lax.broadcasted_iota(jnp.int32, rows.shape, 1) // HD
+    none = jnp.zeros_like(rows)
+    return jnp.concatenate([jnp.where(lanes == at, rows, none) for at in range(heads)], axis=0)
+
+
+def unstack_heads(rows, heads):
+    count = rows.shape[0] // heads
+    merged = rows[:count]
+    lanes = lax.broadcasted_iota(jnp.int32, merged.shape, 1) // HD
+    for at in range(1, heads):
+        merged = jnp.where(lanes == at, rows[at * count : (at + 1) * count], merged)
+    return merged
 
 
 def turned(rows):
@@ -117,23 +132,19 @@
     normed, _ = normalize(rows_in)
     projected[...] = mm(normed.astype(BF), projection[...]).astype(BF)
     balls = rows_in.shape[0] // BALL
-    pairs = features // PAIR
     for ball in range(balls):
         rows = slice(ball * BALL, (ball + 1) * BALL)
         alive = live[:, rows] > 0.5
-        for pair in range(pairs):
+        for pair in range(features // PAIR):
             lanes = slice(pair * PAIR, (pair + 1) * PAIR)
-            query = projected[rows, lanes]
+            query = projected[rows, lanes] * jnp.asarray(HD ** (-0.5), BF)
             key = projected[rows, features + pair * PAIR : features + (pair + 1) * PAIR]
             value = projected[rows, 2 * features + pair * PAIR : 2 * features + (pair + 1) * PAIR]
-            halves = []
-            for half in range(2):
-                scores = mm(scaled_half(query, half), key, (1, 1))
-                head_weights = softmax_rows(jnp.where(alive, scores, -1e30))
-                weights[(ball * pairs + pair) * 2 + half] = head_weights
-                halves.append(mm(head_weights, value))
-            mixed = jnp.where(head_half(halves[0].shape, 0), halves[0], halves[1])
-            mixture[rows, lanes] = mixed.astype(BF)
+            scores = mm(stack_heads(query, 2), key, (1, 1))
+            both = softmax_rows(jnp.where(alive, scores, -1e30))
+            first = (ball * features + pair * PAIR) // HD
+            weights[first : first + 2] = both.reshape(2, BALL, BALL)
+            mixture[rows, lanes] = unstack_heads(mm(both, value), 2).astype(BF)
     result = (rows_in + mm(mixture[...], output[...])).astype(BF)
     send[...] = mm(place, result).astype(BF)
 
@@ -236,7 +247,7 @@
 def coarse_weights_kernel(
     unit, keep, give, own_pack, other_pack, kept, first_half, second_half, *, strides
 ):
-    chip = lax.axis_index("pts")
+    chip, core = lax.axis_index("pts"), lax.axis_index("grp")
     wide = unit.shape[1]
     part = wide // 2
     stacked = jnp.concatenate([keep[...], give[...]], axis=0)
@@ -252,7 +263,7 @@
         for at, passed in enumerate((first_half, second_half)):
             low = terms[:, 2 * at * width : (2 * at + 1) * width]
             high = terms[:, (2 * at + 1) * width : (2 * at + 2) * width]
-            upper = chip // strides[at] % 2 == 1
+            upper = (chip // strides[at] + core) % 2 == 1
             put_blocks(kept, side, at * width, jnp.where(upper, high, low))
             put_blocks(passed, side, 0, jnp.where(upper, low, high))
 
@@ -283,62 +294,133 @@
         for at, block in enumerate((run, step)):
             split = pieces(side, 1 + at).reshape(senders // (2 * block), 2, block, rows, width)
             halves = jnp.sum(jnp.sum(split, axis=2), axis=0)
-            total.extend([halves[0], halves[1]])
+            total.extend([halves[side], halves[1 - side]])
         total.append(jnp.sum(pieces(side, 3), axis=0))
     total = jnp.concatenate(total, axis=1).astype(BF)
     spread[...] = jnp.broadcast_to(total[None], spread.shape)
 
 
-def sums_kernel(
-    own, other, fine_projection, fine_output, pool, projection, output, *, scaling
+def write_half(terms, side, refs, stages, semaphores, scaling):
+    projection, output, pool = refs
+    tall, square = stages
+    wide = pool.shape[0]
+    part, width = wide // 2, wide // 4
+    across = 3 * part // 2
+    copies = []
+
+    def lanes(start, count):
+        values = terms[:, :, start : start + count].astype(F32) * scaling
+        return values.reshape(terms.shape[0] * terms.shape[1], count)
+
+    def send(stage, target):
+        copies.append(pltpu.make_async_copy(stage, target, semaphores.at[len(copies)]))
+        copies[-1].start()
+
+    for heads in range(2):
+        start = 2 * width + heads * (across + 2 * width)
+        for k in range(3):
+            columns = [half * across + k * width for half in range(2)]
+            places = [column // part * wide + heads * part + column % part for column in columns]
+            target = pl.multiple_of(jnp.where(side == 0, places[0], places[1]), width)
+            stage = tall.at[3 * heads + k]
+            stage[...] = lanes(start + k * width, width)
+            send(stage, projection.at[:, pl.ds(target, width)])
+        for at, ref in enumerate((output, pool)):
+            block = lanes(start + across + at * width, width)
+            stage = square.at[2 * heads + at]
+            stage[:, :width] = block[:part]
+            stage[:, width:] = block[part:]
+            target = pl.multiple_of(side * part, part)
+            send(stage, ref.at[heads * part : (heads + 1) * part, pl.ds(target, part)])
+    return copies
+
+
+def own_sums_kernel(own, projection, output, pool, tall, square, semaphores, *, scaling):
+    side = lax.axis_index("grp")
+    refs = (projection, output, pool)
+    for copy in write_half(own, side, refs, (tall, square), semaphores, scaling):
+        copy.wait()
+
+
+def other_sums_kernel(
+    own,
+    other,
+    projection_in,
+    output_in,
+    pool_in,
+    projection,
+    output,
+    pool,
+    fine_projection,
+    fine_output,
+    tall,
+    square,
+    semaphores,
+    fine,
+    fine_square,
+    fine_semaphores,
+    *,
+    scaling,
 ):
+    side = 1 - lax.axis_index("grp")
+    refs = (projection, output, pool)
+    copies = write_half(other, side, refs, (tall, square), semaphores, scaling)
     features = fine_output.shape[0]
-    wide = pool.shape[0]
-    part = wide // 2
-    width = wide // 4
-    across = 3 * part // 2
-
-    owns_low = lax.axis_index("grp") == 0
-
-    def lanes(side, start, count):
-        here, there = own[:, :, start : start + count], other[:, :, start : start + count]
-        low = owns_low if side == 0 else jnp.logical_not(owns_low)
-        values = jnp.where(low, here, there).astype(F32) * scaling
-        return values.reshape(own.shape[0] * own.shape[1], count)
-
-    def start_of(heads):
-        return features + heads * (across + 2 * width)
-
-    for side in range(2):
-        for heads in range(2):
-            for k in range(3):
-                column = side * across + k * width
-                at, inner = column // part, column % part
-                target = at * wide + heads * part + inner
-                projection[:, target : target + width] = lanes(
-                    side, start_of(heads) + k * width, width
-                )
-    projection.flush()
-    for at, ref in enumerate((output, pool)):
-        for side in range(2):
-            for heads in range(2):
-                block = lanes(side, start_of(heads) + across + at * width, width)
-                for k in range(2):
-                    column = (2 * side + k) * width
-                    ref[heads * part : (heads + 1) * part, column : column + width] = block[
-                        k * part : (k + 1) * part
-                    ]
-        ref.flush()
-    for side in range(2):
-        for heads in range(2):
-            block = lanes(side, heads * width, width)
+    width = features // 2
+    for heads in range(2):
+        start = heads * width
+        here, there = own[:, :, start : start + width], other[:, :, start : start + width]
+        for half in range(2):
+            values = jnp.where(side == half, there, here).astype(F32) * scaling
+            block = values.reshape(own.shape[0] * own.shape[1], width)
+            column = (2 * heads + half) * features
             for k in range(2):
-                column = (2 * heads + side) * features + k * width
                 piece = block[k * features : (k + 1) * features]
                 if column < 3 * features:
-                    fine_projection[:, column : column + width] = piece
+                    fine[:, column + k * width : column + (k + 1) * width] = piece
                 else:
-                    fine_output[:, column - 3 * features : column - 3 * features + width] = piece
+                    fine_square[:, k * width : (k + 1) * width] = piece
+    copies.append(pltpu.make_async_copy(fine, fine_projection, fine_semaphores.at[0]))
+    copies.append(pltpu.make_async_copy(fine_square, fine_output, fine_semaphores.at[1]))
+    for copy in copies[-2:]:
+        copy.start()
+    for copy in copies:
+        copy.wait()
+
+
+def write_sums(own, other, features, wide, scaling):
+    part, width = wide // 2, wide // 4
+    shapes = [(wide, 3 * wide), (wide, wide), (wide, wide)]
+    stages = [
+        pltpu.VMEM((6, wide, width), F32),
+        pltpu.VMEM((4, part, part), F32),
+        pltpu.SemaphoreType.DMA((10,)),
+    ]
+    limits = pltpu.CompilerParams(vmem_limit_bytes=16 * 1024 * 1024)
+    firsts = pl.pallas_call(
+        functools.partial(own_sums_kernel, scaling=scaling),
+        out_shape=[pltpu.HBM(shape, F32) for shape in shapes],
+        in_specs=[VMEM],
+        out_specs=[HBM] * 3,
+        scratch_shapes=stages,
+        compiler_params=limits,
+    )(own)
+    shapes += [(features, 3 * features), (features, features)]
+    projection, output, pool, fine_projection, fine_output = pl.pallas_call(
+        functools.partial(other_sums_kernel, scaling=scaling),
+        out_shape=[pltpu.HBM(shape, F32) for shape in shapes],
+        in_specs=[VMEM] * 2 + [HBM] * 3,
+        out_specs=[HBM] * 5,
+        scratch_shapes=stages
+        + [
+            pltpu.VMEM((features, 3 * features), F32),
+            pltpu.VMEM((features, features), F32),
+            pltpu.SemaphoreType.DMA((2,)),
+        ],
+        input_output_aliases={2: 0, 3: 1, 4: 2},
+        compiler_params=limits,
+    )(own, other, *firsts)
+    return fine_projection, fine_output, pool, projection, output
 
 
 def fine_backward_kernel(
@@ -361,28 +443,23 @@
     entering = mm(gradient_rows, output[...], (1, 1)).astype(BF)
     terms = [mm(mixture[...], gradient_rows, (0, 0))]
     balls = rotated.shape[0] // BALL
-    pairs = features // PAIR
+    heads = features // HD
     query_turned, entering_turned = turned(projected[:, :features]), turned(entering)
     turned_parts = ([], [])
     for ball in range(balls):
         rows = slice(ball * BALL, (ball + 1) * BALL)
+        key, value = projected[rows, features : 2 * features], projected[rows, 2 * features :]
+        head_weights = [weights[ball * heads + at] for at in range(heads)]
+        against = mm(stack_heads(entering[rows], heads), value, (1, 1))
+        slopes = slopes_of(jnp.concatenate(head_weights, axis=0), against)
+        query_part = unstack_heads(mm(slopes, key), heads) * HD ** (-0.5)
+        grad_projected[rows, :features] = query_part.astype(BF)
         pieces = ([], [])
-        for pair in range(pairs):
-            lanes = slice(pair * PAIR, (pair + 1) * PAIR)
-            key = projected[rows, features + pair * PAIR : features + (pair + 1) * PAIR]
-            value = projected[rows, 2 * features + pair * PAIR : 2 * features + (pair + 1) * PAIR]
-            query_parts = []
-            for half in range(2):
-                band = slice(pair * PAIR + half * HD, pair * PAIR + (half + 1) * HD)
-                head_weights = weights[(ball * pairs + pair) * 2 + half]
-                against = mm(keep_half(entering[rows, lanes], half), value, (1, 1))
-                slopes = slopes_of(head_weights, against)
-                query_parts.append(mm(slopes, key) * HD ** (-0.5))
-                pieces[0].append(mm(query_turned[band, rows], slopes) * HD ** (-0.5))
-                pieces[1].append(mm(entering_turned[band, rows], head_weights))
-            low, high = query_parts
-            both = jnp.where(head_half(low.shape, 0), low, high).astype(BF)
-            grad_projected[rows, lanes] = both
+        for at in range(heads):
+            band = slice(at * HD, (at + 1) * HD)
+            own = slopes[at * BALL : (at + 1) * BALL]
+            pieces[0].append(mm(query_turned[band, rows], own) * HD ** (-0.5))
+            pieces[1].append(mm(entering_turned[band, rows], head_weights[at]))
         for at in range(2):
             turned_parts[at].append(jnp.concatenate(pieces[at], axis=0))
     for at in range(2):
@@ -532,6 +609,16 @@
 
 def spread_blocks(values, axes):
     return lax.all_to_all(values, axes, split_axis=0, concat_axis=0, tiled=True)
+
+
+def neighbours(owners, stride):
+    pairs = []
+    for chip in range(owners):
+        place = chip // stride % 4
+        for core in range(2):
+            partner = ((place + core ^ 1) - core) % 4
+            pairs.append((2 * chip + core, 2 * (chip + (partner - place) * stride) + core))
+    return pairs
 
 
 def route(values, devices):
@@ -641,8 +728,8 @@
     arrived, first_half, second_half, coarse_gradient = lax.optimization_barrier(
         (arrived, first_half, second_half, coarse_gradient)
     )
-    got_first = lax.ppermute(first_half, "pts", [(i, i ^ run) for i in range(owners)])
-    got_second = lax.ppermute(second_half, "pts", [(i, i ^ step) for i in range(owners)])
+    got_first = lax.ppermute(first_half, ("pts", "grp"), neighbours(owners, run))
+    got_second = lax.ppermute(second_half, ("pts", "grp"), neighbours(owners, step))
     other_gradient = exchange(coarse_gradient)
     tokens, fine_kept, fine_passed = call(
         fine_backward_kernel,
@@ -694,17 +781,7 @@
         take_kernel, (arrived[:, :, :features], send_slot), (Near((count, features)),)
     )
     other_sums = exchange(own_sums)
-    sums = call(
-        functools.partial(sums_kernel, scaling=scaling),
-        (own_sums, other_sums),
-        (
-            Near((features, 3 * features), F32, far=True),
-            Near((features, features), F32, far=True),
-            Near((wide, wide), F32, far=True),
-            Near((wide, 3 * wide), F32, far=True),
-            Near((wide, wide), F32, far=True),
-        ),
-    )
+    sums = write_sums(own_sums, other_sums, features, wide, scaling)
     return (coarse_result, points_gradient, *sums)
 
 

time: 155 us -> 152 us (0.981)
    pallas_call x12 -> x11, Pallas kernels: 24.6 us -> 20.1 us  [call(): pl.pallas_call(body, out_shape=[(pltpu.HBM if out.far else jax.ShapeDtype...]
    pallas_call x0 -> x2, Pallas kernels: none -> 3.53 us  [the longest x1 1.95 us: write_sums(): pl.pallas_call(functools.partial(other_sums_kernel, scaling=scaling), out...]
    ppermute x5, waiting for transfers between devices: 5.01 us -> 2.52 us  [exchange(): return lax.ppermute(values, 'grp', [(0, 1), (1, 0)])]
  transfers between devices with their start and end apart: 7 -> 7, of which waited for: 4 -> 5; matrix products, arithmetic and copies ran while one was open for 0% -> 0% of each run, Pallas kernels for 5% -> 5%
where the time goes in v11:
time: 152 us
  blocking collectives  116 us (76%)
  Pallas kernels  23.7 us (16%)
  starting transfers between devices  8.22 us (5%)
  waiting for transfers between devices  3.62 us (2%)
    all_to_all x5, blocking collectives, spread_blocks(): return lax.all_to_all(values, axes, split_axis=0, concat_axis=0, tiled=True)  116 us
    pallas_call x11, Pallas kernels, call(): pl.pallas_call(body, out_shape=[(pltpu.HBM if out.far else jax.ShapeDtype...  20.1 us
    ppermute x5, starting transfers between devices, exchange(): return lax.ppermute(values, 'grp', [(0, 1), (1, 0)])  6.4 us
  transfers between devices with their start and end apart: 7, of which 5 were waited for; matrix products, arithmetic and copies ran while one was open for 0% of the time, Pallas kernels for 5%

profile of v11, /device:TPU:1, one launch (start us, length us, event | category | flops | bytes accessed | tf_op | source)
XLA Modules:
  0.0 152.1 jit_solution(11787690138430062410)
XLA Ops:
  0.6 2.2 %shard_map.153 = (bf16[1024,256]{1,0:T(8,128)(2,1)S(1)}, s32[1,512]{1,0:T(1,128)S(1)}, s32[1,512]{1,0:T(1,128)S(1)}, s32[1,512]{1,0:T(1,128)S(1)}, f32[1,512]{1,0:T(1,128)S(1)}) custom-call(s32[1,512]{1,0:T(1,128)} %bitcast.19, s32[1,512]{1,0:T(1,128)} %bitcast.20, s32[1,256]{1,0:T(1,128)} %bitcast.21, bf16[512,256]{1,0:T(8,128)(2,1)} %refs_3_.4), custom_call_target="tpu_custom_call" | custom-call | tf_op jit(solution)/shard_map/pallas_call | solution.py:593
  2.8 0.0 copy-start.4
  2.8 25.0 %all_to_all.25 = bf16[128,8,256]{2,1,0:T(8,128)(2,1)S(1)} all-to-all(bf16[128,8,256]{2,1,0:T(8,128)(2,1)S(1)} %bitcast.18), channel_id=1, replica_groups=mesh['pts'=64,'grp'=2] {'pts','grp'}, dimensions={0} | all-to-all | bytes 1048576 | tf_op jit(solution)/shard_map/all_to_all | solution.py:611
  27.8 3.4 %shard_map.154 = (bf16[1024,256]{1,0:T(8,128)(2,1)S(1)}, bf16[512,256]{1,0:T(8,128)(2,1)S(1)}, bf16[512,768]{1,0:T(8,128)(2,1)S(1)}, bf16[512,256]{1,0:T(8,128)(2,1)S(1)}, bf16[8,256,256]{2,1,0:T(8,128)(2,1)S(1)}) custom-call(bf16[1024,256]{1,0:T(8,128)(2,1)S(1)} %bitcast.14, s32[1,512]{1,0:T(1,128)S(1)} %get-tuple-element.47.refs_1_, ...), custom_call_target="tpu_custom_call" | custom-call | tf_op jit(solution)/shard_map/pallas_call | solution.py:593
  31.2 18.1 %all_to_all.26 = bf16[128,8,256]{2,1,0:T(8,128)(2,1)S(1)} all-to-all(bf16[128,8,256]{2,1,0:T(8,128)(2,1)S(1)} %bitcast.16), channel_id=1, replica_groups=mesh['pts'=64,'grp'=2] {'pts','grp'}, dimensions={0} | all-to-all | bytes 1048576 | tf_op jit(solution)/shard_map/all_to_all | solution.py:611
  49.3 0.5 shard_map.155.refs_0_.refs_3_
  49.8 1.2 collective-permute-start
  51.1 1.5 %collective-permute-done.refs_1_.refs_4_ = bf16[256,1024]{1,0:T(8,128)(2,1)S(1)} collective-permute-done((bf16[256,1024]{1,0:T(8,128)(2,1)S(1)}, bf16[256,1024]{1,0:T(8,128)(2,1)S(1)}, u32[]{:S(2)}, u32[]{:S(2)}) %collective-permute-start) | collective-permute-done | bytes 524320 | tf_op jit(solution)/shard_map/ppermute | solution.py:607
  52.6 5.9 %shard_map.156 = (bf16[256,512]{1,0:T(8,128)(2,1)S(1)}, bf16[256,1024]{1,0:T(8,128)(2,1)S(1)}, bf16[256,1024]{1,0:T(8,128)(2,1)S(1)}, bf16[512,512]{1,0:T(8,128)(2,1)S(1)}) custom-call(bf16[256,1024]{1,0:T(8,128)(2,1)S(1)} %shard_map.155.refs_0_.refs_3_, bf16[256,1024]{1,0:T(8,128)(2,1)S(1)} %collective-permute-done.refs_1_.refs_4_, ...), custom_call_target="tpu_custom_call" | custom-call | tf_op jit(solution)/shard_map/pallas_call | solution.py:593
  58.5 0.0 copy-start.2
  58.5 0.6 collective-permute-start.1
  59.1 0.8 shard_map.157
  59.9 0.8 collective-permute-done.1.refs_2_
  60.7 1.5 %shard_map.158 = (bf16[256,512]{1,0:T(8,128)(2,1)}, bf16[256,512]{1,0:T(8,128)(2,1)S(1)}, bf16[1024,256]{1,0:T(8,128)(2,1)S(1)}) custom-call(bf16[256,512]{1,0:T(8,128)(2,1)S(1)} %get-tuple-element.51.refs_0_, bf16[256,1024]{1,0:T(8,128)(2,1)S(1)} %get-tuple-element.52.refs_1_, bf16[256,1024]{1,0:T(8,128)(2,1)S(1)} %collective-permute-done.1.refs_2_, ...), custom_call_target="tpu_custom_call" | custom-call | tf_op jit(solution)/shard_map/pallas_call | solution.py:593
  62.2 17.3 %all_to_all.27 = bf16[128,8,256]{2,1,0:T(8,128)(2,1)S(1)} all-to-all(bf16[128,8,256]{2,1,0:T(8,128)(2,1)S(1)} %bitcast.17), channel_id=1, replica_groups=mesh['pts'=64,'grp'=2] {'pts','grp'}, dimensions={0} | all-to-all | bytes 1048576 | tf_op jit(solution)/shard_map/all_to_all | solution.py:611
  79.5 0.9 collective-permute-start.3
  80.4 1.0 collective-permute-start.4
  81.3 0.5 collective-permute-start.5
  81.9 3.7 %shard_map.159 = (bf16[64,2,8,256]{3,2,1,0:T(8,128)(2,1)S(1)}, f32[256,512]{1,0:T(8,128)S(1)}, bf16[256,512]{1,0:T(8,128)(2,1)S(1)}) custom-call(bf16[1024,256]{1,0:T(8,128)(2,1)S(1)} %bitcast.15, s32[1,512]{1,0:T(1,128)S(1)} %get-tuple-element.47.refs_1_, bf16[512,256]{1,0:T(8,128)(2,1)S(1)} %get-tuple-element.65.refs_2_, ...), custom_call_target="tpu_custom_call" | custom-call | tf_op jit(solution)/shard_map/pallas_call | solution.py:593
  85.6 0.1 collective-permute-start.2
  85.7 0.2 collective-permute-done.3.refs_1_
  85.9 0.9 collective-permute-done.4.refs_2_
  86.8 0.6 shard_map.160.refs_3_
  87.4 0.2 shard_map.161
  87.6 29.9 %all_to_all.28 = bf16[128,8,768]{2,1,0:T(8,128)(2,1)S(1)} all-to-all(bf16[128,8,768]{2,1,0:T(8,128)(2,1)S(1)} %bitcast.12), channel_id=1, replica_groups=mesh['pts'=64,'grp'=2] {'pts','grp'}, dimensions={0} | all-to-all | bytes 3145728 | tf_op jit(solution)/shard_map/all_to_all | solution.py:611
  117.4 0.2 shard_map.163
  117.7 25.3 %all_to_all.29.own = bf16[64,8,1536]{2,1,0:T(8,128)(2,1)S(1)} all-to-all(bf16[64,8,1536]{2,1,0:T(8,128)(2,1)S(1)} %shard_map.163), channel_id=1, replica_groups=mesh['pts'=64,'grp'=2] {'pts'}, dimensions={0} | all-to-all | bytes 3145728 | tf_op jit(solution)/shard_map/all_to_all | solution.py:611
  143.0 3.9 %collective-permute-start.6 = (bf16[64,8,1536]{2,1,0:T(8,128)(2,1)S(1)}, bf16[64,8,1536]{2,1,0:T(8,128)(2,1)S(1)}, u32[]{:S(2)}, u32[]{:S(2)}) collective-permute-start(bf16[64,8,1536]{2,1,0:T(8,128)(2,1)S(1)} %all_to_all.29.own), channel_id=1, source_target_pairs={{0,1},{1,0},{2,3},{3,2},{4,5},{5,4},{6,7},{7,6},{8,9},{9,8},{10,11... | collective-permute-start | bytes 4718600 | tf_op jit(solution)/shard_map/ppermute | solution.py:607
  147.0 1.2 shard_map.162
  148.2 1.6 %shard_map.164 = (f32[512,1536]{1,0:T(8,128)}, f32[512,512]{1,0:T(8,128)}, f32[512,512]{1,0:T(8,128)}) custom-call(bf16[64,8,1536]{2,1,0:T(8,128)(2,1)S(1)} %all_to_all.29.own), custom_call_target="tpu_custom_call" | custom-call | tf_op jit(solution)/shard_map/pallas_call | solution.py:400
  149.7 0.2 collective-permute-done.6.other
  150.0 1.9 %shard_map.165 = (f32[512,1536]{1,0:T(8,128)}, f32[512,512]{1,0:T(8,128)}, f32[512,512]{1,0:T(8,128)}, f32[256,768]{1,0:T(8,128)}, f32[256,256]{1,0:T(8,128)}) custom-call(bf16[64,8,1536]{2,1,0:T(8,128)(2,1)S(1)} %all_to_all.29.own, ...), custom_call_target="tpu_custom_call", output_to_operand_aliasing={{0}: (2, {}), {1}: (3, {}), {2}: (4, {})} | custom-call | tf_op jit(solution)/shard_map/pallas_call | solution.py:409
  (13 shorter events, 0.1 us)
Async XLA Ops:
  0.6 27.2 %copy-start.3 = (bf16[256,768]{1,0:T(8,128)(2,1)S(1)}, bf16[256,768]{1,0:T(8,128)(2,1)}, u32[]{:S(2)}) copy-start(bf16[256,768]{1,0:T(8,128)(2,1)} %refs_6_.3) | copy-start | bytes 1179652
  2.8 46.5 %copy-start.4 = (bf16[256,512]{1,0:T(8,128)(2,1)S(1)}, bf16[256,512]{1,0:T(8,128)(2,1)}, u32[]{:S(2)}) copy-start(bf16[256,512]{1,0:T(8,128)(2,1)} %refs_3_.7) | copy-start | bytes 786436
  27.8 24.8 %copy-start = (bf16[512,1536]{1,0:T(8,128)(2,1)S(1)}, bf16[512,1536]{1,0:T(8,128)(2,1)}, u32[]{:S(2)}) copy-start(bf16[512,1536]{1,0:T(8,128)(2,1)} %refs_5_.1) | copy-start | bytes 4718596
  27.8 24.8 %copy-start.1 = (bf16[512,512]{1,0:T(8,128)(2,1)S(1)}, bf16[512,512]{1,0:T(8,128)(2,1)}, u32[]{:S(2)}) copy-start(bf16[512,512]{1,0:T(8,128)(2,1)} %refs_4_.5) | copy-start | bytes 1572868
  49.8 2.8 %collective-permute-start = (bf16[256,1024]{1,0:T(8,128)(2,1)S(1)}, bf16[256,1024]{1,0:T(8,128)(2,1)S(1)}, u32[]{:S(2)}, u32[]{:S(2)}) collective-permute-start(bf16[256,1024]{1,0:T(8,128)(2,1)S(1)} %shard_map.155.refs_0_.refs_3_), channel_id=1, source_target_pairs={{0,1},{1,0},{2,3},{3,2},{4,5},{5,4},{6,7},{7,6},{8,9},{9,8},{10,11... | collective-permute-start | bytes 1572872 | tf_op jit(solution)/shard_map/ppermute | solution.py:607
  58.5 2.2 %copy-start.2 = (bf16[512,512]{1,0:T(8,128)(2,1)S(1)}, bf16[512,512]{1,0:T(8,128)(2,1)}, u32[]{:S(2)}) copy-start(bf16[512,512]{1,0:T(8,128)(2,1)} %refs_6_.2) | copy-start | bytes 1572868
  58.5 2.2 %collective-permute-start.1 = (bf16[256,1024]{1,0:T(8,128)(2,1)S(1)}, bf16[256,1024]{1,0:T(8,128)(2,1)S(1)}, u32[]{:S(2)}, u32[]{:S(2)}) collective-permute-start(bf16[256,1024]{1,0:T(8,128)(2,1)S(1)} %get-tuple-element.53.refs_2_), channel_id=1, source_target_pairs={{0,1},{1,0},{2,3},{3,2},{4,5},{5,4},{6,7},{7,6},{8,9},{9,8},{10,11... | collective-permute-start | bytes 1572872 | tf_op jit(solution)/shard_map/ppermute | solution.py:607
  60.7 21.2 %copy-start.5 = (bf16[256,256]{1,0:T(8,128)(2,1)S(1)}, bf16[256,256]{1,0:T(8,128)(2,1)}, u32[]{:S(2)}) copy-start(bf16[256,256]{1,0:T(8,128)(2,1)} %refs_7_.1) | copy-start | bytes 393220
  79.5 6.4 %collective-permute-start.3 = (bf16[64,2,8,128]{3,2,1,0:T(8,128)(2,1)S(1)}, bf16[64,2,8,128]{3,2,1,0:T(8,128)(2,1)S(1)}, u32[]{:S(2)}, u32[]{:S(2)}) collective-permute-start(bf16[64,2,8,128]{3,2,1,0:T(8,128)(2,1)S(1)} %get-tuple-element.73), channel_id=1, source_target_pairs={{0,32},{1,97},{2,34},{3,99},{4,36},{5,101},{6,38},{7,103},{8,40},{... | collective-permute-start | bytes 786440 | tf_op jit(solution)/shard_map/ppermute | solution.py:731
  80.4 6.4 %collective-permute-start.4 = (bf16[64,2,8,128]{3,2,1,0:T(8,128)(2,1)S(1)}, bf16[64,2,8,128]{3,2,1,0:T(8,128)(2,1)S(1)}, u32[]{:S(2)}, u32[]{:S(2)}) collective-permute-start(bf16[64,2,8,128]{3,2,1,0:T(8,128)(2,1)S(1)} %get-tuple-element.74), channel_id=1, source_target_pairs={{0,8},{1,25},{2,10},{3,27},{4,12},{5,29},{6,14},{7,31},{8,0},{9,17... | collective-permute-start | bytes 786440 | tf_op jit(solution)/shard_map/ppermute | solution.py:732
  81.3 5.5 %collective-permute-start.5 = (bf16[256,512]{1,0:T(8,128)(2,1)S(1)}, bf16[256,512]{1,0:T(8,128)(2,1)S(1)}, u32[]{:S(2)}, u32[]{:S(2)}) collective-permute-start(bf16[256,512]{1,0:T(8,128)(2,1)S(1)} %get-tuple-element.75.refs_5_), channel_id=1, source_target_pairs={{0,1},{1,0},{2,3},{3,2},{4,5},{5,4},{6,7},{7,6},{8,9},{9,8},{10,11... | collective-permute-start | bytes 786440 | tf_op jit(solution)/shard_map/ppermute | solution.py:607
  85.6 1.8 %collective-permute-start.2 = (bf16[256,512]{1,0:T(8,128)(2,1)S(1)}, bf16[256,512]{1,0:T(8,128)(2,1)S(1)}, u32[]{:S(2)}, u32[]{:S(2)}) collective-permute-start(bf16[256,512]{1,0:T(8,128)(2,1)S(1)} %get-tuple-element.71), channel_id=1, source_target_pairs={{0,1},{1,0},{2,3},{3,2},{4,5},{5,4},{6,7},{7,6},{8,9},{9,8},{10,11... | collective-permute-start | bytes 786440 | tf_op jit(solution)/shard_map/ppermute | solution.py:607
  143.0 6.9 %collective-permute-start.6 = (bf16[64,8,1536]{2,1,0:T(8,128)(2,1)S(1)}, bf16[64,8,1536]{2,1,0:T(8,128)(2,1)S(1)}, u32[]{:S(2)}, u32[]{:S(2)}) collective-permute-start(bf16[64,8,1536]{2,1,0:T(8,128)(2,1)S(1)} %all_to_all.29.own), channel_id=1, source_target_pairs={{0,1},{1,0},{2,3},{3,2},{4,5},{5,4},{6,7},{7,6},{8,9},{9,8},{10,11... | collective-permute-start | bytes 4718600 | tf_op jit(solution)/shard_map/ppermute | solution.py:607

commit v12 on v11

--- a/solution.py
+++ b/solution.py
@@ -41,15 +41,6 @@
     return (lax.broadcasted_iota(jnp.int32, shape, 0) == slots).astype(BF)
 
 
-def head_half(shape, half):
-    lanes = lax.broadcasted_iota(jnp.int32, shape, 1)
-    return (lanes < HD) if half == 0 else (lanes >= HD)
-
-
-def keep_half(rows, half):
-    return jnp.where(head_half(rows.shape, half), rows, jnp.zeros_like(rows))
-
-
 def softmax_rows(scores):
     raised = jnp.exp(scores - jnp.max(scores, axis=-1, keepdims=True))
     return (raised * (1.0 / jnp.sum(raised, axis=-1, keepdims=True))).astype(BF)
@@ -59,10 +50,6 @@
     wide = weights.astype(F32)
     diagonal = jnp.sum(wide * against, axis=-1, keepdims=True)
     return (wide * (against - diagonal)).astype(BF)
-
-
-def scaled_half(rows, half):
-    return keep_half(rows * jnp.asarray(HD ** (-0.5), BF), half)
 
 
 def stack_heads(rows, heads):
@@ -185,22 +172,19 @@
 
     for pair in range(part // PAIR):
         lanes = slice(pair * PAIR, (pair + 1) * PAIR)
-        query, key, value = queries[:, lanes], keys[:, lanes], values[:, lanes]
-        entering = incoming[:, lanes]
-        parts = ([], [])
+        key, value = keys[:, lanes], values[:, lanes]
+        query = queries[:, lanes] * jnp.asarray(HD ** (-0.5), BF)
+        head_weights = softmax_rows(mm(stack_heads(query, 2), key, (1, 1)))
+        against = mm(stack_heads(incoming[:, lanes], 2), value, (1, 1))
+        slopes = slopes_of(head_weights, against)
+        put(pair * PAIR, unstack_heads(mm(head_weights, value), 2).astype(BF))
+        query_part = unstack_heads(mm(slopes, key), 2) * HD ** (-0.5)
+        put(part + pair * PAIR, query_part.astype(BF))
         for half in range(2):
             band = slice(pair * PAIR + half * HD, pair * PAIR + (half + 1) * HD)
-            scores = mm(scaled_half(query, half), key, (1, 1))
-            head_weights = softmax_rows(scores)
-            parts[0].append(mm(head_weights, value))
-            against = mm(keep_half(entering, half), value, (1, 1))
-            slopes = slopes_of(head_weights, against)
-            parts[1].append(mm(slopes, key) * HD ** (-0.5))
-            key_parts.append(mm(queries_turned[band], slopes) * HD ** (-0.5))
-            value_parts.append(mm(incoming_turned[band], head_weights))
-        for at, (low, high) in enumerate(parts):
-            both = jnp.where(head_half(low.shape, 0), low, high).astype(BF)
-            put(at * part + pair * PAIR, both)
+            rows = slice(half * 2 * half_rows, (half + 1) * 2 * half_rows)
+            key_parts.append(mm(queries_turned[band], slopes[rows]) * HD ** (-0.5))
+            value_parts.append(mm(incoming_turned[band], head_weights[rows]))
     put(2 * part, jnp.concatenate(key_parts, axis=0).T.astype(BF))
     put(3 * part, jnp.concatenate(value_parts, axis=0).T.astype(BF))
 
@@ -245,9 +229,10 @@
 
 
 def coarse_weights_kernel(
-    unit, keep, give, own_pack, other_pack, kept, first_half, second_half, *, strides
+    unit, keep, give, own_pack, other_pack, kept, across_x, across_y, across_both, *, strides
 ):
     chip, core = lax.axis_index("pts"), lax.axis_index("grp")
+    roles = [(chip // stride + core) % 2 == 1 for stride in strides]
     wide = unit.shape[1]
     part = wide // 2
     stacked = jnp.concatenate([keep[...], give[...]], axis=0)
@@ -258,14 +243,15 @@
     width = wide // 4
     for side in range(2):
         stack = [output_term[:, (2 * side + k) * width : (2 * side + k + 1) * width] for k in range(2)]
-        columns = projection_term[:, side * across : (side + 1) * across]
-        terms = jnp.concatenate([columns, jnp.concatenate(stack, axis=0)], axis=1)
-        for at, passed in enumerate((first_half, second_half)):
-            low = terms[:, 2 * at * width : (2 * at + 1) * width]
-            high = terms[:, (2 * at + 1) * width : (2 * at + 2) * width]
-            upper = (chip // strides[at] + core) % 2 == 1
-            put_blocks(kept, side, at * width, jnp.where(upper, high, low))
-            put_blocks(passed, side, 0, jnp.where(upper, low, high))
+        first = side * across
+        tiles = [projection_term[:, first + k * width : first + (k + 1) * width] for k in range(3)]
+        tiles.append(jnp.concatenate(stack, axis=0))
+        same = [jnp.where(roles[0], tiles[2 + k], tiles[k]) for k in range(2)]
+        other = [jnp.where(roles[0], tiles[k], tiles[2 + k]) for k in range(2)]
+        put_blocks(kept, side, 0, jnp.where(roles[1], same[1], same[0]))
+        put_blocks(across_y, side, 0, jnp.where(roles[1], same[0], same[1]))
+        put_blocks(across_x, side, 0, jnp.where(roles[1], other[1], other[0]))
+        put_blocks(across_both, side, 0, jnp.where(roles[1], other[0], other[1]))
 
 
 def put_quarters(blocks, lane, term):
@@ -283,7 +269,7 @@
 
 def sum_kernel(arrived, spread, *, tokens, run, step):
     senders, _, rows, across = arrived.shape
-    width = (across - tokens) // 4
+    width = (across - tokens) // 3
 
     def pieces(side, at):
         start = tokens + at * width
@@ -291,11 +277,11 @@
 
     total = [jnp.sum(pieces(side, 0), axis=0) for side in range(2)]
     for side in range(2):
-        for at, block in enumerate((run, step)):
-            split = pieces(side, 1 + at).reshape(senders // (2 * block), 2, block, rows, width)
-            halves = jnp.sum(jnp.sum(split, axis=2), axis=0)
-            total.extend([halves[side], halves[1 - side]])
-        total.append(jnp.sum(pieces(side, 3), axis=0))
+        shape = (senders // (2 * run), 2, run // (2 * step), 2, step, rows, width)
+        split = jnp.sum(jnp.sum(pieces(side, 1).reshape(shape), axis=4), axis=2)
+        split = jnp.sum(split, axis=0)
+        total.extend(split[(x + side) % 2, (y + side) % 2] for x in range(2) for y in range(2))
+        total.append(jnp.sum(pieces(side, 2), axis=0))
     total = jnp.concatenate(total, axis=1).astype(BF)
     spread[...] = jnp.broadcast_to(total[None], spread.shape)
 
@@ -481,18 +467,17 @@
 
 
 def coarse_part_kernel(
-    kept, got_first, got_second, own_pack, other_pack, own_gradient, other_gradient, coarse
-):
-    width = got_first.shape[3]
-    for at, got in enumerate((got_first, got_second)):
-        lanes = slice(at * width, (at + 1) * width)
-        mine = kept[:, :, :, lanes].astype(F32)
-        coarse[:, :, :, lanes] = (mine + got[...].astype(F32)).astype(BF)
+    kept, got_x, got_y, got_both, own_pack, other_pack, own_gradient, other_gradient, coarse
+):
+    width = kept.shape[3]
+    pairs = kept[...].astype(F32) + got_x[...].astype(F32)
+    pairs = pairs + (got_y[...].astype(F32) + got_both[...].astype(F32))
+    coarse[:, :, :, :width] = pairs.astype(BF)
     part = own_gradient.shape[1] // 2
     first = pl.multiple_of(lax.axis_index("grp") * part, part)
     pool_term = mm(own_pack[:, pl.ds(first, part)], own_gradient[...], (0, 0))
     pool_term = pool_term + mm(other_pack[:, pl.ds(first, part)], other_gradient[...], (0, 0))
-    put_quarters(coarse, 2 * width, pool_term)
+    put_quarters(coarse, width, pool_term)
 
 
 def assemble_kernel(tokens, fine_kept, fine_got, coarse, send):
@@ -694,18 +679,12 @@
     )
     got = exchange(give)
     blocks = (owners, 2, slots // devices)
-    kept, first_half, second_half = call(
+    kept, *passed = call(
         functools.partial(coarse_weights_kernel, strides=(run, step)),
         (unit, keep, give, own_pack, other_pack),
-        (
-            Near((*blocks, wide // 2)),
-            Near((*blocks, wide // 4)),
-            Near((*blocks, wide // 4)),
-        ),
-    )
-    got, kept, first_half, second_half = lax.optimization_barrier(
-        (got, kept, first_half, second_half)
-    )
+        (Near((*blocks, wide // 4)),) * 4,
+    )
+    got, kept, passed = lax.optimization_barrier((got, kept, passed))
     coarse_result, coarse_gradient, send = call(
         coarse_finish_kernel,
         (
@@ -725,11 +704,15 @@
         ),
     )
     arrived = route(send, devices)
-    arrived, first_half, second_half, coarse_gradient = lax.optimization_barrier(
-        (arrived, first_half, second_half, coarse_gradient)
-    )
-    got_first = lax.ppermute(first_half, ("pts", "grp"), neighbours(owners, run))
-    got_second = lax.ppermute(second_half, ("pts", "grp"), neighbours(owners, step))
+    arrived, passed, coarse_gradient = lax.optimization_barrier(
+        (arrived, passed, coarse_gradient)
+    )
+    to_x, to_y = neighbours(owners, run), neighbours(owners, step)
+    to_both = [(source, dict(to_y)[target]) for source, target in to_x]
+    received = [
+        lax.ppermute(tile, ("pts", "grp"), pairs)
+        for tile, pairs in zip(passed, (to_x, to_y, to_both))
+    ]
     other_gradient = exchange(coarse_gradient)
     tokens, fine_kept, fine_passed = call(
         fine_backward_kernel,
@@ -755,16 +738,15 @@
         coarse_part_kernel,
         (
             kept,
-            got_first,
-            got_second,
+            *received,
             own_pack,
             other_pack,
             coarse_gradient,
             other_gradient,
         ),
-        (Near((*blocks, 3 * wide // 4)),),
-    )
-    across = features + wide
+        (Near((*blocks, wide // 2)),),
+    )
+    across = features + 3 * wide // 4
     (send,) = call(
         assemble_kernel,
         (tokens, fine_kept, fine_got, coarse_part),

time: 152 us -> 152 us (level)
  blocking collectives: 116 us -> 113 us
  starting transfers between devices: 8.22 us -> 11.2 us
    ppermute x2 -> x3, starting transfers between devices: 1.82 us -> 5.07 us  [on_device(): lax.ppermute(tile, ('pts', 'grp'), pairs)]
    all_to_all x5, blocking collectives: 116 us -> 113 us  [spread_blocks(): return lax.all_to_all(values, axes, split_axis=0, concat_axis=0, tiled=True)]
  transfers between devices with their start and end apart: 7 -> 8, of which waited for: 5 -> 4; matrix products, arithmetic and copies ran while one was open for 0% -> 0% of each run, Pallas kernels for 5% -> 5%
where the time goes in v12:
time: 152 us
  blocking collectives  113 us (74%)
  Pallas kernels  23 us (15%)
  starting transfers between devices  11.2 us (7%)
  waiting for transfers between devices  3.45 us (2%)
    all_to_all x5, blocking collectives, spread_blocks(): return lax.all_to_all(values, axes, split_axis=0, concat_axis=0, tiled=True)  113 us
    pallas_call x11, Pallas kernels, call(): pl.pallas_call(body, out_shape=[(pltpu.HBM if out.far else jax.ShapeDtype...  19.5 us
    ppermute x5, starting transfers between devices, exchange(): return lax.ppermute(values, 'grp', [(0, 1), (1, 0)])  6.17 us
    ppermute x3, starting transfers between devices, on_device(): lax.ppermute(tile, ('pts', 'grp'), pairs)  5.07 us
  transfers between devices with their start and end apart: 8, of which 4 were waited for; matrix products, arithmetic and copies ran while one was open for 0% of the time, Pallas kernels for 5%

profile of v12, /device:TPU:1, one launch (start us, length us, event | category | flops | bytes accessed | tf_op | source)
XLA Modules:
  0.0 151.8 jit_solution(10835009461603283545)
XLA Ops:
  0.6 2.2 %shard_map.153 = (bf16[1024,256]{1,0:T(8,128)(2,1)S(1)}, s32[1,512]{1,0:T(1,128)S(1)}, s32[1,512]{1,0:T(1,128)S(1)}, s32[1,512]{1,0:T(1,128)S(1)}, f32[1,512]{1,0:T(1,128)S(1)}) custom-call(s32[1,512]{1,0:T(1,128)} %bitcast.19, s32[1,512]{1,0:T(1,128)} %bitcast.20, s32[1,256]{1,0:T(1,128)} %bitcast.21, bf16[512,256]{1,0:T(8,128)(2,1)} %refs_3_.4), custom_call_target="tpu_custom_call" | custom-call | tf_op jit(solution)/shard_map/pallas_call | solution.py:578
  2.8 0.0 copy-start.4
  2.8 25.0 %all_to_all.25 = bf16[128,8,256]{2,1,0:T(8,128)(2,1)S(1)} all-to-all(bf16[128,8,256]{2,1,0:T(8,128)(2,1)S(1)} %bitcast.18), channel_id=1, replica_groups=mesh['pts'=64,'grp'=2] {'pts','grp'}, dimensions={0} | all-to-all | bytes 1048576 | tf_op jit(solution)/shard_map/all_to_all | solution.py:596
  27.8 3.4 %shard_map.154 = (bf16[1024,256]{1,0:T(8,128)(2,1)S(1)}, bf16[512,256]{1,0:T(8,128)(2,1)S(1)}, bf16[512,768]{1,0:T(8,128)(2,1)S(1)}, bf16[512,256]{1,0:T(8,128)(2,1)S(1)}, bf16[8,256,256]{2,1,0:T(8,128)(2,1)S(1)}) custom-call(bf16[1024,256]{1,0:T(8,128)(2,1)S(1)} %bitcast.14, s32[1,512]{1,0:T(1,128)S(1)} %get-tuple-element.50.refs_1_, ...), custom_call_target="tpu_custom_call" | custom-call | tf_op jit(solution)/shard_map/pallas_call | solution.py:578
  31.2 18.1 %all_to_all.26 = bf16[128,8,256]{2,1,0:T(8,128)(2,1)S(1)} all-to-all(bf16[128,8,256]{2,1,0:T(8,128)(2,1)S(1)} %bitcast.16), channel_id=1, replica_groups=mesh['pts'=64,'grp'=2] {'pts','grp'}, dimensions={0} | all-to-all | bytes 1048576 | tf_op jit(solution)/shard_map/all_to_all | solution.py:596
  49.3 0.5 shard_map.155.refs_0_.refs_3_.refs_4_
  49.8 1.2 collective-permute-start
  51.1 1.5 %collective-permute-done.refs_1_.refs_4_.refs_5_ = bf16[256,1024]{1,0:T(8,128)(2,1)S(1)} collective-permute-done((bf16[256,1024]{1,0:T(8,128)(2,1)S(1)}, bf16[256,1024]{1,0:T(8,128)(2,1)S(1)}, u32[]{:S(2)}, u32[]{:S(2)}) %collective-permute-start) | collective-permute-done | bytes 524320 | tf_op jit(solution)/shard_map/ppermute | solution.py:592
  52.6 5.3 %shard_map.156 = (bf16[256,512]{1,0:T(8,128)(2,1)S(1)}, bf16[256,1024]{1,0:T(8,128)(2,1)S(1)}, bf16[256,1024]{1,0:T(8,128)(2,1)S(1)}, bf16[512,512]{1,0:T(8,128)(2,1)S(1)}) custom-call(bf16[256,1024]{1,0:T(8,128)(2,1)S(1)} %shard_map.155.refs_0_.refs_3_.refs_4_, bf16[256,1024]{1,0:T(8,128)(2,1)S(1)} %collective-permute-done.refs_1_.refs_4_.refs_5_, ...), custom_call_target="tpu_custom_call" | custom-call | tf_op jit(solution)/shard_map/pallas_call | solution.py:578
  57.9 0.0 copy-start.2
  57.9 0.6 collective-permute-start.1
  58.5 0.8 shard_map.157
  59.3 0.7 collective-permute-done.1.refs_2_
  60.1 1.5 %shard_map.158 = (bf16[256,512]{1,0:T(8,128)(2,1)}, bf16[256,512]{1,0:T(8,128)(2,1)S(1)}, bf16[1024,256]{1,0:T(8,128)(2,1)S(1)}) custom-call(bf16[256,512]{1,0:T(8,128)(2,1)S(1)} %get-tuple-element.54.refs_0_, bf16[256,1024]{1,0:T(8,128)(2,1)S(1)} %get-tuple-element.55.refs_1_, bf16[256,1024]{1,0:T(8,128)(2,1)S(1)} %collective-permute-done.1.refs_2_, ...), custom_call_target="tpu_custom_call" | custom-call | tf_op jit(solution)/shard_map/pallas_call | solution.py:578
  61.6 17.3 %all_to_all.27 = bf16[128,8,256]{2,1,0:T(8,128)(2,1)S(1)} all-to-all(bf16[128,8,256]{2,1,0:T(8,128)(2,1)S(1)} %bitcast.17), channel_id=1, replica_groups=mesh['pts'=64,'grp'=2] {'pts','grp'}, dimensions={0} | all-to-all | bytes 1048576 | tf_op jit(solution)/shard_map/all_to_all | solution.py:596
  78.9 0.9 collective-permute-start.3
  79.8 1.0 collective-permute-start.4
  80.7 3.2 %collective-permute-start.5 = (bf16[64,2,8,128]{3,2,1,0:T(8,128)(2,1)S(1)}, bf16[64,2,8,128]{3,2,1,0:T(8,128)(2,1)S(1)}, u32[]{:S(2)}, u32[]{:S(2)}) collective-permute-start(bf16[64,2,8,128]{3,2,1,0:T(8,128)(2,1)S(1)} %get-tuple-element.80), channel_id=1, source_target_pairs={{0,40},{1,121},{2,42},{3,123},{4,44},{5,125},{6,46},{7,127},{8,32}... | collective-permute-start | bytes 786440 | tf_op jit(solution)/shard_map/ppermute | solution.py:713
  84.0 0.0 collective-permute-start.6
  84.0 3.7 %shard_map.159 = (bf16[64,2,8,256]{3,2,1,0:T(8,128)(2,1)S(1)}, f32[256,512]{1,0:T(8,128)S(1)}, bf16[256,512]{1,0:T(8,128)(2,1)S(1)}) custom-call(bf16[1024,256]{1,0:T(8,128)(2,1)S(1)} %bitcast.15, s32[1,512]{1,0:T(1,128)S(1)} %get-tuple-element.50.refs_1_, bf16[512,256]{1,0:T(8,128)(2,1)S(1)} %get-tuple-element.70.refs_2_, ...), custom_call_target="tpu_custom_call" | custom-call | tf_op jit(solution)/shard_map/pallas_call | solution.py:578
  87.7 0.6 collective-permute-start.2
  88.3 1.0 collective-permute-done.5.refs_3_
  89.3 0.6 shard_map.160.refs_3_
  89.9 0.1 shard_map.161
  90.0 26.9 %all_to_all.28 = bf16[128,8,640]{2,1,0:T(8,128)(2,1)S(1)} all-to-all(bf16[128,8,640]{2,1,0:T(8,128)(2,1)S(1)} %bitcast.12), channel_id=1, replica_groups=mesh['pts'=64,'grp'=2] {'pts','grp'}, dimensions={0} | all-to-all | bytes 2621440 | tf_op jit(solution)/shard_map/all_to_all | solution.py:596
  116.9 0.2 shard_map.163
  117.1 25.8 %all_to_all.29.own = bf16[64,8,1536]{2,1,0:T(8,128)(2,1)S(1)} all-to-all(bf16[64,8,1536]{2,1,0:T(8,128)(2,1)S(1)} %shard_map.163), channel_id=1, replica_groups=mesh['pts'=64,'grp'=2] {'pts'}, dimensions={0} | all-to-all | bytes 3145728 | tf_op jit(solution)/shard_map/all_to_all | solution.py:596
  142.9 3.7 %collective-permute-start.7 = (bf16[64,8,1536]{2,1,0:T(8,128)(2,1)S(1)}, bf16[64,8,1536]{2,1,0:T(8,128)(2,1)S(1)}, u32[]{:S(2)}, u32[]{:S(2)}) collective-permute-start(bf16[64,8,1536]{2,1,0:T(8,128)(2,1)S(1)} %all_to_all.29.own), channel_id=1, source_target_pairs={{0,1},{1,0},{2,3},{3,2},{4,5},{5,4},{6,7},{7,6},{8,9},{9,8},{10,11... | collective-permute-start | bytes 4718600 | tf_op jit(solution)/shard_map/ppermute | solution.py:592
  146.6 1.2 shard_map.162
  147.8 1.6 %shard_map.164 = (f32[512,1536]{1,0:T(8,128)}, f32[512,512]{1,0:T(8,128)}, f32[512,512]{1,0:T(8,128)}) custom-call(bf16[64,8,1536]{2,1,0:T(8,128)(2,1)S(1)} %all_to_all.29.own), custom_call_target="tpu_custom_call" | custom-call | tf_op jit(solution)/shard_map/pallas_call | solution.py:386
  149.4 0.2 collective-permute-done.7.other
  149.6 1.9 %shard_map.165 = (f32[512,1536]{1,0:T(8,128)}, f32[512,512]{1,0:T(8,128)}, f32[512,512]{1,0:T(8,128)}, f32[256,768]{1,0:T(8,128)}, f32[256,256]{1,0:T(8,128)}) custom-call(bf16[64,8,1536]{2,1,0:T(8,128)(2,1)S(1)} %all_to_all.29.own, ...), custom_call_target="tpu_custom_call", output_to_operand_aliasing={{0}: (2, {}), {1}: (3, {}), {2}: (4, {})} | custom-call | tf_op jit(solution)/shard_map/pallas_call | solution.py:395
  (15 shorter events, 0.1 us)
Async XLA Ops:
  0.6 27.2 %copy-start.3 = (bf16[256,768]{1,0:T(8,128)(2,1)S(1)}, bf16[256,768]{1,0:T(8,128)(2,1)}, u32[]{:S(2)}) copy-start(bf16[256,768]{1,0:T(8,128)(2,1)} %refs_6_.3) | copy-start | bytes 1179652
  2.8 46.5 %copy-start.4 = (bf16[256,512]{1,0:T(8,128)(2,1)S(1)}, bf16[256,512]{1,0:T(8,128)(2,1)}, u32[]{:S(2)}) copy-start(bf16[256,512]{1,0:T(8,128)(2,1)} %refs_3_.7) | copy-start | bytes 786436
  27.8 24.8 %copy-start = (bf16[512,1536]{1,0:T(8,128)(2,1)S(1)}, bf16[512,1536]{1,0:T(8,128)(2,1)}, u32[]{:S(2)}) copy-start(bf16[512,1536]{1,0:T(8,128)(2,1)} %refs_5_.1) | copy-start | bytes 4718596
  27.8 24.8 %copy-start.1 = (bf16[512,512]{1,0:T(8,128)(2,1)S(1)}, bf16[512,512]{1,0:T(8,128)(2,1)}, u32[]{:S(2)}) copy-start(bf16[512,512]{1,0:T(8,128)(2,1)} %refs_4_.5) | copy-start | bytes 1572868
  49.8 2.8 %collective-permute-start = (bf16[256,1024]{1,0:T(8,128)(2,1)S(1)}, bf16[256,1024]{1,0:T(8,128)(2,1)S(1)}, u32[]{:S(2)}, u32[]{:S(2)}) collective-permute-start(bf16[256,1024]{1,0:T(8,128)(2,1)S(1)} %shard_map.155.refs_0_.refs_3_.refs_4_), channel_id=1, source_target_pairs={{0,1},{1,0},{2,3},{3,2},{4,5},{5,4},{6,7},{7,6},{8,9},{9,8},{10,11... | collective-permute-start | bytes 1572872 | tf_op jit(solution)/shard_map/ppermute | solution.py:592
  57.9 2.2 %copy-start.2 = (bf16[512,512]{1,0:T(8,128)(2,1)S(1)}, bf16[512,512]{1,0:T(8,128)(2,1)}, u32[]{:S(2)}) copy-start(bf16[512,512]{1,0:T(8,128)(2,1)} %refs_6_.2) | copy-start | bytes 1572868
  57.9 2.2 %collective-permute-start.1 = (bf16[256,1024]{1,0:T(8,128)(2,1)S(1)}, bf16[256,1024]{1,0:T(8,128)(2,1)S(1)}, u32[]{:S(2)}, u32[]{:S(2)}) collective-permute-start(bf16[256,1024]{1,0:T(8,128)(2,1)S(1)} %get-tuple-element.56.refs_2_), channel_id=1, source_target_pairs={{0,1},{1,0},{2,3},{3,2},{4,5},{5,4},{6,7},{7,6},{8,9},{9,8},{10,11... | collective-permute-start | bytes 1572872 | tf_op jit(solution)/shard_map/ppermute | solution.py:592
  60.1 23.9 %copy-start.5 = (bf16[256,256]{1,0:T(8,128)(2,1)S(1)}, bf16[256,256]{1,0:T(8,128)(2,1)}, u32[]{:S(2)}) copy-start(bf16[256,256]{1,0:T(8,128)(2,1)} %refs_7_.1) | copy-start | bytes 393220
  78.9 9.4 %collective-permute-start.3 = (bf16[64,2,8,128]{3,2,1,0:T(8,128)(2,1)S(1)}, bf16[64,2,8,128]{3,2,1,0:T(8,128)(2,1)S(1)}, u32[]{:S(2)}, u32[]{:S(2)}) collective-permute-start(bf16[64,2,8,128]{3,2,1,0:T(8,128)(2,1)S(1)} %get-tuple-element.78), channel_id=1, source_target_pairs={{0,32},{1,97},{2,34},{3,99},{4,36},{5,101},{6,38},{7,103},{8,40},{... | collective-permute-start | bytes 786440 | tf_op jit(solution)/shard_map/ppermute | solution.py:713
  79.8 8.5 %collective-permute-start.4 = (bf16[64,2,8,128]{3,2,1,0:T(8,128)(2,1)S(1)}, bf16[64,2,8,128]{3,2,1,0:T(8,128)(2,1)S(1)}, u32[]{:S(2)}, u32[]{:S(2)}) collective-permute-start(bf16[64,2,8,128]{3,2,1,0:T(8,128)(2,1)S(1)} %get-tuple-element.79), channel_id=1, source_target_pairs={{0,8},{1,25},{2,10},{3,27},{4,12},{5,29},{6,14},{7,31},{8,0},{9,17... | collective-permute-start | bytes 786440 | tf_op jit(solution)/shard_map/ppermute | solution.py:713
  80.7 8.5 %collective-permute-start.5 = (bf16[64,2,8,128]{3,2,1,0:T(8,128)(2,1)S(1)}, bf16[64,2,8,128]{3,2,1,0:T(8,128)(2,1)S(1)}, u32[]{:S(2)}, u32[]{:S(2)}) collective-permute-start(bf16[64,2,8,128]{3,2,1,0:T(8,128)(2,1)S(1)} %get-tuple-element.80), channel_id=1, source_target_pairs={{0,40},{1,121},{2,42},{3,123},{4,44},{5,125},{6,46},{7,127},{8,32}... | collective-permute-start | bytes 786440 | tf_op jit(solution)/shard_map/ppermute | solution.py:713
  84.0 5.3 %collective-permute-start.6 = (bf16[256,512]{1,0:T(8,128)(2,1)S(1)}, bf16[256,512]{1,0:T(8,128)(2,1)S(1)}, u32[]{:S(2)}, u32[]{:S(2)}) collective-permute-start(bf16[256,512]{1,0:T(8,128)(2,1)S(1)} %get-tuple-element.81.refs_6_), channel_id=1, source_target_pairs={{0,1},{1,0},{2,3},{3,2},{4,5},{5,4},{6,7},{7,6},{8,9},{9,8},{10,11... | collective-permute-start | bytes 786440 | tf_op jit(solution)/shard_map/ppermute | solution.py:592
  87.7 2.1 %collective-permute-start.2 = (bf16[256,512]{1,0:T(8,128)(2,1)S(1)}, bf16[256,512]{1,0:T(8,128)(2,1)S(1)}, u32[]{:S(2)}, u32[]{:S(2)}) collective-permute-start(bf16[256,512]{1,0:T(8,128)(2,1)S(1)} %get-tuple-element.76), channel_id=1, source_target_pairs={{0,1},{1,0},{2,3},{3,2},{4,5},{5,4},{6,7},{7,6},{8,9},{9,8},{10,11... | collective-permute-start | bytes 786440 | tf_op jit(solution)/shard_map/ppermute | solution.py:592
  142.9 6.8 %collective-permute-start.7 = (bf16[64,8,1536]{2,1,0:T(8,128)(2,1)S(1)}, bf16[64,8,1536]{2,1,0:T(8,128)(2,1)S(1)}, u32[]{:S(2)}, u32[]{:S(2)}) collective-permute-start(bf16[64,8,1536]{2,1,0:T(8,128)(2,1)S(1)} %all_to_all.29.own), channel_id=1, source_target_pairs={{0,1},{1,0},{2,3},{3,2},{4,5},{5,4},{6,7},{7,6},{8,9},{9,8},{10,11... | collective-permute-start | bytes 4718600 | tf_op jit(solution)/shard_map/ppermute | solution.py:592

commit v13 on v11

--- a/solution.py
+++ b/solution.py
@@ -41,15 +41,6 @@
     return (lax.broadcasted_iota(jnp.int32, shape, 0) == slots).astype(BF)
 
 
-def head_half(shape, half):
-    lanes = lax.broadcasted_iota(jnp.int32, shape, 1)
-    return (lanes < HD) if half == 0 else (lanes >= HD)
-
-
-def keep_half(rows, half):
-    return jnp.where(head_half(rows.shape, half), rows, jnp.zeros_like(rows))
-
-
 def softmax_rows(scores):
     raised = jnp.exp(scores - jnp.max(scores, axis=-1, keepdims=True))
     return (raised * (1.0 / jnp.sum(raised, axis=-1, keepdims=True))).astype(BF)
@@ -59,10 +50,6 @@
     wide = weights.astype(F32)
     diagonal = jnp.sum(wide * against, axis=-1, keepdims=True)
     return (wide * (against - diagonal)).astype(BF)
-
-
-def scaled_half(rows, half):
-    return keep_half(rows * jnp.asarray(HD ** (-0.5), BF), half)
 
 
 def stack_heads(rows, heads):
@@ -185,29 +172,48 @@
 
     for pair in range(part // PAIR):
         lanes = slice(pair * PAIR, (pair + 1) * PAIR)
-        query, key, value = queries[:, lanes], keys[:, lanes], values[:, lanes]
-        entering = incoming[:, lanes]
-        parts = ([], [])
+        key, value = keys[:, lanes], values[:, lanes]
+        query = queries[:, lanes] * jnp.asarray(HD ** (-0.5), BF)
+        head_weights = softmax_rows(mm(stack_heads(query, 2), key, (1, 1)))
+        against = mm(stack_heads(incoming[:, lanes], 2), value, (1, 1))
+        slopes = slopes_of(head_weights, against)
+        put(pair * PAIR, unstack_heads(mm(head_weights, value), 2).astype(BF))
+        query_part = unstack_heads(mm(slopes, key), 2) * HD ** (-0.5)
+        put(part + pair * PAIR, query_part.astype(BF))
         for half in range(2):
             band = slice(pair * PAIR + half * HD, pair * PAIR + (half + 1) * HD)
-            scores = mm(scaled_half(query, half), key, (1, 1))
-            head_weights = softmax_rows(scores)
-            parts[0].append(mm(head_weights, value))
-            against = mm(keep_half(entering, half), value, (1, 1))
-            slopes = slopes_of(head_weights, against)
-            parts[1].append(mm(slopes, key) * HD ** (-0.5))
-            key_parts.append(mm(queries_turned[band], slopes) * HD ** (-0.5))
-            value_parts.append(mm(incoming_turned[band], head_weights))
-        for at, (low, high) in enumerate(parts):
-            both = jnp.where(head_half(low.shape, 0), low, high).astype(BF)
-            put(at * part + pair * PAIR, both)
+            rows = slice(half * 2 * half_rows, (half + 1) * 2 * half_rows)
+            key_parts.append(mm(queries_turned[band], slopes[rows]) * HD ** (-0.5))
+            value_parts.append(mm(incoming_turned[band], head_weights[rows]))
     put(2 * part, jnp.concatenate(key_parts, axis=0).T.astype(BF))
     put(3 * part, jnp.concatenate(value_parts, axis=0).T.astype(BF))
 
 
+def heads_back(grads, index, projection, output):
+    wide = output.shape[1]
+    part = wide // 2
+    first = pl.multiple_of(index * part, part)
+    mixed = mm(grads[:, :part], output[pl.ds(first, part), :])
+    back = jnp.zeros_like(mixed)
+    for at in range(3):
+        back = back + mm(
+            grads[:, (at + 1) * part : (at + 2) * part],
+            projection[:, pl.ds(at * wide + first, part)],
+            (1, 1),
+        )
+    return mixed, back
+
+
+def coarse_own_kernel(coarse, keep, projection, output, mixed, back):
+    own_mixed, own_back = heads_back(keep, lax.axis_index("grp"), projection, output)
+    mixed[...] = coarse[...].astype(F32) + own_mixed
+    back[...] = own_back
+
+
 def coarse_finish_kernel(
     coarse,
-    keep,
+    mixed,
+    back,
     got,
     cotangent,
     pool,
@@ -218,24 +224,12 @@
     gradient,
     send,
 ):
-    half_rows, wide = coarse.shape
-    part = wide // 2
-    mixed = coarse[...].astype(F32)
-    back = jnp.zeros((half_rows, wide), F32)
-    for source, index in ((keep, lax.axis_index("grp")), (got, 1 - lax.axis_index("grp"))):
-        first = pl.multiple_of(index * part, part)
-        mixed = mixed + mm(source[:, :part], output[pl.ds(first, part), :])
-        for at in range(3):
-            back = back + mm(
-                source[:, (at + 1) * part : (at + 2) * part],
-                projection[:, pl.ds(at * wide + first, part)],
-                (1, 1),
-            )
-    result[...] = mixed.astype(BF)
+    other_mixed, other_back = heads_back(got, 1 - lax.axis_index("grp"), projection, output)
+    result[...] = (mixed[...] + other_mixed).astype(BF)
     result.flush()
     normed, inverse = normalize(coarse[...])
     gradient_rows = (
-        cotangent[...].astype(F32) + norm_backward(back, normed, inverse)
+        cotangent[...].astype(F32) + norm_backward(back[...] + other_back, normed, inverse)
     ).astype(BF)
     gradient[...] = gradient_rows
     fine = mm(gradient_rows, pool[...], (1, 1)).astype(BF)
@@ -703,6 +697,11 @@
             Near((*blocks, wide // 4)),
         ),
     )
+    mixed, back = call(
+        coarse_own_kernel,
+        (coarse, keep, coarse_projection, coarse_output),
+        (Near((half_rows, wide), F32), Near((half_rows, wide), F32)),
+    )
     got, kept, first_half, second_half = lax.optimization_barrier(
         (got, kept, first_half, second_half)
     )
@@ -710,7 +709,8 @@
         coarse_finish_kernel,
         (
             coarse,
-            keep,
+            mixed,
+            back,
             got,
             coarse_cotangent,
             pool_weight,

time: 152 us -> 151 us (level)
    pallas_call x11 -> x12, Pallas kernels: 20.1 us -> 19.7 us  [call(): pl.pallas_call(body, out_shape=[(pltpu.HBM if out.far else jax.ShapeDtype...]
where the time goes in v13:
time: 151 us
  blocking collectives  116 us (77%)
  Pallas kernels  23.2 us (15%)
  starting transfers between devices  8.22 us (5%)
  waiting for transfers between devices  3.19 us (2%)
    all_to_all x5, blocking collectives, spread_blocks(): return lax.all_to_all(values, axes, split_axis=0, concat_axis=0, tiled=True)  116 us
    pallas_call x12, Pallas kernels, call(): pl.pallas_call(body, out_shape=[(pltpu.HBM if out.far else jax.ShapeDtype...  19.7 us
    ppermute x5, starting transfers between devices, exchange(): return lax.ppermute(values, 'grp', [(0, 1), (1, 0)])  6.4 us
  transfers between devices with their start and end apart: 7, of which 5 were waited for; matrix products, arithmetic and copies ran while one was open for 0% of the time, Pallas kernels for 5%

profile of v13, /device:TPU:1, one launch (start us, length us, event | category | flops | bytes accessed | tf_op | source)
XLA Modules:
  0.0 151.2 jit_solution(1077052432803199168)
XLA Ops:
  0.6 2.2 %shard_map.153 = (bf16[1024,256]{1,0:T(8,128)(2,1)S(1)}, s32[1,512]{1,0:T(1,128)S(1)}, s32[1,512]{1,0:T(1,128)S(1)}, s32[1,512]{1,0:T(1,128)S(1)}, f32[1,512]{1,0:T(1,128)S(1)}) custom-call(s32[1,512]{1,0:T(1,128)} %bitcast.19, s32[1,512]{1,0:T(1,128)} %bitcast.20, s32[1,256]{1,0:T(1,128)} %bitcast.21, bf16[512,256]{1,0:T(8,128)(2,1)} %refs_3_.4), custom_call_target="tpu_custom_call" | custom-call | tf_op jit(solution)/shard_map/pallas_call | solution.py:587
  2.8 25.0 %all_to_all.25 = bf16[128,8,256]{2,1,0:T(8,128)(2,1)S(1)} all-to-all(bf16[128,8,256]{2,1,0:T(8,128)(2,1)S(1)} %bitcast.18), channel_id=1, replica_groups=mesh['pts'=64,'grp'=2] {'pts','grp'}, dimensions={0} | all-to-all | bytes 1048576 | tf_op jit(solution)/shard_map/all_to_all | solution.py:605
  27.8 3.4 %shard_map.154 = (bf16[1024,256]{1,0:T(8,128)(2,1)S(1)}, bf16[512,256]{1,0:T(8,128)(2,1)S(1)}, bf16[512,768]{1,0:T(8,128)(2,1)S(1)}, bf16[512,256]{1,0:T(8,128)(2,1)S(1)}, bf16[8,256,256]{2,1,0:T(8,128)(2,1)S(1)}) custom-call(bf16[1024,256]{1,0:T(8,128)(2,1)S(1)} %bitcast.14, s32[1,512]{1,0:T(1,128)S(1)} %get-tuple-element.49.refs_1_, ...), custom_call_target="tpu_custom_call" | custom-call | tf_op jit(solution)/shard_map/pallas_call | solution.py:587
  31.2 18.1 %all_to_all.26 = bf16[128,8,256]{2,1,0:T(8,128)(2,1)S(1)} all-to-all(bf16[128,8,256]{2,1,0:T(8,128)(2,1)S(1)} %bitcast.17), channel_id=1, replica_groups=mesh['pts'=64,'grp'=2] {'pts','grp'}, dimensions={0} | all-to-all | bytes 1048576 | tf_op jit(solution)/shard_map/all_to_all | solution.py:605
  49.3 0.5 shard_map.155.refs_0_.refs_3_
  49.8 0.0 copy-start.1
  49.8 1.2 collective-permute-start
  51.1 1.5 %collective-permute-done.refs_1_.refs_4_ = bf16[256,1024]{1,0:T(8,128)(2,1)S(1)} collective-permute-done((bf16[256,1024]{1,0:T(8,128)(2,1)S(1)}, bf16[256,1024]{1,0:T(8,128)(2,1)S(1)}, u32[]{:S(2)}, u32[]{:S(2)}) %collective-permute-start) | collective-permute-done | bytes 524320 | tf_op jit(solution)/shard_map/ppermute | solution.py:601
  52.6 5.3 %shard_map.156 = (bf16[256,512]{1,0:T(8,128)(2,1)S(1)}, bf16[256,1024]{1,0:T(8,128)(2,1)S(1)}, bf16[256,1024]{1,0:T(8,128)(2,1)S(1)}, bf16[512,512]{1,0:T(8,128)(2,1)S(1)}) custom-call(bf16[256,1024]{1,0:T(8,128)(2,1)S(1)} %shard_map.155.refs_0_.refs_3_, bf16[256,1024]{1,0:T(8,128)(2,1)S(1)} %collective-permute-done.refs_1_.refs_4_, ...), custom_call_target="tpu_custom_call" | custom-call | tf_op jit(solution)/shard_map/pallas_call | solution.py:587
  57.9 0.6 collective-permute-start.1
  58.5 0.4 shard_map.157
  59.0 0.7 shard_map.158
  59.7 0.3 collective-permute-done.1.refs_3_
  60.1 1.2 shard_map.159
  61.3 17.3 %all_to_all.27 = bf16[128,8,256]{2,1,0:T(8,128)(2,1)S(1)} all-to-all(bf16[128,8,256]{2,1,0:T(8,128)(2,1)S(1)} %bitcast.16), channel_id=1, replica_groups=mesh['pts'=64,'grp'=2] {'pts','grp'}, dimensions={0} | all-to-all | bytes 1048576 | tf_op jit(solution)/shard_map/all_to_all | solution.py:605
  78.6 0.9 collective-permute-start.3
  79.5 1.0 collective-permute-start.4
  80.5 0.5 collective-permute-start.5
  81.0 3.7 %shard_map.160 = (bf16[64,2,8,256]{3,2,1,0:T(8,128)(2,1)S(1)}, f32[256,512]{1,0:T(8,128)S(1)}, bf16[256,512]{1,0:T(8,128)(2,1)S(1)}) custom-call(bf16[1024,256]{1,0:T(8,128)(2,1)S(1)} %bitcast.15, s32[1,512]{1,0:T(1,128)S(1)} %get-tuple-element.49.refs_1_, bf16[512,256]{1,0:T(8,128)(2,1)S(1)} %get-tuple-element.69.refs_2_, ...), custom_call_target="tpu_custom_call" | custom-call | tf_op jit(solution)/shard_map/pallas_call | solution.py:587
  84.7 0.1 collective-permute-start.2
  84.8 0.2 collective-permute-done.3.refs_1_
  85.1 0.9 collective-permute-done.4.refs_2_
  85.9 0.6 shard_map.161.refs_3_
  86.5 0.2 shard_map.162
  86.7 29.9 %all_to_all.28 = bf16[128,8,768]{2,1,0:T(8,128)(2,1)S(1)} all-to-all(bf16[128,8,768]{2,1,0:T(8,128)(2,1)S(1)} %bitcast.12), channel_id=1, replica_groups=mesh['pts'=64,'grp'=2] {'pts','grp'}, dimensions={0} | all-to-all | bytes 3145728 | tf_op jit(solution)/shard_map/all_to_all | solution.py:605
  116.6 0.2 shard_map.164
  116.8 25.3 %all_to_all.29.own = bf16[64,8,1536]{2,1,0:T(8,128)(2,1)S(1)} all-to-all(bf16[64,8,1536]{2,1,0:T(8,128)(2,1)S(1)} %shard_map.164), channel_id=1, replica_groups=mesh['pts'=64,'grp'=2] {'pts'}, dimensions={0} | all-to-all | bytes 3145728 | tf_op jit(solution)/shard_map/all_to_all | solution.py:605
  142.1 3.9 %collective-permute-start.6 = (bf16[64,8,1536]{2,1,0:T(8,128)(2,1)S(1)}, bf16[64,8,1536]{2,1,0:T(8,128)(2,1)S(1)}, u32[]{:S(2)}, u32[]{:S(2)}) collective-permute-start(bf16[64,8,1536]{2,1,0:T(8,128)(2,1)S(1)} %all_to_all.29.own), channel_id=1, source_target_pairs={{0,1},{1,0},{2,3},{3,2},{4,5},{5,4},{6,7},{7,6},{8,9},{9,8},{10,11... | collective-permute-start | bytes 4718600 | tf_op jit(solution)/shard_map/ppermute | solution.py:601
  146.1 1.2 shard_map.163
  147.3 1.6 %shard_map.165 = (f32[512,1536]{1,0:T(8,128)}, f32[512,512]{1,0:T(8,128)}, f32[512,512]{1,0:T(8,128)}) custom-call(bf16[64,8,1536]{2,1,0:T(8,128)(2,1)S(1)} %all_to_all.29.own), custom_call_target="tpu_custom_call" | custom-call | tf_op jit(solution)/shard_map/pallas_call | solution.py:394
  148.9 0.2 collective-permute-done.6.other
  149.1 1.9 %shard_map.166 = (f32[512,1536]{1,0:T(8,128)}, f32[512,512]{1,0:T(8,128)}, f32[512,512]{1,0:T(8,128)}, f32[256,768]{1,0:T(8,128)}, f32[256,256]{1,0:T(8,128)}) custom-call(bf16[64,8,1536]{2,1,0:T(8,128)(2,1)S(1)} %all_to_all.29.own, ...), custom_call_target="tpu_custom_call", output_to_operand_aliasing={{0}: (2, {}), {1}: (3, {}), {2}: (4, {})} | custom-call | tf_op jit(solution)/shard_map/pallas_call | solution.py:403
  (14 shorter events, 0.1 us)
Async XLA Ops:
  0.6 27.2 %copy-start.3 = (bf16[256,768]{1,0:T(8,128)(2,1)S(1)}, bf16[256,768]{1,0:T(8,128)(2,1)}, u32[]{:S(2)}) copy-start(bf16[256,768]{1,0:T(8,128)(2,1)} %refs_6_.3) | copy-start | bytes 1179652
  2.8 46.5 %copy-start.4 = (bf16[256,512]{1,0:T(8,128)(2,1)S(1)}, bf16[256,512]{1,0:T(8,128)(2,1)}, u32[]{:S(2)}) copy-start(bf16[256,512]{1,0:T(8,128)(2,1)} %refs_4_.5) | copy-start | bytes 786436
  27.8 24.8 %copy-start = (bf16[512,1536]{1,0:T(8,128)(2,1)S(1)}, bf16[512,1536]{1,0:T(8,128)(2,1)}, u32[]{:S(2)}) copy-start(bf16[512,1536]{1,0:T(8,128)(2,1)} %refs_6_.2) | copy-start | bytes 4718596
  27.8 24.8 %copy-start.2 = (bf16[512,512]{1,0:T(8,128)(2,1)S(1)}, bf16[512,512]{1,0:T(8,128)(2,1)}, u32[]{:S(2)}) copy-start(bf16[512,512]{1,0:T(8,128)(2,1)} %refs_5_.1) | copy-start | bytes 1572868
  49.8 8.7 %copy-start.1 = (bf16[512,512]{1,0:T(8,128)(2,1)S(1)}, bf16[512,512]{1,0:T(8,128)(2,1)}, u32[]{:S(2)}) copy-start(bf16[512,512]{1,0:T(8,128)(2,1)} %refs_7_.2) | copy-start | bytes 1572868
  49.8 2.8 %collective-permute-start = (bf16[256,1024]{1,0:T(8,128)(2,1)S(1)}, bf16[256,1024]{1,0:T(8,128)(2,1)S(1)}, u32[]{:S(2)}, u32[]{:S(2)}) collective-permute-start(bf16[256,1024]{1,0:T(8,128)(2,1)S(1)} %shard_map.155.refs_0_.refs_3_), channel_id=1, source_target_pairs={{0,1},{1,0},{2,3},{3,2},{4,5},{5,4},{6,7},{7,6},{8,9},{9,8},{10,11... | collective-permute-start | bytes 1572872 | tf_op jit(solution)/shard_map/ppermute | solution.py:601
  57.9 2.2 %collective-permute-start.1 = (bf16[256,1024]{1,0:T(8,128)(2,1)S(1)}, bf16[256,1024]{1,0:T(8,128)(2,1)S(1)}, u32[]{:S(2)}, u32[]{:S(2)}) collective-permute-start(bf16[256,1024]{1,0:T(8,128)(2,1)S(1)} %get-tuple-element.57.refs_2_), channel_id=1, source_target_pairs={{0,1},{1,0},{2,3},{3,2},{4,5},{5,4},{6,7},{7,6},{8,9},{9,8},{10,11... | collective-permute-start | bytes 1572872 | tf_op jit(solution)/shard_map/ppermute | solution.py:601
  60.1 20.9 %copy-start.5 = (bf16[256,256]{1,0:T(8,128)(2,1)S(1)}, bf16[256,256]{1,0:T(8,128)(2,1)}, u32[]{:S(2)}) copy-start(bf16[256,256]{1,0:T(8,128)(2,1)} %refs_7_.3) | copy-start | bytes 393220
  78.6 6.4 %collective-permute-start.3 = (bf16[64,2,8,128]{3,2,1,0:T(8,128)(2,1)S(1)}, bf16[64,2,8,128]{3,2,1,0:T(8,128)(2,1)S(1)}, u32[]{:S(2)}, u32[]{:S(2)}) collective-permute-start(bf16[64,2,8,128]{3,2,1,0:T(8,128)(2,1)S(1)} %get-tuple-element.77), channel_id=1, source_target_pairs={{0,32},{1,97},{2,34},{3,99},{4,36},{5,101},{6,38},{7,103},{8,40},{... | collective-permute-start | bytes 786440 | tf_op jit(solution)/shard_map/ppermute | solution.py:731
  79.5 6.4 %collective-permute-start.4 = (bf16[64,2,8,128]{3,2,1,0:T(8,128)(2,1)S(1)}, bf16[64,2,8,128]{3,2,1,0:T(8,128)(2,1)S(1)}, u32[]{:S(2)}, u32[]{:S(2)}) collective-permute-start(bf16[64,2,8,128]{3,2,1,0:T(8,128)(2,1)S(1)} %get-tuple-element.78), channel_id=1, source_target_pairs={{0,8},{1,25},{2,10},{3,27},{4,12},{5,29},{6,14},{7,31},{8,0},{9,17... | collective-permute-start | bytes 786440 | tf_op jit(solution)/shard_map/ppermute | solution.py:732
  80.5 5.5 %collective-permute-start.5 = (bf16[256,512]{1,0:T(8,128)(2,1)S(1)}, bf16[256,512]{1,0:T(8,128)(2,1)S(1)}, u32[]{:S(2)}, u32[]{:S(2)}) collective-permute-start(bf16[256,512]{1,0:T(8,128)(2,1)S(1)} %get-tuple-element.79.refs_5_), channel_id=1, source_target_pairs={{0,1},{1,0},{2,3},{3,2},{4,5},{5,4},{6,7},{7,6},{8,9},{9,8},{10,11... | collective-permute-start | bytes 786440 | tf_op jit(solution)/shard_map/ppermute | solution.py:601
  84.7 1.8 %collective-permute-start.2 = (bf16[256,512]{1,0:T(8,128)(2,1)S(1)}, bf16[256,512]{1,0:T(8,128)(2,1)S(1)}, u32[]{:S(2)}, u32[]{:S(2)}) collective-permute-start(bf16[256,512]{1,0:T(8,128)(2,1)S(1)} %get-tuple-element.75), channel_id=1, source_target_pairs={{0,1},{1,0},{2,3},{3,2},{4,5},{5,4},{6,7},{7,6},{8,9},{9,8},{10,11... | collective-permute-start | bytes 786440 | tf_op jit(solution)/shard_map/ppermute | solution.py:601
  142.1 6.9 %collective-permute-start.6 = (bf16[64,8,1536]{2,1,0:T(8,128)(2,1)S(1)}, bf16[64,8,1536]{2,1,0:T(8,128)(2,1)S(1)}, u32[]{:S(2)}, u32[]{:S(2)}) collective-permute-start(bf16[64,8,1536]{2,1,0:T(8,128)(2,1)S(1)} %all_to_all.29.own), channel_id=1, source_target_pairs={{0,1},{1,0},{2,3},{3,2},{4,5},{5,4},{6,7},{7,6},{8,9},{9,8},{10,11... | collective-permute-start | bytes 4718600 | tf_op jit(solution)/shard_map/ppermute | solution.py:601

commit v14 on v13

--- a/solution.py
+++ b/solution.py
@@ -275,26 +275,30 @@
     blocks[:, side, :, lane : lane + width] = pieces.astype(BF)
 
 
-def sum_kernel(arrived, spread, *, tokens, run, step):
-    senders, _, rows, across = arrived.shape
+def sum_kernel(arrived, spread, own_tokens, passed_tokens, *, tokens, run, step):
+    senders, sides, rows, across = arrived.shape
     width = (across - tokens) // 4
+    upper = lax.axis_index("grp") == 1
+    low_tokens, high_tokens = arrived[:, 0, :, :tokens], arrived[:, 1, :, :tokens]
+    own_tokens[...] = jnp.where(upper, high_tokens, low_tokens)
+    passed_tokens[...] = jnp.where(upper, low_tokens, high_tokens)
 
     def pieces(side, at):
         start = tokens + at * width
         return arrived[:, side, :, start : start + width].astype(F32)
 
-    total = [jnp.sum(pieces(side, 0), axis=0) for side in range(2)]
-    for side in range(2):
+    for side in range(sides):
+        total = [jnp.sum(pieces(side, 0), axis=0)]
         for at, block in enumerate((run, step)):
             split = pieces(side, 1 + at).reshape(senders // (2 * block), 2, block, rows, width)
-            halves = jnp.sum(jnp.sum(split, axis=2), axis=0)
-            total.extend([halves[side], halves[1 - side]])
+            even, odd = jnp.sum(jnp.sum(split, axis=2), axis=0)
+            total.extend([jnp.where(upper, odd, even), jnp.where(upper, even, odd)])
         total.append(jnp.sum(pieces(side, 3), axis=0))
-    total = jnp.concatenate(total, axis=1).astype(BF)
-    spread[...] = jnp.broadcast_to(total[None], spread.shape)
-
-
-def write_half(terms, side, refs, stages, semaphores, scaling):
+        total = jnp.concatenate(total, axis=1).astype(BF)
+        spread[:, side] = jnp.broadcast_to(total[None], (senders, rows, total.shape[1]))
+
+
+def write_heads(terms, heads, refs, stages, semaphores, scaling):
     projection, output, pool = refs
     tall, square = stages
     wide = pool.shape[0]
@@ -302,37 +306,37 @@
     across = 3 * part // 2
     copies = []
 
-    def lanes(start, count):
-        values = terms[:, :, start : start + count].astype(F32) * scaling
-        return values.reshape(terms.shape[0] * terms.shape[1], count)
+    def lanes(side, start, count):
+        values = terms[:, side, :, start : start + count].astype(F32) * scaling
+        return values.reshape(wide, count)
 
     def send(stage, target):
         copies.append(pltpu.make_async_copy(stage, target, semaphores.at[len(copies)]))
         copies[-1].start()
 
-    for heads in range(2):
-        start = 2 * width + heads * (across + 2 * width)
+    for side in range(2):
         for k in range(3):
-            columns = [half * across + k * width for half in range(2)]
-            places = [column // part * wide + heads * part + column % part for column in columns]
-            target = pl.multiple_of(jnp.where(side == 0, places[0], places[1]), width)
-            stage = tall.at[3 * heads + k]
-            stage[...] = lanes(start + k * width, width)
+            column = side * across + k * width
+            place = column // part * wide + column % part
+            target = pl.multiple_of(place + heads * part, width)
+            stage = tall.at[3 * side + k]
+            stage[...] = lanes(side, width + k * width, width)
             send(stage, projection.at[:, pl.ds(target, width)])
-        for at, ref in enumerate((output, pool)):
-            block = lanes(start + across + at * width, width)
-            stage = square.at[2 * heads + at]
-            stage[:, :width] = block[:part]
-            stage[:, width:] = block[part:]
-            target = pl.multiple_of(side * part, part)
-            send(stage, ref.at[heads * part : (heads + 1) * part, pl.ds(target, part)])
+    for at, ref in enumerate((output, pool)):
+        stage = square.at[at]
+        for side in range(2):
+            block = lanes(side, width + across + at * width, width)
+            for k in range(2):
+                first = (2 * side + k) * width
+                stage[:, first : first + width] = block[k * part : (k + 1) * part]
+        send(stage, ref.at[pl.ds(pl.multiple_of(heads * part, part), part), :])
     return copies
 
 
 def own_sums_kernel(own, projection, output, pool, tall, square, semaphores, *, scaling):
-    side = lax.axis_index("grp")
     refs = (projection, output, pool)
-    for copy in write_half(own, side, refs, (tall, square), semaphores, scaling):
+    heads = lax.axis_index("grp")
+    for copy in write_heads(own, heads, refs, (tall, square), semaphores, scaling):
         copy.wait()
 
 
@@ -356,18 +360,17 @@
     *,
     scaling,
 ):
-    side = 1 - lax.axis_index("grp")
+    heads = 1 - lax.axis_index("grp")
     refs = (projection, output, pool)
-    copies = write_half(other, side, refs, (tall, square), semaphores, scaling)
+    copies = write_heads(other, heads, refs, (tall, square), semaphores, scaling)
     features = fine_output.shape[0]
     width = features // 2
-    for heads in range(2):
-        start = heads * width
-        here, there = own[:, :, start : start + width], other[:, :, start : start + width]
-        for half in range(2):
-            values = jnp.where(side == half, there, here).astype(F32) * scaling
-            block = values.reshape(own.shape[0] * own.shape[1], width)
-            column = (2 * heads + half) * features
+    for at in range(2):
+        for side in range(2):
+            here, there = own[:, side, :, :width], other[:, side, :, :width]
+            values = jnp.where(heads == at, there, here).astype(F32) * scaling
+            block = values.reshape(2 * features, width)
+            column = (2 * at + side) * features
             for k in range(2):
                 piece = block[k * features : (k + 1) * features]
                 if column < 3 * features:
@@ -387,8 +390,8 @@
     shapes = [(wide, 3 * wide), (wide, wide), (wide, wide)]
     stages = [
         pltpu.VMEM((6, wide, width), F32),
-        pltpu.VMEM((4, part, part), F32),
-        pltpu.SemaphoreType.DMA((10,)),
+        pltpu.VMEM((2, part, wide), F32),
+        pltpu.SemaphoreType.DMA((8,)),
     ]
     limits = pltpu.CompilerParams(vmem_limit_bytes=16 * 1024 * 1024)
     firsts = pl.pallas_call(
@@ -496,10 +499,15 @@
     send[:, :, :, send.shape[3] - coarse.shape[3] :] = coarse[...]
 
 
-def take_kernel(arrived, slots, rows_out):
-    place = one_hot(slots[...], slots.shape[1] * 2)
-    rows = arrived[...].reshape(place.shape[0], arrived.shape[-1])
-    rows_out[...] = mm(place, rows, (0, 0)).astype(BF)
+def take_parts_kernel(own, got, slots, rows_out):
+    upper = lax.axis_index("grp") == 1
+    senders, rows, features = own.shape
+    shape = (senders, 1, rows, features)
+    first = jnp.where(upper, got[...], own[...]).astype(F32).reshape(shape)
+    second = jnp.where(upper, own[...], got[...]).astype(F32).reshape(shape)
+    both = jnp.concatenate([first, second], axis=1).reshape(2 * senders * rows, features)
+    place = one_hot(slots[...], both.shape[0])
+    rows_out[...] = mm(place, both.astype(BF), (0, 0)).astype(BF)
 
 
 VMEM = pl.BlockSpec(memory_space=pltpu.VMEM)
@@ -770,17 +778,25 @@
         (tokens, fine_kept, fine_got, coarse_part),
         (Near((*blocks, across)),),
     )
-    arrived = spread_blocks(send.reshape(devices, slots // devices, across), ("pts", "grp"))
-    (spread,) = call(
+    arrived = spread_blocks(send, "pts")
+    spread, own_tokens, passed_tokens = call(
         functools.partial(sum_kernel, tokens=features, run=run, step=step),
-        (arrived.reshape(send.shape),),
-        (Near((owners, slots // devices, features + 5 * wide // 2)),),
+        (arrived,),
+        (
+            Near((*blocks, 3 * wide // 2)),
+            Near((owners, slots // devices, features)),
+            Near((owners, slots // devices, features)),
+        ),
     )
     own_sums = spread_blocks(spread, "pts")
+    own_sums, own_tokens, passed_tokens = lax.optimization_barrier(
+        (own_sums, own_tokens, passed_tokens)
+    )
+    other_sums = exchange(own_sums)
+    got_tokens = exchange(passed_tokens)
     (points_gradient,) = call(
-        take_kernel, (arrived[:, :, :features], send_slot), (Near((count, features)),)
-    )
-    other_sums = exchange(own_sums)
+        take_parts_kernel, (own_tokens, got_tokens, send_slot), (Near((count, features)),)
+    )
     sums = write_sums(own_sums, other_sums, features, wide, scaling)
     return (coarse_result, points_gradient, *sums)
 

time: 151 us -> 153 us (1.013)
  waiting for transfers between devices: 3.19 us -> 4.82 us
    ppermute x5 -> x6, waiting for transfers between devices: 2.09 us -> 3.71 us  [exchange(): return lax.ppermute(values, 'grp', [(0, 1), (1, 0)])]
    ppermute x5 -> x6, starting transfers between devices: 6.4 us -> 6.19 us  [exchange(): return lax.ppermute(values, 'grp', [(0, 1), (1, 0)])]
  transfers between devices with their start and end apart: 7 -> 8, of which waited for: 5 -> 5; matrix products, arithmetic and copies ran while one was open for 0% -> 0% of each run, Pallas kernels for 5% -> 5%
where the time goes in v14:
time: 153 us
  blocking collectives  116 us (76%)
  Pallas kernels  23.2 us (15%)
  starting transfers between devices  8.01 us (5%)
  waiting for transfers between devices  4.82 us (3%)
    all_to_all x5, blocking collectives, spread_blocks(): return lax.all_to_all(values, axes, split_axis=0, concat_axis=0, tiled=True)  116 us
    pallas_call x12, Pallas kernels, call(): pl.pallas_call(body, out_shape=[(pltpu.HBM if out.far else jax.ShapeDtype...  19.7 us
    ppermute x6, starting transfers between devices, exchange(): return lax.ppermute(values, 'grp', [(0, 1), (1, 0)])  6.19 us
    ppermute x6, waiting for transfers between devices, exchange(): return lax.ppermute(values, 'grp', [(0, 1), (1, 0)])  3.71 us
  transfers between devices with their start and end apart: 8, of which 5 were waited for; matrix products, arithmetic and copies ran while one was open for 0% of the time, Pallas kernels for 5%

profile of v14, /device:TPU:1, one launch (start us, length us, event | category | flops | bytes accessed | tf_op | source)
XLA Modules:
  0.0 152.8 jit_solution(13537285836507285751)
XLA Ops:
  0.6 2.2 %shard_map.153 = (bf16[1024,256]{1,0:T(8,128)(2,1)S(1)}, s32[1,512]{1,0:T(1,128)S(1)}, s32[1,512]{1,0:T(1,128)S(1)}, s32[1,512]{1,0:T(1,128)S(1)}, f32[1,512]{1,0:T(1,128)S(1)}) custom-call(s32[1,512]{1,0:T(1,128)} %bitcast.15, s32[1,512]{1,0:T(1,128)} %bitcast.16, s32[1,256]{1,0:T(1,128)} %bitcast.17, bf16[512,256]{1,0:T(8,128)(2,1)} %refs_3_.4), custom_call_target="tpu_custom_call" | custom-call | tf_op jit(solution)/shard_map/pallas_call | solution.py:595
  2.8 25.0 %all_to_all.25 = bf16[128,8,256]{2,1,0:T(8,128)(2,1)S(1)} all-to-all(bf16[128,8,256]{2,1,0:T(8,128)(2,1)S(1)} %bitcast.14), channel_id=1, replica_groups=mesh['pts'=64,'grp'=2] {'pts','grp'}, dimensions={0} | all-to-all | bytes 1048576 | tf_op jit(solution)/shard_map/all_to_all | solution.py:613
  27.8 3.4 %shard_map.154 = (bf16[1024,256]{1,0:T(8,128)(2,1)S(1)}, bf16[512,256]{1,0:T(8,128)(2,1)S(1)}, bf16[512,768]{1,0:T(8,128)(2,1)S(1)}, bf16[512,256]{1,0:T(8,128)(2,1)S(1)}, bf16[8,256,256]{2,1,0:T(8,128)(2,1)S(1)}) custom-call(bf16[1024,256]{1,0:T(8,128)(2,1)S(1)} %bitcast.10, s32[1,512]{1,0:T(1,128)S(1)} %get-tuple-element.55.refs_1_, ...), custom_call_target="tpu_custom_call" | custom-call | tf_op jit(solution)/shard_map/pallas_call | solution.py:595
  31.2 18.1 %all_to_all.26 = bf16[128,8,256]{2,1,0:T(8,128)(2,1)S(1)} all-to-all(bf16[128,8,256]{2,1,0:T(8,128)(2,1)S(1)} %bitcast.13), channel_id=1, replica_groups=mesh['pts'=64,'grp'=2] {'pts','grp'}, dimensions={0} | all-to-all | bytes 1048576 | tf_op jit(solution)/shard_map/all_to_all | solution.py:613
  49.3 0.5 shard_map.155.refs_0_.refs_3_
  49.8 0.0 copy-start.1
  49.8 1.2 collective-permute-start
  51.1 1.5 %collective-permute-done.refs_1_.refs_4_ = bf16[256,1024]{1,0:T(8,128)(2,1)S(1)} collective-permute-done((bf16[256,1024]{1,0:T(8,128)(2,1)S(1)}, bf16[256,1024]{1,0:T(8,128)(2,1)S(1)}, u32[]{:S(2)}, u32[]{:S(2)}) %collective-permute-start) | collective-permute-done | bytes 524320 | tf_op jit(solution)/shard_map/ppermute | solution.py:609
  52.6 5.3 %shard_map.156 = (bf16[256,512]{1,0:T(8,128)(2,1)S(1)}, bf16[256,1024]{1,0:T(8,128)(2,1)S(1)}, bf16[256,1024]{1,0:T(8,128)(2,1)S(1)}, bf16[512,512]{1,0:T(8,128)(2,1)S(1)}) custom-call(bf16[256,1024]{1,0:T(8,128)(2,1)S(1)} %shard_map.155.refs_0_.refs_3_, bf16[256,1024]{1,0:T(8,128)(2,1)S(1)} %collective-permute-done.refs_1_.refs_4_, ...), custom_call_target="tpu_custom_call" | custom-call | tf_op jit(solution)/shard_map/pallas_call | solution.py:595
  57.9 0.6 collective-permute-start.1
  58.5 0.4 shard_map.157
  59.0 0.7 shard_map.158
  59.7 0.3 collective-permute-done.1.refs_3_
  60.1 1.2 shard_map.159
  61.3 17.3 %all_to_all.27 = bf16[128,8,256]{2,1,0:T(8,128)(2,1)S(1)} all-to-all(bf16[128,8,256]{2,1,0:T(8,128)(2,1)S(1)} %bitcast.12), channel_id=1, replica_groups=mesh['pts'=64,'grp'=2] {'pts','grp'}, dimensions={0} | all-to-all | bytes 1048576 | tf_op jit(solution)/shard_map/all_to_all | solution.py:613
  78.6 0.9 collective-permute-start.3
  79.5 1.0 collective-permute-start.4
  80.5 0.5 collective-permute-start.5
  81.0 3.7 %shard_map.160 = (bf16[64,2,8,256]{3,2,1,0:T(8,128)(2,1)S(1)}, f32[256,512]{1,0:T(8,128)S(1)}, bf16[256,512]{1,0:T(8,128)(2,1)S(1)}) custom-call(bf16[1024,256]{1,0:T(8,128)(2,1)S(1)} %bitcast.11, s32[1,512]{1,0:T(1,128)S(1)} %get-tuple-element.55.refs_1_, bf16[512,256]{1,0:T(8,128)(2,1)S(1)} %get-tuple-element.75.refs_2_, ...), custom_call_target="tpu_custom_call" | custom-call | tf_op jit(solution)/shard_map/pallas_call | solution.py:595
  84.7 0.1 collective-permute-start.2
  84.8 0.2 collective-permute-done.3.refs_1_
  85.1 0.9 collective-permute-done.4.refs_2_
  85.9 0.6 shard_map.161.refs_3_
  86.5 0.2 shard_map.162
  86.7 28.0 %all_to_all.28.refs_0_ = bf16[64,2,8,768]{3,2,1,0:T(8,128)(2,1)S(1)} all-to-all(bf16[64,2,8,768]{3,2,1,0:T(8,128)(2,1)S(1)} %shard_map.162), channel_id=1, replica_groups=mesh['pts'=64,'grp'=2] {'pts'}, dimensions={0} | all-to-all | bytes 3145728 | tf_op jit(solution)/shard_map/all_to_all | solution.py:613
  114.7 0.3 shard_map.163
  115.0 27.4 %all_to_all.29.own = bf16[64,2,8,768]{3,2,1,0:T(8,128)(2,1)S(1)} all-to-all(bf16[64,2,8,768]{3,2,1,0:T(8,128)(2,1)S(1)} %get-tuple-element.86), channel_id=1, replica_groups=mesh['pts'=64,'grp'=2] {'pts'}, dimensions={0} | all-to-all | bytes 3145728 | tf_op jit(solution)/shard_map/all_to_all | solution.py:613
  142.4 3.7 %collective-permute-start.7 = (bf16[64,2,8,768]{3,2,1,0:T(8,128)(2,1)S(1)}, bf16[64,2,8,768]{3,2,1,0:T(8,128)(2,1)S(1)}, u32[]{:S(2)}, u32[]{:S(2)}) collective-permute-start(bf16[64,2,8,768]{3,2,1,0:T(8,128)(2,1)S(1)} %all_to_all.29.own), channel_id=1, source_target_pairs={{0,1},{1,0},{2,3},{3,2},{4,5},{5,4},{6,7},{7,6},{8,9},{9,8},{10,11... | collective-permute-start | bytes 4718600 | tf_op jit(solution)/shard_map/ppermute | solution.py:609
  146.1 1.6 %shard_map.165 = (f32[512,1536]{1,0:T(8,128)}, f32[512,512]{1,0:T(8,128)}, f32[512,512]{1,0:T(8,128)}) custom-call(bf16[64,2,8,768]{3,2,1,0:T(8,128)(2,1)S(1)} %all_to_all.29.own), custom_call_target="tpu_custom_call" | custom-call | tf_op jit(solution)/shard_map/pallas_call | solution.py:397
  147.7 1.8 %collective-permute-done.6.refs_1_ = bf16[64,8,256]{2,1,0:T(8,128)(2,1)S(1)} collective-permute-done((bf16[64,8,256]{2,1,0:T(8,128)(2,1)S(1)}, bf16[64,8,256]{2,1,0:T(8,128)(2,1)S(1)}, u32[]{:S(2)}, u32[]{:S(2)}) %collective-permute-start.6) | collective-permute-done | bytes 262176 | tf_op jit(solution)/shard_map/ppermute | solution.py:609
  149.5 1.2 shard_map.164
  150.7 1.9 %shard_map.166 = (f32[512,1536]{1,0:T(8,128)}, f32[512,512]{1,0:T(8,128)}, f32[512,512]{1,0:T(8,128)}, f32[256,768]{1,0:T(8,128)}, f32[256,256]{1,0:T(8,128)}) custom-call(bf16[64,2,8,768]{3,2,1,0:T(8,128)(2,1)S(1)} %all_to_all.29.own, ...), custom_call_target="tpu_custom_call", output_to_operand_aliasing={{0}: (2, {}), {1}: (3, {}), {2}: (4, {})} | custom-call | tf_op jit(solution)/shard_map/pallas_call | solution.py:406
  (15 shorter events, 0.0 us)
Async XLA Ops:
  0.6 27.2 %copy-start.3 = (bf16[256,768]{1,0:T(8,128)(2,1)S(1)}, bf16[256,768]{1,0:T(8,128)(2,1)}, u32[]{:S(2)}) copy-start(bf16[256,768]{1,0:T(8,128)(2,1)} %refs_6_.3) | copy-start | bytes 1179652
  2.8 46.5 %copy-start.4 = (bf16[256,512]{1,0:T(8,128)(2,1)S(1)}, bf16[256,512]{1,0:T(8,128)(2,1)}, u32[]{:S(2)}) copy-start(bf16[256,512]{1,0:T(8,128)(2,1)} %refs_4_.5) | copy-start | bytes 786436
  27.8 24.8 %copy-start = (bf16[512,1536]{1,0:T(8,128)(2,1)S(1)}, bf16[512,1536]{1,0:T(8,128)(2,1)}, u32[]{:S(2)}) copy-start(bf16[512,1536]{1,0:T(8,128)(2,1)} %refs_6_.2) | copy-start | bytes 4718596
  27.8 24.8 %copy-start.2 = (bf16[512,512]{1,0:T(8,128)(2,1)S(1)}, bf16[512,512]{1,0:T(8,128)(2,1)}, u32[]{:S(2)}) copy-start(bf16[512,512]{1,0:T(8,128)(2,1)} %refs_5_.1) | copy-start | bytes 1572868
  49.8 8.7 %copy-start.1 = (bf16[512,512]{1,0:T(8,128)(2,1)S(1)}, bf16[512,512]{1,0:T(8,128)(2,1)}, u32[]{:S(2)}) copy-start(bf16[512,512]{1,0:T(8,128)(2,1)} %refs_7_.2) | copy-start | bytes 1572868
  49.8 2.8 %collective-permute-start = (bf16[256,1024]{1,0:T(8,128)(2,1)S(1)}, bf16[256,1024]{1,0:T(8,128)(2,1)S(1)}, u32[]{:S(2)}, u32[]{:S(2)}) collective-permute-start(bf16[256,1024]{1,0:T(8,128)(2,1)S(1)} %shard_map.155.refs_0_.refs_3_), channel_id=1, source_target_pairs={{0,1},{1,0},{2,3},{3,2},{4,5},{5,4},{6,7},{7,6},{8,9},{9,8},{10,11... | collective-permute-start | bytes 1572872 | tf_op jit(solution)/shard_map/ppermute | solution.py:609
  57.9 2.2 %collective-permute-start.1 = (bf16[256,1024]{1,0:T(8,128)(2,1)S(1)}, bf16[256,1024]{1,0:T(8,128)(2,1)S(1)}, u32[]{:S(2)}, u32[]{:S(2)}) collective-permute-start(bf16[256,1024]{1,0:T(8,128)(2,1)S(1)} %get-tuple-element.63.refs_2_), channel_id=1, source_target_pairs={{0,1},{1,0},{2,3},{3,2},{4,5},{5,4},{6,7},{7,6},{8,9},{9,8},{10,11... | collective-permute-start | bytes 1572872 | tf_op jit(solution)/shard_map/ppermute | solution.py:609
  60.1 20.9 %copy-start.5 = (bf16[256,256]{1,0:T(8,128)(2,1)S(1)}, bf16[256,256]{1,0:T(8,128)(2,1)}, u32[]{:S(2)}) copy-start(bf16[256,256]{1,0:T(8,128)(2,1)} %refs_7_.3) | copy-start | bytes 393220
  78.6 6.4 %collective-permute-start.3 = (bf16[64,2,8,128]{3,2,1,0:T(8,128)(2,1)S(1)}, bf16[64,2,8,128]{3,2,1,0:T(8,128)(2,1)S(1)}, u32[]{:S(2)}, u32[]{:S(2)}) collective-permute-start(bf16[64,2,8,128]{3,2,1,0:T(8,128)(2,1)S(1)} %get-tuple-element.83), channel_id=1, source_target_pairs={{0,32},{1,97},{2,34},{3,99},{4,36},{5,101},{6,38},{7,103},{8,40},{... | collective-permute-start | bytes 786440 | tf_op jit(solution)/shard_map/ppermute | solution.py:739
  79.5 6.4 %collective-permute-start.4 = (bf16[64,2,8,128]{3,2,1,0:T(8,128)(2,1)S(1)}, bf16[64,2,8,128]{3,2,1,0:T(8,128)(2,1)S(1)}, u32[]{:S(2)}, u32[]{:S(2)}) collective-permute-start(bf16[64,2,8,128]{3,2,1,0:T(8,128)(2,1)S(1)} %get-tuple-element.84), channel_id=1, source_target_pairs={{0,8},{1,25},{2,10},{3,27},{4,12},{5,29},{6,14},{7,31},{8,0},{9,17... | collective-permute-start | bytes 786440 | tf_op jit(solution)/shard_map/ppermute | solution.py:740
  80.5 5.5 %collective-permute-start.5 = (bf16[256,512]{1,0:T(8,128)(2,1)S(1)}, bf16[256,512]{1,0:T(8,128)(2,1)S(1)}, u32[]{:S(2)}, u32[]{:S(2)}) collective-permute-start(bf16[256,512]{1,0:T(8,128)(2,1)S(1)} %get-tuple-element.85.refs_5_), channel_id=1, source_target_pairs={{0,1},{1,0},{2,3},{3,2},{4,5},{5,4},{6,7},{7,6},{8,9},{9,8},{10,11... | collective-permute-start | bytes 786440 | tf_op jit(solution)/shard_map/ppermute | solution.py:609
  84.7 1.8 %collective-permute-start.2 = (bf16[256,512]{1,0:T(8,128)(2,1)S(1)}, bf16[256,512]{1,0:T(8,128)(2,1)S(1)}, u32[]{:S(2)}, u32[]{:S(2)}) collective-permute-start(bf16[256,512]{1,0:T(8,128)(2,1)S(1)} %get-tuple-element.81), channel_id=1, source_target_pairs={{0,1},{1,0},{2,3},{3,2},{4,5},{5,4},{6,7},{7,6},{8,9},{9,8},{10,11... | collective-permute-start | bytes 786440 | tf_op jit(solution)/shard_map/ppermute | solution.py:609
  142.4 8.3 %collective-permute-start.7 = (bf16[64,2,8,768]{3,2,1,0:T(8,128)(2,1)S(1)}, bf16[64,2,8,768]{3,2,1,0:T(8,128)(2,1)S(1)}, u32[]{:S(2)}, u32[]{:S(2)}) collective-permute-start(bf16[64,2,8,768]{3,2,1,0:T(8,128)(2,1)S(1)} %all_to_all.29.own), channel_id=1, source_target_pairs={{0,1},{1,0},{2,3},{3,2},{4,5},{5,4},{6,7},{7,6},{8,9},{9,8},{10,11... | collective-permute-start | bytes 4718600 | tf_op jit(solution)/shard_map/ppermute | solution.py:609
  146.1 3.4 %collective-permute-start.6 = (bf16[64,8,256]{2,1,0:T(8,128)(2,1)S(1)}, bf16[64,8,256]{2,1,0:T(8,128)(2,1)S(1)}, u32[]{:S(2)}, u32[]{:S(2)}) collective-permute-start(bf16[64,8,256]{2,1,0:T(8,128)(2,1)S(1)} %get-tuple-element.90), channel_id=1, source_target_pairs={{0,1},{1,0},{2,3},{3,2},{4,5},{5,4},{6,7},{7,6},{8,9},{9,8},{10,11... | collective-permute-start | bytes 786440 | tf_op jit(solution)/shard_map/ppermute | solution.py:609

commit v15 on v13

--- a/solution.py
+++ b/solution.py
@@ -145,23 +145,43 @@
     pack[:, wide:] = cotangent[...]
 
 
-def coarse_kernel(
-    own_pack, other_pack, pool, projection, output, coarse, keep, give, unit
-):
-    half_rows, wide = coarse.shape
+def project_rows(joined, cotangent, pool, projection, output):
+    wide = pool.shape[1]
     part = wide // 2
     first = pl.multiple_of(lax.axis_index("grp") * part, part)
-    joined = jnp.concatenate([own_pack[:, :wide], other_pack[:, :wide]], axis=0)
     tokens = mm(joined, pool[...]).astype(BF)
-    coarse[...] = tokens[:half_rows]
     normed, _ = normalize(tokens)
-    unit_rows = normed.astype(BF)
+    unit = normed.astype(BF)
+    rows = [
+        mm(unit, projection[:, pl.ds(at * wide + first, part)]).astype(BF) for at in range(3)
+    ]
+    rows.append(mm(cotangent, output[pl.ds(first, part), :], (1, 1)).astype(BF))
+    return tokens, unit, rows
+
+
+def coarse_own_rows_kernel(own_pack, pool, projection, output, coarse, unit, rows_out):
+    wide = pool.shape[1]
+    tokens, unit_rows, rows = project_rows(
+        own_pack[:, :wide], own_pack[:, wide:], pool, projection, output
+    )
+    coarse[...] = tokens
     unit[...] = unit_rows
-    queries = mm(unit_rows, projection[:, pl.ds(first, part)]).astype(BF)
-    keys = mm(unit_rows, projection[:, pl.ds(wide + first, part)]).astype(BF)
-    values = mm(unit_rows, projection[:, pl.ds(2 * wide + first, part)]).astype(BF)
-    cotangent = jnp.concatenate([own_pack[:, wide:], other_pack[:, wide:]], axis=0)
-    incoming = mm(cotangent, output[pl.ds(first, part), :], (1, 1)).astype(BF)
+    for at, values in enumerate(rows):
+        rows_out[:, at * wide // 2 : (at + 1) * wide // 2] = values
+
+
+def coarse_kernel(other_pack, own_rows, pool, projection, output, keep, give, unit):
+    wide = pool.shape[1]
+    part = wide // 2
+    half_rows = own_rows.shape[0]
+    _, unit_rows, rows = project_rows(
+        other_pack[:, :wide], other_pack[:, wide:], pool, projection, output
+    )
+    unit[...] = unit_rows
+    queries, keys, values, incoming = [
+        jnp.concatenate([own_rows[:, at * part : (at + 1) * part], rows[at]], axis=0)
+        for at in range(4)
+    ]
     queries_turned, incoming_turned = turned(queries), turned(incoming)
     key_parts, value_parts = [], []
 
@@ -239,14 +259,25 @@
 
 
 def coarse_weights_kernel(
-    unit, keep, give, own_pack, other_pack, kept, first_half, second_half, *, strides
+    own_unit,
+    other_unit,
+    keep,
+    give,
+    own_pack,
+    other_pack,
+    kept,
+    first_half,
+    second_half,
+    *,
+    strides,
 ):
     chip, core = lax.axis_index("pts"), lax.axis_index("grp")
-    wide = unit.shape[1]
+    wide = own_unit.shape[1]
     part = wide // 2
+    unit = jnp.concatenate([own_unit[...], other_unit[...]], axis=0)
     stacked = jnp.concatenate([keep[...], give[...]], axis=0)
     cotangent = jnp.concatenate([own_pack[:, wide:], other_pack[:, wide:]], axis=0)
-    projection_term = mm(unit[...], stacked[:, part:], (0, 0))
+    projection_term = mm(unit, stacked[:, part:], (0, 0))
     output_term = mm(stacked[:, :part], cotangent, (0, 0))
     across = projection_term.shape[1] // 2
     width = wide // 4
@@ -474,19 +505,21 @@
     tokens[...] = mm(place, result.astype(BF)).reshape(tokens.shape).astype(BF)
 
 
-def coarse_part_kernel(
-    kept, got_first, got_second, own_pack, other_pack, own_gradient, other_gradient, coarse
-):
+def pool_kernel(own_pack, other_pack, own_gradient, other_gradient, blocks):
+    part = own_gradient.shape[1] // 2
+    first = pl.multiple_of(lax.axis_index("grp") * part, part)
+    term = mm(own_pack[:, pl.ds(first, part)], own_gradient[...], (0, 0))
+    term = term + mm(other_pack[:, pl.ds(first, part)], other_gradient[...], (0, 0))
+    put_quarters(blocks, 0, term)
+
+
+def coarse_part_kernel(kept, got_first, got_second, pool, coarse):
     width = got_first.shape[3]
     for at, got in enumerate((got_first, got_second)):
         lanes = slice(at * width, (at + 1) * width)
         mine = kept[:, :, :, lanes].astype(F32)
         coarse[:, :, :, lanes] = (mine + got[...].astype(F32)).astype(BF)
-    part = own_gradient.shape[1] // 2
-    first = pl.multiple_of(lax.axis_index("grp") * part, part)
-    pool_term = mm(own_pack[:, pl.ds(first, part)], own_gradient[...], (0, 0))
-    pool_term = pool_term + mm(other_pack[:, pl.ds(first, part)], other_gradient[...], (0, 0))
-    put_quarters(coarse, 2 * width, pool_term)
+    coarse[:, :, :, 2 * width :] = pool[...]
 
 
 def assemble_kernel(tokens, fine_kept, fine_got, coarse, send):
@@ -676,21 +709,29 @@
         join_kernel, (arrived, pair_slot, coarse_cotangent), (Near((half_rows, 2 * wide)),)
     )
     other_pack = exchange(own_pack)
-    coarse, keep, give, unit = call(
-        coarse_kernel,
-        (own_pack, other_pack, pool_weight, coarse_projection, Far(coarse_output)),
-        (
+    coarse, own_unit, own_rows = call(
+        coarse_own_rows_kernel,
+        (own_pack, pool_weight, coarse_projection, Far(coarse_output)),
+        (
+            Near((half_rows, wide)),
             Near((half_rows, wide)),
             Near((half_rows, 2 * wide)),
+        ),
+    )
+    keep, give, other_unit = call(
+        coarse_kernel,
+        (other_pack, own_rows, pool_weight, coarse_projection, coarse_output),
+        (
             Near((half_rows, 2 * wide)),
-            Near((count, wide)),
+            Near((half_rows, 2 * wide)),
+            Near((half_rows, wide)),
         ),
     )
     got = exchange(give)
     blocks = (owners, 2, slots // devices)
     kept, first_half, second_half = call(
         functools.partial(coarse_weights_kernel, strides=(run, step)),
-        (unit, keep, give, own_pack, other_pack),
+        (own_unit, other_unit, keep, give, own_pack, other_pack),
         (
             Near((*blocks, wide // 2)),
             Near((*blocks, wide // 4)),
@@ -751,17 +792,14 @@
         scratch=(pltpu.VMEM((count, 3 * features), BF),),
     )
     fine_got = exchange(fine_passed)
+    (pool_part,) = call(
+        pool_kernel,
+        (own_pack, other_pack, coarse_gradient, other_gradient),
+        (Near((*blocks, wide // 4)),),
+    )
     (coarse_part,) = call(
         coarse_part_kernel,
-        (
-            kept,
-            got_first,
-            got_second,
-            own_pack,
-            other_pack,
-            coarse_gradient,
-            other_gradient,
-        ),
+        (kept, got_first, got_second, pool_part),
         (Near((*blocks, 3 * wide // 4)),),
     )
     across = features + wide

time: 151 us -> 150 us (level)
  waiting for transfers between devices: 3.19 us -> 1.64 us
    pallas_call x12 -> x14, Pallas kernels: 19.7 us -> 20.3 us  [call(): pl.pallas_call(body, out_shape=[(pltpu.HBM if out.far else jax.ShapeDtype...]
  transfers between devices with their start and end apart: 7 -> 7, of which waited for: 5 -> 4; matrix products, arithmetic and copies ran while one was open for 0% -> 0% of each run, Pallas kernels for 5% -> 7%
where the time goes in v15:
time: 150 us
  blocking collectives  115 us (77%)
  Pallas kernels  23.9 us (16%)
  starting transfers between devices  8.09 us (5%)
  waiting for transfers between devices  1.64 us (1%)
    all_to_all x5, blocking collectives, spread_blocks(): return lax.all_to_all(values, axes, split_axis=0, concat_axis=0, tiled=True)  115 us
    pallas_call x14, Pallas kernels, call(): pl.pallas_call(body, out_shape=[(pltpu.HBM if out.far else jax.ShapeDtype...  20.3 us
    ppermute x5, starting transfers between devices, exchange(): return lax.ppermute(values, 'grp', [(0, 1), (1, 0)])  6.27 us
  transfers between devices with their start and end apart: 7, of which 4 were waited for; matrix products, arithmetic and copies ran while one was open for 0% of the time, Pallas kernels for 7%

profile of v15, /device:TPU:1, one launch (start us, length us, event | category | flops | bytes accessed | tf_op | source)
XLA Modules:
  0.0 149.9 jit_solution(4375601826884792487)
XLA Ops:
  0.6 2.2 %shard_map.153 = (bf16[1024,256]{1,0:T(8,128)(2,1)S(1)}, s32[1,512]{1,0:T(1,128)S(1)}, s32[1,512]{1,0:T(1,128)S(1)}, s32[1,512]{1,0:T(1,128)S(1)}, f32[1,512]{1,0:T(1,128)S(1)}) custom-call(s32[1,512]{1,0:T(1,128)} %bitcast.19, s32[1,512]{1,0:T(1,128)} %bitcast.20, s32[1,256]{1,0:T(1,128)} %bitcast.21, bf16[512,256]{1,0:T(8,128)(2,1)} %refs_3_.5), custom_call_target="tpu_custom_call" | custom-call | tf_op jit(solution)/shard_map/pallas_call | solution.py:620
  2.8 25.0 %all_to_all.25 = bf16[128,8,256]{2,1,0:T(8,128)(2,1)S(1)} all-to-all(bf16[128,8,256]{2,1,0:T(8,128)(2,1)S(1)} %bitcast.18), channel_id=1, replica_groups=mesh['pts'=64,'grp'=2] {'pts','grp'}, dimensions={0} | all-to-all | bytes 1048576 | tf_op jit(solution)/shard_map/all_to_all | solution.py:638
  27.8 3.4 %shard_map.154 = (bf16[1024,256]{1,0:T(8,128)(2,1)S(1)}, bf16[512,256]{1,0:T(8,128)(2,1)S(1)}, bf16[512,768]{1,0:T(8,128)(2,1)S(1)}, bf16[512,256]{1,0:T(8,128)(2,1)S(1)}, bf16[8,256,256]{2,1,0:T(8,128)(2,1)S(1)}) custom-call(bf16[1024,256]{1,0:T(8,128)(2,1)S(1)} %bitcast.14, s32[1,512]{1,0:T(1,128)S(1)} %get-tuple-element.51.refs_1_, ...), custom_call_target="tpu_custom_call" | custom-call | tf_op jit(solution)/shard_map/pallas_call | solution.py:620
  31.2 18.1 %all_to_all.26 = bf16[128,8,256]{2,1,0:T(8,128)(2,1)S(1)} all-to-all(bf16[128,8,256]{2,1,0:T(8,128)(2,1)S(1)} %bitcast.17), channel_id=1, replica_groups=mesh['pts'=64,'grp'=2] {'pts','grp'}, dimensions={0} | all-to-all | bytes 1048576 | tf_op jit(solution)/shard_map/all_to_all | solution.py:638
  49.3 0.5 shard_map.155.refs_0_.refs_4_
  49.8 1.2 collective-permute-start
  51.1 1.6 %shard_map.156 = (bf16[256,512]{1,0:T(8,128)(2,1)S(1)}, bf16[256,512]{1,0:T(8,128)(2,1)S(1)}, bf16[256,1024]{1,0:T(8,128)(2,1)S(1)}) custom-call(bf16[256,1024]{1,0:T(8,128)(2,1)S(1)} %shard_map.155.refs_0_.refs_4_, bf16[512,512]{1,0:T(8,128)(2,1)S(1)} %copy-done.2, bf16[512,1536]{1,0:T(8,128)(2,1)S(1)} %copy-done, bf16[512,512]{1,0:T(8,128)(2,1)} %refs_7_.2), custom_call_target="tpu_custom_call" | custom-call | tf_op jit(solution)/shard_map/pallas_call | solution.py:620
  52.7 4.4 %shard_map.157 = (bf16[256,1024]{1,0:T(8,128)(2,1)S(1)}, bf16[256,1024]{1,0:T(8,128)(2,1)S(1)}, bf16[256,512]{1,0:T(8,128)(2,1)S(1)}) custom-call(bf16[256,1024]{1,0:T(8,128)(2,1)S(1)} %collective-permute-done.refs_0_.refs_5_.refs_1_, bf16[256,1024]{1,0:T(8,128)(2,1)S(1)} %get-tuple-element.56.refs_1_, bf16[512,512]{1,0:T(8,128)(2,1)S(1)} %copy-done.2, ...), custom_call_target="tpu_custom_call" | custom-call | tf_op jit(solution)/shard_map/pallas_call | solution.py:620
  57.1 0.5 collective-permute-start.1
  57.6 0.4 shard_map.158
  58.0 0.7 shard_map.159
  58.8 0.5 collective-permute-done.1.refs_3_
  59.3 1.2 shard_map.160
  60.5 17.2 %all_to_all.27 = bf16[128,8,256]{2,1,0:T(8,128)(2,1)S(1)} all-to-all(bf16[128,8,256]{2,1,0:T(8,128)(2,1)S(1)} %bitcast.16), channel_id=1, replica_groups=mesh['pts'=64,'grp'=2] {'pts','grp'}, dimensions={0} | all-to-all | bytes 1048576 | tf_op jit(solution)/shard_map/all_to_all | solution.py:638
  77.7 0.9 collective-permute-start.3
  78.6 1.0 collective-permute-start.4
  79.5 0.5 collective-permute-start.5
  80.1 3.7 %shard_map.161 = (bf16[64,2,8,256]{3,2,1,0:T(8,128)(2,1)S(1)}, f32[256,512]{1,0:T(8,128)S(1)}, bf16[256,512]{1,0:T(8,128)(2,1)S(1)}) custom-call(bf16[1024,256]{1,0:T(8,128)(2,1)S(1)} %bitcast.15, s32[1,512]{1,0:T(1,128)S(1)} %get-tuple-element.51.refs_1_, bf16[512,256]{1,0:T(8,128)(2,1)S(1)} %get-tuple-element.73.refs_2_, ...), custom_call_target="tpu_custom_call" | custom-call | tf_op jit(solution)/shard_map/pallas_call | solution.py:620
  83.8 0.1 collective-permute-start.2
  83.9 0.3 shard_map.162.refs_3_
  84.3 0.7 collective-permute-done.4.refs_2_
  85.0 0.2 shard_map.163.refs_3_
  85.2 0.2 collective-permute-done.2.refs_2_
  85.4 0.2 shard_map.164
  85.6 29.6 %all_to_all.28 = bf16[128,8,768]{2,1,0:T(8,128)(2,1)S(1)} all-to-all(bf16[128,8,768]{2,1,0:T(8,128)(2,1)S(1)} %bitcast.12), channel_id=1, replica_groups=mesh['pts'=64,'grp'=2] {'pts','grp'}, dimensions={0} | all-to-all | bytes 3145728 | tf_op jit(solution)/shard_map/all_to_all | solution.py:638
  115.2 0.2 shard_map.166
  115.5 25.3 %all_to_all.29.own = bf16[64,8,1536]{2,1,0:T(8,128)(2,1)S(1)} all-to-all(bf16[64,8,1536]{2,1,0:T(8,128)(2,1)S(1)} %shard_map.166), channel_id=1, replica_groups=mesh['pts'=64,'grp'=2] {'pts'}, dimensions={0} | all-to-all | bytes 3145728 | tf_op jit(solution)/shard_map/all_to_all | solution.py:638
  140.8 3.9 %collective-permute-start.6 = (bf16[64,8,1536]{2,1,0:T(8,128)(2,1)S(1)}, bf16[64,8,1536]{2,1,0:T(8,128)(2,1)S(1)}, u32[]{:S(2)}, u32[]{:S(2)}) collective-permute-start(bf16[64,8,1536]{2,1,0:T(8,128)(2,1)S(1)} %all_to_all.29.own), channel_id=1, source_target_pairs={{0,1},{1,0},{2,3},{3,2},{4,5},{5,4},{6,7},{7,6},{8,9},{9,8},{10,11... | collective-permute-start | bytes 4718600 | tf_op jit(solution)/shard_map/ppermute | solution.py:634
  144.7 1.2 shard_map.165
  145.9 1.6 %shard_map.167 = (f32[512,1536]{1,0:T(8,128)}, f32[512,512]{1,0:T(8,128)}, f32[512,512]{1,0:T(8,128)}) custom-call(bf16[64,8,1536]{2,1,0:T(8,128)(2,1)S(1)} %all_to_all.29.own), custom_call_target="tpu_custom_call" | custom-call | tf_op jit(solution)/shard_map/pallas_call | solution.py:425
  147.5 0.2 collective-permute-done.6.other
  147.7 1.9 %shard_map.168 = (f32[512,1536]{1,0:T(8,128)}, f32[512,512]{1,0:T(8,128)}, f32[512,512]{1,0:T(8,128)}, f32[256,768]{1,0:T(8,128)}, f32[256,256]{1,0:T(8,128)}) custom-call(bf16[64,8,1536]{2,1,0:T(8,128)(2,1)S(1)} %all_to_all.29.own, ...), custom_call_target="tpu_custom_call", output_to_operand_aliasing={{0}: (2, {}), {1}: (3, {}), {2}: (4, {})} | custom-call | tf_op jit(solution)/shard_map/pallas_call | solution.py:434
  (16 shorter events, 0.1 us)
Async XLA Ops:
  0.6 27.2 %copy-start.3 = (bf16[256,768]{1,0:T(8,128)(2,1)S(1)}, bf16[256,768]{1,0:T(8,128)(2,1)}, u32[]{:S(2)}) copy-start(bf16[256,768]{1,0:T(8,128)(2,1)} %refs_6_.3) | copy-start | bytes 1179652
  2.8 46.5 %copy-start.4 = (bf16[256,512]{1,0:T(8,128)(2,1)S(1)}, bf16[256,512]{1,0:T(8,128)(2,1)}, u32[]{:S(2)}) copy-start(bf16[256,512]{1,0:T(8,128)(2,1)} %refs_4_.5) | copy-start | bytes 786436
  27.8 23.3 %copy-start = (bf16[512,1536]{1,0:T(8,128)(2,1)S(1)}, bf16[512,1536]{1,0:T(8,128)(2,1)}, u32[]{:S(2)}) copy-start(bf16[512,1536]{1,0:T(8,128)(2,1)} %refs_6_.2) | copy-start | bytes 4718596
  27.8 23.3 %copy-start.2 = (bf16[512,512]{1,0:T(8,128)(2,1)S(1)}, bf16[512,512]{1,0:T(8,128)(2,1)}, u32[]{:S(2)}) copy-start(bf16[512,512]{1,0:T(8,128)(2,1)} %refs_5_.1) | copy-start | bytes 1572868
  49.8 2.9 %copy-start.1 = (bf16[512,512]{1,0:T(8,128)(2,1)S(1)}, bf16[512,512]{1,0:T(8,128)(2,1)}, u32[]{:S(2)}) copy-start(bf16[512,512]{1,0:T(8,128)(2,1)} %refs_7_.2) | copy-start | bytes 1572868
  49.8 2.9 %collective-permute-start = (bf16[256,1024]{1,0:T(8,128)(2,1)S(1)}, bf16[256,1024]{1,0:T(8,128)(2,1)S(1)}, u32[]{:S(2)}, u32[]{:S(2)}) collective-permute-start(bf16[256,1024]{1,0:T(8,128)(2,1)S(1)} %shard_map.155.refs_0_.refs_4_), channel_id=1, source_target_pairs={{0,1},{1,0},{2,3},{3,2},{4,5},{5,4},{6,7},{7,6},{8,9},{9,8},{10,11... | collective-permute-start | bytes 1572872 | tf_op jit(solution)/shard_map/ppermute | solution.py:634
  57.1 2.2 %collective-permute-start.1 = (bf16[256,1024]{1,0:T(8,128)(2,1)S(1)}, bf16[256,1024]{1,0:T(8,128)(2,1)S(1)}, u32[]{:S(2)}, u32[]{:S(2)}) collective-permute-start(bf16[256,1024]{1,0:T(8,128)(2,1)S(1)} %get-tuple-element.60.refs_3_), channel_id=1, source_target_pairs={{0,1},{1,0},{2,3},{3,2},{4,5},{5,4},{6,7},{7,6},{8,9},{9,8},{10,11... | collective-permute-start | bytes 1572872 | tf_op jit(solution)/shard_map/ppermute | solution.py:634
  59.3 20.8 %copy-start.5 = (bf16[256,256]{1,0:T(8,128)(2,1)S(1)}, bf16[256,256]{1,0:T(8,128)(2,1)}, u32[]{:S(2)}) copy-start(bf16[256,256]{1,0:T(8,128)(2,1)} %refs_7_.3) | copy-start | bytes 393220
  77.7 6.5 %collective-permute-start.3 = (bf16[64,2,8,128]{3,2,1,0:T(8,128)(2,1)S(1)}, bf16[64,2,8,128]{3,2,1,0:T(8,128)(2,1)S(1)}, u32[]{:S(2)}, u32[]{:S(2)}) collective-permute-start(bf16[64,2,8,128]{3,2,1,0:T(8,128)(2,1)S(1)} %get-tuple-element.81), channel_id=1, source_target_pairs={{0,32},{1,97},{2,34},{3,99},{4,36},{5,101},{6,38},{7,103},{8,40},{... | collective-permute-start | bytes 786440 | tf_op jit(solution)/shard_map/ppermute | solution.py:772
  78.6 6.4 %collective-permute-start.4 = (bf16[64,2,8,128]{3,2,1,0:T(8,128)(2,1)S(1)}, bf16[64,2,8,128]{3,2,1,0:T(8,128)(2,1)S(1)}, u32[]{:S(2)}, u32[]{:S(2)}) collective-permute-start(bf16[64,2,8,128]{3,2,1,0:T(8,128)(2,1)S(1)} %get-tuple-element.82), channel_id=1, source_target_pairs={{0,8},{1,25},{2,10},{3,27},{4,12},{5,29},{6,14},{7,31},{8,0},{9,17... | collective-permute-start | bytes 786440 | tf_op jit(solution)/shard_map/ppermute | solution.py:773
  79.5 4.4 %collective-permute-start.5 = (bf16[256,512]{1,0:T(8,128)(2,1)S(1)}, bf16[256,512]{1,0:T(8,128)(2,1)S(1)}, u32[]{:S(2)}, u32[]{:S(2)}) collective-permute-start(bf16[256,512]{1,0:T(8,128)(2,1)S(1)} %get-tuple-element.83.refs_2_), channel_id=1, source_target_pairs={{0,1},{1,0},{2,3},{3,2},{4,5},{5,4},{6,7},{7,6},{8,9},{9,8},{10,11... | collective-permute-start | bytes 786440 | tf_op jit(solution)/shard_map/ppermute | solution.py:634
  83.8 1.6 %collective-permute-start.2 = (bf16[256,512]{1,0:T(8,128)(2,1)S(1)}, bf16[256,512]{1,0:T(8,128)(2,1)S(1)}, u32[]{:S(2)}, u32[]{:S(2)}) collective-permute-start(bf16[256,512]{1,0:T(8,128)(2,1)S(1)} %get-tuple-element.79), channel_id=1, source_target_pairs={{0,1},{1,0},{2,3},{3,2},{4,5},{5,4},{6,7},{7,6},{8,9},{9,8},{10,11... | collective-permute-start | bytes 786440 | tf_op jit(solution)/shard_map/ppermute | solution.py:634
  140.8 6.9 %collective-permute-start.6 = (bf16[64,8,1536]{2,1,0:T(8,128)(2,1)S(1)}, bf16[64,8,1536]{2,1,0:T(8,128)(2,1)S(1)}, u32[]{:S(2)}, u32[]{:S(2)}) collective-permute-start(bf16[64,8,1536]{2,1,0:T(8,128)(2,1)S(1)} %all_to_all.29.own), channel_id=1, source_target_pairs={{0,1},{1,0},{2,3},{3,2},{4,5},{5,4},{6,7},{7,6},{8,9},{9,8},{10,11... | collective-permute-start | bytes 4718600 | tf_op jit(solution)/shard_map/ppermute | solution.py:634

commit v16 on v15

--- a/solution.py
+++ b/solution.py
@@ -195,9 +195,12 @@
         key, value = keys[:, lanes], values[:, lanes]
         query = queries[:, lanes] * jnp.asarray(HD ** (-0.5), BF)
         head_weights = softmax_rows(mm(stack_heads(query, 2), key, (1, 1)))
-        against = mm(stack_heads(incoming[:, lanes], 2), value, (1, 1))
-        slopes = slopes_of(head_weights, against)
-        put(pair * PAIR, unstack_heads(mm(head_weights, value), 2).astype(BF))
+        entering = stack_heads(incoming[:, lanes], 2)
+        mixed = mm(head_weights, value)
+        put(pair * PAIR, unstack_heads(mixed, 2).astype(BF))
+        diagonal = jnp.sum(entering.astype(F32) * mixed, axis=-1, keepdims=True)
+        against = mm(entering, value, (1, 1))
+        slopes = (head_weights.astype(F32) * (against - diagonal)).astype(BF)
         query_part = unstack_heads(mm(slopes, key), 2) * HD ** (-0.5)
         put(part + pair * PAIR, query_part.astype(BF))
         for half in range(2):

time: 150 us -> 150 us (level)
  no operation moved by 1% of the time
where the time goes in v16:
time: 150 us
  blocking collectives  115 us (77%)
  Pallas kernels  24.1 us (16%)
  starting transfers between devices  8.09 us (5%)
  waiting for transfers between devices  1.64 us (1%)
    all_to_all x5, blocking collectives, spread_blocks(): return lax.all_to_all(values, axes, split_axis=0, concat_axis=0, tiled=True)  115 us
    pallas_call x14, Pallas kernels, call(): pl.pallas_call(body, out_shape=[(pltpu.HBM if out.far else jax.ShapeDtype...  20.5 us
    ppermute x5, starting transfers between devices, exchange(): return lax.ppermute(values, 'grp', [(0, 1), (1, 0)])  6.27 us
  transfers between devices with their start and end apart: 7, of which 4 were waited for; matrix products, arithmetic and copies ran while one was open for 0% of the time, Pallas kernels for 7%

profile of v16, /device:TPU:1, one launch (start us, length us, event | category | flops | bytes accessed | tf_op | source)
XLA Modules:
  0.0 150.0 jit_solution(14493551494592268673)
XLA Ops:
  0.6 2.2 %shard_map.153 = (bf16[1024,256]{1,0:T(8,128)(2,1)S(1)}, s32[1,512]{1,0:T(1,128)S(1)}, s32[1,512]{1,0:T(1,128)S(1)}, s32[1,512]{1,0:T(1,128)S(1)}, f32[1,512]{1,0:T(1,128)S(1)}) custom-call(s32[1,512]{1,0:T(1,128)} %bitcast.19, s32[1,512]{1,0:T(1,128)} %bitcast.20, s32[1,256]{1,0:T(1,128)} %bitcast.21, bf16[512,256]{1,0:T(8,128)(2,1)} %refs_3_.5), custom_call_target="tpu_custom_call" | custom-call | tf_op jit(solution)/shard_map/pallas_call | solution.py:623
  2.8 25.0 %all_to_all.25 = bf16[128,8,256]{2,1,0:T(8,128)(2,1)S(1)} all-to-all(bf16[128,8,256]{2,1,0:T(8,128)(2,1)S(1)} %bitcast.18), channel_id=1, replica_groups=mesh['pts'=64,'grp'=2] {'pts','grp'}, dimensions={0} | all-to-all | bytes 1048576 | tf_op jit(solution)/shard_map/all_to_all | solution.py:641
  27.8 3.4 %shard_map.154 = (bf16[1024,256]{1,0:T(8,128)(2,1)S(1)}, bf16[512,256]{1,0:T(8,128)(2,1)S(1)}, bf16[512,768]{1,0:T(8,128)(2,1)S(1)}, bf16[512,256]{1,0:T(8,128)(2,1)S(1)}, bf16[8,256,256]{2,1,0:T(8,128)(2,1)S(1)}) custom-call(bf16[1024,256]{1,0:T(8,128)(2,1)S(1)} %bitcast.14, s32[1,512]{1,0:T(1,128)S(1)} %get-tuple-element.51.refs_1_, ...), custom_call_target="tpu_custom_call" | custom-call | tf_op jit(solution)/shard_map/pallas_call | solution.py:623
  31.2 18.1 %all_to_all.26 = bf16[128,8,256]{2,1,0:T(8,128)(2,1)S(1)} all-to-all(bf16[128,8,256]{2,1,0:T(8,128)(2,1)S(1)} %bitcast.17), channel_id=1, replica_groups=mesh['pts'=64,'grp'=2] {'pts','grp'}, dimensions={0} | all-to-all | bytes 1048576 | tf_op jit(solution)/shard_map/all_to_all | solution.py:641
  49.3 0.5 shard_map.155.refs_0_.refs_4_
  49.8 1.2 collective-permute-start
  51.1 1.6 %shard_map.156 = (bf16[256,512]{1,0:T(8,128)(2,1)S(1)}, bf16[256,512]{1,0:T(8,128)(2,1)S(1)}, bf16[256,1024]{1,0:T(8,128)(2,1)S(1)}) custom-call(bf16[256,1024]{1,0:T(8,128)(2,1)S(1)} %shard_map.155.refs_0_.refs_4_, bf16[512,512]{1,0:T(8,128)(2,1)S(1)} %copy-done.2, bf16[512,1536]{1,0:T(8,128)(2,1)S(1)} %copy-done, bf16[512,512]{1,0:T(8,128)(2,1)} %refs_7_.2), custom_call_target="tpu_custom_call" | custom-call | tf_op jit(solution)/shard_map/pallas_call | solution.py:623
  52.7 4.5 %shard_map.157 = (bf16[256,1024]{1,0:T(8,128)(2,1)S(1)}, bf16[256,1024]{1,0:T(8,128)(2,1)S(1)}, bf16[256,512]{1,0:T(8,128)(2,1)S(1)}) custom-call(bf16[256,1024]{1,0:T(8,128)(2,1)S(1)} %collective-permute-done.refs_0_.refs_5_.refs_1_, bf16[256,1024]{1,0:T(8,128)(2,1)S(1)} %get-tuple-element.56.refs_1_, bf16[512,512]{1,0:T(8,128)(2,1)S(1)} %copy-done.2, ...), custom_call_target="tpu_custom_call" | custom-call | tf_op jit(solution)/shard_map/pallas_call | solution.py:623
  57.3 0.5 collective-permute-start.1
  57.8 0.4 shard_map.158
  58.2 0.7 shard_map.159
  59.0 0.5 collective-permute-done.1.refs_3_
  59.4 1.2 shard_map.160
  60.7 17.2 %all_to_all.27 = bf16[128,8,256]{2,1,0:T(8,128)(2,1)S(1)} all-to-all(bf16[128,8,256]{2,1,0:T(8,128)(2,1)S(1)} %bitcast.16), channel_id=1, replica_groups=mesh['pts'=64,'grp'=2] {'pts','grp'}, dimensions={0} | all-to-all | bytes 1048576 | tf_op jit(solution)/shard_map/all_to_all | solution.py:641
  77.9 0.9 collective-permute-start.3
  78.8 1.0 collective-permute-start.4
  79.7 0.5 collective-permute-start.5
  80.3 3.7 %shard_map.161 = (bf16[64,2,8,256]{3,2,1,0:T(8,128)(2,1)S(1)}, f32[256,512]{1,0:T(8,128)S(1)}, bf16[256,512]{1,0:T(8,128)(2,1)S(1)}) custom-call(bf16[1024,256]{1,0:T(8,128)(2,1)S(1)} %bitcast.15, s32[1,512]{1,0:T(1,128)S(1)} %get-tuple-element.51.refs_1_, bf16[512,256]{1,0:T(8,128)(2,1)S(1)} %get-tuple-element.73.refs_2_, ...), custom_call_target="tpu_custom_call" | custom-call | tf_op jit(solution)/shard_map/pallas_call | solution.py:623
  84.0 0.1 collective-permute-start.2
  84.1 0.3 shard_map.162.refs_3_
  84.5 0.7 collective-permute-done.4.refs_2_
  85.2 0.2 shard_map.163.refs_3_
  85.4 0.2 collective-permute-done.2.refs_2_
  85.6 0.2 shard_map.164
  85.8 29.6 %all_to_all.28 = bf16[128,8,768]{2,1,0:T(8,128)(2,1)S(1)} all-to-all(bf16[128,8,768]{2,1,0:T(8,128)(2,1)S(1)} %bitcast.12), channel_id=1, replica_groups=mesh['pts'=64,'grp'=2] {'pts','grp'}, dimensions={0} | all-to-all | bytes 3145728 | tf_op jit(solution)/shard_map/all_to_all | solution.py:641
  115.4 0.2 shard_map.166
  115.7 25.3 %all_to_all.29.own = bf16[64,8,1536]{2,1,0:T(8,128)(2,1)S(1)} all-to-all(bf16[64,8,1536]{2,1,0:T(8,128)(2,1)S(1)} %shard_map.166), channel_id=1, replica_groups=mesh['pts'=64,'grp'=2] {'pts'}, dimensions={0} | all-to-all | bytes 3145728 | tf_op jit(solution)/shard_map/all_to_all | solution.py:641
  141.0 3.9 %collective-permute-start.6 = (bf16[64,8,1536]{2,1,0:T(8,128)(2,1)S(1)}, bf16[64,8,1536]{2,1,0:T(8,128)(2,1)S(1)}, u32[]{:S(2)}, u32[]{:S(2)}) collective-permute-start(bf16[64,8,1536]{2,1,0:T(8,128)(2,1)S(1)} %all_to_all.29.own), channel_id=1, source_target_pairs={{0,1},{1,0},{2,3},{3,2},{4,5},{5,4},{6,7},{7,6},{8,9},{9,8},{10,11... | collective-permute-start | bytes 4718600 | tf_op jit(solution)/shard_map/ppermute | solution.py:637
  144.9 1.2 shard_map.165
  146.1 1.6 %shard_map.167 = (f32[512,1536]{1,0:T(8,128)}, f32[512,512]{1,0:T(8,128)}, f32[512,512]{1,0:T(8,128)}) custom-call(bf16[64,8,1536]{2,1,0:T(8,128)(2,1)S(1)} %all_to_all.29.own), custom_call_target="tpu_custom_call" | custom-call | tf_op jit(solution)/shard_map/pallas_call | solution.py:428
  147.7 0.2 collective-permute-done.6.other
  147.9 1.9 %shard_map.168 = (f32[512,1536]{1,0:T(8,128)}, f32[512,512]{1,0:T(8,128)}, f32[512,512]{1,0:T(8,128)}, f32[256,768]{1,0:T(8,128)}, f32[256,256]{1,0:T(8,128)}) custom-call(bf16[64,8,1536]{2,1,0:T(8,128)(2,1)S(1)} %all_to_all.29.own, ...), custom_call_target="tpu_custom_call", output_to_operand_aliasing={{0}: (2, {}), {1}: (3, {}), {2}: (4, {})} | custom-call | tf_op jit(solution)/shard_map/pallas_call | solution.py:437
  (16 shorter events, 0.1 us)
Async XLA Ops:
  0.6 27.2 %copy-start.3 = (bf16[256,768]{1,0:T(8,128)(2,1)S(1)}, bf16[256,768]{1,0:T(8,128)(2,1)}, u32[]{:S(2)}) copy-start(bf16[256,768]{1,0:T(8,128)(2,1)} %refs_6_.3) | copy-start | bytes 1179652
  2.8 46.5 %copy-start.4 = (bf16[256,512]{1,0:T(8,128)(2,1)S(1)}, bf16[256,512]{1,0:T(8,128)(2,1)}, u32[]{:S(2)}) copy-start(bf16[256,512]{1,0:T(8,128)(2,1)} %refs_4_.5) | copy-start | bytes 786436
  27.8 23.3 %copy-start = (bf16[512,1536]{1,0:T(8,128)(2,1)S(1)}, bf16[512,1536]{1,0:T(8,128)(2,1)}, u32[]{:S(2)}) copy-start(bf16[512,1536]{1,0:T(8,128)(2,1)} %refs_6_.2) | copy-start | bytes 4718596
  27.8 23.3 %copy-start.2 = (bf16[512,512]{1,0:T(8,128)(2,1)S(1)}, bf16[512,512]{1,0:T(8,128)(2,1)}, u32[]{:S(2)}) copy-start(bf16[512,512]{1,0:T(8,128)(2,1)} %refs_5_.1) | copy-start | bytes 1572868
  49.8 2.9 %copy-start.1 = (bf16[512,512]{1,0:T(8,128)(2,1)S(1)}, bf16[512,512]{1,0:T(8,128)(2,1)}, u32[]{:S(2)}) copy-start(bf16[512,512]{1,0:T(8,128)(2,1)} %refs_7_.2) | copy-start | bytes 1572868
  49.8 2.9 %collective-permute-start = (bf16[256,1024]{1,0:T(8,128)(2,1)S(1)}, bf16[256,1024]{1,0:T(8,128)(2,1)S(1)}, u32[]{:S(2)}, u32[]{:S(2)}) collective-permute-start(bf16[256,1024]{1,0:T(8,128)(2,1)S(1)} %shard_map.155.refs_0_.refs_4_), channel_id=1, source_target_pairs={{0,1},{1,0},{2,3},{3,2},{4,5},{5,4},{6,7},{7,6},{8,9},{9,8},{10,11... | collective-permute-start | bytes 1572872 | tf_op jit(solution)/shard_map/ppermute | solution.py:637
  57.3 2.2 %collective-permute-start.1 = (bf16[256,1024]{1,0:T(8,128)(2,1)S(1)}, bf16[256,1024]{1,0:T(8,128)(2,1)S(1)}, u32[]{:S(2)}, u32[]{:S(2)}) collective-permute-start(bf16[256,1024]{1,0:T(8,128)(2,1)S(1)} %get-tuple-element.60.refs_3_), channel_id=1, source_target_pairs={{0,1},{1,0},{2,3},{3,2},{4,5},{5,4},{6,7},{7,6},{8,9},{9,8},{10,11... | collective-permute-start | bytes 1572872 | tf_op jit(solution)/shard_map/ppermute | solution.py:637
  59.4 20.8 %copy-start.5 = (bf16[256,256]{1,0:T(8,128)(2,1)S(1)}, bf16[256,256]{1,0:T(8,128)(2,1)}, u32[]{:S(2)}) copy-start(bf16[256,256]{1,0:T(8,128)(2,1)} %refs_7_.3) | copy-start | bytes 393220
  77.9 6.5 %collective-permute-start.3 = (bf16[64,2,8,128]{3,2,1,0:T(8,128)(2,1)S(1)}, bf16[64,2,8,128]{3,2,1,0:T(8,128)(2,1)S(1)}, u32[]{:S(2)}, u32[]{:S(2)}) collective-permute-start(bf16[64,2,8,128]{3,2,1,0:T(8,128)(2,1)S(1)} %get-tuple-element.81), channel_id=1, source_target_pairs={{0,32},{1,97},{2,34},{3,99},{4,36},{5,101},{6,38},{7,103},{8,40},{... | collective-permute-start | bytes 786440 | tf_op jit(solution)/shard_map/ppermute | solution.py:775
  78.8 6.4 %collective-permute-start.4 = (bf16[64,2,8,128]{3,2,1,0:T(8,128)(2,1)S(1)}, bf16[64,2,8,128]{3,2,1,0:T(8,128)(2,1)S(1)}, u32[]{:S(2)}, u32[]{:S(2)}) collective-permute-start(bf16[64,2,8,128]{3,2,1,0:T(8,128)(2,1)S(1)} %get-tuple-element.82), channel_id=1, source_target_pairs={{0,8},{1,25},{2,10},{3,27},{4,12},{5,29},{6,14},{7,31},{8,0},{9,17... | collective-permute-start | bytes 786440 | tf_op jit(solution)/shard_map/ppermute | solution.py:776
  79.7 4.4 %collective-permute-start.5 = (bf16[256,512]{1,0:T(8,128)(2,1)S(1)}, bf16[256,512]{1,0:T(8,128)(2,1)S(1)}, u32[]{:S(2)}, u32[]{:S(2)}) collective-permute-start(bf16[256,512]{1,0:T(8,128)(2,1)S(1)} %get-tuple-element.83.refs_2_), channel_id=1, source_target_pairs={{0,1},{1,0},{2,3},{3,2},{4,5},{5,4},{6,7},{7,6},{8,9},{9,8},{10,11... | collective-permute-start | bytes 786440 | tf_op jit(solution)/shard_map/ppermute | solution.py:637
  84.0 1.6 %collective-permute-start.2 = (bf16[256,512]{1,0:T(8,128)(2,1)S(1)}, bf16[256,512]{1,0:T(8,128)(2,1)S(1)}, u32[]{:S(2)}, u32[]{:S(2)}) collective-permute-start(bf16[256,512]{1,0:T(8,128)(2,1)S(1)} %get-tuple-element.79), channel_id=1, source_target_pairs={{0,1},{1,0},{2,3},{3,2},{4,5},{5,4},{6,7},{7,6},{8,9},{9,8},{10,11... | collective-permute-start | bytes 786440 | tf_op jit(solution)/shard_map/ppermute | solution.py:637
  141.0 6.9 %collective-permute-start.6 = (bf16[64,8,1536]{2,1,0:T(8,128)(2,1)S(1)}, bf16[64,8,1536]{2,1,0:T(8,128)(2,1)S(1)}, u32[]{:S(2)}, u32[]{:S(2)}) collective-permute-start(bf16[64,8,1536]{2,1,0:T(8,128)(2,1)S(1)} %all_to_all.29.own), channel_id=1, source_target_pairs={{0,1},{1,0},{2,3},{3,2},{4,5},{5,4},{6,7},{7,6},{8,9},{9,8},{10,11... | collective-permute-start | bytes 4718600 | tf_op jit(solution)/shard_map/ppermute | solution.py:637

commit v17 on v15

--- a/solution.py
+++ b/solution.py
@@ -326,7 +326,7 @@
 
 
 def write_half(terms, side, refs, stages, semaphores, scaling):
-    projection, output, pool = refs
+    projection, output, pool, fine_projection, fine_output = refs
     tall, square = stages
     wide = pool.shape[0]
     part, width = wide // 2, wide // 4
@@ -337,10 +337,16 @@
         values = terms[:, :, start : start + count].astype(F32) * scaling
         return values.reshape(terms.shape[0] * terms.shape[1], count)
 
-    def send(stage, target):
+    def prepare(stage, target):
         copies.append(pltpu.make_async_copy(stage, target, semaphores.at[len(copies)]))
-        copies[-1].start()
-
+        return copies[-1]
+
+    def fill(stage, start):
+        block = lanes(start, width)
+        stage[:, :width] = block[:part]
+        stage[:, width:] = block[part:]
+
+    place = pl.multiple_of(side * part, part)
     for heads in range(2):
         start = 2 * width + heads * (across + 2 * width)
         for k in range(3):
@@ -349,102 +355,71 @@
             target = pl.multiple_of(jnp.where(side == 0, places[0], places[1]), width)
             stage = tall.at[3 * heads + k]
             stage[...] = lanes(start + k * width, width)
-            send(stage, projection.at[:, pl.ds(target, width)])
+            prepare(stage, projection.at[:, pl.ds(target, width)]).start()
         for at, ref in enumerate((output, pool)):
-            block = lanes(start + across + at * width, width)
             stage = square.at[2 * heads + at]
-            stage[:, :width] = block[:part]
-            stage[:, width:] = block[part:]
-            target = pl.multiple_of(side * part, part)
-            send(stage, ref.at[heads * part : (heads + 1) * part, pl.ds(target, part)])
-    return copies
-
-
-def own_sums_kernel(own, projection, output, pool, tall, square, semaphores, *, scaling):
-    side = lax.axis_index("grp")
-    refs = (projection, output, pool)
-    for copy in write_half(own, side, refs, (tall, square), semaphores, scaling):
-        copy.wait()
-
-
-def other_sums_kernel(
-    own,
-    other,
-    projection_in,
-    output_in,
-    pool_in,
-    projection,
-    output,
-    pool,
-    fine_projection,
-    fine_output,
-    tall,
-    square,
-    semaphores,
-    fine,
-    fine_square,
-    fine_semaphores,
-    *,
-    scaling,
-):
-    side = 1 - lax.axis_index("grp")
-    refs = (projection, output, pool)
-    copies = write_half(other, side, refs, (tall, square), semaphores, scaling)
-    features = fine_output.shape[0]
-    width = features // 2
-    for heads in range(2):
-        start = heads * width
-        here, there = own[:, :, start : start + width], other[:, :, start : start + width]
-        for half in range(2):
-            values = jnp.where(side == half, there, here).astype(F32) * scaling
-            block = values.reshape(own.shape[0] * own.shape[1], width)
-            column = (2 * heads + half) * features
-            for k in range(2):
-                piece = block[k * features : (k + 1) * features]
-                if column < 3 * features:
-                    fine[:, column + k * width : column + (k + 1) * width] = piece
-                else:
-                    fine_square[:, k * width : (k + 1) * width] = piece
-    copies.append(pltpu.make_async_copy(fine, fine_projection, fine_semaphores.at[0]))
-    copies.append(pltpu.make_async_copy(fine_square, fine_output, fine_semaphores.at[1]))
-    for copy in copies[-2:]:
-        copy.start()
+            fill(stage, start + across + at * width)
+            target = ref.at[heads * part : (heads + 1) * part, pl.ds(place, part)]
+            prepare(stage, target).start()
+    fill(square.at[4], 0)
+    prepare(square.at[4], fine_projection.at[:, pl.ds(place, part)]).start()
+    fill(square.at[5], width)
+    last = semaphores.at[len(copies)]
+    to_projection = pltpu.make_async_copy(
+        square.at[5], fine_projection.at[:, 2 * part : 3 * part], last
+    )
+    to_output = pltpu.make_async_copy(square.at[5], fine_output, last)
+
+    @pl.when(side == 0)
+    def _():
+        to_projection.start()
+        to_projection.wait()
+
+    @pl.when(side != 0)
+    def _():
+        to_output.start()
+        to_output.wait()
+
     for copy in copies:
         copy.wait()
+
+
+def own_sums_kernel(terms, *refs, scaling):
+    write_half(terms, lax.axis_index("grp"), refs[:5], refs[5:7], refs[7], scaling)
+
+
+def other_sums_kernel(terms, *refs, scaling):
+    write_half(terms, 1 - lax.axis_index("grp"), refs[5:10], refs[10:12], refs[12], scaling)
 
 
 def write_sums(own, other, features, wide, scaling):
     part, width = wide // 2, wide // 4
     shapes = [(wide, 3 * wide), (wide, wide), (wide, wide)]
+    shapes += [(features, 3 * features), (features, features)]
     stages = [
         pltpu.VMEM((6, wide, width), F32),
-        pltpu.VMEM((4, part, part), F32),
-        pltpu.SemaphoreType.DMA((10,)),
+        pltpu.VMEM((6, part, part), F32),
+        pltpu.SemaphoreType.DMA((12,)),
     ]
     limits = pltpu.CompilerParams(vmem_limit_bytes=16 * 1024 * 1024)
+    outputs = [pltpu.HBM(shape, F32) for shape in shapes]
     firsts = pl.pallas_call(
         functools.partial(own_sums_kernel, scaling=scaling),
-        out_shape=[pltpu.HBM(shape, F32) for shape in shapes],
+        out_shape=outputs,
         in_specs=[VMEM],
-        out_specs=[HBM] * 3,
+        out_specs=[HBM] * 5,
         scratch_shapes=stages,
         compiler_params=limits,
     )(own)
-    shapes += [(features, 3 * features), (features, features)]
     projection, output, pool, fine_projection, fine_output = pl.pallas_call(
         functools.partial(other_sums_kernel, scaling=scaling),
-        out_shape=[pltpu.HBM(shape, F32) for shape in shapes],
-        in_specs=[VMEM] * 2 + [HBM] * 3,
+        out_shape=outputs,
+        in_specs=[VMEM] + [HBM] * 5,
         out_specs=[HBM] * 5,
-        scratch_shapes=stages
-        + [
-            pltpu.VMEM((features, 3 * features), F32),
-            pltpu.VMEM((features, features), F32),
-            pltpu.SemaphoreType.DMA((2,)),
-        ],
-        input_output_aliases={2: 0, 3: 1, 4: 2},
+        scratch_shapes=stages,
+        input_output_aliases={at + 1: at for at in range(5)},
         compiler_params=limits,
-    )(own, other, *firsts)
+    )(other, *firsts)
     return fine_projection, fine_output, pool, projection, output
 
 

time: 150 us -> 150 us (level)
  transfers between devices with their start and end apart: 7 -> 7, of which waited for: 4 -> 3; matrix products, arithmetic and copies ran while one was open for 0% -> 0% of each run, Pallas kernels for 7% -> 7%
where the time goes in v17:
time: 150 us
  blocking collectives  115 us (77%)
  Pallas kernels  23.9 us (16%)
  starting transfers between devices  8.09 us (5%)
    all_to_all x5, blocking collectives, spread_blocks(): return lax.all_to_all(values, axes, split_axis=0, concat_axis=0, tiled=True)  115 us
    pallas_call x14, Pallas kernels, call(): pl.pallas_call(body, out_shape=[(pltpu.HBM if out.far else jax.ShapeDtype...  20.3 us
    ppermute x5, starting transfers between devices, exchange(): return lax.ppermute(values, 'grp', [(0, 1), (1, 0)])  6.27 us
  transfers between devices with their start and end apart: 7, of which 3 were waited for; matrix products, arithmetic and copies ran while one was open for 0% of the time, Pallas kernels for 7%

profile of v17, /device:TPU:1, one launch (start us, length us, event | category | flops | bytes accessed | tf_op | source)
XLA Modules:
  0.0 149.7 jit_solution(3746723482046066235)
XLA Ops:
  0.6 2.2 %shard_map.153 = (bf16[1024,256]{1,0:T(8,128)(2,1)S(1)}, s32[1,512]{1,0:T(1,128)S(1)}, s32[1,512]{1,0:T(1,128)S(1)}, s32[1,512]{1,0:T(1,128)S(1)}, f32[1,512]{1,0:T(1,128)S(1)}) custom-call(s32[1,512]{1,0:T(1,128)} %bitcast.19, s32[1,512]{1,0:T(1,128)} %bitcast.20, s32[1,256]{1,0:T(1,128)} %bitcast.21, bf16[512,256]{1,0:T(8,128)(2,1)} %refs_3_.5), custom_call_target="tpu_custom_call" | custom-call | tf_op jit(solution)/shard_map/pallas_call | solution.py:595
  2.8 25.0 %all_to_all.25 = bf16[128,8,256]{2,1,0:T(8,128)(2,1)S(1)} all-to-all(bf16[128,8,256]{2,1,0:T(8,128)(2,1)S(1)} %bitcast.18), channel_id=1, replica_groups=mesh['pts'=64,'grp'=2] {'pts','grp'}, dimensions={0} | all-to-all | bytes 1048576 | tf_op jit(solution)/shard_map/all_to_all | solution.py:613
  27.8 3.4 %shard_map.154 = (bf16[1024,256]{1,0:T(8,128)(2,1)S(1)}, bf16[512,256]{1,0:T(8,128)(2,1)S(1)}, bf16[512,768]{1,0:T(8,128)(2,1)S(1)}, bf16[512,256]{1,0:T(8,128)(2,1)S(1)}, bf16[8,256,256]{2,1,0:T(8,128)(2,1)S(1)}) custom-call(bf16[1024,256]{1,0:T(8,128)(2,1)S(1)} %bitcast.14, s32[1,512]{1,0:T(1,128)S(1)} %get-tuple-element.53.refs_1_, ...), custom_call_target="tpu_custom_call" | custom-call | tf_op jit(solution)/shard_map/pallas_call | solution.py:595
  31.2 18.1 %all_to_all.26 = bf16[128,8,256]{2,1,0:T(8,128)(2,1)S(1)} all-to-all(bf16[128,8,256]{2,1,0:T(8,128)(2,1)S(1)} %bitcast.17), channel_id=1, replica_groups=mesh['pts'=64,'grp'=2] {'pts','grp'}, dimensions={0} | all-to-all | bytes 1048576 | tf_op jit(solution)/shard_map/all_to_all | solution.py:613
  49.3 0.5 shard_map.155.refs_0_.refs_4_
  49.8 0.0 copy-start.1
  49.8 1.2 collective-permute-start
  51.1 1.6 %shard_map.156 = (bf16[256,512]{1,0:T(8,128)(2,1)S(1)}, bf16[256,512]{1,0:T(8,128)(2,1)S(1)}, bf16[256,1024]{1,0:T(8,128)(2,1)S(1)}) custom-call(bf16[256,1024]{1,0:T(8,128)(2,1)S(1)} %shard_map.155.refs_0_.refs_4_, bf16[512,512]{1,0:T(8,128)(2,1)S(1)} %copy-done.2, bf16[512,1536]{1,0:T(8,128)(2,1)S(1)} %copy-done, bf16[512,512]{1,0:T(8,128)(2,1)} %refs_7_.2), custom_call_target="tpu_custom_call" | custom-call | tf_op jit(solution)/shard_map/pallas_call | solution.py:595
  52.7 4.4 %shard_map.157 = (bf16[256,1024]{1,0:T(8,128)(2,1)S(1)}, bf16[256,1024]{1,0:T(8,128)(2,1)S(1)}, bf16[256,512]{1,0:T(8,128)(2,1)S(1)}) custom-call(bf16[256,1024]{1,0:T(8,128)(2,1)S(1)} %collective-permute-done.refs_0_.refs_5_.refs_1_, bf16[256,1024]{1,0:T(8,128)(2,1)S(1)} %get-tuple-element.58.refs_1_, bf16[512,512]{1,0:T(8,128)(2,1)S(1)} %copy-done.2, ...), custom_call_target="tpu_custom_call" | custom-call | tf_op jit(solution)/shard_map/pallas_call | solution.py:595
  57.1 0.5 collective-permute-start.1
  57.6 0.4 shard_map.158
  58.0 0.7 shard_map.159
  58.8 0.5 collective-permute-done.1.refs_3_
  59.3 1.2 shard_map.160
  60.5 17.2 %all_to_all.27 = bf16[128,8,256]{2,1,0:T(8,128)(2,1)S(1)} all-to-all(bf16[128,8,256]{2,1,0:T(8,128)(2,1)S(1)} %bitcast.16), channel_id=1, replica_groups=mesh['pts'=64,'grp'=2] {'pts','grp'}, dimensions={0} | all-to-all | bytes 1048576 | tf_op jit(solution)/shard_map/all_to_all | solution.py:613
  77.7 0.9 collective-permute-start.3
  78.6 1.0 collective-permute-start.4
  79.5 0.5 collective-permute-start.5
  80.1 3.7 %shard_map.161 = (bf16[64,2,8,256]{3,2,1,0:T(8,128)(2,1)S(1)}, f32[256,512]{1,0:T(8,128)S(1)}, bf16[256,512]{1,0:T(8,128)(2,1)S(1)}) custom-call(bf16[1024,256]{1,0:T(8,128)(2,1)S(1)} %bitcast.15, s32[1,512]{1,0:T(1,128)S(1)} %get-tuple-element.53.refs_1_, bf16[512,256]{1,0:T(8,128)(2,1)S(1)} %get-tuple-element.75.refs_2_, ...), custom_call_target="tpu_custom_call" | custom-call | tf_op jit(solution)/shard_map/pallas_call | solution.py:595
  83.8 0.1 collective-permute-start.2
  83.9 0.3 shard_map.162.refs_3_
  84.3 0.7 collective-permute-done.4.refs_2_
  85.0 0.2 shard_map.163.refs_3_
  85.2 0.2 collective-permute-done.2.refs_2_
  85.4 0.2 shard_map.164
  85.6 29.6 %all_to_all.28 = bf16[128,8,768]{2,1,0:T(8,128)(2,1)S(1)} all-to-all(bf16[128,8,768]{2,1,0:T(8,128)(2,1)S(1)} %bitcast.12), channel_id=1, replica_groups=mesh['pts'=64,'grp'=2] {'pts','grp'}, dimensions={0} | all-to-all | bytes 3145728 | tf_op jit(solution)/shard_map/all_to_all | solution.py:613
  115.2 0.2 shard_map.166
  115.5 25.3 %all_to_all.29.terms = bf16[64,8,1536]{2,1,0:T(8,128)(2,1)S(1)} all-to-all(bf16[64,8,1536]{2,1,0:T(8,128)(2,1)S(1)} %shard_map.166), channel_id=1, replica_groups=mesh['pts'=64,'grp'=2] {'pts'}, dimensions={0} | all-to-all | bytes 3145728 | tf_op jit(solution)/shard_map/all_to_all | solution.py:613
  140.8 3.9 %collective-permute-start.6 = (bf16[64,8,1536]{2,1,0:T(8,128)(2,1)S(1)}, bf16[64,8,1536]{2,1,0:T(8,128)(2,1)S(1)}, u32[]{:S(2)}, u32[]{:S(2)}) collective-permute-start(bf16[64,8,1536]{2,1,0:T(8,128)(2,1)S(1)} %all_to_all.29.terms), channel_id=1, source_target_pairs={{0,1},{1,0},{2,3},{3,2},{4,5},{5,4},{6,7},{7,6},{8,9},{9,8},{10,11... | collective-permute-start | bytes 4718600 | tf_op jit(solution)/shard_map/ppermute | solution.py:609
  144.7 1.2 shard_map.165
  145.9 1.8 %shard_map.167 = (f32[512,1536]{1,0:T(8,128)}, f32[512,512]{1,0:T(8,128)}, f32[512,512]{1,0:T(8,128)}, f32[256,768]{1,0:T(8,128)}, f32[256,256]{1,0:T(8,128)}) custom-call(bf16[64,8,1536]{2,1,0:T(8,128)(2,1)S(1)} %all_to_all.29.terms), custom_call_target="tpu_custom_call" | custom-call | tf_op jit(solution)/shard_map/pallas_call | solution.py:406
  147.8 1.8 %shard_map.168 = (f32[512,1536]{1,0:T(8,128)}, f32[512,512]{1,0:T(8,128)}, f32[512,512]{1,0:T(8,128)}, f32[256,768]{1,0:T(8,128)}, f32[256,256]{1,0:T(8,128)}) custom-call(bf16[64,8,1536]{2,1,0:T(8,128)(2,1)S(1)} %collective-permute-done.6.terms, ...), custom_call_target="tpu_custom_call", output_to_operand_aliasing={{0}: (1, {}), {1}: (2, {}), {2}: (3, {}), {3}: (4, {}), {4}... | custom-call | tf_op jit(solution)/shard_map/pallas_call | solution.py:414
  (16 shorter events, 0.1 us)
Async XLA Ops:
  0.6 27.2 %copy-start.3 = (bf16[256,768]{1,0:T(8,128)(2,1)S(1)}, bf16[256,768]{1,0:T(8,128)(2,1)}, u32[]{:S(2)}) copy-start(bf16[256,768]{1,0:T(8,128)(2,1)} %refs_6_.3) | copy-start | bytes 1179652
  2.8 46.5 %copy-start.4 = (bf16[256,512]{1,0:T(8,128)(2,1)S(1)}, bf16[256,512]{1,0:T(8,128)(2,1)}, u32[]{:S(2)}) copy-start(bf16[256,512]{1,0:T(8,128)(2,1)} %refs_4_.5) | copy-start | bytes 786436
  27.8 23.3 %copy-start = (bf16[512,1536]{1,0:T(8,128)(2,1)S(1)}, bf16[512,1536]{1,0:T(8,128)(2,1)}, u32[]{:S(2)}) copy-start(bf16[512,1536]{1,0:T(8,128)(2,1)} %refs_6_.2) | copy-start | bytes 4718596
  27.8 23.3 %copy-start.2 = (bf16[512,512]{1,0:T(8,128)(2,1)S(1)}, bf16[512,512]{1,0:T(8,128)(2,1)}, u32[]{:S(2)}) copy-start(bf16[512,512]{1,0:T(8,128)(2,1)} %refs_5_.1) | copy-start | bytes 1572868
  49.8 2.9 %copy-start.1 = (bf16[512,512]{1,0:T(8,128)(2,1)S(1)}, bf16[512,512]{1,0:T(8,128)(2,1)}, u32[]{:S(2)}) copy-start(bf16[512,512]{1,0:T(8,128)(2,1)} %refs_7_.2) | copy-start | bytes 1572868
  49.8 2.9 %collective-permute-start = (bf16[256,1024]{1,0:T(8,128)(2,1)S(1)}, bf16[256,1024]{1,0:T(8,128)(2,1)S(1)}, u32[]{:S(2)}, u32[]{:S(2)}) collective-permute-start(bf16[256,1024]{1,0:T(8,128)(2,1)S(1)} %shard_map.155.refs_0_.refs_4_), channel_id=1, source_target_pairs={{0,1},{1,0},{2,3},{3,2},{4,5},{5,4},{6,7},{7,6},{8,9},{9,8},{10,11... | collective-permute-start | bytes 1572872 | tf_op jit(solution)/shard_map/ppermute | solution.py:609
  57.1 2.2 %collective-permute-start.1 = (bf16[256,1024]{1,0:T(8,128)(2,1)S(1)}, bf16[256,1024]{1,0:T(8,128)(2,1)S(1)}, u32[]{:S(2)}, u32[]{:S(2)}) collective-permute-start(bf16[256,1024]{1,0:T(8,128)(2,1)S(1)} %get-tuple-element.62.refs_3_), channel_id=1, source_target_pairs={{0,1},{1,0},{2,3},{3,2},{4,5},{5,4},{6,7},{7,6},{8,9},{9,8},{10,11... | collective-permute-start | bytes 1572872 | tf_op jit(solution)/shard_map/ppermute | solution.py:609
  59.3 20.8 %copy-start.5 = (bf16[256,256]{1,0:T(8,128)(2,1)S(1)}, bf16[256,256]{1,0:T(8,128)(2,1)}, u32[]{:S(2)}) copy-start(bf16[256,256]{1,0:T(8,128)(2,1)} %refs_7_.3) | copy-start | bytes 393220
  77.7 6.5 %collective-permute-start.3 = (bf16[64,2,8,128]{3,2,1,0:T(8,128)(2,1)S(1)}, bf16[64,2,8,128]{3,2,1,0:T(8,128)(2,1)S(1)}, u32[]{:S(2)}, u32[]{:S(2)}) collective-permute-start(bf16[64,2,8,128]{3,2,1,0:T(8,128)(2,1)S(1)} %get-tuple-element.83), channel_id=1, source_target_pairs={{0,32},{1,97},{2,34},{3,99},{4,36},{5,101},{6,38},{7,103},{8,40},{... | collective-permute-start | bytes 786440 | tf_op jit(solution)/shard_map/ppermute | solution.py:747
  78.6 6.4 %collective-permute-start.4 = (bf16[64,2,8,128]{3,2,1,0:T(8,128)(2,1)S(1)}, bf16[64,2,8,128]{3,2,1,0:T(8,128)(2,1)S(1)}, u32[]{:S(2)}, u32[]{:S(2)}) collective-permute-start(bf16[64,2,8,128]{3,2,1,0:T(8,128)(2,1)S(1)} %get-tuple-element.84), channel_id=1, source_target_pairs={{0,8},{1,25},{2,10},{3,27},{4,12},{5,29},{6,14},{7,31},{8,0},{9,17... | collective-permute-start | bytes 786440 | tf_op jit(solution)/shard_map/ppermute | solution.py:748
  79.5 4.4 %collective-permute-start.5 = (bf16[256,512]{1,0:T(8,128)(2,1)S(1)}, bf16[256,512]{1,0:T(8,128)(2,1)S(1)}, u32[]{:S(2)}, u32[]{:S(2)}) collective-permute-start(bf16[256,512]{1,0:T(8,128)(2,1)S(1)} %get-tuple-element.85.refs_2_), channel_id=1, source_target_pairs={{0,1},{1,0},{2,3},{3,2},{4,5},{5,4},{6,7},{7,6},{8,9},{9,8},{10,11... | collective-permute-start | bytes 786440 | tf_op jit(solution)/shard_map/ppermute | solution.py:609
  83.8 1.6 %collective-permute-start.2 = (bf16[256,512]{1,0:T(8,128)(2,1)S(1)}, bf16[256,512]{1,0:T(8,128)(2,1)S(1)}, u32[]{:S(2)}, u32[]{:S(2)}) collective-permute-start(bf16[256,512]{1,0:T(8,128)(2,1)S(1)} %get-tuple-element.81), channel_id=1, source_target_pairs={{0,1},{1,0},{2,3},{3,2},{4,5},{5,4},{6,7},{7,6},{8,9},{9,8},{10,11... | collective-permute-start | bytes 786440 | tf_op jit(solution)/shard_map/ppermute | solution.py:609
  140.8 6.9 %collective-permute-start.6 = (bf16[64,8,1536]{2,1,0:T(8,128)(2,1)S(1)}, bf16[64,8,1536]{2,1,0:T(8,128)(2,1)S(1)}, u32[]{:S(2)}, u32[]{:S(2)}) collective-permute-start(bf16[64,8,1536]{2,1,0:T(8,128)(2,1)S(1)} %all_to_all.29.terms), channel_id=1, source_target_pairs={{0,1},{1,0},{2,3},{3,2},{4,5},{5,4},{6,7},{7,6},{8,9},{9,8},{10,11... | collective-permute-start | bytes 4718600 | tf_op jit(solution)/shard_map/ppermute | solution.py:609

commit v18 on v15

--- a/solution.py
+++ b/solution.py
@@ -170,7 +170,9 @@
         rows_out[:, at * wide // 2 : (at + 1) * wide // 2] = values
 
 
-def coarse_kernel(other_pack, own_rows, pool, projection, output, keep, give, unit):
+def coarse_kernel(
+    other_pack, own_rows, pool, projection, output, keep, give, give_mixed, unit
+):
     wide = pool.shape[1]
     part = wide // 2
     half_rows = own_rows.shape[0]
@@ -188,7 +190,10 @@
     def put(at, rows):
         target = slice(at, at + rows.shape[1])
         keep[:, target] = rows[:half_rows]
-        give[:, target] = rows[half_rows:]
+        if at < part:
+            give_mixed[:, target] = rows[half_rows:]
+        else:
+            give[:, at - part : at - part + rows.shape[1]] = rows[half_rows:]
 
     for pair in range(part // PAIR):
         lanes = slice(pair * PAIR, (pair + 1) * PAIR)
@@ -209,49 +214,36 @@
     put(3 * part, jnp.concatenate(value_parts, axis=0).T.astype(BF))
 
 
-def heads_back(grads, index, projection, output):
-    wide = output.shape[1]
+def heads_back(grads, start, index, projection):
+    wide = projection.shape[0]
     part = wide // 2
     first = pl.multiple_of(index * part, part)
-    mixed = mm(grads[:, :part], output[pl.ds(first, part), :])
-    back = jnp.zeros_like(mixed)
+    back = jnp.zeros((grads.shape[0], wide), F32)
     for at in range(3):
         back = back + mm(
-            grads[:, (at + 1) * part : (at + 2) * part],
+            grads[:, start + at * part : start + (at + 1) * part],
             projection[:, pl.ds(at * wide + first, part)],
             (1, 1),
         )
-    return mixed, back
-
-
-def coarse_own_kernel(coarse, keep, projection, output, mixed, back):
-    own_mixed, own_back = heads_back(keep, lax.axis_index("grp"), projection, output)
-    mixed[...] = coarse[...].astype(F32) + own_mixed
-    back[...] = own_back
+    return back
+
+
+def coarse_own_kernel(keep, projection, back):
+    part = projection.shape[0] // 2
+    back[...] = heads_back(keep, part, lax.axis_index("grp"), projection)
 
 
 def coarse_finish_kernel(
-    coarse,
-    mixed,
-    back,
-    got,
-    cotangent,
-    pool,
-    projection,
-    output,
-    pair_slot,
-    result,
-    gradient,
-    send,
+    coarse, back, got, cotangent, pool, projection, pair_slot, give_mixed, pack, send
 ):
-    other_mixed, other_back = heads_back(got, 1 - lax.axis_index("grp"), projection, output)
-    result[...] = (mixed[...] + other_mixed).astype(BF)
-    result.flush()
+    other_back = heads_back(got, 0, 1 - lax.axis_index("grp"), projection)
     normed, inverse = normalize(coarse[...])
     gradient_rows = (
         cotangent[...].astype(F32) + norm_backward(back[...] + other_back, normed, inverse)
     ).astype(BF)
-    gradient[...] = gradient_rows
+    wide = pool.shape[1]
+    pack[:, :wide] = gradient_rows
+    pack[:, wide:] = give_mixed[...]
     fine = mm(gradient_rows, pool[...], (1, 1)).astype(BF)
     features = send.shape[1]
     stacked = jnp.concatenate([fine[:, :features], fine[:, features:]], axis=0)
@@ -263,6 +255,7 @@
     other_unit,
     keep,
     give,
+    give_mixed,
     own_pack,
     other_pack,
     kept,
@@ -275,7 +268,8 @@
     wide = own_unit.shape[1]
     part = wide // 2
     unit = jnp.concatenate([own_unit[...], other_unit[...]], axis=0)
-    stacked = jnp.concatenate([keep[...], give[...]], axis=0)
+    given = jnp.concatenate([give_mixed[...], give[...]], axis=1)
+    stacked = jnp.concatenate([keep[...], given], axis=0)
     cotangent = jnp.concatenate([own_pack[:, wide:], other_pack[:, wide:]], axis=0)
     projection_term = mm(unit, stacked[:, part:], (0, 0))
     output_term = mm(stacked[:, :part], cotangent, (0, 0))
@@ -505,11 +499,20 @@
     tokens[...] = mm(place, result.astype(BF)).reshape(tokens.shape).astype(BF)
 
 
-def pool_kernel(own_pack, other_pack, own_gradient, other_gradient, blocks):
-    part = own_gradient.shape[1] // 2
-    first = pl.multiple_of(lax.axis_index("grp") * part, part)
-    term = mm(own_pack[:, pl.ds(first, part)], own_gradient[...], (0, 0))
-    term = term + mm(other_pack[:, pl.ds(first, part)], other_gradient[...], (0, 0))
+def pool_kernel(
+    own_pack, other_pack, own_gradient, other_gradient, coarse, keep, output, blocks, result
+):
+    wide = coarse.shape[1]
+    part = wide // 2
+    core = lax.axis_index("grp")
+    first = pl.multiple_of(core * part, part)
+    second = pl.multiple_of((1 - core) * part, part)
+    mixed = mm(keep[:, :part], output[pl.ds(first, part), :])
+    mixed = mixed + mm(other_gradient[:, wide:], output[pl.ds(second, part), :])
+    result[...] = (coarse[...].astype(F32) + mixed).astype(BF)
+    result.flush()
+    term = mm(own_pack[:, pl.ds(first, part)], own_gradient[:, :wide], (0, 0))
+    term = term + mm(other_pack[:, pl.ds(first, part)], other_gradient[:, :wide], (0, 0))
     put_quarters(blocks, 0, term)
 
 
@@ -718,12 +721,13 @@
             Near((half_rows, 2 * wide)),
         ),
     )
-    keep, give, other_unit = call(
+    keep, give, give_mixed, other_unit = call(
         coarse_kernel,
         (other_pack, own_rows, pool_weight, coarse_projection, coarse_output),
         (
             Near((half_rows, 2 * wide)),
-            Near((half_rows, 2 * wide)),
+            Near((half_rows, 3 * wide // 2)),
+            Near((half_rows, wide // 2)),
             Near((half_rows, wide)),
         ),
     )
@@ -731,39 +735,30 @@
     blocks = (owners, 2, slots // devices)
     kept, first_half, second_half = call(
         functools.partial(coarse_weights_kernel, strides=(run, step)),
-        (own_unit, other_unit, keep, give, own_pack, other_pack),
+        (own_unit, other_unit, keep, give, give_mixed, own_pack, other_pack),
         (
             Near((*blocks, wide // 2)),
             Near((*blocks, wide // 4)),
             Near((*blocks, wide // 4)),
         ),
     )
-    mixed, back = call(
-        coarse_own_kernel,
-        (coarse, keep, coarse_projection, coarse_output),
-        (Near((half_rows, wide), F32), Near((half_rows, wide), F32)),
-    )
+    (back,) = call(coarse_own_kernel, (keep, coarse_projection), (Near((half_rows, wide), F32),))
     got, kept, first_half, second_half = lax.optimization_barrier(
         (got, kept, first_half, second_half)
     )
-    coarse_result, coarse_gradient, send = call(
+    coarse_gradient, send = call(
         coarse_finish_kernel,
         (
             coarse,
-            mixed,
             back,
             got,
             coarse_cotangent,
             pool_weight,
             coarse_projection,
-            coarse_output,
             pair_slot,
-        ),
-        (
-            Near((half_rows, wide), far=True),
-            Near((half_rows, wide)),
-            Near((slots, features)),
-        ),
+            give_mixed,
+        ),
+        (Near((half_rows, 3 * wide // 2)), Near((slots, features))),
     )
     arrived = route(send, devices)
     arrived, first_half, second_half, coarse_gradient = lax.optimization_barrier(
@@ -792,10 +787,18 @@
         scratch=(pltpu.VMEM((count, 3 * features), BF),),
     )
     fine_got = exchange(fine_passed)
-    (pool_part,) = call(
+    pool_part, coarse_result = call(
         pool_kernel,
-        (own_pack, other_pack, coarse_gradient, other_gradient),
-        (Near((*blocks, wide // 4)),),
+        (
+            own_pack,
+            other_pack,
+            coarse_gradient,
+            other_gradient,
+            coarse,
+            keep,
+            coarse_output,
+        ),
+        (Near((*blocks, wide // 4)), Near((half_rows, wide), far=True)),
     )
     (coarse_part,) = call(
         coarse_part_kernel,

time: 150 us -> 150 us (level)
  no operation moved by 1% of the time
where the time goes in v18:
time: 150 us
  blocking collectives  115 us (77%)
  Pallas kernels  24.4 us (16%)
  starting transfers between devices  8.07 us (5%)
  waiting for transfers between devices  1.8 us (1%)
    all_to_all x5, blocking collectives, spread_blocks(): return lax.all_to_all(values, axes, split_axis=0, concat_axis=0, tiled=True)  115 us
    pallas_call x14, Pallas kernels, call(): pl.pallas_call(body, out_shape=[(pltpu.HBM if out.far else jax.ShapeDtype...  20.9 us
    ppermute x5, starting transfers between devices, exchange(): return lax.ppermute(values, 'grp', [(0, 1), (1, 0)])  6.96 us
  transfers between devices with their start and end apart: 7, of which 4 were waited for; matrix products, arithmetic and copies ran while one was open for 0% of the time, Pallas kernels for 7%

profile of v18, /device:TPU:1, one launch (start us, length us, event | category | flops | bytes accessed | tf_op | source)
XLA Modules:
  0.0 149.8 jit_solution(6469268561574732395)
XLA Ops:
  0.6 2.2 %shard_map.153 = (bf16[1024,256]{1,0:T(8,128)(2,1)S(1)}, s32[1,512]{1,0:T(1,128)S(1)}, s32[1,512]{1,0:T(1,128)S(1)}, s32[1,512]{1,0:T(1,128)S(1)}, f32[1,512]{1,0:T(1,128)S(1)}) custom-call(s32[1,512]{1,0:T(1,128)} %bitcast.19, s32[1,512]{1,0:T(1,128)} %bitcast.20, s32[1,256]{1,0:T(1,128)} %bitcast.21, bf16[512,256]{1,0:T(8,128)(2,1)} %refs_3_.5), custom_call_target="tpu_custom_call" | custom-call | tf_op jit(solution)/shard_map/pallas_call | solution.py:623
  2.8 25.0 %all_to_all.25 = bf16[128,8,256]{2,1,0:T(8,128)(2,1)S(1)} all-to-all(bf16[128,8,256]{2,1,0:T(8,128)(2,1)S(1)} %bitcast.18), channel_id=1, replica_groups=mesh['pts'=64,'grp'=2] {'pts','grp'}, dimensions={0} | all-to-all | bytes 1048576 | tf_op jit(solution)/shard_map/all_to_all | solution.py:641
  27.8 3.4 %shard_map.154 = (bf16[1024,256]{1,0:T(8,128)(2,1)S(1)}, bf16[512,256]{1,0:T(8,128)(2,1)S(1)}, bf16[512,768]{1,0:T(8,128)(2,1)S(1)}, bf16[512,256]{1,0:T(8,128)(2,1)S(1)}, bf16[8,256,256]{2,1,0:T(8,128)(2,1)S(1)}) custom-call(bf16[1024,256]{1,0:T(8,128)(2,1)S(1)} %bitcast.14, s32[1,512]{1,0:T(1,128)S(1)} %get-tuple-element.51.refs_1_, ...), custom_call_target="tpu_custom_call" | custom-call | tf_op jit(solution)/shard_map/pallas_call | solution.py:623
  31.2 18.1 %all_to_all.26 = bf16[128,8,256]{2,1,0:T(8,128)(2,1)S(1)} all-to-all(bf16[128,8,256]{2,1,0:T(8,128)(2,1)S(1)} %bitcast.16), channel_id=1, replica_groups=mesh['pts'=64,'grp'=2] {'pts','grp'}, dimensions={0} | all-to-all | bytes 1048576 | tf_op jit(solution)/shard_map/all_to_all | solution.py:641
  49.3 0.5 shard_map.155.refs_0_.refs_5_
  49.8 1.2 collective-permute-start
  51.1 1.6 %shard_map.156 = (bf16[256,512]{1,0:T(8,128)(2,1)S(1)}, bf16[256,512]{1,0:T(8,128)(2,1)S(1)}, bf16[256,1024]{1,0:T(8,128)(2,1)S(1)}) custom-call(bf16[256,1024]{1,0:T(8,128)(2,1)S(1)} %shard_map.155.refs_0_.refs_5_, bf16[512,512]{1,0:T(8,128)(2,1)S(1)} %copy-done.1, bf16[512,1536]{1,0:T(8,128)(2,1)S(1)} %copy-done, bf16[512,512]{1,0:T(8,128)(2,1)} %refs_6_.2), custom_call_target="tpu_custom_call" | custom-call | tf_op jit(solution)/shard_map/pallas_call | solution.py:623
  52.7 4.4 %shard_map.157 = (bf16[256,1024]{1,0:T(8,128)(2,1)S(1)}, bf16[256,768]{1,0:T(8,128)(2,1)S(1)}, bf16[256,256]{1,0:T(8,128)(2,1)S(1)}, bf16[256,512]{1,0:T(8,128)(2,1)S(1)}) custom-call(bf16[256,1024]{1,0:T(8,128)(2,1)S(1)} %collective-permute-done.refs_0_.refs_6_.refs_1_, bf16[256,1024]{1,0:T(8,128)(2,1)S(1)} %get-tuple-element.56.refs_1_, ...), custom_call_target="tpu_custom_call" | custom-call | tf_op jit(solution)/shard_map/pallas_call | solution.py:623
  57.1 0.5 collective-permute-start.1
  57.6 0.4 shard_map.158.refs_1_
  58.0 0.8 shard_map.159
  58.8 0.3 collective-permute-done.1.refs_2_
  59.1 1.2 shard_map.160
  60.2 17.2 %all_to_all.27 = bf16[128,8,256]{2,1,0:T(8,128)(2,1)S(1)} all-to-all(bf16[128,8,256]{2,1,0:T(8,128)(2,1)S(1)} %bitcast.17), channel_id=1, replica_groups=mesh['pts'=64,'grp'=2] {'pts','grp'}, dimensions={0} | all-to-all | bytes 1048576 | tf_op jit(solution)/shard_map/all_to_all | solution.py:641
  77.4 1.1 collective-permute-start.2
  78.6 0.9 collective-permute-start.4
  79.5 0.2 collective-permute-start.5
  79.7 3.7 %shard_map.162 = (bf16[64,2,8,256]{3,2,1,0:T(8,128)(2,1)S(1)}, f32[256,512]{1,0:T(8,128)S(1)}, bf16[256,512]{1,0:T(8,128)(2,1)S(1)}) custom-call(bf16[1024,256]{1,0:T(8,128)(2,1)S(1)} %bitcast.15, s32[1,512]{1,0:T(1,128)S(1)} %get-tuple-element.51.refs_1_, bf16[512,256]{1,0:T(8,128)(2,1)S(1)} %get-tuple-element.73.refs_2_, ...), custom_call_target="tpu_custom_call" | custom-call | tf_op jit(solution)/shard_map/pallas_call | solution.py:623
  83.4 0.2 collective-permute-start.3
  83.6 1.0 shard_map.161
  84.6 0.4 collective-permute-done.4.refs_1_
  85.0 0.9 collective-permute-done.5.refs_2_
  85.9 0.2 shard_map.163.refs_3_
  86.1 0.2 shard_map.164
  86.2 29.0 %all_to_all.28 = bf16[128,8,768]{2,1,0:T(8,128)(2,1)S(1)} all-to-all(bf16[128,8,768]{2,1,0:T(8,128)(2,1)S(1)} %bitcast.12), channel_id=1, replica_groups=mesh['pts'=64,'grp'=2] {'pts','grp'}, dimensions={0} | all-to-all | bytes 3145728 | tf_op jit(solution)/shard_map/all_to_all | solution.py:641
  115.2 0.2 shard_map.166
  115.5 25.3 %all_to_all.29.own = bf16[64,8,1536]{2,1,0:T(8,128)(2,1)S(1)} all-to-all(bf16[64,8,1536]{2,1,0:T(8,128)(2,1)S(1)} %shard_map.166), channel_id=1, replica_groups=mesh['pts'=64,'grp'=2] {'pts'}, dimensions={0} | all-to-all | bytes 3145728 | tf_op jit(solution)/shard_map/all_to_all | solution.py:641
  140.8 3.9 %collective-permute-start.6 = (bf16[64,8,1536]{2,1,0:T(8,128)(2,1)S(1)}, bf16[64,8,1536]{2,1,0:T(8,128)(2,1)S(1)}, u32[]{:S(2)}, u32[]{:S(2)}) collective-permute-start(bf16[64,8,1536]{2,1,0:T(8,128)(2,1)S(1)} %all_to_all.29.own), channel_id=1, source_target_pairs={{0,1},{1,0},{2,3},{3,2},{4,5},{5,4},{6,7},{7,6},{8,9},{9,8},{10,11... | collective-permute-start | bytes 4718600 | tf_op jit(solution)/shard_map/ppermute | solution.py:637
  144.7 1.2 shard_map.165
  145.9 1.6 %shard_map.167 = (f32[512,1536]{1,0:T(8,128)}, f32[512,512]{1,0:T(8,128)}, f32[512,512]{1,0:T(8,128)}) custom-call(bf16[64,8,1536]{2,1,0:T(8,128)(2,1)S(1)} %all_to_all.29.own), custom_call_target="tpu_custom_call" | custom-call | tf_op jit(solution)/shard_map/pallas_call | solution.py:419
  147.5 0.2 collective-permute-done.6.other
  147.7 1.9 %shard_map.168 = (f32[512,1536]{1,0:T(8,128)}, f32[512,512]{1,0:T(8,128)}, f32[512,512]{1,0:T(8,128)}, f32[256,768]{1,0:T(8,128)}, f32[256,256]{1,0:T(8,128)}) custom-call(bf16[64,8,1536]{2,1,0:T(8,128)(2,1)S(1)} %all_to_all.29.own, ...), custom_call_target="tpu_custom_call", output_to_operand_aliasing={{0}: (2, {}), {1}: (3, {}), {2}: (4, {})} | custom-call | tf_op jit(solution)/shard_map/pallas_call | solution.py:428
  (16 shorter events, 0.1 us)
Async XLA Ops:
  0.6 27.2 %copy-start.3 = (bf16[256,768]{1,0:T(8,128)(2,1)S(1)}, bf16[256,768]{1,0:T(8,128)(2,1)}, u32[]{:S(2)}) copy-start(bf16[256,768]{1,0:T(8,128)(2,1)} %refs_6_.3) | copy-start | bytes 1179652
  2.8 46.5 %copy-start.4 = (bf16[256,512]{1,0:T(8,128)(2,1)S(1)}, bf16[256,512]{1,0:T(8,128)(2,1)}, u32[]{:S(2)}) copy-start(bf16[256,512]{1,0:T(8,128)(2,1)} %refs_3_.9) | copy-start | bytes 786436
  27.8 23.2 %copy-start = (bf16[512,1536]{1,0:T(8,128)(2,1)S(1)}, bf16[512,1536]{1,0:T(8,128)(2,1)}, u32[]{:S(2)}) copy-start(bf16[512,1536]{1,0:T(8,128)(2,1)} %refs_5_.1) | copy-start | bytes 4718596
  27.8 23.2 %copy-start.1 = (bf16[512,512]{1,0:T(8,128)(2,1)S(1)}, bf16[512,512]{1,0:T(8,128)(2,1)}, u32[]{:S(2)}) copy-start(bf16[512,512]{1,0:T(8,128)(2,1)} %refs_4_.5) | copy-start | bytes 1572868
  49.8 2.9 %copy-start.2 = (bf16[512,512]{1,0:T(8,128)(2,1)S(1)}, bf16[512,512]{1,0:T(8,128)(2,1)}, u32[]{:S(2)}) copy-start(bf16[512,512]{1,0:T(8,128)(2,1)} %refs_6_.2) | copy-start | bytes 1572868
  49.8 2.9 %collective-permute-start = (bf16[256,1024]{1,0:T(8,128)(2,1)S(1)}, bf16[256,1024]{1,0:T(8,128)(2,1)S(1)}, u32[]{:S(2)}, u32[]{:S(2)}) collective-permute-start(bf16[256,1024]{1,0:T(8,128)(2,1)S(1)} %shard_map.155.refs_0_.refs_5_), channel_id=1, source_target_pairs={{0,1},{1,0},{2,3},{3,2},{4,5},{5,4},{6,7},{7,6},{8,9},{9,8},{10,11... | collective-permute-start | bytes 1572872 | tf_op jit(solution)/shard_map/ppermute | solution.py:637
  57.1 2.0 %collective-permute-start.1 = (bf16[256,768]{1,0:T(8,128)(2,1)S(1)}, bf16[256,768]{1,0:T(8,128)(2,1)S(1)}, u32[]{:S(2)}, u32[]{:S(2)}) collective-permute-start(bf16[256,768]{1,0:T(8,128)(2,1)S(1)} %get-tuple-element.58.refs_3_), channel_id=1, source_target_pairs={{0,1},{1,0},{2,3},{3,2},{4,5},{5,4},{6,7},{7,6},{8,9},{9,8},{10,11... | collective-permute-start | bytes 1179656 | tf_op jit(solution)/shard_map/ppermute | solution.py:637
  59.1 20.6 %copy-start.5 = (bf16[256,256]{1,0:T(8,128)(2,1)S(1)}, bf16[256,256]{1,0:T(8,128)(2,1)}, u32[]{:S(2)}) copy-start(bf16[256,256]{1,0:T(8,128)(2,1)} %refs_7_.1) | copy-start | bytes 393220
  77.4 6.1 %collective-permute-start.2 = (bf16[256,768]{1,0:T(8,128)(2,1)S(1)}, bf16[256,768]{1,0:T(8,128)(2,1)S(1)}, u32[]{:S(2)}, u32[]{:S(2)}) collective-permute-start(bf16[256,768]{1,0:T(8,128)(2,1)S(1)} %get-tuple-element.70.refs_2_), channel_id=1, source_target_pairs={{0,1},{1,0},{2,3},{3,2},{4,5},{5,4},{6,7},{7,6},{8,9},{9,8},{10,11... | collective-permute-start | bytes 1179656 | tf_op jit(solution)/shard_map/ppermute | solution.py:637
  78.6 6.4 %collective-permute-start.4 = (bf16[64,2,8,128]{3,2,1,0:T(8,128)(2,1)S(1)}, bf16[64,2,8,128]{3,2,1,0:T(8,128)(2,1)S(1)}, u32[]{:S(2)}, u32[]{:S(2)}) collective-permute-start(bf16[64,2,8,128]{3,2,1,0:T(8,128)(2,1)S(1)} %get-tuple-element.81), channel_id=1, source_target_pairs={{0,32},{1,97},{2,34},{3,99},{4,36},{5,101},{6,38},{7,103},{8,40},{... | collective-permute-start | bytes 786440 | tf_op jit(solution)/shard_map/ppermute | solution.py:767
  79.5 6.4 %collective-permute-start.5 = (bf16[64,2,8,128]{3,2,1,0:T(8,128)(2,1)S(1)}, bf16[64,2,8,128]{3,2,1,0:T(8,128)(2,1)S(1)}, u32[]{:S(2)}, u32[]{:S(2)}) collective-permute-start(bf16[64,2,8,128]{3,2,1,0:T(8,128)(2,1)S(1)} %get-tuple-element.82), channel_id=1, source_target_pairs={{0,8},{1,25},{2,10},{3,27},{4,12},{5,29},{6,14},{7,31},{8,0},{9,17... | collective-permute-start | bytes 786440 | tf_op jit(solution)/shard_map/ppermute | solution.py:768
  83.4 2.7 %collective-permute-start.3 = (bf16[256,512]{1,0:T(8,128)(2,1)S(1)}, bf16[256,512]{1,0:T(8,128)(2,1)S(1)}, u32[]{:S(2)}, u32[]{:S(2)}) collective-permute-start(bf16[256,512]{1,0:T(8,128)(2,1)S(1)} %get-tuple-element.79), channel_id=1, source_target_pairs={{0,1},{1,0},{2,3},{3,2},{4,5},{5,4},{6,7},{7,6},{8,9},{9,8},{10,11... | collective-permute-start | bytes 786440 | tf_op jit(solution)/shard_map/ppermute | solution.py:637
  140.8 6.9 %collective-permute-start.6 = (bf16[64,8,1536]{2,1,0:T(8,128)(2,1)S(1)}, bf16[64,8,1536]{2,1,0:T(8,128)(2,1)S(1)}, u32[]{:S(2)}, u32[]{:S(2)}) collective-permute-start(bf16[64,8,1536]{2,1,0:T(8,128)(2,1)S(1)} %all_to_all.29.own), channel_id=1, source_target_pairs={{0,1},{1,0},{2,3},{3,2},{4,5},{5,4},{6,7},{7,6},{8,9},{9,8},{10,11... | collective-permute-start | bytes 4718600 | tf_op jit(solution)/shard_map/ppermute | solution.py:637

commit v19 on v17

--- a/solution.py
+++ b/solution.py
@@ -170,7 +170,9 @@
         rows_out[:, at * wide // 2 : (at + 1) * wide // 2] = values
 
 
-def coarse_kernel(other_pack, own_rows, pool, projection, output, keep, give, unit):
+def coarse_kernel(
+    other_pack, own_rows, pool, projection, output, keep, give, give_mixed, unit
+):
     wide = pool.shape[1]
     part = wide // 2
     half_rows = own_rows.shape[0]
@@ -188,7 +190,10 @@
     def put(at, rows):
         target = slice(at, at + rows.shape[1])
         keep[:, target] = rows[:half_rows]
-        give[:, target] = rows[half_rows:]
+        if at < part:
+            give_mixed[:, target] = rows[half_rows:]
+        else:
+            give[:, at - part : at - part + rows.shape[1]] = rows[half_rows:]
 
     for pair in range(part // PAIR):
         lanes = slice(pair * PAIR, (pair + 1) * PAIR)
@@ -209,49 +214,36 @@
     put(3 * part, jnp.concatenate(value_parts, axis=0).T.astype(BF))
 
 
-def heads_back(grads, index, projection, output):
-    wide = output.shape[1]
+def heads_back(grads, start, index, projection):
+    wide = projection.shape[0]
     part = wide // 2
     first = pl.multiple_of(index * part, part)
-    mixed = mm(grads[:, :part], output[pl.ds(first, part), :])
-    back = jnp.zeros_like(mixed)
+    back = jnp.zeros((grads.shape[0], wide), F32)
     for at in range(3):
         back = back + mm(
-            grads[:, (at + 1) * part : (at + 2) * part],
+            grads[:, start + at * part : start + (at + 1) * part],
             projection[:, pl.ds(at * wide + first, part)],
             (1, 1),
         )
-    return mixed, back
-
-
-def coarse_own_kernel(coarse, keep, projection, output, mixed, back):
-    own_mixed, own_back = heads_back(keep, lax.axis_index("grp"), projection, output)
-    mixed[...] = coarse[...].astype(F32) + own_mixed
-    back[...] = own_back
+    return back
+
+
+def coarse_own_kernel(keep, projection, back):
+    part = projection.shape[0] // 2
+    back[...] = heads_back(keep, part, lax.axis_index("grp"), projection)
 
 
 def coarse_finish_kernel(
-    coarse,
-    mixed,
-    back,
-    got,
-    cotangent,
-    pool,
-    projection,
-    output,
-    pair_slot,
-    result,
-    gradient,
-    send,
+    coarse, back, got, cotangent, pool, projection, pair_slot, give_mixed, pack, send
 ):
-    other_mixed, other_back = heads_back(got, 1 - lax.axis_index("grp"), projection, output)
-    result[...] = (mixed[...] + other_mixed).astype(BF)
-    result.flush()
+    other_back = heads_back(got, 0, 1 - lax.axis_index("grp"), projection)
     normed, inverse = normalize(coarse[...])
     gradient_rows = (
         cotangent[...].astype(F32) + norm_backward(back[...] + other_back, normed, inverse)
     ).astype(BF)
-    gradient[...] = gradient_rows
+    wide = pool.shape[1]
+    pack[:, :wide] = gradient_rows
+    pack[:, wide:] = give_mixed[...]
     fine = mm(gradient_rows, pool[...], (1, 1)).astype(BF)
     features = send.shape[1]
     stacked = jnp.concatenate([fine[:, :features], fine[:, features:]], axis=0)
@@ -263,6 +255,7 @@
     other_unit,
     keep,
     give,
+    give_mixed,
     own_pack,
     other_pack,
     kept,
@@ -275,7 +268,8 @@
     wide = own_unit.shape[1]
     part = wide // 2
     unit = jnp.concatenate([own_unit[...], other_unit[...]], axis=0)
-    stacked = jnp.concatenate([keep[...], give[...]], axis=0)
+    given = jnp.concatenate([give_mixed[...], give[...]], axis=1)
+    stacked = jnp.concatenate([keep[...], given], axis=0)
     cotangent = jnp.concatenate([own_pack[:, wide:], other_pack[:, wide:]], axis=0)
     projection_term = mm(unit, stacked[:, part:], (0, 0))
     output_term = mm(stacked[:, :part], cotangent, (0, 0))
@@ -480,11 +474,20 @@
     tokens[...] = mm(place, result.astype(BF)).reshape(tokens.shape).astype(BF)
 
 
-def pool_kernel(own_pack, other_pack, own_gradient, other_gradient, blocks):
-    part = own_gradient.shape[1] // 2
-    first = pl.multiple_of(lax.axis_index("grp") * part, part)
-    term = mm(own_pack[:, pl.ds(first, part)], own_gradient[...], (0, 0))
-    term = term + mm(other_pack[:, pl.ds(first, part)], other_gradient[...], (0, 0))
+def pool_kernel(
+    own_pack, other_pack, own_gradient, other_gradient, coarse, keep, output, blocks, result
+):
+    wide = coarse.shape[1]
+    part = wide // 2
+    core = lax.axis_index("grp")
+    first = pl.multiple_of(core * part, part)
+    second = pl.multiple_of((1 - core) * part, part)
+    mixed = mm(keep[:, :part], output[pl.ds(first, part), :])
+    mixed = mixed + mm(other_gradient[:, wide:], output[pl.ds(second, part), :])
+    result[...] = (coarse[...].astype(F32) + mixed).astype(BF)
+    result.flush()
+    term = mm(own_pack[:, pl.ds(first, part)], own_gradient[:, :wide], (0, 0))
+    term = term + mm(other_pack[:, pl.ds(first, part)], other_gradient[:, :wide], (0, 0))
     put_quarters(blocks, 0, term)
 
 
@@ -693,12 +696,13 @@
             Near((half_rows, 2 * wide)),
         ),
     )
-    keep, give, other_unit = call(
+    keep, give, give_mixed, other_unit = call(
         coarse_kernel,
         (other_pack, own_rows, pool_weight, coarse_projection, coarse_output),
         (
             Near((half_rows, 2 * wide)),
-            Near((half_rows, 2 * wide)),
+            Near((half_rows, 3 * wide // 2)),
+            Near((half_rows, wide // 2)),
             Near((half_rows, wide)),
         ),
     )
@@ -706,39 +710,30 @@
     blocks = (owners, 2, slots // devices)
     kept, first_half, second_half = call(
         functools.partial(coarse_weights_kernel, strides=(run, step)),
-        (own_unit, other_unit, keep, give, own_pack, other_pack),
+        (own_unit, other_unit, keep, give, give_mixed, own_pack, other_pack),
         (
             Near((*blocks, wide // 2)),
             Near((*blocks, wide // 4)),
             Near((*blocks, wide // 4)),
         ),
     )
-    mixed, back = call(
-        coarse_own_kernel,
-        (coarse, keep, coarse_projection, coarse_output),
-        (Near((half_rows, wide), F32), Near((half_rows, wide), F32)),
-    )
+    (back,) = call(coarse_own_kernel, (keep, coarse_projection), (Near((half_rows, wide), F32),))
     got, kept, first_half, second_half = lax.optimization_barrier(
         (got, kept, first_half, second_half)
     )
-    coarse_result, coarse_gradient, send = call(
+    coarse_gradient, send = call(
         coarse_finish_kernel,
         (
             coarse,
-            mixed,
             back,
             got,
             coarse_cotangent,
             pool_weight,
             coarse_projection,
-            coarse_output,
             pair_slot,
-        ),
-        (
-            Near((half_rows, wide), far=True),
-            Near((half_rows, wide)),
-            Near((slots, features)),
-        ),
+            give_mixed,
+        ),
+        (Near((half_rows, 3 * wide // 2)), Near((slots, features))),
     )
     arrived = route(send, devices)
     arrived, first_half, second_half, coarse_gradient = lax.optimization_barrier(
@@ -767,10 +762,18 @@
         scratch=(pltpu.VMEM((count, 3 * features), BF),),
     )
     fine_got = exchange(fine_passed)
-    (pool_part,) = call(
+    pool_part, coarse_result = call(
         pool_kernel,
-        (own_pack, other_pack, coarse_gradient, other_gradient),
-        (Near((*blocks, wide // 4)),),
+        (
+            own_pack,
+            other_pack,
+            coarse_gradient,
+            other_gradient,
+            coarse,
+            keep,
+            coarse_output,
+        ),
+        (Near((*blocks, wide // 4)), Near((half_rows, wide), far=True)),
     )
     (coarse_part,) = call(
         coarse_part_kernel,

time: 150 us -> 150 us (level)
  no operation moved by 1% of the time
where the time goes in v19:
time: 150 us
  blocking collectives  115 us (77%)
  Pallas kernels  24.5 us (16%)
  starting transfers between devices  8.07 us (5%)
  waiting for transfers between devices  1.59 us (1%)
    all_to_all x5, blocking collectives, spread_blocks(): return lax.all_to_all(values, axes, split_axis=0, concat_axis=0, tiled=True)  115 us
    pallas_call x14, Pallas kernels, call(): pl.pallas_call(body, out_shape=[(pltpu.HBM if out.far else jax.ShapeDtype...  20.9 us
    ppermute x5, starting transfers between devices, exchange(): return lax.ppermute(values, 'grp', [(0, 1), (1, 0)])  6.96 us
  transfers between devices with their start and end apart: 7, of which 3 were waited for; matrix products, arithmetic and copies ran while one was open for 0% of the time, Pallas kernels for 7%

profile of v19, /device:TPU:1, one launch (start us, length us, event | category | flops | bytes accessed | tf_op | source)
XLA Modules:
  0.0 149.7 jit_solution(11596738436550103787)
XLA Ops:
  0.6 2.2 %shard_map.153 = (bf16[1024,256]{1,0:T(8,128)(2,1)S(1)}, s32[1,512]{1,0:T(1,128)S(1)}, s32[1,512]{1,0:T(1,128)S(1)}, s32[1,512]{1,0:T(1,128)S(1)}, f32[1,512]{1,0:T(1,128)S(1)}) custom-call(s32[1,512]{1,0:T(1,128)} %bitcast.19, s32[1,512]{1,0:T(1,128)} %bitcast.20, s32[1,256]{1,0:T(1,128)} %bitcast.21, bf16[512,256]{1,0:T(8,128)(2,1)} %refs_3_.5), custom_call_target="tpu_custom_call" | custom-call | tf_op jit(solution)/shard_map/pallas_call | solution.py:598
  2.8 25.0 %all_to_all.25 = bf16[128,8,256]{2,1,0:T(8,128)(2,1)S(1)} all-to-all(bf16[128,8,256]{2,1,0:T(8,128)(2,1)S(1)} %bitcast.18), channel_id=1, replica_groups=mesh['pts'=64,'grp'=2] {'pts','grp'}, dimensions={0} | all-to-all | bytes 1048576 | tf_op jit(solution)/shard_map/all_to_all | solution.py:616
  27.8 3.4 %shard_map.154 = (bf16[1024,256]{1,0:T(8,128)(2,1)S(1)}, bf16[512,256]{1,0:T(8,128)(2,1)S(1)}, bf16[512,768]{1,0:T(8,128)(2,1)S(1)}, bf16[512,256]{1,0:T(8,128)(2,1)S(1)}, bf16[8,256,256]{2,1,0:T(8,128)(2,1)S(1)}) custom-call(bf16[1024,256]{1,0:T(8,128)(2,1)S(1)} %bitcast.14, s32[1,512]{1,0:T(1,128)S(1)} %get-tuple-element.53.refs_1_, ...), custom_call_target="tpu_custom_call" | custom-call | tf_op jit(solution)/shard_map/pallas_call | solution.py:598
  31.2 18.1 %all_to_all.26 = bf16[128,8,256]{2,1,0:T(8,128)(2,1)S(1)} all-to-all(bf16[128,8,256]{2,1,0:T(8,128)(2,1)S(1)} %bitcast.16), channel_id=1, replica_groups=mesh['pts'=64,'grp'=2] {'pts','grp'}, dimensions={0} | all-to-all | bytes 1048576 | tf_op jit(solution)/shard_map/all_to_all | solution.py:616
  49.3 0.5 shard_map.155.refs_0_.refs_5_
  49.8 0.0 copy-start.2
  49.8 1.2 collective-permute-start
  51.1 1.6 %shard_map.156 = (bf16[256,512]{1,0:T(8,128)(2,1)S(1)}, bf16[256,512]{1,0:T(8,128)(2,1)S(1)}, bf16[256,1024]{1,0:T(8,128)(2,1)S(1)}) custom-call(bf16[256,1024]{1,0:T(8,128)(2,1)S(1)} %shard_map.155.refs_0_.refs_5_, bf16[512,512]{1,0:T(8,128)(2,1)S(1)} %copy-done.1, bf16[512,1536]{1,0:T(8,128)(2,1)S(1)} %copy-done, bf16[512,512]{1,0:T(8,128)(2,1)} %refs_6_.2), custom_call_target="tpu_custom_call" | custom-call | tf_op jit(solution)/shard_map/pallas_call | solution.py:598
  52.7 4.4 %shard_map.157 = (bf16[256,1024]{1,0:T(8,128)(2,1)S(1)}, bf16[256,768]{1,0:T(8,128)(2,1)S(1)}, bf16[256,256]{1,0:T(8,128)(2,1)S(1)}, bf16[256,512]{1,0:T(8,128)(2,1)S(1)}) custom-call(bf16[256,1024]{1,0:T(8,128)(2,1)S(1)} %collective-permute-done.refs_0_.refs_6_.refs_1_, bf16[256,1024]{1,0:T(8,128)(2,1)S(1)} %get-tuple-element.58.refs_1_, ...), custom_call_target="tpu_custom_call" | custom-call | tf_op jit(solution)/shard_map/pallas_call | solution.py:598
  57.1 0.5 collective-permute-start.1
  57.6 0.4 shard_map.158.refs_1_
  58.0 0.8 shard_map.159
  58.8 0.3 collective-permute-done.1.refs_2_
  59.1 1.2 shard_map.160
  60.2 17.2 %all_to_all.27 = bf16[128,8,256]{2,1,0:T(8,128)(2,1)S(1)} all-to-all(bf16[128,8,256]{2,1,0:T(8,128)(2,1)S(1)} %bitcast.17), channel_id=1, replica_groups=mesh['pts'=64,'grp'=2] {'pts','grp'}, dimensions={0} | all-to-all | bytes 1048576 | tf_op jit(solution)/shard_map/all_to_all | solution.py:616
  77.4 1.1 collective-permute-start.2
  78.6 0.9 collective-permute-start.4
  79.5 0.2 collective-permute-start.5
  79.7 3.7 %shard_map.162 = (bf16[64,2,8,256]{3,2,1,0:T(8,128)(2,1)S(1)}, f32[256,512]{1,0:T(8,128)S(1)}, bf16[256,512]{1,0:T(8,128)(2,1)S(1)}) custom-call(bf16[1024,256]{1,0:T(8,128)(2,1)S(1)} %bitcast.15, s32[1,512]{1,0:T(1,128)S(1)} %get-tuple-element.53.refs_1_, bf16[512,256]{1,0:T(8,128)(2,1)S(1)} %get-tuple-element.75.refs_2_, ...), custom_call_target="tpu_custom_call" | custom-call | tf_op jit(solution)/shard_map/pallas_call | solution.py:598
  83.4 0.2 collective-permute-start.3
  83.6 1.0 shard_map.161
  84.6 0.4 collective-permute-done.4.refs_1_
  85.0 0.9 collective-permute-done.5.refs_2_
  85.9 0.2 shard_map.163.refs_3_
  86.1 0.2 shard_map.164
  86.2 29.0 %all_to_all.28 = bf16[128,8,768]{2,1,0:T(8,128)(2,1)S(1)} all-to-all(bf16[128,8,768]{2,1,0:T(8,128)(2,1)S(1)} %bitcast.12), channel_id=1, replica_groups=mesh['pts'=64,'grp'=2] {'pts','grp'}, dimensions={0} | all-to-all | bytes 3145728 | tf_op jit(solution)/shard_map/all_to_all | solution.py:616
  115.2 0.2 shard_map.166
  115.5 25.3 %all_to_all.29.terms = bf16[64,8,1536]{2,1,0:T(8,128)(2,1)S(1)} all-to-all(bf16[64,8,1536]{2,1,0:T(8,128)(2,1)S(1)} %shard_map.166), channel_id=1, replica_groups=mesh['pts'=64,'grp'=2] {'pts'}, dimensions={0} | all-to-all | bytes 3145728 | tf_op jit(solution)/shard_map/all_to_all | solution.py:616
  140.8 3.9 %collective-permute-start.6 = (bf16[64,8,1536]{2,1,0:T(8,128)(2,1)S(1)}, bf16[64,8,1536]{2,1,0:T(8,128)(2,1)S(1)}, u32[]{:S(2)}, u32[]{:S(2)}) collective-permute-start(bf16[64,8,1536]{2,1,0:T(8,128)(2,1)S(1)} %all_to_all.29.terms), channel_id=1, source_target_pairs={{0,1},{1,0},{2,3},{3,2},{4,5},{5,4},{6,7},{7,6},{8,9},{9,8},{10,11... | collective-permute-start | bytes 4718600 | tf_op jit(solution)/shard_map/ppermute | solution.py:612
  144.7 1.2 shard_map.165
  145.9 1.8 %shard_map.167 = (f32[512,1536]{1,0:T(8,128)}, f32[512,512]{1,0:T(8,128)}, f32[512,512]{1,0:T(8,128)}, f32[256,768]{1,0:T(8,128)}, f32[256,256]{1,0:T(8,128)}) custom-call(bf16[64,8,1536]{2,1,0:T(8,128)(2,1)S(1)} %all_to_all.29.terms), custom_call_target="tpu_custom_call" | custom-call | tf_op jit(solution)/shard_map/pallas_call | solution.py:400
  147.7 1.8 %shard_map.168 = (f32[512,1536]{1,0:T(8,128)}, f32[512,512]{1,0:T(8,128)}, f32[512,512]{1,0:T(8,128)}, f32[256,768]{1,0:T(8,128)}, f32[256,256]{1,0:T(8,128)}) custom-call(bf16[64,8,1536]{2,1,0:T(8,128)(2,1)S(1)} %collective-permute-done.6.terms, ...), custom_call_target="tpu_custom_call", output_to_operand_aliasing={{0}: (1, {}), {1}: (2, {}), {2}: (3, {}), {3}: (4, {}), {4}... | custom-call | tf_op jit(solution)/shard_map/pallas_call | solution.py:408
  (16 shorter events, 0.1 us)
Async XLA Ops:
  0.6 27.2 %copy-start.3 = (bf16[256,768]{1,0:T(8,128)(2,1)S(1)}, bf16[256,768]{1,0:T(8,128)(2,1)}, u32[]{:S(2)}) copy-start(bf16[256,768]{1,0:T(8,128)(2,1)} %refs_6_.3) | copy-start | bytes 1179652
  2.8 46.5 %copy-start.4 = (bf16[256,512]{1,0:T(8,128)(2,1)S(1)}, bf16[256,512]{1,0:T(8,128)(2,1)}, u32[]{:S(2)}) copy-start(bf16[256,512]{1,0:T(8,128)(2,1)} %refs_3_.9) | copy-start | bytes 786436
  27.8 23.2 %copy-start = (bf16[512,1536]{1,0:T(8,128)(2,1)S(1)}, bf16[512,1536]{1,0:T(8,128)(2,1)}, u32[]{:S(2)}) copy-start(bf16[512,1536]{1,0:T(8,128)(2,1)} %refs_5_.1) | copy-start | bytes 4718596
  27.8 23.2 %copy-start.1 = (bf16[512,512]{1,0:T(8,128)(2,1)S(1)}, bf16[512,512]{1,0:T(8,128)(2,1)}, u32[]{:S(2)}) copy-start(bf16[512,512]{1,0:T(8,128)(2,1)} %refs_4_.5) | copy-start | bytes 1572868
  49.8 2.9 %copy-start.2 = (bf16[512,512]{1,0:T(8,128)(2,1)S(1)}, bf16[512,512]{1,0:T(8,128)(2,1)}, u32[]{:S(2)}) copy-start(bf16[512,512]{1,0:T(8,128)(2,1)} %refs_6_.2) | copy-start | bytes 1572868
  49.8 2.9 %collective-permute-start = (bf16[256,1024]{1,0:T(8,128)(2,1)S(1)}, bf16[256,1024]{1,0:T(8,128)(2,1)S(1)}, u32[]{:S(2)}, u32[]{:S(2)}) collective-permute-start(bf16[256,1024]{1,0:T(8,128)(2,1)S(1)} %shard_map.155.refs_0_.refs_5_), channel_id=1, source_target_pairs={{0,1},{1,0},{2,3},{3,2},{4,5},{5,4},{6,7},{7,6},{8,9},{9,8},{10,11... | collective-permute-start | bytes 1572872 | tf_op jit(solution)/shard_map/ppermute | solution.py:612
  57.1 2.0 %collective-permute-start.1 = (bf16[256,768]{1,0:T(8,128)(2,1)S(1)}, bf16[256,768]{1,0:T(8,128)(2,1)S(1)}, u32[]{:S(2)}, u32[]{:S(2)}) collective-permute-start(bf16[256,768]{1,0:T(8,128)(2,1)S(1)} %get-tuple-element.60.refs_3_), channel_id=1, source_target_pairs={{0,1},{1,0},{2,3},{3,2},{4,5},{5,4},{6,7},{7,6},{8,9},{9,8},{10,11... | collective-permute-start | bytes 1179656 | tf_op jit(solution)/shard_map/ppermute | solution.py:612
  59.1 20.6 %copy-start.5 = (bf16[256,256]{1,0:T(8,128)(2,1)S(1)}, bf16[256,256]{1,0:T(8,128)(2,1)}, u32[]{:S(2)}) copy-start(bf16[256,256]{1,0:T(8,128)(2,1)} %refs_7_.1) | copy-start | bytes 393220
  77.4 6.1 %collective-permute-start.2 = (bf16[256,768]{1,0:T(8,128)(2,1)S(1)}, bf16[256,768]{1,0:T(8,128)(2,1)S(1)}, u32[]{:S(2)}, u32[]{:S(2)}) collective-permute-start(bf16[256,768]{1,0:T(8,128)(2,1)S(1)} %get-tuple-element.72.refs_2_), channel_id=1, source_target_pairs={{0,1},{1,0},{2,3},{3,2},{4,5},{5,4},{6,7},{7,6},{8,9},{9,8},{10,11... | collective-permute-start | bytes 1179656 | tf_op jit(solution)/shard_map/ppermute | solution.py:612
  78.6 6.4 %collective-permute-start.4 = (bf16[64,2,8,128]{3,2,1,0:T(8,128)(2,1)S(1)}, bf16[64,2,8,128]{3,2,1,0:T(8,128)(2,1)S(1)}, u32[]{:S(2)}, u32[]{:S(2)}) collective-permute-start(bf16[64,2,8,128]{3,2,1,0:T(8,128)(2,1)S(1)} %get-tuple-element.83), channel_id=1, source_target_pairs={{0,32},{1,97},{2,34},{3,99},{4,36},{5,101},{6,38},{7,103},{8,40},{... | collective-permute-start | bytes 786440 | tf_op jit(solution)/shard_map/ppermute | solution.py:742
  79.5 6.4 %collective-permute-start.5 = (bf16[64,2,8,128]{3,2,1,0:T(8,128)(2,1)S(1)}, bf16[64,2,8,128]{3,2,1,0:T(8,128)(2,1)S(1)}, u32[]{:S(2)}, u32[]{:S(2)}) collective-permute-start(bf16[64,2,8,128]{3,2,1,0:T(8,128)(2,1)S(1)} %get-tuple-element.84), channel_id=1, source_target_pairs={{0,8},{1,25},{2,10},{3,27},{4,12},{5,29},{6,14},{7,31},{8,0},{9,17... | collective-permute-start | bytes 786440 | tf_op jit(solution)/shard_map/ppermute | solution.py:743
  83.4 2.7 %collective-permute-start.3 = (bf16[256,512]{1,0:T(8,128)(2,1)S(1)}, bf16[256,512]{1,0:T(8,128)(2,1)S(1)}, u32[]{:S(2)}, u32[]{:S(2)}) collective-permute-start(bf16[256,512]{1,0:T(8,128)(2,1)S(1)} %get-tuple-element.81), channel_id=1, source_target_pairs={{0,1},{1,0},{2,3},{3,2},{4,5},{5,4},{6,7},{7,6},{8,9},{9,8},{10,11... | collective-permute-start | bytes 786440 | tf_op jit(solution)/shard_map/ppermute | solution.py:612
  140.8 6.9 %collective-permute-start.6 = (bf16[64,8,1536]{2,1,0:T(8,128)(2,1)S(1)}, bf16[64,8,1536]{2,1,0:T(8,128)(2,1)S(1)}, u32[]{:S(2)}, u32[]{:S(2)}) collective-permute-start(bf16[64,8,1536]{2,1,0:T(8,128)(2,1)S(1)} %all_to_all.29.terms), channel_id=1, source_target_pairs={{0,1},{1,0},{2,3},{3,2},{4,5},{5,4},{6,7},{7,6},{8,9},{9,8},{10,11... | collective-permute-start | bytes 4718600 | tf_op jit(solution)/shard_map/ppermute | solution.py:612
